TPU v7x, 32 devices: a whole 2x2x4 slice. The times are simulated.
32 devices in a mesh: dp: 8 (over y, x, core), bucket: 4 (over z).
Axes of the slice: x: 2, y: 2, z: 4, core: 2. Of those that a mesh axis runs over, the one named last changes fastest.
Arguments:
- feats: float32 [65536, 400], P(('dp', 'bucket'))
- labels: int32 [65536], P(('dp', 'bucket')), may hold values from 0 to 46
- valid: int32 [65536], P(('dp', 'bucket')), may hold values from 0 to 1, as said below
- branch_w: float32 [4, 100, 512], replicated, may hold values from -0.625 to 0.625
- branch_gain: float32 [4, 512], replicated, may hold values from 0.5 to 1.5
- branch_shift: float32 [4, 512], replicated, may hold values from -3 to 3
- branch_slope: float32 [4, 512], replicated, may hold values from 0.05 to 0.5
- mix_slope: float32 [2048], replicated, may hold values from 0.05 to 0.5
- mix_w: float32 [2048, 512], replicated, may hold values from -0.125 to 0.125
- mix_gain: float32 [512], replicated, may hold values from 0.5 to 1.5
- mix_shift: float32 [512], replicated, may hold values from -3 to 3
- out_slope: float32 [512], replicated, may hold values from 0.05 to 0.5
- head_w: float32 [512, 47], replicated, may hold values from -0.25 to 0.25
- head_bias: float32 [47], replicated, may hold values from -3 to 3
Outputs:
- loss: float32 [], replicated
- feats_grad: float32 [65536, 400], P(('dp', 'bucket'))
- branch_w_grad: float32 [4, 100, 512], replicated
- branch_gain_grad: float32 [4, 512], replicated
- branch_shift_grad: float32 [4, 512], replicated
- branch_slope_grad: float32 [4, 512], replicated
- mix_slope_grad: float32 [2048], replicated
- mix_w_grad: float32 [2048, 512], replicated
- mix_gain_grad: float32 [512], replicated
- mix_shift_grad: float32 [512], replicated
- out_slope_grad: float32 [512], replicated
- head_w_grad: float32 [512, 47], replicated
- head_bias_grad: float32 [47], replicated
Inputs may be any that keep to these rules, and one draw needn't show every extreme that they name: `valid`: within each device's 2048 node slots the training nodes form one leading block; its length varies between devices (two may be equal), and some device's block fills all 2048 slots.
All inputs are finite; a program needn't handle non-finite values.
Results may differ from a plain program's by a relative error of at most 0.0003.
Values sent between devices are 32-bit elements; how exact they have to be, the bound alone decides.
No kernel may reach another device: no remote copies, remote signals or barrier semaphores. Data moves between devices by JAX's collectives and lax.ppermute only.
A program may use at most 192 MiB of HBM per device.

v0:
```python
import jax
import jax.numpy as jnp
from jax import lax
from jax.sharding import PartitionSpec as P

HIGH = lax.Precision.HIGHEST
EPS = 1e-05


def matmul(a, b):
    return jnp.dot(a, b, precision=HIGH, preferred_element_type=jnp.float32)


def smooth_act(y, slope):
    return slope * y + (1.0 - slope) * jax.nn.softplus(y)


def smooth_back(y, slope, grad):
    d_input = grad * (slope + (1.0 - slope) * jax.nn.sigmoid(y))
    d_slope = jnp.sum(grad * (y - jax.nn.softplus(y)), axis=0)
    return (d_input, d_slope)


def per_device(
    feats,
    labels,
    valid,
    branch_w,
    branch_gain,
    branch_shift,
    branch_slope,
    mix_slope,
    mix_w,
    mix_gain,
    mix_shift,
    out_slope,
    head_w,
    head_bias,
):
    rows = feats.shape[0]
    width = feats.shape[1]
    hops = branch_w.shape[0]
    in_w = branch_w.shape[1]
    hidden = branch_w.shape[2]
    classes = head_w.shape[1]
    local_x, local_lab, local_ok = (feats, labels, valid)
    mask = local_ok.astype(jnp.float32)[:, None]
    x_hops = local_x.reshape(rows, hops, in_w)
    z = jnp.einsum(
        "mhi,hio->mho", x_hops, branch_w, precision=HIGH, preferred_element_type=jnp.float32
    )
    mask3 = mask[:, :, None]
    sum_one, sum_two, count = lax.psum(
        (jnp.sum(mask3 * z, axis=0), jnp.sum(mask3 * z * z, axis=0), jnp.sum(mask)),
        ("dp", "bucket"),
    )
    mean = sum_one / count
    rstd = lax.rsqrt(sum_two / count - mean * mean + EPS)
    z_norm = (z - mean) * rstd
    y = branch_gain * z_norm + branch_shift
    joined = smooth_act(y, branch_slope).reshape(rows, hops * hidden)
    mixed_in = smooth_act(joined, mix_slope)
    mixed = matmul(mixed_in, mix_w)
    mix_one, mix_two = lax.psum(
        (jnp.sum(mask * mixed, axis=0), jnp.sum(mask * mixed * mixed, axis=0)), ("dp", "bucket")
    )
    mix_mean = mix_one / count
    mix_rstd = lax.rsqrt(mix_two / count - mix_mean * mix_mean + EPS)
    mix_norm = (mixed - mix_mean) * mix_rstd
    y2 = mix_gain * mix_norm + mix_shift
    final = smooth_act(y2, out_slope)
    logits = matmul(final, head_w) + head_bias
    total = jax.nn.logsumexp(logits, axis=1)
    hit = (local_lab[:, None] == jnp.arange(classes, dtype=jnp.int32)[None, :]).astype(jnp.float32)
    picked = jnp.sum(logits * hit, axis=1)
    loss_part = jnp.sum(mask[:, 0] * (total - picked))
    d_logits = mask * (jnp.exp(logits - total[:, None]) - hit) / count
    head_w_part = matmul(final.T, d_logits)
    head_bias_part = jnp.sum(d_logits, axis=0)
    d_final = matmul(d_logits, head_w.T)
    d_y2, out_slope_part = smooth_back(y2, out_slope, d_final)
    mix_gain_grad, mix_shift_grad = lax.psum(
        (jnp.sum(d_y2 * mix_norm, axis=0), jnp.sum(d_y2, axis=0)), ("dp", "bucket")
    )
    d_norm2 = d_y2 * mix_gain
    d_mixed = mix_rstd * (
        d_norm2 - mask * (mix_gain * mix_shift_grad + mix_norm * mix_gain * mix_gain_grad) / count
    )
    d_mixed_in = matmul(d_mixed, mix_w.T)
    mix_w_part = matmul(mixed_in.T, d_mixed)
    d_joined, mix_slope_part = smooth_back(joined, mix_slope, d_mixed_in)
    d_y, branch_slope_part = smooth_back(y, branch_slope, d_joined.reshape(rows, hops, hidden))
    branch_gain_grad, branch_shift_grad = lax.psum(
        (jnp.sum(d_y * z_norm, axis=0), jnp.sum(d_y, axis=0)), ("dp", "bucket")
    )
    d_norm = d_y * branch_gain
    d_z = rstd * (
        d_norm
        - mask3
        * (branch_gain * branch_shift_grad + z_norm * branch_gain * branch_gain_grad)
        / count
    )
    d_x = jnp.einsum(
        "mho,hio->mhi", d_z, branch_w, precision=HIGH, preferred_element_type=jnp.float32
    ).reshape(rows, width)
    branch_w_part = jnp.einsum(
        "mhi,mho->hio", x_hops, d_z, precision=HIGH, preferred_element_type=jnp.float32
    )
    (
        loss_sum,
        branch_w_grad,
        mix_w_grad,
        branch_slope_grad,
        mix_slope_grad,
        head_w_grad,
        head_bias_grad,
        out_slope_grad,
    ) = lax.psum(
        (
            loss_part,
            branch_w_part,
            mix_w_part,
            branch_slope_part,
            mix_slope_part,
            head_w_part,
            head_bias_part,
            out_slope_part,
        ),
        ("dp", "bucket"),
    )
    loss = loss_sum / count
    return (
        loss,
        d_x,
        branch_w_grad,
        branch_gain_grad,
        branch_shift_grad,
        branch_slope_grad,
        mix_slope_grad,
        mix_w_grad,
        mix_gain_grad,
        mix_shift_grad,
        out_slope_grad,
        head_w_grad,
        head_bias_grad,
    )


def solution(mesh):
    in_specs = (
        P(("dp", "bucket"), None),
        P(("dp", "bucket")),
        P(("dp", "bucket")),
        P(),
        P(),
        P(),
        P(),
        P(),
        P(),
        P(),
        P(),
        P(),
        P(),
        P(),
    )
    out_specs = (
        P(),
        P(("dp", "bucket"), None),
        P(),
        P(),
        P(),
        P(),
        P(),
        P(),
        P(),
        P(),
        P(),
        P(),
        P(),
    )
    return jax.shard_map(
        per_device, mesh=mesh, in_specs=in_specs, out_specs=out_specs, check_vma=False
    )
```

profile of v0, /device:TPU:0, one launch (start us, length us, event | category | flops | bytes accessed | tf_op | source)
XLA Modules:
  0.0 660.5 jit_solution(7913612612918637448)
XLA Ops:
  7.2 0.0 copy-start
  7.2 0.0 all-reduce.7.cloned.1.call-start
  7.2 1.3 convert_reduce_fusion
  8.5 0.7 convert_element_type.6
  9.2 1.3 broadcast_subtract_fusion.2
  10.5 1.3 broadcast_subtract_fusion
  11.8 2.1 reshape.71
  13.9 20.5 %multiply_reduce_fusion = (f32[4,512]{1,0:T(4,128)S(1)}, f32[4,512]{1,0:T(4,128)S(1)}, f32[4,512,2048]{2,1,0:T(8,128)}) fusion(f32[2048]{0:T(1024)S(1)} %convert_element_type.6, f32[2048,4,100]{0,2,1:T(8,128)S(1)} %reshape.71, f32[4,100,512]{2,0,1:T(4,128)} %param.17), kind=kOutput, calls=%fused_computation.3 | convolution fusion | flops 5049937920 | bytes 20897792 | tf_op jit(solution)/shard_map/mhi,hio->mho/dot_general | solution.py:49
  34.5 42.4 %all-reduce.3 = (f32[4,512]{1,0:T(4,128)}, f32[]{:T(128)}, f32[4,512]{1,0:T(4,128)}) all-reduce(f32[4,512]{1,0:T(4,128)S(1)} %get-tuple-element.42, f32[]{:T(128)} %convert_reduce_fusion, f32[4,512]{1,0:T(4,128)S(1)} %get-tuple-element.41), channel_id=1, replica_groups=mesh['dp'=8,'bucket'=4] {'dp','bucket'}, use_global_device_ids=true, to_apply=%region_5.0 | all-reduce | flops 4097 | bytes 32776 | tf_op jit(solution)/shard_map/psum | solution.py:53
  76.9 1.4 broadcast_divide_fusion
  78.3 0.0 copy-start.15
  78.3 0.0 copy-start.17
  78.3 17.5 %multiply_add_fusion = f32[2048,4,512]{0,2,1:T(8,128)S(1)} fusion(f32[4,512,2048]{2,1,0:T(8,128)} %get-tuple-element.74, f32[4,512]{1,0:T(4,128)S(1)} %get-tuple-element.80, f32[4,512]{1,0:T(4,128)} %param.19, f32[4,512]{1,0:T(4,128)S(1)} %get-tuple-element.71, f32[4,512]{1,0:T(4,128)S(1)} %get-tuple-element.70, f32[4,512]{1,0:T(4,128)S(1)} %copy-done.8, ...), kind=kLoop, calls=%fused_computation.30 | loop fusion | flops 54525952 | bytes 33603584 | tf_op jit(solution)/shard_map/add | solution.py:15
  95.8 5.7 copy-done.2
  101.5 12.5 %fusion.1 = f32[2048,2048]{0,1:T(8,128)S(1)} fusion(f32[2048,4,512]{0,2,1:T(8,128)S(1)} %multiply_add_fusion, f32[2048]{0:T(1024)S(1)} %copy-done.17, f32[2048]{0:T(1024)S(1)} %copy-done.15), kind=kLoop, calls=%fused_computation.10 | loop fusion | flops 37748736 | bytes 33570816 | tf_op jit(solution)/shard_map/add | solution.py:15
  114.0 58.3 %multiply_reduce_fusion.3 = (f32[512]{0:T(512)}, f32[512]{0:T(512)}, f32[2048,512]{1,0:T(8,128)}) fusion(f32[2048]{0:T(1024)S(1)} %convert_element_type.6, f32[2048,2048]{0,1:T(8,128)S(1)} %fusion.1, f32[2048,512]{1,0:T(8,128)} %param.22), kind=kOutput, calls=%fused_computation.34 | convolution fusion | flops 25773998080 | bytes 25178112 | tf_op jit(solution)/shard_map/dot_general | solution.py:11
  172.3 40.9 %all-reduce.2 = (f32[512]{0:T(512)}, f32[512]{0:T(512)}) all-reduce(f32[512]{0:T(512)} %get-tuple-element.48, f32[512]{0:T(512)} %get-tuple-element.47), channel_id=1, replica_groups=mesh['dp'=8,'bucket'=4] {'dp','bucket'}, use_global_device_ids=true, to_apply=%region_9.10 | all-reduce | flops 1024 | bytes 8192 | tf_op jit(solution)/shard_map/psum | solution.py:64
  213.1 1.4 broadcast_divide_fusion.1
  214.5 0.0 copy-start.21
  214.5 0.0 copy-start.5
  214.5 0.0 copy-start.30
  214.5 0.0 copy-start.36
  214.6 9.0 %fusion.29 = (f32[2048]{0:T(1024)S(1)}, f32[2048,47]{0,1:T(8,128)S(1)}) fusion(f32[47]{0:T(128)} %param.27, f32[512,47]{0,1:T(8,128)S(1)} %copy-done, f32[2048,512]{1,0:T(8,128)} %get-tuple-element.75, f32[512]{0:T(512)} %broadcast_subtract_fusion.2, f32[512]{0:T(512)} %param.24, f32[512]{0:T(512)S(1)} %get-tuple-element.73, f32[512]{0:T(512)S(1)} %get-tuple-element.72, ...), kind=kOutput, calls=%fused_computation.74 | convolution fusion | flops 605218816 | bytes 4696252 | tf_op jit(solution)/shard_map/dot_general | solution.py:11
  223.6 0.1 exponential_reduce_fusion
  223.7 0.0 copy-start.12
  223.7 1.5 fusion.23
  225.3 7.2 %fusion.20 = f32[512,47]{0,1:T(8,128)} fusion(f32[2048,512]{1,0:T(8,128)S(1)} %copy-done.5, f32[512]{0:T(512)S(1)} %copy-done.30, f32[512]{0:T(512)S(1)} %copy-done.36, f32[512]{0:T(512)S(1)} %get-tuple-element.73, f32[512]{0:T(512)S(1)} %get-tuple-element.72, f32[512]{0:T(512)S(1)} %copy-done.22, f32[512]{0:T(512)S(1)} %copy-done.28, ...), kind=kOutput, calls=%fused_computation.49 | convolution fusion | flops 605605888 | bytes 4712452 | tf_op jit(solution)/shard_map/dot_general | solution.py:11
  232.5 10.6 %fusion.27 = (f32[512]{0:T(512)}, f32[512]{0:T(512)}, f32[512]{0:T(512)}, f32[2048,512]{1,0:T(8,128)}) fusion(f32[512]{0:T(512)S(1)} %copy-done.36, f32[512]{0:T(512)S(1)} %get-tuple-element.73, f32[2048,512]{1,0:T(8,128)S(1)} %copy-done.5, f32[512]{0:T(512)S(1)} %get-tuple-element.72, f32[512]{0:T(512)S(1)} %copy-done.22, f32[512]{0:T(512)S(1)} %copy-done.30, ...), kind=kOutput, calls=%fused_computation.73 | convolution fusion | flops 615041536 | bytes 8912900 | tf_op jit(solution)/shard_map/dot_general | solution.py:11
  243.1 40.7 %all-reduce.1 = (f32[512]{0:T(512)S(1)}, f32[512]{0:T(512)S(1)}) all-reduce(f32[512]{0:T(512)} %get-tuple-element.45, f32[512]{0:T(512)} %get-tuple-element.44), channel_id=1, replica_groups=mesh['dp'=8,'bucket'=4] {'dp','bucket'}, use_global_device_ids=true, to_apply=%region_18.19 | all-reduce | flops 1024 | bytes 8192 | tf_op jit(solution)/shard_map/psum | solution.py:82
  283.8 0.7 mul.273
  284.6 0.0 copy-start.37
  284.6 37.8 %fusion.25 = f32[2048,512]{1,0:T(8,128)} fusion(f32[2048,2048]{0,1:T(8,128)} %copy-done.4, f32[2048,512]{1,0:T(8,128)} %get-tuple-element.75, f32[]{:T(128)} %get-tuple-element.63, f32[512]{0:T(512)S(1)} %get-tuple-element.89, f32[512]{0:T(512)S(1)} %mul.273, f32[512]{0:T(512)} %copy-done.26, f32[512]{0:T(512)} %copy-done.24, ...), kind=kOutput, calls=%fused_computation.71 | convolution fusion | flops 25787629568 | bytes 29384708 | tf_op jit(solution)/shard_map/dot_general | solution.py:11
  322.5 4.5 subtract_multiply_fusion.4.clone.4
  327.0 0.6 multiply_reduce_fusion.6
  327.6 45.8 %add_multiply_fusion = (f32[2048,4,512]{0,2,1:T(8,128)}, f32[2048,2048]{0,1:T(8,128)}, f32[2048,2048]{0,1:T(8,128)}) fusion(f32[4,512,2048]{2,1,0:T(8,128)} %get-tuple-element.74, f32[4,512]{1,0:T(4,128)S(1)} %get-tuple-element.80, f32[4,512]{1,0:T(4,128)S(1)} %copy-done.14, f32[4,512]{1,0:T(4,128)S(1)} %get-tuple-element.71, ...), kind=kOutput, calls=%fused_computation.29 | convolution fusion | flops 25836912640 | bytes 92340224 | tf_op jit(solution)/shard_map/dot_general | solution.py:11
  373.5 16.0 %fusion.3 = f32[2048]{0:T(1024)S(1)} fusion(f32[2048,2048]{0,1:T(8,128)} %get-tuple-element.79, f32[2048,4,512]{0,2,1:T(8,128)} %copy-done.2), kind=kLoop, calls=%fused_computation.12 | loop fusion | flops 37746688 | bytes 33562624 | tf_op jit(solution)/shard_map/reduce_sum | solution.py:20
  389.6 18.9 %multiply_reduce_fusion.1 = (f32[4,512]{1,0:T(4,128)S(1)}, f32[4,512]{1,0:T(4,128)S(1)}, f32[4,512]{1,0:T(4,128)S(1)}) fusion(f32[2048,4,512]{0,2,1:T(8,128)} %bitcast.86, f32[4,512,2048]{2,1,0:T(8,128)S(1)} %bitcast.85, f32[4,512]{1,0:T(4,128)S(1)} %copy-done.14, f32[4,512]{1,0:T(4,128)S(1)} %get-tuple-element.71, f32[4,512]{1,0:T(4,128)S(1)} %get-tuple-element.70, ...), kind=kLoop, calls=%fused_computation.26 | loop fusion | flops 67102720 | bytes 50388992 | tf_op jit(solution)/shard_map/reduce_sum | solution.py:20
  408.5 41.4 %all-reduce = (f32[]{:T(128)}, f32[4,512]{1,0:T(4,128)S(1)}, f32[4,512]{1,0:T(4,128)S(1)}, f32[4,512]{1,0:T(4,128)}, f32[2048]{0:T(1024)}, /*index=5*/f32[512]{0:T(512)}, f32[47]{0:T(128)}) all-reduce(f32[]{:T(128)} %multiply_reduce_fusion.6, ...), channel_id=1, replica_groups=mesh['dp'=8,'bucket'=4] {'dp','bucket'}, use_global_device_ids=true, to_apply=%region_14.15 | all-reduce | flops 8752 | bytes 70016 | tf_op jit(solution)/shard_map/psum | solution.py:118
  449.9 23.0 %subtract_multiply_fusion = f32[2048,4,512]{0,2,1:T(8,128)S(1)} fusion(f32[2048,4,512]{0,2,1:T(8,128)} %get-tuple-element.68, f32[4,512,2048]{2,1,0:T(8,128)} %get-tuple-element.74, f32[]{:T(128)} %get-tuple-element.63, f32[4,512]{1,0:T(4,128)S(1)} %get-tuple-element.84, f32[4,512]{1,0:T(4,128)S(1)} %mul.284, f32[4,512]{1,0:T(4,128)S(1)} %get-tuple-element.71, ...), kind=kLoop, calls=%fused_computation.27 | loop fusion | flops 41943040 | bytes 50380804 | tf_op jit(solution)/shard_map/mul | solution.py:97
  472.9 5.7 copy-done.3
  478.7 17.5 %convolution_bitcast_fusion.1 = f32[4,100,512]{2,1,0:T(8,128)} fusion(f32[2048,4,512]{0,2,1:T(8,128)S(1)} %subtract_multiply_fusion, f32[2048,4,100]{0,2,1:T(8,128)S(1)} %reshape.71), kind=kOutput, calls=%fused_computation.45 | convolution fusion | flops 5033164800 | bytes 20873216 | tf_op jit(solution)/shard_map/mhi,mho->hio/dot_general | solution.py:106
  496.1 0.0 all-reduce.7.cloned.1.call-update
  497.5 13.7 %convolution_bitcast_fusion = f32[2048,4,100]{0,2,1:T(8,128)S(1)} fusion(f32[2048,4,512]{0,2,1:T(8,128)} %copy-done.3, f32[4,100,512]{2,0,1:T(4,128)} %param.17), kind=kOutput, calls=%fused_computation.43 | convolution fusion | flops 5033164800 | bytes 20873216 | tf_op jit(solution)/shard_map/mho,hio->mhi/dot_general | solution.py:103
  511.2 1.9 reshape.74
  513.1 131.0 %all-reduce.7.cloned.1.call-done = (f32[4,100,512]{2,1,0:T(8,128)}, f32[2048,512]{1,0:T(8,128)}, f32[512,47]{0,1:T(8,128)}) async-done(((f32[4,100,512]{2,1,0:T(8,128)}, f32[2048,512]{1,0:T(8,128)}, f32[512,47]{0,1:T(8,128)}), (f32[4,100,512]{2,1,0:T(8,128)}, f32[2048,512]{1,0:T(8,128)}, f32[512,47]{0,1:T(8,128)})) %all-reduce.7.cloned.1.call-update) | async-done | bytes 5109776 | tf_op jit(solution)/shard_map/psum | solution.py:118
  644.1 2.6 copy.36
  646.7 4.7 copy.48
  651.4 0.6 copy.49
  (79 shorter events, 0.2 us)
Async XLA Ops:
  7.2 207.3 %copy-start = (f32[512,47]{0,1:T(8,128)S(1)}, f32[512,47]{0,1:T(8,128)}, u32[]{:S(2)}) copy-start(f32[512,47]{0,1:T(8,128)} %param.26) | copy-start | bytes 288772
  7.2 636.9 %all-reduce.7.cloned.1.call-start = ((), (), s32[]{:S(2)}) async-start(), calls=%async_computation | async-start | bytes 10289152 | tf_op jit(solution)/shard_map/psum | solution.py:118
  13.9 63.0 %copy-start.10 = (f32[4,512]{1,0:T(4,128)S(1)}, f32[4,512]{1,0:T(4,128)}, u32[]{:S(2)}) copy-start(f32[4,512]{1,0:T(4,128)} %param.20) | copy-start | bytes 24580
  13.9 64.4 %copy-start.8 = (f32[4,512]{1,0:T(4,128)S(1)}, f32[4,512]{1,0:T(4,128)}, u32[]{:S(2)}) copy-start(f32[4,512]{1,0:T(4,128)} %param.18) | copy-start | bytes 24580
  78.3 23.2 %copy-start.15 = (f32[2048]{0:T(1024)S(1)}, f32[2048]{0:T(1024)}, u32[]{:S(2)}) copy-start(f32[2048]{0:T(1024)} %param.21) | copy-start | bytes 24580
  78.3 23.2 %copy-start.17 = (f32[2048]{0:T(1024)S(1)}, f32[2048]{0:T(1024)}, u32[]{:S(2)}) copy-start(f32[2048]{0:T(1024)} %broadcast_subtract_fusion) | copy-start | bytes 24580
  95.8 5.7 copy-start.2
  114.0 58.3 %copy-start.4 = (f32[2048,2048]{0,1:T(8,128)}, f32[2048,2048]{0,1:T(8,128)S(1)}, u32[]{:S(2)}) copy-start(f32[2048,2048]{0,1:T(8,128)S(1)} %fusion.1) | copy-start | bytes 50331652
  214.5 18.0 %copy-start.24 = (f32[512]{0:T(512)}, f32[512]{0:T(512)S(1)}, u32[]{:S(2)}) copy-start(f32[512]{0:T(512)S(1)} %get-tuple-element.72) | copy-start | bytes 6148
  214.5 18.0 %copy-start.26 = (f32[512]{0:T(512)}, f32[512]{0:T(512)S(1)}, u32[]{:S(2)}) copy-start(f32[512]{0:T(512)S(1)} %get-tuple-element.73) | copy-start | bytes 6148
  214.5 9.2 %copy-start.21 = (s32[2048]{0:T(1024)S(1)}, s32[2048]{0:T(1024)}, u32[]{:S(2)}) copy-start(s32[2048]{0:T(1024)} %param.15) | copy-start | bytes 24580
  214.5 10.8 %copy-start.5 = (f32[2048,512]{1,0:T(8,128)S(1)}, f32[2048,512]{1,0:T(8,128)}, u32[]{:S(2)}) copy-start(f32[2048,512]{1,0:T(8,128)} %get-tuple-element.75) | copy-start | bytes 12582916
  214.5 10.7 %copy-start.22 = (f32[512]{0:T(512)S(1)}, f32[512]{0:T(512)}, u32[]{:S(2)}) copy-start(f32[512]{0:T(512)} %param.23) | copy-start | bytes 6148
  214.5 10.7 %copy-start.28 = (f32[512]{0:T(512)S(1)}, f32[512]{0:T(512)}, u32[]{:S(2)}) copy-start(f32[512]{0:T(512)} %param.25) | copy-start | bytes 6148
  214.5 10.7 %copy-start.30 = (f32[512]{0:T(512)S(1)}, f32[512]{0:T(512)}, u32[]{:S(2)}) copy-start(f32[512]{0:T(512)} %broadcast_subtract_fusion.2) | copy-start | bytes 6148
  214.5 10.7 %copy-start.36 = (f32[512]{0:T(512)S(1)}, f32[512]{0:T(512)}, u32[]{:S(2)}) copy-start(f32[512]{0:T(512)} %param.24) | copy-start | bytes 6148
  223.7 8.8 %copy-start.12 = (f32[2048]{0:T(1024)}, f32[2048]{0:T(1024)S(1)}, u32[]{:S(2)}) copy-start(f32[2048]{0:T(1024)S(1)} %log_add_fusion) | copy-start | bytes 24580
  283.8 0.7 copy-start.34
  283.8 38.5 %copy-start.38 = (f32[512]{0:T(512)}, f32[512]{0:T(512)S(1)}, u32[]{:S(2)}) copy-start(f32[512]{0:T(512)S(1)} %get-tuple-element.89) | copy-start | bytes 6148
  284.5 37.8 %copy-start.6 = (f32[2048,512]{1,0:T(8,128)S(1)}, f32[2048,512]{1,0:T(8,128)}, u32[]{:S(2)}) copy-start(f32[2048,512]{1,0:T(8,128)} %get-tuple-element.75) | copy-start | bytes 12582916
  284.5 37.9 %copy-start.7 = (f32[2048,512]{1,0:T(8,128)S(1)}, f32[2048,512]{1,0:T(8,128)}, u32[]{:S(2)}) copy-start(f32[2048,512]{1,0:T(8,128)} %get-tuple-element.78) | copy-start | bytes 12582916
  284.5 37.9 %copy-start.23 = (f32[512]{0:T(512)S(1)}, f32[512]{0:T(512)}, u32[]{:S(2)}) copy-start(f32[512]{0:T(512)} %param.23) | copy-start | bytes 6148
  284.5 37.9 %copy-start.25 = (f32[512]{0:T(512)S(1)}, f32[512]{0:T(512)}, u32[]{:S(2)}) copy-start(f32[512]{0:T(512)} %copy-done.24) | copy-start | bytes 6148
  284.5 37.9 %copy-start.27 = (f32[512]{0:T(512)S(1)}, f32[512]{0:T(512)}, u32[]{:S(2)}) copy-start(f32[512]{0:T(512)} %copy-done.26) | copy-start | bytes 6148
  284.5 37.9 %copy-start.29 = (f32[512]{0:T(512)S(1)}, f32[512]{0:T(512)}, u32[]{:S(2)}) copy-start(f32[512]{0:T(512)} %param.25) | copy-start | bytes 6148
  284.5 37.9 %copy-start.31 = (f32[512]{0:T(512)S(1)}, f32[512]{0:T(512)}, u32[]{:S(2)}) copy-start(f32[512]{0:T(512)} %broadcast_subtract_fusion.2) | copy-start | bytes 6148
  284.6 37.8 %copy-start.37 = (f32[512]{0:T(512)S(1)}, f32[512]{0:T(512)}, u32[]{:S(2)}) copy-start(f32[512]{0:T(512)} %param.24) | copy-start | bytes 6148
  322.4 4.6 copy-start.11
  322.4 4.6 copy-start.13
  322.4 4.6 copy-start.19
  322.4 5.2 copy-start.14
  322.5 5.2 copy-start.16
  322.5 5.2 copy-start.18
  373.5 16.0 %slice-start = ((s8[16777216]{0:T(1024)(128)(4,1)}), s8[4194304]{0:T(1024)(128)(4,1)S(1)}, s32[]{:S(2)}) async-start(s8[16777216]{0:T(1024)(128)(4,1)} %bitcast.84), calls=%async_computation.1 | async-start | bytes 8388608
  373.5 16.0 %slice-start.1 = ((s8[16777216]{0:T(1024)(128)(4,1)}), s8[4194304]{0:T(1024)(128)(4,1)S(1)}, s32[]{:S(2)}) async-start(s8[16777216]{0:T(1024)(128)(4,1)} %bitcast.84), calls=%async_computation.2 | async-start | bytes 8388608
  373.5 16.0 %slice-start.2 = ((s8[16777216]{0:T(1024)(128)(4,1)}), s8[4194304]{0:T(1024)(128)(4,1)S(1)}, s32[]{:S(2)}) async-start(s8[16777216]{0:T(1024)(128)(4,1)} %bitcast.84), calls=%async_computation.3 | async-start | bytes 8388608
  373.5 16.0 %slice-start.3 = ((s8[16777216]{0:T(1024)(128)(4,1)}), s8[4194304]{0:T(1024)(128)(4,1)S(1)}, s32[]{:S(2)}) async-start(s8[16777216]{0:T(1024)(128)(4,1)} %bitcast.84), calls=%async_computation.4 | async-start | bytes 8388608
  389.5 19.0 %copy-start.33 = (f32[47]{0:T(128)S(1)}, f32[47]{0:T(128)}, u32[]{:S(2)}) copy-start(f32[47]{0:T(128)} %get-tuple-element.49) | copy-start | bytes 568
  389.5 19.0 %copy-start.35 = (f32[512]{0:T(512)S(1)}, f32[512]{0:T(512)}, u32[]{:S(2)}) copy-start(f32[512]{0:T(512)} %get-tuple-element.46) | copy-start | bytes 6148
  449.9 23.1 %copy-start.20 = (f32[4,512]{1,0:T(4,128)}, f32[4,512]{1,0:T(4,128)S(1)}, u32[]{:S(2)}) copy-start(f32[4,512]{1,0:T(4,128)S(1)} %get-tuple-element.85) | copy-start | bytes 24580
  449.9 23.1 %copy-start.32 = (f32[4,512]{1,0:T(4,128)}, f32[4,512]{1,0:T(4,128)S(1)}, u32[]{:S(2)}) copy-start(f32[4,512]{1,0:T(4,128)S(1)} %get-tuple-element.84) | copy-start | bytes 24580
  472.9 5.7 copy-start.3
  646.7 5.3 copy-start.1
  646.7 4.7 copy-start.9
Sparse Core Ops, SparseCore 0:
  496.3 147.8 all-reduce.6
where the time goes:
time: 669 us; the launch traced here: 660 us
  matrix products  220 us (33%)
  blocking collectives  165 us (25%)
  waiting for transfers between devices  131 us (20%)
  other arithmetic  103 us (15%)
  local copies, waits for them, and re-layouts  23.5 us (4%)
  between operations  17.5 us (3%)
    dot_general x6, matrix products, matmul(): return jnp.dot(a, b, precision=HIGH, preferred_element_type=jnp.float32)  169 us
    psum x1, waiting for transfers between devices, per_device(): lax.psum((loss_part, branch_w_part, mix_w_part, branch_slope_part, mix_sl...  131 us
    psum x1, blocking collectives, per_device(): lax.psum((jnp.sum(mask3 * z, axis=0), jnp.sum(mask3 * z * z, axis=0), jnp...  42.4 us
    psum x1, blocking collectives, per_device(): lax.psum((loss_part, branch_w_part, mix_w_part, branch_slope_part, mix_sl...  41.4 us
    psum x1, blocking collectives, per_device(): lax.psum((jnp.sum(mask * mixed, axis=0), jnp.sum(mask * mixed * mixed, ax...  40.9 us
    psum x1, blocking collectives, per_device(): lax.psum((jnp.sum(d_y2 * mix_norm, axis=0), jnp.sum(d_y2, axis=0)), ('dp'...  40.7 us
    reduce_sum x2, other arithmetic, smooth_back(): d_slope = jnp.sum(grad * (y - jax.nn.softplus(y)), axis=0)  34.9 us
    add x2, other arithmetic, smooth_act(): return slope * y + (1.0 - slope) * jax.nn.softplus(y)  29.9 us
  transfers between devices with their start and end apart: 1, of which 1 were waited for; matrix products, arithmetic and copies ran while one was open for 2% of the time, Pallas kernels for 0%

commit v1 on v0

v1 whole, which is shorter than its diff:
```python
import functools

import jax
import jax.numpy as jnp
from jax import lax
from jax.experimental import pallas as pl
from jax.experimental.pallas import tpu as pltpu
from jax.sharding import PartitionSpec as P

EPS = 1e-05
F32 = jnp.float32
BF16 = jnp.bfloat16
LANES = 128
VMEM = 56 * 1024 * 1024
TILE = 256
NN = (((1,), (0,)), ((), ()))
NT = (((1,), (1,)), ((), ()))
TN = (((0,), (0,)), ((), ()))


def split(x):
    hi = x.astype(BF16)
    return hi, (x - hi.astype(F32)).astype(BF16)


def dot3(a, b, dims=NN):
    ah, al = a
    bh, bl = b
    dot = functools.partial(lax.dot_general, dimension_numbers=dims, preferred_element_type=F32)
    return dot(ah, bh) + (dot(ah, bl) + dot(al, bh))


def soft(y):
    return jnp.maximum(y, 0.0) + jnp.log(1.0 + jnp.exp(-jnp.abs(y)))


def windows(hops, in_w, width):
    out = []
    for h in range(hops):
        lo = h * in_w // LANES * LANES
        hi = min(-(-(h + 1) * in_w // LANES) * LANES, width)
        out.append((lo, hi))
    return out


def params(**kw):
    return pltpu.CompilerParams(vmem_limit_bytes=VMEM, **kw)


def whole(x):
    return pl.BlockSpec(x.shape, lambda *_: (0,) * len(x.shape))


def row_mask(valid_ref, step, tile):
    n = jnp.sum(valid_ref[...])
    row = step * tile + lax.broadcasted_iota(jnp.int32, (tile, 1), 0)
    return row < n


def branch_kernel(wins, valid_ref, x_ref, wh_ref, wl_ref, z_ref, st_ref):
    step = pl.program_id(0)
    tile = x_ref.shape[0]
    hid = wh_ref.shape[2]
    mask = row_mask(valid_ref, step, tile)

    @pl.when(step == 0)
    def _():
        st_ref[...] = jnp.zeros_like(st_ref)
        n = jnp.sum(valid_ref[...]).astype(F32)
        st_ref[2:3, :] = jnp.broadcast_to(n, (1, st_ref.shape[1]))

    for h, (lo, hi) in enumerate(wins):
        xs = split(x_ref[:, lo:hi])
        z = dot3(xs, (wh_ref[h, : hi - lo, :], wl_ref[h, : hi - lo, :]))
        cols = slice(h * hid, (h + 1) * hid)
        z_ref[:, cols] = z
        zm = jnp.where(mask, z, 0.0)
        st_ref[0:1, cols] += jnp.sum(zm, axis=0, keepdims=True)
        st_ref[1:2, cols] += jnp.sum(zm * zm, axis=0, keepdims=True)


def branch(valid, x, wh, wl, wins):
    rows, width = x.shape
    hops, _, hid = wh.shape
    mix = hops * hid
    return pl.pallas_call(
        functools.partial(branch_kernel, wins),
        grid=(rows // TILE,),
        in_specs=[
            whole(valid),
            pl.BlockSpec((TILE, width), lambda i: (i, 0)),
            whole(wh),
            whole(wl),
        ],
        out_specs=[
            pl.BlockSpec((TILE, mix), lambda i: (i, 0)),
            pl.BlockSpec((3, mix), lambda i: (0, 0)),
        ],
        out_shape=[
            jax.ShapeDtypeStruct((rows, mix), F32),
            jax.ShapeDtypeStruct((3, mix), F32),
        ],
        compiler_params=params(),
        name="branch",
    )(valid, x, wh, wl)


def gram_kernel(wins, valid_ref, x_ref, g_ref, xm_ref):
    step = pl.program_id(0)
    mask = row_mask(valid_ref, step, x_ref.shape[0])

    @pl.when(step == 0)
    def _():
        g_ref[...] = jnp.zeros_like(g_ref)
        xm_ref[...] = jnp.zeros_like(xm_ref)

    x = jnp.where(mask, x_ref[...], 0.0)
    xm_ref[...] += jnp.sum(x, axis=0, keepdims=True)
    xh, xl = split(x)
    for h, (lo, hi) in enumerate(wins):
        xs = xh[:, lo:hi], xl[:, lo:hi]
        g_ref[h, : hi - lo, : hi - lo] += dot3(xs, xs, TN)


def gram(valid, x, wins):
    rows, width = x.shape
    kw = max(hi - lo for lo, hi in wins)
    return pl.pallas_call(
        functools.partial(gram_kernel, wins),
        grid=(rows // TILE,),
        in_specs=[whole(valid), pl.BlockSpec((TILE, width), lambda i: (i, 0))],
        out_specs=[
            pl.BlockSpec((len(wins), kw, kw), lambda i: (0, 0, 0)),
            pl.BlockSpec((1, width), lambda i: (0, 0)),
        ],
        out_shape=[
            jax.ShapeDtypeStruct((len(wins), kw, kw), F32),
            jax.ShapeDtypeStruct((1, width), F32),
        ],
        compiler_params=params(),
        name="gram",
    )(valid, x)


def norm_of(st_ref, cols):
    count = st_ref[2:3, cols]
    mean = st_ref[0:1, cols] / count
    var = st_ref[1:2, cols] / count - mean * mean
    return mean, lax.rsqrt(var + EPS)


def forward_kernel(
    valid_ref, z_ref, st_ref, gain_ref, shift_ref, slope_ref, mslope_ref, w_ref,
    j_ref, uh_ref, ul_ref, v_ref, st2_ref, wh_ref, wl_ref,
):
    step = pl.program_id(0)
    tile = z_ref.shape[0]
    hops, hid = gain_ref.shape
    mask = row_mask(valid_ref, step, tile)

    @pl.when(step == 0)
    def _():
        st2_ref[...] = jnp.zeros_like(st2_ref)
        for h in range(hops):
            rows = slice(h * hid, (h + 1) * hid)
            wh_ref[rows, :], wl_ref[rows, :] = split(w_ref[rows, :])

    v = None
    for h in range(hops):
        cols = slice(h * hid, (h + 1) * hid)
        mean, rstd = norm_of(st_ref, cols)
        a = gain_ref[h : h + 1, :] * rstd
        b = shift_ref[h : h + 1, :] - mean * a
        s1 = slope_ref[h : h + 1, :]
        s2 = mslope_ref[h : h + 1, :]
        y = z_ref[:, cols] * a + b
        j = s1 * y + (1.0 - s1) * soft(y)
        u = s2 * j + (1.0 - s2) * soft(j)
        j_ref[:, cols] = j
        us = split(u)
        uh_ref[:, cols], ul_ref[:, cols] = us
        part = dot3(us, (wh_ref[cols, :], wl_ref[cols, :]))
        v = part if v is None else v + part
    v_ref[...] = v
    vm = jnp.where(mask, v, 0.0)
    st2_ref[0:1, :] += jnp.sum(vm, axis=0, keepdims=True)
    st2_ref[1:2, :] += jnp.sum(vm * vm, axis=0, keepdims=True)


def forward(valid, z, st, gain, shift, slope, mslope, w):
    rows, mix = z.shape
    hid = w.shape[1]
    tile = lambda n: pl.BlockSpec((TILE, n), lambda i: (i, 0))
    return pl.pallas_call(
        forward_kernel,
        grid=(rows // TILE,),
        in_specs=[whole(valid), tile(mix)] + [whole(t) for t in (st, gain, shift, slope, mslope, w)],
        out_specs=[tile(mix), tile(mix), tile(mix), tile(hid)]
        + [pl.BlockSpec(s, lambda i: (0, 0)) for s in ((2, hid), (mix, hid), (mix, hid))],
        out_shape=[
            jax.ShapeDtypeStruct((rows, mix), F32),
            jax.ShapeDtypeStruct((rows, mix), BF16),
            jax.ShapeDtypeStruct((rows, mix), BF16),
            jax.ShapeDtypeStruct((rows, hid), F32),
            jax.ShapeDtypeStruct((2, hid), F32),
            jax.ShapeDtypeStruct((mix, hid), BF16),
            jax.ShapeDtypeStruct((mix, hid), BF16),
        ],
        compiler_params=params(),
        name="forward",
    )(valid, z, st, gain, shift, slope, mslope, w)


def head_kernel(
    valid_ref, labels_ref, v_ref, st_ref, cnt_ref, gain_ref, shift_ref, slope_ref, hw_ref, hb_ref,
    dy_ref, st3_ref, misc_ref,
):
    step = pl.program_id(0)
    tile, hid = v_ref.shape
    classes = hw_ref.shape[1]
    mask = row_mask(valid_ref, step, tile)
    count = cnt_ref[2:3, 0:1]

    @pl.when(step == 0)
    def _():
        st3_ref[...] = jnp.zeros_like(st3_ref)
        misc_ref[...] = jnp.zeros_like(misc_ref)

    mean = st_ref[0:1, :] / count
    rstd = lax.rsqrt(st_ref[1:2, :] / count - mean * mean + EPS)
    s = slope_ref[...]
    zn = (v_ref[...] - mean) * rstd
    y = gain_ref[...] * zn + shift_ref[...]
    sp = soft(y)
    w = s * y + (1.0 - s) * sp
    ws = split(w)
    hw = split(hw_ref[...])
    logits = dot3(ws, hw) + hb_ref[...]
    peak = jnp.max(logits, axis=1, keepdims=True)
    ex = jnp.exp(logits - peak)
    tot = jnp.sum(ex, axis=1, keepdims=True)
    lab = labels_ref[pl.ds(step * (tile // LANES), tile // LANES), :]
    lab = jnp.concatenate(
        [jnp.broadcast_to(lab[k : k + 1, :], (LANES, LANES)).T for k in range(tile // LANES)], axis=0
    )
    hit = lab[:, :classes] == lax.broadcasted_iota(jnp.int32, (tile, classes), 1)
    picked = jnp.sum(jnp.where(hit, logits, 0.0), axis=1, keepdims=True)
    loss = jnp.sum(jnp.where(mask, peak + jnp.log(tot) - picked, 0.0))
    dl = jnp.where(mask, (ex / tot - hit.astype(F32)) / count, 0.0)
    dls = split(dl)
    misc_ref[0:classes, :] += dot3(dls, ws, TN)
    misc_ref[classes : classes + 1, 0:classes] += jnp.sum(dl, axis=0, keepdims=True)
    misc_ref[classes : classes + 1, LANES : 2 * LANES] += jnp.broadcast_to(loss, (1, LANES))
    dw = dot3(dls, hw, NT)
    dy = dw * (1.0 - (1.0 - s) * jnp.exp(-sp))
    dy_ref[...] = dy
    misc_ref[classes + 1 : classes + 2, :] += jnp.sum(dw * (y - sp), axis=0, keepdims=True)
    st3_ref[0:1, :] += jnp.sum(dy, axis=0, keepdims=True)
    st3_ref[1:2, :] += jnp.sum(dy * zn, axis=0, keepdims=True)


def head(valid, labels, v, st2, st, gain, shift, slope, hw, hb):
    rows, hid = v.shape
    tile = lambda n: pl.BlockSpec((TILE, n), lambda i: (i, 0))
    misc = -(-(hw.shape[1] + 2) // 8) * 8
    return pl.pallas_call(
        head_kernel,
        grid=(rows // TILE,),
        in_specs=[whole(valid), whole(labels), tile(hid)]
        + [whole(t) for t in (st2, st, gain, shift, slope, hw, hb)],
        out_specs=[
            tile(hid),
            pl.BlockSpec((2, hid), lambda i: (0, 0)),
            pl.BlockSpec((misc, hid), lambda i: (0, 0)),
        ],
        out_shape=[
            jax.ShapeDtypeStruct((rows, hid), F32),
            jax.ShapeDtypeStruct((2, hid), F32),
            jax.ShapeDtypeStruct((misc, hid), F32),
        ],
        compiler_params=params(),
        name="head",
    )(valid, labels, v, st2, st, gain, shift, slope, hw, hb)


def mix_kernel(
    valid_ref, dy_ref, v_ref, st2_ref, cnt_ref, st3_ref, gain_ref, uh_ref, ul_ref,
    m_ref, dvh_ref, dvl_ref,
):
    step = pl.program_id(0)
    tile = dy_ref.shape[0]
    mask = row_mask(valid_ref, step, tile)
    count = cnt_ref[2:3, 0:1]
    mean = st2_ref[0:1, :] / count
    rstd = lax.rsqrt(st2_ref[1:2, :] / count - mean * mean + EPS)
    a = gain_ref[...] * rstd
    c1 = a * st3_ref[0:1, :] / count
    c2 = a * st3_ref[1:2, :] / count
    zn = (v_ref[...] - mean) * rstd
    dv = jnp.where(mask, a * dy_ref[...] - (c1 + zn * c2), 0.0)
    dvs = split(dv)
    dvh_ref[...], dvl_ref[...] = dvs

    @pl.when(step == 0)
    def _():
        m_ref[...] = jnp.zeros_like(m_ref)

    hid = dy_ref.shape[1]
    for h in range(uh_ref.shape[1] // hid):
        cols = slice(h * hid, (h + 1) * hid)
        m_ref[cols, :] += dot3((uh_ref[:, cols], ul_ref[:, cols]), dvs, TN)


def mix_back(valid, dy, v, st2, st, st3, gain, uh, ul):
    rows, hid = dy.shape
    mix = uh.shape[1]
    tile = lambda n: pl.BlockSpec((TILE, n), lambda i: (i, 0))
    return pl.pallas_call(
        mix_kernel,
        grid=(rows // TILE,),
        in_specs=[whole(valid), tile(hid), tile(hid)]
        + [whole(t) for t in (st2, st, st3, gain)]
        + [tile(mix), tile(mix)],
        out_specs=[pl.BlockSpec((mix, hid), lambda i: (0, 0)), tile(hid), tile(hid)],
        out_shape=[
            jax.ShapeDtypeStruct((mix, hid), F32),
            jax.ShapeDtypeStruct((rows, hid), BF16),
            jax.ShapeDtypeStruct((rows, hid), BF16),
        ],
        compiler_params=params(),
        name="mix_back",
    )(valid, dy, v, st2, st, st3, gain, uh, ul)


def hop_kernel(
    h, lo, hi, st_ref, gain_ref, shift_ref, slope_ref, mslope_ref, dvh_ref, dvl_ref, mwh_ref, mwl_ref,
    z_ref, j_ref, uh_ref, ul_ref, x_ref, bwh_ref, bwl_ref,
    dx_ref, bw_ref, sums_ref,
):
    step = pl.program_id(0)

    @pl.when(step == 0)
    def _():
        bw_ref[...] = jnp.zeros_like(bw_ref)
        sums_ref[...] = jnp.zeros_like(sums_ref)

    mean, rstd = norm_of(st_ref, slice(None))
    gain = gain_ref[h : h + 1, :]
    a = gain * rstd
    b = shift_ref[h : h + 1, :] - mean * a
    s1 = slope_ref[h : h + 1, :]
    s2 = mslope_ref[h : h + 1, :]
    y = z_ref[...] * a + b
    j = j_ref[...]
    u = uh_ref[...].astype(F32) + ul_ref[...].astype(F32)
    du = dot3((dvh_ref[...], dvl_ref[...]), (mwh_ref[...], mwl_ref[...]), NT)
    r2 = 1.0 / (1.0 - s2)
    r1 = 1.0 / (1.0 - s1)
    dj = du * (1.0 - (1.0 - s2) * jnp.exp((s2 * r2) * j - r2 * u))
    dy = dj * (1.0 - (1.0 - s1) * jnp.exp((s1 * r1) * y - r1 * j))
    row = lambda t: jnp.sum(t, axis=0, keepdims=True)
    sums_ref[0:1, :] += row(dy)
    sums_ref[1:2, :] += row(dy * y)
    sums_ref[2:3, :] += row(dj * (y - j)) * r1
    sums_ref[3:4, :] += row(du * (j - u)) * r2
    dys = split(dy * a)
    wb = bwh_ref[0, : hi - lo, :], bwl_ref[0, : hi - lo, :]
    dx_ref[...] = dot3(dys, wb, NT)
    bw_ref[...] += dot3(split(x_ref[:, lo:hi]), dys, TN)


def hop_back(h, lo, hi, st, gain, shift, slope, mslope, dvh, dvl, mwh, mwl, z, j, uh, ul, x, bwh, bwl):
    rows, width = x.shape
    hid = dvh.shape[1]
    kw = bwh.shape[1]
    tile = lambda n, k=0: pl.BlockSpec((TILE, n), lambda i: (i, k))
    block = lambda r: pl.BlockSpec((r, hid), lambda i: (h, 0))
    return pl.pallas_call(
        functools.partial(hop_kernel, h, lo, hi),
        grid=(rows // TILE,),
        in_specs=[pl.BlockSpec((3, hid), lambda i: (0, h))]
        + [whole(t) for t in (gain, shift, slope, mslope)]
        + [tile(hid), tile(hid), block(hid), block(hid)]
        + [tile(hid, h)] * 4
        + [tile(width)]
        + [pl.BlockSpec((1, kw, hid), lambda i: (h, 0, 0))] * 2,
        out_specs=[
            tile(hi - lo),
            pl.BlockSpec((hi - lo, hid), lambda i: (0, 0)),
            pl.BlockSpec((4, hid), lambda i: (0, 0)),
        ],
        out_shape=[
            jax.ShapeDtypeStruct((rows, hi - lo), F32),
            jax.ShapeDtypeStruct((hi - lo, hid), F32),
            jax.ShapeDtypeStruct((4, hid), F32),
        ],
        compiler_params=params(),
        name=f"hop_back_{h}",
    )(st, gain, shift, slope, mslope, dvh, dvl, mwh, mwl, z, j, uh, ul, x, bwh, bwl)


def branch_fix_kernel(
    wins, in_w, st_ref, tot_ref, own_ref, gain_ref, shift_ref, g_ref, xm_ref, wh_ref, wl_ref,
    *refs,
):
    hops = len(wins)
    bws, (misc_ref, out_ref, q_ref, r_ref, gs_ref) = refs[:hops], refs[hops:]
    hid = gain_ref.shape[1]
    pad = -(-in_w // 8) * 8
    out_ref[...] = jnp.zeros_like(out_ref)
    for h, (lo, hi) in enumerate(wins):
        cols = slice(h * hid, (h + 1) * hid)
        n = hi - lo
        off = h * in_w - lo
        mean, rstd = norm_of(st_ref, cols)
        count = st_ref[2:3, cols]
        gain = gain_ref[h : h + 1, :]
        total = tot_ref[4 * h : 4 * h + 1, :]
        gsum = (tot_ref[4 * h + 1 : 4 * h + 2, :] - shift_ref[h : h + 1, :] * total) / gain
        gs_ref[h : h + 1, :] = gsum
        a = gain * rstd
        c1 = a * total / count
        c2 = a * gsum * rstd / count
        wh, wl = wh_ref[h, :n, :], wl_ref[h, :n, :]
        w = wh.astype(F32) + wl.astype(F32)
        wc = split(w * c2)
        k0 = c1 - mean * c2
        q_ref[h, :n, :n] = dot3((wh, wl), wc, NT)
        r_ref[h : h + 1, :n] = dot3(split(jnp.broadcast_to(k0, (8, hid))), (wh, wl), NT)[0:1, :]
        xm = jnp.broadcast_to(xm_ref[0:1, lo:hi], (LANES, n)).T[:, 0:1]
        bw = bws[h][...] - dot3(split(g_ref[h, :n, :n]), wc) - xm * k0
        out_ref[h * pad : h * pad + in_w, :] = bw[off : off + in_w, :]
    base = hops * pad
    k = misc_ref.shape[0]
    out_ref[base : base + k, :] = misc_ref[...]
    out_ref[base + k : base + k + 4 * hops, :] = own_ref[...]


def branch_fix(st, tot, own, gain, shift, g, xm, wh, wl, bws, misc, wins, in_w):
    hops, hid = gain.shape
    kw = g.shape[1]
    rows = hops * (-(-in_w // 8) * 8) + misc.shape[0] + 4 * hops
    rows = -(-rows // 512) * 512
    args = (st, tot, own, gain, shift, g, xm, wh, wl, *bws, misc)
    shapes = ((rows, hid), (hops, kw, kw), (hops, kw), (hops, hid))
    return pl.pallas_call(
        functools.partial(branch_fix_kernel, wins, in_w),
        out_shape=[jax.ShapeDtypeStruct(s, F32) for s in shapes],
        compiler_params=params(),
        name="branch_fix",
    )(*args)


def feats_kernel(wins, valid_ref, x_ref, q_ref, r_ref, *refs):
    dxs, out_ref = refs[:-1], refs[-1]
    tile = x_ref.shape[0]
    mask = row_mask(valid_ref, pl.program_id(0), tile)
    xh, xl = split(x_ref[...])
    pieces = {}
    for h, (lo, hi) in enumerate(wins):
        n = hi - lo
        fix = dot3((xh[:, lo:hi], xl[:, lo:hi]), split(q_ref[h, :n, :n]), NT) + r_ref[h : h + 1, :n]
        d = dxs[h][...] - jnp.where(mask, fix, 0.0)
        for c in range(lo, hi, LANES):
            e = min(c + LANES, hi)
            part = d[:, c - lo : e - lo]
            pieces[c, e] = pieces[c, e] + part if (c, e) in pieces else part
    for (c, e), part in pieces.items():
        out_ref[:, c:e] = part


def feats_fix(valid, x, q, r, dxs, wins):
    rows, width = x.shape
    tile = lambda n: pl.BlockSpec((TILE, n), lambda i: (i, 0))
    return pl.pallas_call(
        functools.partial(feats_kernel, wins),
        grid=(rows // TILE,),
        in_specs=[whole(valid), tile(width), whole(q), whole(r)] + [tile(d.shape[1]) for d in dxs],
        out_specs=tile(width),
        out_shape=jax.ShapeDtypeStruct((rows, width), F32),
        compiler_params=params(),
        name="feats_fix",
    )(valid, x, q, r, *dxs)


def flip(v, axis, size, k):
    return lax.ppermute(v, axis, [(i, i ^ k) for i in range(size)])


def sum_small(v, sizes):
    steps = []
    for axis, size in sizes.items():
        k = 1
        if axis == "dp" and size >= 2:
            steps.append((axis, size, 1, 2))
            k = 2
        while k < size:
            wide = 4 if 4 * k <= size else 2
            steps.append((axis, size, k, wide))
            k *= wide
    for axis, size, k, wide in steps:
        if wide == 2:
            v = v + flip(v, axis, size, k)
        else:
            p1, p2, p3 = (flip(v, axis, size, k * m) for m in (1, 2, 3))
            v = (v + p1) + (p2 + p3)
    return v


def halve(v, axis, size, k):
    bit = lax.axis_index(axis) // k % 2
    n = v.shape[0] // 2
    got = flip(lax.dynamic_slice_in_dim(v, (1 - bit) * n, n, 0), axis, size, k)
    return lax.dynamic_slice_in_dim(v, bit * n, n, 0) + got


def double(v, axis, size, k):
    bit = lax.axis_index(axis) // k % 2
    got = flip(v, axis, size, k)
    return jnp.where(bit == 0, jnp.concatenate([v, got], 0), jnp.concatenate([got, v], 0))


def sum_along(v, order):
    for s in order:
        v = halve(v, *s)
    for s in reversed(order):
        v = double(v, *s)
    return v


def sum_large(v, sizes):
    dp, bucket = sizes["dp"], sizes["bucket"]
    bits = lambda n: [1 << i for i in range(n.bit_length() - 1)]
    core = [("dp", dp, 1)] if dp > 1 else []
    square = [("dp", dp, k) for k in bits(dp) if k > 1]
    depth = [("bucket", bucket, k) for k in bits(bucket)]
    for s in core:
        v = halve(v, *s)
    n = v.shape[0] // 2
    v = jnp.concatenate(
        [sum_along(v[:n], square + depth), sum_along(v[n:], square[::-1] + depth)], 0
    )
    for s in core:
        v = double(v, *s)
    return v


def per_device(sizes, feats, labels, valid, branch_w, branch_gain, branch_shift, branch_slope, mix_slope,
               mix_w, mix_gain, mix_shift, out_slope, head_w, head_bias):
    rows, width = feats.shape
    hops, in_w, hid = branch_w.shape
    classes = head_w.shape[1]
    mix = hops * hid
    wins = windows(hops, in_w, width)
    kw = max(hi - lo for lo, hi in wins)
    valid = valid.reshape(rows // LANES, LANES)
    labels = labels.reshape(rows // LANES, LANES)
    mslope = mix_slope.reshape(hops, hid)
    row = lambda t: t.reshape(1, -1)
    wide = jnp.stack(
        [
            jnp.pad(branch_w[h], ((h * in_w - lo, kw - (h * in_w - lo) - in_w), (0, 0)))
            for h, (lo, hi) in enumerate(wins)
        ]
    )
    hi_part = lax.reduce_precision(wide, 8, 7)
    bwh = hi_part.astype(BF16)
    bwl = (wide - hi_part).astype(BF16)

    z, st = branch(valid, feats, bwh, bwl, wins)
    st = sum_small(st, sizes)
    g, xm = gram(valid, feats, wins)
    j, uh, ul, v, st2, mwh, mwl = forward(
        valid, z, st, branch_gain, branch_shift, branch_slope, mslope, mix_w
    )
    st2 = sum_small(st2, sizes)
    dy2, st3, misc = head(
        valid, labels, v, st2, st, row(mix_gain), row(mix_shift), row(out_slope), head_w, row(head_bias)
    )
    st3 = sum_small(st3, sizes)
    m, dvh, dvl = mix_back(valid, dy2, v, st2, st, st3, row(mix_gain), uh, ul)
    dxs, bws, sums = [], [], []
    for h, (lo, hi) in enumerate(wins):
        dx, bw, s = hop_back(
            h, lo, hi, st, branch_gain, branch_shift, branch_slope, mslope, dvh, dvl, mwh, mwl,
            z, j, uh, ul, feats, bwh, bwl,
        )
        dxs.append(dx)
        bws.append(bw)
        sums.append(s)
    m = sum_large(m, sizes)
    own = jnp.concatenate(sums, 0)
    tot = sum_small(own, sizes)
    packed, q, r, branch_gain_grad = branch_fix(
        st, tot, own, branch_gain, branch_shift, g, xm, bwh, bwl, bws, misc, wins, in_w
    )
    packed = sum_large(packed, sizes)
    d_x = feats_fix(valid, feats, q, r, dxs, wins)

    count = st[2, 0]
    pad = -(-in_w // 8) * 8
    base = hops * pad
    k = misc.shape[0]
    tail = packed[base : base + k + 4 * hops]
    per_hop = tail[k:].reshape(hops, 4, hid)
    return (
        tail[classes, LANES] / count,
        d_x,
        packed[:base].reshape(hops, pad, hid)[:, :in_w, :],
        branch_gain_grad,
        per_hop[:, 0, :],
        per_hop[:, 2, :],
        per_hop[:, 3, :].reshape(mix),
        m,
        st3[1],
        st3[0],
        tail[classes + 1],
        tail[:classes].T,
        tail[classes, :classes],
    )


def solution(mesh):
    sizes = {axis: mesh.shape[axis] for axis in ("dp", "bucket")}
    split_rows = P(("dp", "bucket"), None)
    in_specs = (split_rows, P(("dp", "bucket")), P(("dp", "bucket"))) + (P(),) * 11
    out_specs = (P(), split_rows) + (P(),) * 11
    return jax.shard_map(
        functools.partial(per_device, sizes),
        mesh=mesh,
        in_specs=in_specs,
        out_specs=out_specs,
        check_vma=False,
    )
```

time: 669 us -> 369 us (0.55)
  matrix products: 220 us -> 0 us
  Pallas kernels: 0 us -> 177 us
  blocking collectives: 165 us -> 0 us
  other arithmetic: 103 us -> 18.1 us
  starting transfers between devices: 0.04 us -> 67.9 us
  waiting for transfers between devices: 131 us -> 74.7 us
  between operations: 17.5 us -> 3.79 us
    dot_general x9 -> x0, matrix products: 220 us -> none  [the longest x6 169 us: matmul(): return jnp.dot(a, b, precision=HIGH, preferred_element_type=jnp.float32)]
    pallas_call x0 -> x11, Pallas kernels: none -> 177 us  [the longest x4 65.7 us: hop_back(): pl.pallas_call(functools.partial(hop_kernel, h, lo, hi), grid=(rows // TI...]
    psum x4 -> x0, blocking collectives: 165 us -> none  [the longest x1 42.4 us: per_device(): lax.psum((jnp.sum(mask3 * z, axis=0), jnp.sum(mask3 * z * z, axis=0), jnp...]
    psum x1 -> x0, waiting for transfers between devices: 131 us -> none  [per_device(): lax.psum((loss_part, branch_w_part, mix_w_part, branch_slope_part, mix_sl...]
    ppermute x0 -> x64, waiting for transfers between devices: none -> 74.7 us  [flip(): return lax.ppermute(v, axis, [(i, i ^ k) for i in range(size)])]
    ppermute x0 -> x64, starting transfers between devices: none -> 67.9 us  [flip(): return lax.ppermute(v, axis, [(i, i ^ k) for i in range(size)])]
    reduce_sum x6 -> x0, other arithmetic: 38.4 us -> none  [the longest x2 34.9 us: smooth_back(): d_slope = jnp.sum(grad * (y - jax.nn.softplus(y)), axis=0)]
    mul x4 -> x0, other arithmetic: 28.3 us -> none  [the longest x1 23 us: per_device(): rstd * (d_norm - mask3 * (branch_gain * branch_shift_grad + z_norm * bran...]
  transfers between devices with their start and end apart: 1 -> 64, of which waited for: 1 -> 41; matrix products, arithmetic and copies ran while one was open for 2% -> 6% of each run, Pallas kernels for 0% -> 5%
where the time goes in v1:
time: 369 us; the launch traced here: 367 us
  Pallas kernels  177 us (48%)
  waiting for transfers between devices  74.7 us (20%)
  starting transfers between devices  67.9 us (18%)
  local copies, waits for them, and re-layouts  25.4 us (7%)
  other arithmetic  18.1 us (5%)
  between operations  3.79 us (1%)
    ppermute x64, waiting for transfers between devices, flip(): return lax.ppermute(v, axis, [(i, i ^ k) for i in range(size)])  74.7 us
    ppermute x64, starting transfers between devices, flip(): return lax.ppermute(v, axis, [(i, i ^ k) for i in range(size)])  67.9 us
    pallas_call x4, Pallas kernels, hop_back(): pl.pallas_call(functools.partial(hop_kernel, h, lo, hi), grid=(rows // TI...  65.7 us
    pallas_call x1, Pallas kernels, forward(): pl.pallas_call(forward_kernel, grid=(rows // TILE,), in_specs=[whole(vali...  33.7 us
    pallas_call x1, Pallas kernels, mix_back(): pl.pallas_call(mix_kernel, grid=(rows // TILE,), in_specs=[whole(valid),...  22.9 us
    pallas_call x1, Pallas kernels, head(): pl.pallas_call(head_kernel, grid=(rows // TILE,), in_specs=[whole(valid),...  16.5 us
    unnamed x26, local copies, waits for them, and re-layouts  14.4 us
    pallas_call x1, Pallas kernels, branch(): pl.pallas_call(functools.partial(branch_kernel, wins), grid=(rows // TILE...  13.4 us
  transfers between devices with their start and end apart: 64, of which 41 were waited for; matrix products, arithmetic and copies ran while one was open for 6% of the time, Pallas kernels for 5%

profile of v1, /device:TPU:0, one launch (start us, length us, event | category | flops | bytes accessed | tf_op | source)
XLA Modules:
  0.0 366.7 jit_solution(16639007348729485086)
XLA Ops:
  0.7 5.1 %copy.31.x_ref = f32[2048,400]{1,0:T(8,128)} copy(f32[2048,400]{0,1:T(8,128)} %param.14) | data formatting | bytes 6553600 | tf_op args[0]
  6.6 1.8 fusion
  8.4 13.4 %branch.1 = (f32[2048,2048]{1,0:T(8,128)}, f32[3,2048]{1,0:T(4,128)}) custom-call(s32[16,128]{1,0:T(8,128)} %bitcast.40, f32[2048,400]{1,0:T(8,128)} %copy.31.x_ref, bf16[4,256,512]{2,1,0:T(8,128)(2,1)} %get-tuple-element.95.wh_ref.bwh_ref, bf16[4,256,512]{2,1,0:T(8,128)(2,1)} %get-tuple-element.94.wl_ref.bwl_ref), custom_call_target="tpu_custom_call" | custom-call | tf_op jit(solution)/shard_map/branch/pallas_call | solution.py:86
  24.1 2.9 collective-permute-start.2
  28.9 3.1 collective-permute-done.3
  32.4 2.7 collective-permute-start.5
  37.5 3.3 collective-permute-done.6
  41.4 33.7 %forward.1 = (f32[2048,2048]{1,0:T(8,128)}, bf16[2048,2048]{1,0:T(8,128)(2,1)}, bf16[2048,2048]{1,0:T(8,128)(2,1)}, f32[2048,512]{1,0:T(8,128)}, f32[2,512]{1,0:...) custom-call(s32[16,128]{1,0:T(8,128)} %bitcast.41, f32[2048,2048]{1,0:T(8,128)} %get-tuple-element.47.z_ref, ...), custom_call_target="tpu_custom_call" | custom-call | tf_op jit(solution)/shard_map/forward/pallas_call | solution.py:194
  80.8 2.5 collective-permute-done.10
  87.8 2.1 collective-permute-done.13
  90.5 16.5 %head.1 = (f32[2048,512]{1,0:T(8,128)}, f32[2,512]{1,0:T(2,128)}, f32[56,512]{1,0:T(8,128)}) custom-call(s32[16,128]{1,0:T(8,128)} %bitcast.42, s32[16,128]{1,0:T(8,128)} %bitcast.46, f32[2048,512]{1,0:T(8,128)} %get-tuple-element.48.v_ref, f32[2,512]{1,0:T(2,128)} %add_add_fusion.6.st_ref.st2_ref, f32[3,2048]{1,0:T(4,128)} %add_add_fusion.2.st_ref.cnt_ref, ...), custom_call_target="tpu_custom_call" | custom-call | tf_op jit(solution)/shard_map/head/pallas_call | solution.py:266
  112.7 2.0 collective-permute-done.17
  116.4 1.8 collective-permute-start.20
  119.9 1.9 collective-permute-done.20
  122.4 22.9 %mix_back.1 = (f32[2048,512]{1,0:T(8,128)}, bf16[2048,512]{1,0:T(8,128)(2,1)}, bf16[2048,512]{1,0:T(8,128)(2,1)}) custom-call(s32[16,128]{1,0:T(8,128)} %bitcast.43, f32[2048,512]{1,0:T(8,128)} %get-tuple-element.50.dy_ref, f32[2048,512]{1,0:T(8,128)} %get-tuple-element.48.v_ref, f32[2,512]{1,0:T(2,128)} %add_add_fusion.6.st_ref.st2_ref, ...), custom_call_target="tpu_custom_call" | custom-call | tf_op jit(solution)/shard_map/mix_back/pallas_call | solution.py:318
  145.3 16.3 %hop_back_3.1 = (f32[2048,144]{1,0:T(8,128)}, f32[144,512]{1,0:T(8,128)}, f32[4,512]{1,0:T(4,128)}) custom-call(f32[3,2048]{1,0:T(4,128)} %add_add_fusion.2.st_ref.cnt_ref, f32[4,512]{1,0:T(4,128)} %gain_ref.11, f32[4,512]{1,0:T(4,128)} %shift_ref.11, f32[4,512]{1,0:T(4,128)} %slope_ref.9, f32[4,512]{1,0:T(4,128)} %reshape.56.mslope_ref, ...), custom_call_target="tpu_custom_call" | custom-call | tf_op jit(solution)/shard_map/hop_back_3/pallas_call | solution.py:378
  161.6 16.8 %hop_back_2.1 = (f32[2048,256]{1,0:T(8,128)}, f32[256,512]{1,0:T(8,128)}, f32[4,512]{1,0:T(4,128)}) custom-call(f32[3,2048]{1,0:T(4,128)} %add_add_fusion.2.st_ref.cnt_ref, f32[4,512]{1,0:T(4,128)} %gain_ref.11, f32[4,512]{1,0:T(4,128)} %shift_ref.11, f32[4,512]{1,0:T(4,128)} %slope_ref.9, f32[4,512]{1,0:T(4,128)} %reshape.56.mslope_ref, ...), custom_call_target="tpu_custom_call" | custom-call | tf_op jit(solution)/shard_map/hop_back_2/pallas_call | solution.py:378
  178.4 16.9 %hop_back_1.1 = (f32[2048,256]{1,0:T(8,128)}, f32[256,512]{1,0:T(8,128)}, f32[4,512]{1,0:T(4,128)}) custom-call(f32[3,2048]{1,0:T(4,128)} %add_add_fusion.2.st_ref.cnt_ref, f32[4,512]{1,0:T(4,128)} %gain_ref.11, f32[4,512]{1,0:T(4,128)} %shift_ref.11, f32[4,512]{1,0:T(4,128)} %slope_ref.9, f32[4,512]{1,0:T(4,128)} %reshape.56.mslope_ref, ...), custom_call_target="tpu_custom_call" | custom-call | tf_op jit(solution)/shard_map/hop_back_1/pallas_call | solution.py:378
  195.3 15.8 %hop_back_0.1 = (f32[2048,128]{1,0:T(8,128)}, f32[128,512]{1,0:T(8,128)}, f32[4,512]{1,0:T(4,128)}) custom-call(f32[3,2048]{1,0:T(4,128)} %add_add_fusion.2.st_ref.cnt_ref, f32[4,512]{1,0:T(4,128)} %gain_ref.11, f32[4,512]{1,0:T(4,128)} %shift_ref.11, f32[4,512]{1,0:T(4,128)} %slope_ref.9, f32[4,512]{1,0:T(4,128)} %reshape.56.mslope_ref, ...), custom_call_target="tpu_custom_call" | custom-call | tf_op jit(solution)/shard_map/hop_back_0/pallas_call | solution.py:378
  213.8 1.6 collective-permute-start.23
  217.8 2.4 collective-permute-done.24
  221.5 1.8 collective-permute-start.27
  223.8 8.7 %gram.1 = (f32[4,256,256]{2,1,0:T(8,128)}, f32[1,400]{1,0:T(1,128)}) custom-call(s32[16,128]{1,0:T(8,128)} %bitcast.44, f32[2048,400]{1,0:T(8,128)} %copy.31.x_ref), custom_call_target="tpu_custom_call" | custom-call | tf_op jit(solution)/shard_map/gram/pallas_call | solution.py:128
  233.1 5.7 %branch_fix.1 = (f32[512,512]{1,0:T(8,128)}, f32[4,256,256]{2,1,0:T(8,128)}, f32[4,256]{1,0:T(4,128)}, f32[4,512]{1,0:T(4,128)}) custom-call(f32[3,2048]{1,0:T(4,128)} %add_add_fusion.2.st_ref.cnt_ref, f32[16,512]{1,0:T(8,128)} %add_add_fusion.tot_ref, f32[16,512]{1,0:T(8,128)} %copy-done.3, f32[4,512]{1,0:T(4,128)} %gain_ref.11, f32[4,512]{1,0:T(4,128)} %shift_ref.11, ...), custom_call_target="tpu_custom_call" | custom-call | tf_op jit(solution)/shard_map/branch_fix/pallas_call | solution.py:446
  240.0 3.2 constant_dynamic-slice_fusion.8
  246.5 2.8 collective-permute-done.37
  250.5 1.6 collective-permute-start.30
  256.5 2.1 dynamic-slice_add_fusion
  263.2 7.1 %collective-permute-done.55 = f32[256,512]{1,0:T(8,128)S(1)} collective-permute-done((f32[256,512]{1,0:T(8,128)S(1)}, f32[256,512]{1,0:T(8,128)S(1)}, u32[]{:S(2)}, u32[]{:S(2)}) %collective-permute-start.55) | collective-permute-done | bytes 524320 | tf_op jit(solution)/shard_map/ppermute | solution.py:487
  271.6 4.0 %collective-permute-done.47 = f32[256,512]{1,0:T(8,128)S(1)} collective-permute-done((f32[256,512]{1,0:T(8,128)S(1)}, f32[256,512]{1,0:T(8,128)S(1)}, u32[]{:S(2)}, u32[]{:S(2)}) %collective-permute-start.47) | collective-permute-done | bytes 524320 | tf_op jit(solution)/shard_map/ppermute | solution.py:487
  275.8 2.6 collective-permute-done.56
  278.4 1.6 collective-permute-start.57
  280.0 2.1 collective-permute-done.48
  283.8 2.5 collective-permute-start.58
  287.3 2.3 collective-permute-start.50
  289.6 2.2 collective-permute-done.58
  293.1 1.8 collective-permute-start.51
  294.9 2.9 collective-permute-done.59
  300.0 2.3 collective-permute-start.32
  305.8 6.2 %collective-permute-done.61 = f32[128,512]{1,0:T(8,128)S(1)} collective-permute-done((f32[128,512]{1,0:T(8,128)S(1)}, f32[128,512]{1,0:T(8,128)S(1)}, u32[]{:S(2)}, u32[]{:S(2)}) %collective-permute-start.61) | collective-permute-done | bytes 262176 | tf_op jit(solution)/shard_map/ppermute | solution.py:487
  315.9 1.8 collective-permute-done.33
  318.2 3.1 collective-permute-done.62
  323.7 2.0 collective-permute-start.35
  325.8 2.4 collective-permute-done.43
  330.4 3.0 collective-permute-done.44
  337.4 10.4 %feats_fix.1 = f32[2048,400]{1,0:T(8,128)} custom-call(s32[16,128]{1,0:T(8,128)} %bitcast.45, f32[2048,400]{1,0:T(8,128)} %copy.31.x_ref, f32[4,256,256]{2,1,0:T(8,128)} %get-tuple-element.71.q_ref, f32[4,256]{1,0:T(4,128)} %get-tuple-element.72.r_ref, f32[2048,128]{1,0:T(8,128)} %get-tuple-element.73.refs_0_, f32[2048,256]{1,0:T(8,128)} %get-tuple-element.74.refs_1_, ...), custom_call_target="tpu_custom_call" | custom-call | tf_op jit(solution)/shard_map/feats_fix/pallas_call | solution.py:475
  347.8 5.2 %copy.42 = f32[2048,400]{0,1:T(8,128)} copy(f32[2048,400]{1,0:T(8,128)} %feats_fix.1) | data formatting | bytes 6553600
  361.5 4.1 %maximum_select_fusion = f32[2048,512]{1,0:T(8,128)} fusion(f32[1024,512]{1,0:T(8,128)} %collective-permute-done.63, f32[512,512]{1,0:T(8,128)S(1)} %maximum_select_fusion.3, f32[512,512]{1,0:T(8,128)S(1)} %maximum_select_fusion.2, pred[]{:T(512)S(6)} %eq.65), kind=kLoop, calls=%fused_computation | loop fusion | flops 5242880 | bytes 8388609 | tf_op jit(solution)/shard_map/jit(_where)/select_n | solution.py:520
  (207 shorter events, 82.3 us)
Async XLA Ops:
  24.1 4.8 %collective-permute-start.2 = (f32[3,2048]{1,0:T(4,128)S(1)}, f32[3,2048]{1,0:T(4,128)S(1)}, u32[]{:S(2)}, u32[]{:S(2)}) collective-permute-start(f32[3,2048]{1,0:T(4,128)S(1)} %add.295), channel_id=1, source_target_pairs={{0,16},{4,20},{8,24},{12,28},{16,0},{20,4},{24,8},{28,12},{1,17},{... | collective-permute-start | bytes 73736 | tf_op jit(solution)/shard_map/ppermute | solution.py:487
  27.0 5.0 %collective-permute-start.3 = (f32[3,2048]{1,0:T(4,128)S(1)}, f32[3,2048]{1,0:T(4,128)S(1)}, u32[]{:S(2)}, u32[]{:S(2)}) collective-permute-start(f32[3,2048]{1,0:T(4,128)S(1)} %add.295), channel_id=1, source_target_pairs={{0,24},{4,28},{8,16},{12,20},{16,8},{20,12},{24,0},{28,4},{1,25},{... | collective-permute-start | bytes 73736 | tf_op jit(solution)/shard_map/ppermute | solution.py:487
  32.4 5.1 %collective-permute-start.5 = (f32[3,2048]{1,0:T(4,128)S(1)}, f32[3,2048]{1,0:T(4,128)S(1)}, u32[]{:S(2)}, u32[]{:S(2)}) collective-permute-start(f32[3,2048]{1,0:T(4,128)S(1)} %add_add_fusion.3), channel_id=1, source_target_pairs={{0,2},{1,3},{2,0},{3,1},{4,6},{5,7},{6,4},{7,5},{8,10},{9,11},{10,... | collective-permute-start | bytes 73736 | tf_op jit(solution)/shard_map/ppermute | solution.py:487
  35.0 5.7 %collective-permute-start.6 = (f32[3,2048]{1,0:T(4,128)S(1)}, f32[3,2048]{1,0:T(4,128)S(1)}, u32[]{:S(2)}, u32[]{:S(2)}) collective-permute-start(f32[3,2048]{1,0:T(4,128)S(1)} %add_add_fusion.3), channel_id=1, source_target_pairs={{0,3},{1,2},{2,1},{3,0},{4,7},{5,6},{6,5},{7,4},{8,11},{9,10},{10,... | collective-permute-start | bytes 73736 | tf_op jit(solution)/shard_map/ppermute | solution.py:487
  78.7 4.5 %collective-permute-start.10 = (f32[2,512]{1,0:T(2,128)S(1)}, f32[2,512]{1,0:T(2,128)S(1)}, u32[]{:S(2)}, u32[]{:S(2)}) collective-permute-start(f32[2,512]{1,0:T(2,128)S(1)} %add.302), channel_id=1, source_target_pairs={{0,24},{4,28},{8,16},{12,20},{16,8},{20,12},{24,0},{28,4},{1,25},{... | collective-permute-start | bytes 12296 | tf_op jit(solution)/shard_map/ppermute | solution.py:487
  83.2 4.6 %collective-permute-start.12 = (f32[2,512]{1,0:T(2,128)S(1)}, f32[2,512]{1,0:T(2,128)S(1)}, u32[]{:S(2)}, u32[]{:S(2)}) collective-permute-start(f32[2,512]{1,0:T(2,128)S(1)} %add_add_fusion.7), channel_id=1, source_target_pairs={{0,2},{1,3},{2,0},{3,1},{4,6},{5,7},{6,4},{7,5},{8,10},{9,11},{10,... | collective-permute-start | bytes 12296 | tf_op jit(solution)/shard_map/ppermute | solution.py:487
  84.5 5.4 %collective-permute-start.13 = (f32[2,512]{1,0:T(2,128)S(1)}, f32[2,512]{1,0:T(2,128)S(1)}, u32[]{:S(2)}, u32[]{:S(2)}) collective-permute-start(f32[2,512]{1,0:T(2,128)S(1)} %add_add_fusion.7), channel_id=1, source_target_pairs={{0,3},{1,2},{2,1},{3,0},{4,7},{5,6},{6,5},{7,4},{8,11},{9,10},{10,... | collective-permute-start | bytes 12296 | tf_op jit(solution)/shard_map/ppermute | solution.py:487
  110.2 4.5 %collective-permute-start.17 = (f32[2,512]{1,0:T(2,128)S(1)}, f32[2,512]{1,0:T(2,128)S(1)}, u32[]{:S(2)}, u32[]{:S(2)}) collective-permute-start(f32[2,512]{1,0:T(2,128)S(1)} %add.309), channel_id=1, source_target_pairs={{0,24},{4,28},{8,16},{12,20},{16,8},{20,12},{24,0},{28,4},{1,25},{... | collective-permute-start | bytes 12296 | tf_op jit(solution)/shard_map/ppermute | solution.py:487
  115.3 4.6 %collective-permute-start.19 = (f32[2,512]{1,0:T(2,128)S(1)}, f32[2,512]{1,0:T(2,128)S(1)}, u32[]{:S(2)}, u32[]{:S(2)}) collective-permute-start(f32[2,512]{1,0:T(2,128)S(1)} %add_add_fusion.5), channel_id=1, source_target_pairs={{0,2},{1,3},{2,0},{3,1},{4,6},{5,7},{6,4},{7,5},{8,10},{9,11},{10,... | collective-permute-start | bytes 12296 | tf_op jit(solution)/shard_map/ppermute | solution.py:487
  116.4 5.4 %collective-permute-start.20 = (f32[2,512]{1,0:T(2,128)S(1)}, f32[2,512]{1,0:T(2,128)S(1)}, u32[]{:S(2)}, u32[]{:S(2)}) collective-permute-start(f32[2,512]{1,0:T(2,128)S(1)} %add_add_fusion.5), channel_id=1, source_target_pairs={{0,3},{1,2},{2,1},{3,0},{4,7},{5,6},{6,5},{7,4},{8,11},{9,10},{10,... | collective-permute-start | bytes 12296 | tf_op jit(solution)/shard_map/ppermute | solution.py:487
  215.4 4.8 %collective-permute-start.24 = (f32[16,512]{1,0:T(8,128)S(1)}, f32[16,512]{1,0:T(8,128)S(1)}, u32[]{:S(2)}, u32[]{:S(2)}) collective-permute-start(f32[16,512]{1,0:T(8,128)S(1)} %fusion.1), channel_id=1, source_target_pairs={{0,24},{4,28},{8,16},{12,20},{16,8},{20,12},{24,0},{28,4},{1,25},{... | collective-permute-start | bytes 98312 | tf_op jit(solution)/shard_map/ppermute | solution.py:487
  220.3 12.2 %collective-permute-start.26 = (f32[16,512]{1,0:T(8,128)S(1)}, f32[16,512]{1,0:T(8,128)S(1)}, u32[]{:S(2)}, u32[]{:S(2)}) collective-permute-start(f32[16,512]{1,0:T(8,128)S(1)} %add_add_fusion.1), channel_id=1, source_target_pairs={{0,2},{1,3},{2,0},{3,1},{4,6},{5,7},{6,4},{7,5},{8,10},{9,11},{10,... | collective-permute-start | bytes 98312 | tf_op jit(solution)/shard_map/ppermute | solution.py:487
  221.5 11.0 %collective-permute-start.27 = (f32[16,512]{1,0:T(8,128)S(1)}, f32[16,512]{1,0:T(8,128)S(1)}, u32[]{:S(2)}, u32[]{:S(2)}) collective-permute-start(f32[16,512]{1,0:T(8,128)S(1)} %add_add_fusion.1), channel_id=1, source_target_pairs={{0,3},{1,2},{2,1},{3,0},{4,7},{5,6},{6,5},{7,4},{8,11},{9,10},{10,... | collective-permute-start | bytes 98312 | tf_op jit(solution)/shard_map/ppermute | solution.py:487
  223.3 9.2 %collective-permute-start.25 = (f32[16,512]{1,0:T(8,128)S(1)}, f32[16,512]{1,0:T(8,128)S(1)}, u32[]{:S(2)}, u32[]{:S(2)}) collective-permute-start(f32[16,512]{1,0:T(8,128)S(1)} %add_add_fusion.1), channel_id=1, source_target_pairs={{0,1},{1,0},{2,3},{3,2},{4,5},{5,4},{6,7},{7,6},{8,9},{9,8},{10,11... | collective-permute-start | bytes 98312 | tf_op jit(solution)/shard_map/ppermute | solution.py:487
  243.2 13.3 %collective-permute-start.46 = (f32[1024,512]{1,0:T(8,128)}, f32[1024,512]{1,0:T(8,128)S(1)}, u32[]{:S(2)}, u32[]{:S(2)}) collective-permute-start(f32[1024,512]{1,0:T(8,128)} %constant_dynamic-slice_fusion.8), channel_id=1, source_target_pairs={{0,4},{4,0},{8,12},{12,8},{16,20},{20,16},{24,28},{28,24},{1,5},{5... | collective-permute-start | bytes 6291464 | tf_op jit(solution)/shard_map/ppermute | solution.py:487
  243.8 5.5 %collective-permute-start.37 = (f32[64,512]{1,0:T(8,128)S(1)}, f32[64,512]{1,0:T(8,128)S(1)}, u32[]{:S(2)}, u32[]{:S(2)}) collective-permute-start(f32[64,512]{1,0:T(8,128)S(1)} %constant_dynamic-slice_fusion.12), channel_id=1, source_target_pairs={{0,16},{4,20},{8,24},{12,28},{16,0},{20,4},{24,8},{28,12},{1,17},{... | collective-permute-start | bytes 393224 | tf_op jit(solution)/shard_map/ppermute | solution.py:487
  244.9 5.6 %collective-permute-start.29 = (f32[64,512]{1,0:T(8,128)S(1)}, f32[64,512]{1,0:T(8,128)S(1)}, u32[]{:S(2)}, u32[]{:S(2)}) collective-permute-start(f32[64,512]{1,0:T(8,128)S(1)} %constant_dynamic-slice_fusion.16), channel_id=1, source_target_pairs={{0,8},{4,12},{8,0},{12,4},{16,24},{20,28},{24,16},{28,20},{1,9},{5... | collective-permute-start | bytes 393224 | tf_op jit(solution)/shard_map/ppermute | solution.py:487
  250.5 4.8 %collective-permute-start.30 = (f32[32,512]{1,0:T(8,128)S(1)}, f32[32,512]{1,0:T(8,128)S(1)}, u32[]{:S(2)}, u32[]{:S(2)}) collective-permute-start(f32[32,512]{1,0:T(8,128)S(1)} %constant_dynamic-slice_fusion.15), channel_id=1, source_target_pairs={{0,16},{4,20},{8,24},{12,28},{16,0},{20,4},{24,8},{28,12},{1,17},{... | collective-permute-start | bytes 196616 | tf_op jit(solution)/shard_map/ppermute | solution.py:487
  253.8 6.6 %collective-permute-start.39 = (f32[16,512]{1,0:T(8,128)S(1)}, f32[16,512]{1,0:T(8,128)S(1)}, u32[]{:S(2)}, u32[]{:S(2)}) collective-permute-start(f32[16,512]{1,0:T(8,128)S(1)} %constant_dynamic-slice_fusion.10), channel_id=1, source_target_pairs={{0,1},{1,0},{2,3},{3,2},{4,5},{5,4},{6,7},{7,6},{8,9},{9,8},{10,11... | collective-permute-start | bytes 98312 | tf_op jit(solution)/shard_map/ppermute | solution.py:487
  255.4 7.8 %collective-permute-start.31 = (f32[16,512]{1,0:T(8,128)S(1)}, f32[16,512]{1,0:T(8,128)S(1)}, u32[]{:S(2)}, u32[]{:S(2)}) collective-permute-start(f32[16,512]{1,0:T(8,128)S(1)} %constant_dynamic-slice_fusion.14), channel_id=1, source_target_pairs={{0,1},{1,0},{2,3},{3,2},{4,5},{5,4},{6,7},{7,6},{8,9},{9,8},{10,11... | collective-permute-start | bytes 98312 | tf_op jit(solution)/shard_map/ppermute | solution.py:487
  258.8 11.5 %collective-permute-start.55 = (f32[256,512]{1,0:T(8,128)S(1)}, f32[256,512]{1,0:T(8,128)S(1)}, u32[]{:S(2)}, u32[]{:S(2)}) collective-permute-start(f32[256,512]{1,0:T(8,128)S(1)} %constant_dynamic-slice_fusion.3), channel_id=1, source_target_pairs={{0,16},{4,20},{8,24},{12,28},{16,0},{20,4},{24,8},{28,12},{1,17},{... | collective-permute-start | bytes 1572872 | tf_op jit(solution)/shard_map/ppermute | solution.py:487
  260.4 45.2 %collective-permute-start.40 = (f32[8,512]{1,0:T(8,128)S(1)}, f32[8,512]{1,0:T(8,128)S(1)}, u32[]{:S(2)}, u32[]{:S(2)}) collective-permute-start(f32[8,512]{1,0:T(8,128)S(1)} %constant_dynamic-slice_fusion.9), channel_id=1, source_target_pairs={{0,2},{1,3},{2,0},{3,1},{4,6},{5,7},{6,4},{7,5},{8,10},{9,11},{10,... | collective-permute-start | bytes 49160 | tf_op jit(solution)/shard_map/ppermute | solution.py:487
  261.6 13.9 %collective-permute-start.47 = (f32[256,512]{1,0:T(8,128)S(1)}, f32[256,512]{1,0:T(8,128)S(1)}, u32[]{:S(2)}, u32[]{:S(2)}) collective-permute-start(f32[256,512]{1,0:T(8,128)S(1)} %constant_dynamic-slice_fusion.7), channel_id=1, source_target_pairs={{0,8},{4,12},{8,0},{12,4},{16,24},{20,28},{24,16},{28,20},{1,9},{5... | collective-permute-start | bytes 1572872 | tf_op jit(solution)/shard_map/ppermute | solution.py:487
  270.4 7.9 %collective-permute-start.56 = (f32[128,512]{1,0:T(8,128)S(1)}, f32[128,512]{1,0:T(8,128)S(1)}, u32[]{:S(2)}, u32[]{:S(2)}) collective-permute-start(f32[128,512]{1,0:T(8,128)S(1)} %constant_dynamic-slice_fusion.2), channel_id=1, source_target_pairs={{0,8},{4,12},{8,0},{12,4},{16,24},{20,28},{24,16},{28,20},{1,9},{5... | collective-permute-start | bytes 786440 | tf_op jit(solution)/shard_map/ppermute | solution.py:487
  275.7 6.4 %collective-permute-start.48 = (f32[128,512]{1,0:T(8,128)S(1)}, f32[128,512]{1,0:T(8,128)S(1)}, u32[]{:S(2)}, u32[]{:S(2)}) collective-permute-start(f32[128,512]{1,0:T(8,128)S(1)} %constant_dynamic-slice_fusion.6), channel_id=1, source_target_pairs={{0,16},{4,20},{8,24},{12,28},{16,0},{20,4},{24,8},{28,12},{1,17},{... | collective-permute-start | bytes 786440 | tf_op jit(solution)/shard_map/ppermute | solution.py:487
  278.4 5.4 %collective-permute-start.57 = (f32[64,512]{1,0:T(8,128)S(1)}, f32[64,512]{1,0:T(8,128)S(1)}, u32[]{:S(2)}, u32[]{:S(2)}) collective-permute-start(f32[64,512]{1,0:T(8,128)S(1)} %constant_dynamic-slice_fusion.1), channel_id=1, source_target_pairs={{0,1},{1,0},{2,3},{3,2},{4,5},{5,4},{6,7},{7,6},{8,9},{9,8},{10,11... | collective-permute-start | bytes 393224 | tf_op jit(solution)/shard_map/ppermute | solution.py:487
  282.2 5.0 %collective-permute-start.49 = (f32[64,512]{1,0:T(8,128)S(1)}, f32[64,512]{1,0:T(8,128)S(1)}, u32[]{:S(2)}, u32[]{:S(2)}) collective-permute-start(f32[64,512]{1,0:T(8,128)S(1)} %constant_dynamic-slice_fusion.5), channel_id=1, source_target_pairs={{0,1},{1,0},{2,3},{3,2},{4,5},{5,4},{6,7},{7,6},{8,9},{9,8},{10,11... | collective-permute-start | bytes 393224 | tf_op jit(solution)/shard_map/ppermute | solution.py:487
  283.8 7.9 %collective-permute-start.58 = (f32[32,512]{1,0:T(8,128)S(1)}, f32[32,512]{1,0:T(8,128)S(1)}, u32[]{:S(2)}, u32[]{:S(2)}) collective-permute-start(f32[32,512]{1,0:T(8,128)S(1)} %constant_dynamic-slice_fusion), channel_id=1, source_target_pairs={{0,2},{1,3},{2,0},{3,1},{4,6},{5,7},{6,4},{7,5},{8,10},{9,11},{10,... | collective-permute-start | bytes 196616 | tf_op jit(solution)/shard_map/ppermute | solution.py:487
  287.3 5.8 %collective-permute-start.50 = (f32[32,512]{1,0:T(8,128)S(1)}, f32[32,512]{1,0:T(8,128)S(1)}, u32[]{:S(2)}, u32[]{:S(2)}) collective-permute-start(f32[32,512]{1,0:T(8,128)S(1)} %constant_dynamic-slice_fusion.4), channel_id=1, source_target_pairs={{0,2},{1,3},{2,0},{3,1},{4,6},{5,7},{6,4},{7,5},{8,10},{9,11},{10,... | collective-permute-start | bytes 196616 | tf_op jit(solution)/shard_map/ppermute | solution.py:487
  291.8 6.0 %collective-permute-start.59 = (f32[32,512]{1,0:T(8,128)S(1)}, f32[32,512]{1,0:T(8,128)S(1)}, u32[]{:S(2)}, u32[]{:S(2)}) collective-permute-start(f32[32,512]{1,0:T(8,128)S(1)} %dynamic-slice_add_fusion.10), channel_id=1, source_target_pairs={{0,2},{1,3},{2,0},{3,1},{4,6},{5,7},{6,4},{7,5},{8,10},{9,11},{10,... | collective-permute-start | bytes 196616 | tf_op jit(solution)/shard_map/ppermute | solution.py:487
  293.1 6.2 %collective-permute-start.51 = (f32[32,512]{1,0:T(8,128)S(1)}, f32[32,512]{1,0:T(8,128)S(1)}, u32[]{:S(2)}, u32[]{:S(2)}) collective-permute-start(f32[32,512]{1,0:T(8,128)S(1)} %dynamic-slice_add_fusion.11), channel_id=1, source_target_pairs={{0,2},{1,3},{2,0},{3,1},{4,6},{5,7},{6,4},{7,5},{8,10},{9,11},{10,... | collective-permute-start | bytes 196616 | tf_op jit(solution)/shard_map/ppermute | solution.py:487
  297.8 5.2 %collective-permute-start.60 = (f32[64,512]{1,0:T(8,128)S(1)}, f32[64,512]{1,0:T(8,128)S(1)}, u32[]{:S(2)}, u32[]{:S(2)}) collective-permute-start(f32[64,512]{1,0:T(8,128)S(1)} %maximum_select_fusion.13), channel_id=1, source_target_pairs={{0,1},{1,0},{2,3},{3,2},{4,5},{5,4},{6,7},{7,6},{8,9},{9,8},{10,11... | collective-permute-start | bytes 393224 | tf_op jit(solution)/shard_map/ppermute | solution.py:487
  299.3 5.1 %collective-permute-start.52 = (f32[64,512]{1,0:T(8,128)S(1)}, f32[64,512]{1,0:T(8,128)S(1)}, u32[]{:S(2)}, u32[]{:S(2)}) collective-permute-start(f32[64,512]{1,0:T(8,128)S(1)} %maximum_select_fusion.12), channel_id=1, source_target_pairs={{0,1},{1,0},{2,3},{3,2},{4,5},{5,4},{6,7},{7,6},{8,9},{9,8},{10,11... | collective-permute-start | bytes 393224 | tf_op jit(solution)/shard_map/ppermute | solution.py:487
  300.0 12.8 %collective-permute-start.32 = (f32[8,512]{1,0:T(8,128)S(1)}, f32[8,512]{1,0:T(8,128)S(1)}, u32[]{:S(2)}, u32[]{:S(2)}) collective-permute-start(f32[8,512]{1,0:T(8,128)S(1)} %constant_dynamic-slice_fusion.13), channel_id=1, source_target_pairs={{0,2},{1,3},{2,0},{3,1},{4,6},{5,7},{6,4},{7,5},{8,10},{9,11},{10,... | collective-permute-start | bytes 49160 | tf_op jit(solution)/shard_map/ppermute | solution.py:487
  303.1 8.9 %collective-permute-start.61 = (f32[128,512]{1,0:T(8,128)S(1)}, f32[128,512]{1,0:T(8,128)S(1)}, u32[]{:S(2)}, u32[]{:S(2)}) collective-permute-start(f32[128,512]{1,0:T(8,128)S(1)} %maximum_select_fusion.9), channel_id=1, source_target_pairs={{0,8},{4,12},{8,0},{12,4},{16,24},{20,28},{24,16},{28,20},{1,9},{5... | collective-permute-start | bytes 786440 | tf_op jit(solution)/shard_map/ppermute | solution.py:487
  304.5 8.2 %collective-permute-start.53 = (f32[128,512]{1,0:T(8,128)S(1)}, f32[128,512]{1,0:T(8,128)S(1)}, u32[]{:S(2)}, u32[]{:S(2)}) collective-permute-start(f32[128,512]{1,0:T(8,128)S(1)} %maximum_select_fusion.8), channel_id=1, source_target_pairs={{0,16},{4,20},{8,24},{12,28},{16,0},{20,4},{24,8},{28,12},{1,17},{... | collective-permute-start | bytes 786440 | tf_op jit(solution)/shard_map/ppermute | solution.py:487
  305.6 8.9 %collective-permute-start.41 = (f32[8,512]{1,0:T(8,128)S(1)}, f32[8,512]{1,0:T(8,128)S(1)}, u32[]{:S(2)}, u32[]{:S(2)}) collective-permute-start(f32[8,512]{1,0:T(8,128)S(1)} %dynamic-slice_add_fusion.16), channel_id=1, source_target_pairs={{0,2},{1,3},{2,0},{3,1},{4,6},{5,7},{6,4},{7,5},{8,10},{9,11},{10,... | collective-permute-start | bytes 49160 | tf_op jit(solution)/shard_map/ppermute | solution.py:487
  312.1 9.2 %collective-permute-start.62 = (f32[256,512]{1,0:T(8,128)S(1)}, f32[256,512]{1,0:T(8,128)S(1)}, u32[]{:S(2)}, u32[]{:S(2)}) collective-permute-start(f32[256,512]{1,0:T(8,128)S(1)} %maximum_select_fusion.5), channel_id=1, source_target_pairs={{0,16},{4,20},{8,24},{12,28},{16,0},{20,4},{24,8},{28,12},{1,17},{... | collective-permute-start | bytes 1572872 | tf_op jit(solution)/shard_map/ppermute | solution.py:487
  312.7 9.2 %collective-permute-start.54 = (f32[256,512]{1,0:T(8,128)S(1)}, f32[256,512]{1,0:T(8,128)S(1)}, u32[]{:S(2)}, u32[]{:S(2)}) collective-permute-start(f32[256,512]{1,0:T(8,128)S(1)} %maximum_select_fusion.4), channel_id=1, source_target_pairs={{0,8},{4,12},{8,0},{12,4},{16,24},{20,28},{24,16},{28,20},{1,9},{5... | collective-permute-start | bytes 1572872 | tf_op jit(solution)/shard_map/ppermute | solution.py:487
  312.9 4.9 %collective-permute-start.33 = (f32[8,512]{1,0:T(8,128)S(1)}, f32[8,512]{1,0:T(8,128)S(1)}, u32[]{:S(2)}, u32[]{:S(2)}) collective-permute-start(f32[8,512]{1,0:T(8,128)S(1)} %dynamic-slice_add_fusion.17), channel_id=1, source_target_pairs={{0,2},{1,3},{2,0},{3,1},{4,6},{5,7},{6,4},{7,5},{8,10},{9,11},{10,... | collective-permute-start | bytes 49160 | tf_op jit(solution)/shard_map/ppermute | solution.py:487
  314.4 9.1 %collective-permute-start.42 = (f32[16,512]{1,0:T(8,128)S(1)}, f32[16,512]{1,0:T(8,128)S(1)}, u32[]{:S(2)}, u32[]{:S(2)}) collective-permute-start(f32[16,512]{1,0:T(8,128)S(1)} %maximum_select_fusion.17), channel_id=1, source_target_pairs={{0,1},{1,0},{2,3},{3,2},{4,5},{5,4},{6,7},{7,6},{8,9},{9,8},{10,11... | collective-permute-start | bytes 98312 | tf_op jit(solution)/shard_map/ppermute | solution.py:487
  317.7 6.0 %collective-permute-start.34 = (f32[16,512]{1,0:T(8,128)S(1)}, f32[16,512]{1,0:T(8,128)S(1)}, u32[]{:S(2)}, u32[]{:S(2)}) collective-permute-start(f32[16,512]{1,0:T(8,128)S(1)} %maximum_select_fusion.16), channel_id=1, source_target_pairs={{0,1},{1,0},{2,3},{3,2},{4,5},{5,4},{6,7},{7,6},{8,9},{9,8},{10,11... | collective-permute-start | bytes 98312 | tf_op jit(solution)/shard_map/ppermute | solution.py:487
  323.6 37.9 %collective-permute-start.63 = (f32[1024,512]{1,0:T(8,128)}, f32[1024,512]{1,0:T(8,128)}, u32[]{:S(2)}, u32[]{:S(2)}) collective-permute-start(f32[1024,512]{1,0:T(8,128)} %pad_maximum_fusion.1), channel_id=1, source_target_pairs={{0,4},{4,0},{8,12},{12,8},{16,20},{20,16},{24,28},{28,24},{1,5},{5... | collective-permute-start | bytes 6291464 | tf_op jit(solution)/shard_map/ppermute | solution.py:487
  323.6 4.6 %collective-permute-start.43 = (f32[32,512]{1,0:T(8,128)S(1)}, f32[32,512]{1,0:T(8,128)S(1)}, u32[]{:S(2)}, u32[]{:S(2)}) collective-permute-start(f32[32,512]{1,0:T(8,128)S(1)} %maximum_select_fusion.15), channel_id=1, source_target_pairs={{0,8},{4,12},{8,0},{12,4},{16,24},{20,28},{24,16},{28,20},{1,9},{5... | collective-permute-start | bytes 196616 | tf_op jit(solution)/shard_map/ppermute | solution.py:487
  323.7 6.0 %collective-permute-start.35 = (f32[32,512]{1,0:T(8,128)S(1)}, f32[32,512]{1,0:T(8,128)S(1)}, u32[]{:S(2)}, u32[]{:S(2)}) collective-permute-start(f32[32,512]{1,0:T(8,128)S(1)} %maximum_select_fusion.14), channel_id=1, source_target_pairs={{0,16},{4,20},{8,24},{12,28},{16,0},{20,4},{24,8},{28,12},{1,17},{... | collective-permute-start | bytes 196616 | tf_op jit(solution)/shard_map/ppermute | solution.py:487
  328.2 5.2 %collective-permute-start.44 = (f32[64,512]{1,0:T(8,128)S(1)}, f32[64,512]{1,0:T(8,128)S(1)}, u32[]{:S(2)}, u32[]{:S(2)}) collective-permute-start(f32[64,512]{1,0:T(8,128)S(1)} %maximum_select_fusion.11), channel_id=1, source_target_pairs={{0,16},{4,20},{8,24},{12,28},{16,0},{20,4},{24,8},{28,12},{1,17},{... | collective-permute-start | bytes 393224 | tf_op jit(solution)/shard_map/ppermute | solution.py:487
  329.7 5.0 %collective-permute-start.36 = (f32[64,512]{1,0:T(8,128)S(1)}, f32[64,512]{1,0:T(8,128)S(1)}, u32[]{:S(2)}, u32[]{:S(2)}) collective-permute-start(f32[64,512]{1,0:T(8,128)S(1)} %maximum_select_fusion.10), channel_id=1, source_target_pairs={{0,8},{4,12},{8,0},{12,4},{16,24},{20,28},{24,16},{28,20},{1,9},{5... | collective-permute-start | bytes 393224 | tf_op jit(solution)/shard_map/ppermute | solution.py:487
  335.5 17.4 %collective-permute-start.45 = (f32[256,512]{1,0:T(8,128)S(1)}, f32[256,512]{1,0:T(8,128)}, u32[]{:S(2)}, u32[]{:S(2)}) collective-permute-start(f32[256,512]{1,0:T(8,128)S(1)} %pad_maximum_fusion.2), channel_id=1, source_target_pairs={{0,4},{4,0},{8,12},{12,8},{16,20},{20,16},{24,28},{28,24},{1,5},{5... | collective-permute-start | bytes 1572872 | tf_op jit(solution)/shard_map/ppermute | solution.py:487
  (26 other events, 216.7 us)

commit v2 on v1

v2 whole, which is shorter than its diff:
```python
import functools

import jax
import jax.numpy as jnp
from jax import lax
from jax.experimental import pallas as pl
from jax.experimental.pallas import tpu as pltpu
from jax.sharding import PartitionSpec as P

EPS = 1e-05
F32 = jnp.float32
BF16 = jnp.bfloat16
LANES = 128
VMEM = 56 * 1024 * 1024
LOG2E = 1.4426950408889634
LN2 = 0.6931471805599453
TILES = {"gram": 1024, "forward": 512, "head": 512, "mix": 512, "hop": 512, "fix": 512}
HOP_STAGES = 3
PACK_STAGES = 2
SUB = 256
CHUNK = 512
NN = (((1,), (0,)), ((), ()))
NT = (((1,), (1,)), ((), ()))
TN = (((0,), (0,)), ((), ()))


def split(x):
    hi = x.astype(BF16)
    return hi, (x - hi.astype(F32)).astype(BF16)


def dot3(a, b, dims=NN):
    ah, al = a
    bh, bl = b
    dot = functools.partial(lax.dot_general, dimension_numbers=dims, preferred_element_type=F32)
    return dot(ah, bh) + (dot(ah, bl) + dot(al, bh))


def act2(y, slope, rest):
    return jnp.maximum(slope * y + rest * jnp.log(1.0 + jnp.exp2(jnp.minimum(y, 30.0))), y)


def cost(us):
    return pl.CostEstimate(flops=0, bytes_accessed=int(us * 3.69e6), transcendentals=0)


def params(**kw):
    return pltpu.CompilerParams(vmem_limit_bytes=VMEM, **kw)


def whole(x):
    return pl.BlockSpec(x.shape, lambda *_: (0,) * len(x.shape))


def row_mask(valid_ref, step, tile, axis=0):
    n = jnp.sum(valid_ref[...])
    shape = (tile, 1) if axis == 0 else (1, tile)
    return step * tile + lax.broadcasted_iota(jnp.int32, shape, axis) < n


def hop_rows(x_ref, h, in_w, extra=None):
    x = x_ref[h * in_w : (h + 1) * in_w, :]
    pad = -(-(in_w + 1) // 16) * 16 - in_w
    tail = jnp.zeros((pad, x.shape[1]), F32)
    if extra is not None:
        first = lax.broadcasted_iota(jnp.int32, tail.shape, 0) == 0
        tail = jnp.where(first, extra, 0.0)
    return jnp.concatenate([x, tail], axis=0)


def stack3(a):
    hi, lo = split(a)
    return jnp.concatenate([hi, lo, hi], axis=0)


def gram_kernel(in_w, valid_ref, x_ref, w_ref, g_ref, st_ref, wp_ref):
    step = pl.program_id(0)
    tile = x_ref.shape[1]
    hops, hid = w_ref.shape[1:]
    mask = row_mask(valid_ref, step, tile, 1)

    @pl.when(step == 0)
    def _():
        g_ref[...] = jnp.zeros_like(g_ref)

    for h in range(hops):
        x = jnp.where(mask, hop_rows(x_ref, h, in_w, 1.0), 0.0)
        hi, lo = split(x)
        n = x.shape[0]
        dot = functools.partial(lax.dot_general, dimension_numbers=NT, preferred_element_type=F32)
        cross = dot(hi, lo)
        g_ref[h, :, :n] += dot(hi, hi) + (cross + cross.T)

    @pl.when(step == pl.num_programs(0) - 1)
    def _():
        for h in range(hops):
            n = g_ref.shape[1]
            w = w_ref[:, h, :]
            w = jnp.concatenate([w, jnp.zeros((n - in_w, hid), F32)], axis=0)
            ws = split(w)
            g = g_ref[h, :, :n]
            gw = dot3(split(g), ws)
            cols = slice(h * hid, (h + 1) * hid)
            st_ref[0:1, cols] = gw[in_w : in_w + 1, :]
            st_ref[1:2, cols] = jnp.sum(w * gw, axis=0, keepdims=True)
            wp_ref[h] = jnp.concatenate([ws[0], ws[0], ws[1]], axis=0)
        st_ref[:, hops * hid :] = jnp.broadcast_to(g_ref[0, in_w : in_w + 1, in_w : in_w + 1], (2, LANES))


def gram(valid, x, w, tile):
    width, rows = x.shape
    in_w, hops, hid = w.shape
    n = -(-(in_w + 1) // 16) * 16
    shapes = ((hops, n, LANES), F32), ((2, hops * hid + LANES), F32), ((hops, 3 * n, hid), BF16)
    return pl.pallas_call(
        functools.partial(gram_kernel, in_w),
        grid=(rows // tile,),
        in_specs=[whole(valid), pl.BlockSpec((width, tile), lambda i: (0, i)), whole(w)],
        out_specs=[pl.BlockSpec(s, lambda i, s=s: (0,) * len(s)) for s, _ in shapes],
        out_shape=[jax.ShapeDtypeStruct(*s) for s in shapes],
        compiler_params=params(),
        name="gram",
        cost_estimate=cost(5),
    )(valid, x, w)


def count_of(st_ref):
    return st_ref[0:1, st_ref.shape[1] - 1 :]


def norm_of(st_ref, cols):
    count = count_of(st_ref)
    mean = st_ref[0:1, cols] / count
    var = st_ref[1:2, cols] / count - mean * mean
    return mean, lax.rsqrt(var + EPS)


def scale_of(st_ref, cols, gain_ref, shift_ref, h):
    mean, rstd = norm_of(st_ref, cols)
    a = gain_ref[h : h + 1, :] * rstd
    return LOG2E * a, LOG2E * (shift_ref[h : h + 1, :] - mean * a)


def forward_kernel(
    in_w, valid_ref, x_ref, wp_ref, st_ref, gain_ref, shift_ref, slope_ref, mslope_ref, w_ref,
    j_ref, uh_ref, ul_ref, v_ref, st2_ref, wh_ref, wl_ref,
):
    step = pl.program_id(0)
    tile = x_ref.shape[1]
    hops, hid = gain_ref.shape
    mask = row_mask(valid_ref, step, tile)

    @pl.when(step == 0)
    def _():
        st2_ref[...] = jnp.zeros_like(st2_ref)
        for h in range(hops):
            rows = slice(h * hid, (h + 1) * hid)
            wh_ref[rows, :], wl_ref[rows, :] = split(w_ref[rows, :])

    dot = functools.partial(lax.dot_general, preferred_element_type=F32)
    chunks = [(h, slice(r, r + CHUNK)) for h in range(hops) for r in range(0, tile, CHUNK)]
    scales, xs = {}, {}

    def project(i):
        h, rows = chunks[i]
        if h not in xs:
            xs[h] = stack3(hop_rows(x_ref, h, in_w))
        return dot(xs[h][:, rows], wp_ref[h], TN)

    def activate(i, z):
        h, rows = chunks[i]
        cols = slice(h * hid, (h + 1) * hid)
        if h not in scales:
            scales[h] = scale_of(st_ref, cols, gain_ref, shift_ref, h)
        a, b = scales[h]
        s1 = slope_ref[h : h + 1, :]
        s2 = mslope_ref[h : h + 1, :]
        j = act2(z * a + b, s1, LOG2E * (1.0 - s1))
        u = act2(j, s2, LOG2E * (1.0 - s2))
        j_ref[rows, cols] = j
        us = split(u)
        uh_ref[rows, cols], ul_ref[rows, cols] = us
        return us

    def mix(i, us):
        h, rows = chunks[i]
        cols = slice(h * hid, (h + 1) * hid)
        both = dot(jnp.concatenate(us, axis=0), wh_ref[cols, :], NN)
        part = both[:CHUNK] + both[CHUNK:] + dot(us[0], wl_ref[cols, :], NN)
        v_ref[rows, :] = part if h == 0 else v_ref[rows, :] + part

    z = project(0)
    before = None
    for i in range(len(chunks)):
        ahead = project(i + 1) if i + 1 < len(chunks) else None
        if before is not None:
            mix(i - 1, before)
        before = activate(i, z)
        z = ahead
    mix(len(chunks) - 1, before)
    v = v_ref[...]
    v = LN2 * v
    v_ref[...] = v
    vm = jnp.where(mask, v, 0.0)
    st2_ref[0:1, :] += jnp.sum(vm, axis=0, keepdims=True)
    st2_ref[1:2, :] += jnp.sum(vm * vm, axis=0, keepdims=True)


def forward(valid, x, wp, st, gain, shift, slope, mslope, w, in_w, tile):
    width, rows = x.shape
    mix, hid = w.shape
    by = lambda n: pl.BlockSpec((tile, n), lambda i: (i, 0))
    return pl.pallas_call(
        functools.partial(forward_kernel, in_w),
        grid=(rows // tile,),
        in_specs=[whole(valid), pl.BlockSpec((width, tile), lambda i: (0, i))]
        + [whole(t) for t in (wp, st, gain, shift, slope, mslope, w)],
        out_specs=[by(mix), by(mix), by(mix), by(hid)]
        + [pl.BlockSpec(s, lambda i: (0, 0)) for s in ((2, hid), (mix, hid), (mix, hid))],
        out_shape=[
            jax.ShapeDtypeStruct((rows, mix), F32),
            jax.ShapeDtypeStruct((rows, mix), BF16),
            jax.ShapeDtypeStruct((rows, mix), BF16),
            jax.ShapeDtypeStruct((rows, hid), F32),
            jax.ShapeDtypeStruct((2, hid), F32),
            jax.ShapeDtypeStruct((mix, hid), BF16),
            jax.ShapeDtypeStruct((mix, hid), BF16),
        ],
        compiler_params=params(),
        name="forward",
        cost_estimate=cost(30),
    )(valid, x, wp, st, gain, shift, slope, mslope, w)


def as_column(row):
    n = row.shape[1]
    same = lax.broadcasted_iota(jnp.int32, (n, n), 0) == lax.broadcasted_iota(jnp.int32, (n, n), 1)
    return jnp.sum(jnp.where(same, jnp.broadcast_to(row, (n, n)), 0.0), axis=1, keepdims=True)


def as_row(col):
    n = col.shape[0]
    same = lax.broadcasted_iota(jnp.int32, (n, n), 0) == lax.broadcasted_iota(jnp.int32, (n, n), 1)
    return jnp.sum(jnp.where(same, jnp.broadcast_to(col, (n, n)), 0.0), axis=0, keepdims=True)


def head_kernel(
    valid_ref, labels_ref, v_ref, st_ref, cnt_ref, gain_ref, shift_ref, slope_ref, hw_ref, hb_ref,
    dy_ref, st3_ref, misc_ref,
):
    step = pl.program_id(0)
    tile, hid = v_ref.shape
    classes = hw_ref.shape[0]
    padded = -(-classes // 16) * 16
    mask = row_mask(valid_ref, step, tile, 1)
    count = count_of(cnt_ref)

    @pl.when(step == 0)
    def _():
        st3_ref[...] = jnp.zeros_like(st3_ref)
        misc_ref[...] = jnp.zeros_like(misc_ref)

    mean = st_ref[0:1, :] / count
    rstd = lax.rsqrt(st_ref[1:2, :] / count - mean * mean + EPS)
    s = slope_ref[...]
    zn = (v_ref[...] - mean) * rstd
    y = gain_ref[...] * zn + shift_ref[...]
    e1 = 1.0 + jnp.exp(jnp.minimum(y, 20.0))
    sp = jnp.maximum(jnp.log(e1), y)
    w = s * y + (1.0 - s) * sp
    ws = split(w)
    hw = hw_ref[...]
    if padded > classes:
        hw = jnp.concatenate([hw, jnp.zeros((padded - classes, hid), F32)], axis=0)
    hh, hl = split(hw)
    dot = functools.partial(lax.dot_general, dimension_numbers=NT, preferred_element_type=F32)
    both = dot(jnp.concatenate([hh, hl], axis=0), ws[0])
    logits = both[:padded] + both[padded:] + dot(hh, ws[1])
    logits = logits[:classes] + as_column(hb_ref[...])
    peak = jnp.max(logits, axis=0, keepdims=True)
    ex = jnp.exp(logits - peak)
    tot = jnp.sum(ex, axis=0, keepdims=True)
    per = tile // LANES
    lab = jnp.concatenate([labels_ref[pl.ds(step * per + k, 1), :] for k in range(per)], axis=1)
    hit = lab == lax.broadcasted_iota(jnp.int32, (classes, tile), 0)
    picked = jnp.sum(jnp.where(hit, logits, 0.0), axis=0, keepdims=True)
    loss = jnp.sum(jnp.where(mask, peak + jnp.log(tot) - picked, 0.0))
    dl = jnp.where(mask, (ex / tot - hit.astype(F32)) / count, 0.0)
    bias = as_row(jnp.sum(dl, axis=1, keepdims=True))
    if padded > classes:
        dl = jnp.concatenate([dl, jnp.zeros((padded - classes, tile), F32)], axis=0)
    dh, dlo = split(dl)
    dot = functools.partial(lax.dot_general, dimension_numbers=NN, preferred_element_type=F32)
    both = dot(jnp.concatenate([dh, dlo], axis=0), ws[0])
    hwg = both[:padded] + both[padded:] + dot(dh, ws[1])
    misc_ref[0:classes, :] += hwg[:classes]
    misc_ref[classes : classes + 1, 0:classes] += bias
    misc_ref[classes : classes + 1, LANES : 2 * LANES] += jnp.broadcast_to(loss, (1, LANES))
    dw = lax.dot_general(
        jnp.concatenate([dh, dlo, dh], axis=0),
        jnp.concatenate([hh, hh, hl], axis=0),
        TN,
        preferred_element_type=F32,
    )
    dy = dw * (1.0 - (1.0 - s) / e1)
    dy_ref[...] = dy
    row = lambda t: jnp.sum(t, axis=0, keepdims=True)
    misc_ref[classes + 1 : classes + 2, :] += row(dw * (y - sp))
    st3_ref[0:1, :] += row(dy)
    st3_ref[1:2, :] += row(dy * zn)


def head(valid, labels, v, st2, st, gain, shift, slope, hw, hb, tile):
    rows, hid = v.shape
    by = lambda n: pl.BlockSpec((tile, n), lambda i: (i, 0))
    misc = -(-(hw.shape[0] + 2) // 8) * 8
    return pl.pallas_call(
        head_kernel,
        grid=(rows // tile,),
        in_specs=[whole(valid), whole(labels), by(hid)]
        + [whole(t) for t in (st2, st, gain, shift, slope, hw, hb)],
        out_specs=[
            by(hid),
            pl.BlockSpec((2, hid), lambda i: (0, 0)),
            pl.BlockSpec((misc, hid), lambda i: (0, 0)),
        ],
        out_shape=[
            jax.ShapeDtypeStruct((rows, hid), F32),
            jax.ShapeDtypeStruct((2, hid), F32),
            jax.ShapeDtypeStruct((misc, hid), F32),
        ],
        compiler_params=params(),
        name="head",
        cost_estimate=cost(9),
    )(valid, labels, v, st2, st, gain, shift, slope, hw, hb)


def mix_dv(valid_ref, dy_ref, v_ref, st2_ref, cnt_ref, st3_ref, gain_ref):
    mask = row_mask(valid_ref, pl.program_id(0), dy_ref.shape[0])
    count = count_of(cnt_ref)
    mean = st2_ref[0:1, :] / count
    rstd = lax.rsqrt(st2_ref[1:2, :] / count - mean * mean + EPS)
    a = LN2 * gain_ref[...] * rstd
    c1 = a * st3_ref[0:1, :] / count
    c2 = a * st3_ref[1:2, :] / count
    zn = (v_ref[...] - mean) * rstd
    return split(jnp.where(mask, a * dy_ref[...] - (c1 + zn * c2), 0.0))


def mix_product(dvs, uh_ref, ul_ref, m_ref):
    @pl.when(pl.program_id(0) == 0)
    def _():
        m_ref[...] = jnp.zeros_like(m_ref)

    hid = dvs[0].shape[1]
    for h in range(uh_ref.shape[1] // hid):
        cols = slice(h * hid, (h + 1) * hid)
        m_ref[cols, :] += dot3((uh_ref[:, cols], ul_ref[:, cols]), dvs, TN)


def mix_first_kernel(half_ref, *refs):
    ins, (uh_ref, ul_ref, m_ref, dvh_ref, dvl_ref) = refs[:7], refs[7:]
    dvs = mix_dv(*ins)
    dvh_ref[...], dvl_ref[...] = dvs
    mix_product(dvs, uh_ref, ul_ref, m_ref)


def mix_second_kernel(half_ref, dvh_ref, dvl_ref, uh_ref, ul_ref, m_ref):
    mix_product((dvh_ref[...], dvl_ref[...]), uh_ref, ul_ref, m_ref)


def mix_back(half, valid, dy, v, st2, st, st3, gain, uh, ul, tile):
    rows, hid = dy.shape
    part = uh.shape[1] // 2
    by = lambda n: pl.BlockSpec((tile, n), lambda i, half: (i, 0))
    return pl.pallas_call(
        mix_first_kernel,
        grid_spec=pltpu.PrefetchScalarGridSpec(
            num_scalar_prefetch=1,
            grid=(rows // tile,),
            in_specs=[whole(valid), by(hid), by(hid)]
            + [whole(t) for t in (st2, st, st3, gain)]
            + [pl.BlockSpec((tile, part), lambda i, half: (i, half[0]))] * 2,
            out_specs=[pl.BlockSpec((part, hid), lambda i, half: (0, 0)), by(hid), by(hid)],
        ),
        out_shape=[
            jax.ShapeDtypeStruct((part, hid), F32),
            jax.ShapeDtypeStruct((rows, hid), BF16),
            jax.ShapeDtypeStruct((rows, hid), BF16),
        ],
        compiler_params=params(),
        name="mix_back",
        cost_estimate=cost(14),
    )(half, valid, dy, v, st2, st, st3, gain, uh, ul)


def mix_back_rest(half, dvh, dvl, uh, ul, tile):
    rows, hid = dvh.shape
    part = uh.shape[1] // 2
    by = lambda n: pl.BlockSpec((tile, n), lambda i, half: (i, 0))
    return pl.pallas_call(
        mix_second_kernel,
        grid_spec=pltpu.PrefetchScalarGridSpec(
            num_scalar_prefetch=1,
            grid=(rows // tile,),
            in_specs=[by(hid), by(hid)]
            + [pl.BlockSpec((tile, part), lambda i, half: (i, half[0]))] * 2,
            out_specs=pl.BlockSpec((part, hid), lambda i, half: (0, 0)),
        ),
        out_shape=jax.ShapeDtypeStruct((part, hid), F32),
        compiler_params=params(),
        name="mix_back_rest",
        cost_estimate=cost(12),
    )(half, dvh, dvl, uh, ul)


def hop_kernel(
    h, in_w, x_ref, wp_ref, st_ref, gain_ref, shift_ref, slope_ref, mslope_ref, dvh_ref, dvl_ref, mwh_ref, mwl_ref,
    j_ref, uh_ref, ul_ref,
    dx_ref, bw_ref, sums_ref,
):
    step = pl.program_id(0)
    n = wp_ref.shape[1] // 3
    hid = gain_ref.shape[1]

    @pl.when(step == 0)
    def _():
        bw_ref[...] = jnp.zeros_like(bw_ref)
        sums_ref[...] = jnp.zeros_like(sums_ref)

    a, b = scale_of(st_ref, slice(h * hid, (h + 1) * hid), gain_ref, shift_ref, h)
    s1 = slope_ref[h : h + 1, :]
    s2 = mslope_ref[h : h + 1, :]
    xall = stack3(hop_rows(x_ref, h, in_w))
    wp = wp_ref[0]
    r2 = 1.0 / (1.0 - s2)
    r1 = 1.0 / (1.0 - s1)
    wh, wl = split((wp[:n].astype(F32) + wp[2 * n :].astype(F32)) * a)
    whl = jnp.concatenate([wh, wl], axis=0)
    dot = functools.partial(lax.dot_general, preferred_element_type=F32)
    row = lambda t: jnp.sum(t, axis=0, keepdims=True)
    sums = [0.0] * 4
    tile = x_ref.shape[1]
    parts = [slice(k, k + SUB) for k in range(0, tile, SUB)]

    def products(rs):
        y = dot(xall[:, rs], wp, TN)
        return y, dot3((dvh_ref[rs, :], dvl_ref[rs, :]), (mwh_ref[...], mwl_ref[...]), NT)

    def middle(rs, z, du):
        y = z * a + b
        j = j_ref[rs, :]
        u = uh_ref[rs, :].astype(F32) + ul_ref[rs, :].astype(F32)
        dj = du * (1.0 - (1.0 - s2) * jnp.exp2((s2 * r2) * j - r2 * u))
        dy = dj * (1.0 - (1.0 - s1) * jnp.exp2((s1 * r1) * y - r1 * j))
        for q, t in enumerate((dy, dy * y, dj * (y - j), du * (j - u))):
            sums[q] = sums[q] + row(t)
        return split(dy)

    def results(rs, dys):
        dh, dl = dys
        xs = xall[: 2 * n, rs]
        both = dot(xs, dh, NN)
        bw_ref[...] += both[:n] + both[n:] + dot(xs[:n], dl, NN)
        both = dot(whl, dh, NT)
        dx_ref[:, rs] = both[:n] + both[n:] + dot(wh, dl, NT)

    now = products(parts[0])
    before = None
    for k, rs in enumerate(parts):
        ahead = products(parts[k + 1]) if k + 1 < len(parts) else None
        if before is not None:
            results(parts[k - 1], before)
        before = middle(rs, *now)
        now = ahead
    results(parts[-1], before)
    for q, f in enumerate((1.0, 1.0, r1, r2)):
        sums_ref[q : q + 1, :] += sums[q] * f

    @pl.when(step == pl.num_programs(0) - 1)
    def _():
        bw_ref[...] = bw_ref[...] * a


def hop_back(h, in_w, x, wp, st, gain, shift, slope, mslope, dvh, dvl, mwh, mwl, j, uh, ul, tile):
    width, rows = x.shape
    hid = dvh.shape[1]
    n = wp.shape[1] // 3
    by = lambda w, k=0: pl.BlockSpec((tile, w), lambda i: (i, k))
    block = lambda r: pl.BlockSpec((r, hid), lambda i: (h, 0))
    return pl.pallas_call(
        functools.partial(hop_kernel, h, in_w),
        grid=(rows // tile,),
        in_specs=[
            pl.BlockSpec((width, tile), lambda i: (0, i)),
            pl.BlockSpec((1, 3 * n, hid), lambda i: (h, 0, 0)),
            whole(st),
        ]
        + [whole(t) for t in (gain, shift, slope, mslope)]
        + [by(hid), by(hid), block(hid), block(hid)]
        + [by(hid, h)] * 3,
        out_specs=[
            pl.BlockSpec((n, tile), lambda i: (0, i)),
            pl.BlockSpec((n, hid), lambda i: (0, 0)),
            pl.BlockSpec((4, hid), lambda i: (0, 0)),
        ],
        out_shape=[
            jax.ShapeDtypeStruct((n, rows), F32),
            jax.ShapeDtypeStruct((n, hid), F32),
            jax.ShapeDtypeStruct((4, hid), F32),
        ],
        compiler_params=params(),
        name=f"hop_back_{h}",
        cost_estimate=cost(14),
    )(x, wp, st, gain, shift, slope, mslope, dvh, dvl, mwh, mwl, j, uh, ul)


def pack_rows(n, hops, misc, unit=1):
    base = hops * n
    gram_at = base + misc + 4 * hops
    used = gram_at + hops * n // 4
    return base, gram_at, -(-used // unit) * unit


def pack_kernel(g_ref, misc_ref, *refs):
    hops = g_ref.shape[0]
    n = g_ref.shape[1]
    out_ref = refs[-1]
    base, gram_at, _ = pack_rows(n, hops, misc_ref.shape[0])
    total = out_ref.shape[0]
    for h in range(hops):
        out_ref[h * n : (h + 1) * n, :] = refs[h][...]
        k = base + misc_ref.shape[0] + 4 * h
        out_ref[k : k + 4, :] = refs[hops + h][...]
        for q in range(4):
            k = gram_at + h * n // 4
            out_ref[k : k + n // 4, q * LANES : (q + 1) * LANES] = g_ref[h, q * n // 4 : (q + 1) * n // 4, :]
    out_ref[base : base + misc_ref.shape[0], :] = misc_ref[...]
    used = gram_at + hops * n // 4
    if used < total:
        out_ref[used:, :] = jnp.zeros((total - used, out_ref.shape[1]), F32)


def pack(g, misc, bws, sums, unit):
    hid = misc.shape[1]
    total = pack_rows(g.shape[1], g.shape[0], misc.shape[0], unit)[2]
    return pl.pallas_call(
        pack_kernel,
        out_shape=jax.ShapeDtypeStruct((total, hid), F32),
        compiler_params=params(),
        name="pack",
        cost_estimate=cost(3),
    )(g, misc, *bws, *sums)


def fix_kernel(in_w, classes, misc, valid_ref, x_ref, p_ref, st_ref, gain_ref, shift_ref, wp_ref, *refs):
    step = pl.program_id(0)
    hops, hid = gain_ref.shape
    tile = x_ref.shape[1]
    n = wp_ref.shape[1] // 3
    dxs, rest = refs[:hops], refs[hops:]
    dx_ref, bw_ref, gain_out, shift_out, slope_out, mslope_out, oslope_out, hw_out, hb_out, loss_out, q_ref = rest
    base, gram_at, _ = pack_rows(n, hops, misc)
    mask = row_mask(valid_ref, step, tile, 1)

    @pl.when(step == 0)
    def _():
        count = count_of(st_ref)
        hw_out[...] = p_ref[base : base + classes, :]
        hb_out[...] = p_ref[base + classes : base + classes + 1, :classes]
        loss_out[...] = p_ref[base + classes : base + classes + 1, LANES : LANES + 1] / count
        oslope_out[...] = p_ref[base + classes + 1 : base + classes + 2, :]
        for h in range(hops):
            cols = slice(h * hid, (h + 1) * hid)
            mean, rstd = norm_of(st_ref, cols)
            gain = gain_ref[h : h + 1, :]
            at = base + misc + 4 * h
            total = LOG2E * p_ref[at : at + 1, :]
            gsum = (p_ref[at + 1 : at + 2, :] - shift_ref[h : h + 1, :] * total) / gain
            gain_out[h : h + 1, :] = gsum
            shift_out[h : h + 1, :] = total
            slope_out[h : h + 1, :] = p_ref[at + 2 : at + 3, :]
            mslope_out[h : h + 1, :] = p_ref[at + 3 : at + 4, :]
            a = gain * rstd / count
            c2 = a * gsum * rstd
            k0 = a * total - mean * c2
            wh, wl = wp_ref[h, :n, :], wp_ref[h, 2 * n :, :]
            wc = (wh.astype(F32) + wl.astype(F32)) * c2
            mask_row = lax.broadcasted_iota(jnp.int32, (n, hid), 0) == in_w
            wc = split(jnp.where(mask_row, k0, wc))
            q_ref[h, :, :n] = dot3((wh, wl), wc, NT)
            k = gram_at + h * n // 4
            g = jnp.concatenate(
                [p_ref[k : k + n // 4, q * LANES : q * LANES + n] for q in range(4)], axis=0
            )
            bw = p_ref[h * n : (h + 1) * n, :] - dot3(split(g), wc)
            bw_ref[:, h, :] = bw[:in_w]

    for h in range(hops):
        x = jnp.where(mask, hop_rows(x_ref, h, in_w, 1.0), 0.0)
        fix = dot3(split(q_ref[h, :, :n]), split(x))
        dx_ref[h * in_w : (h + 1) * in_w, :] = (dxs[h][...] - fix)[:in_w]


def fix(valid, x, packed, st, gain, shift, wp, dxs, in_w, classes, misc, tile):
    width, rows = x.shape
    hops, hid = gain.shape
    n = wp.shape[1] // 3
    cols = lambda r: pl.BlockSpec((r, tile), lambda i: (0, i))
    shapes = ((in_w, hops, hid),) + ((hops, hid),) * 4 + ((1, hid), (classes, hid), (1, classes), (1, 1))
    return pl.pallas_call(
        functools.partial(fix_kernel, in_w, classes, misc),
        grid=(rows // tile,),
        in_specs=[whole(valid), cols(width)]
        + [whole(t) for t in (packed, st, gain, shift, wp)]
        + [cols(n)] * hops,
        out_specs=[cols(width)] + [pl.BlockSpec(s, lambda i, s=s: (0,) * len(s)) for s in shapes],
        out_shape=[jax.ShapeDtypeStruct(s, F32) for s in ((width, rows),) + shapes],
        scratch_shapes=[pltpu.VMEM((hops, n, LANES), F32)],
        compiler_params=params(),
        name="fix",
        cost_estimate=cost(8),
    )(valid, x, packed, st, gain, shift, wp, *dxs)


def flip(v, axis, size, k):
    return lax.ppermute(v, axis, [(i, i ^ k) for i in range(size)])


def sum_small(v, sizes):
    steps = []
    for axis, size in sizes.items():
        k = 1
        if axis == "dp" and size >= 2:
            steps.append((axis, size, 1, 2))
            k = 2
        while k < size:
            wide = 4 if 4 * k <= size else 2
            steps.append((axis, size, k, wide))
            k *= wide
    for axis, size, k, wide in steps:
        if wide == 2:
            v = v + flip(v, axis, size, k)
        else:
            p1, p2, p3 = (flip(v, axis, size, k * m) for m in (1, 2, 3))
            v = (v + p1) + (p2 + p3)
    return v


def sum_tiny(v, sizes):
    n = sizes["dp"] * sizes["bucket"]
    copies = jnp.broadcast_to(v[None], (n,) + v.shape)
    return jnp.sum(lax.all_to_all(copies, ("dp", "bucket"), 0, 0, tiled=True), axis=0)


def pieces(v, n):
    size = v.shape[0] // n
    return [v[i * size : (i + 1) * size] for i in range(n)]


def take(v, index, n):
    size = v.shape[0] // n
    return lax.dynamic_slice_in_dim(v, index * size, size, 0)


def halve(v, axis, size, k):
    bit = lax.axis_index(axis) // k % 2
    return take(v, bit, 2) + flip(take(v, 1 - bit, 2), axis, size, k)


def double(v, axis, size, k):
    bit = lax.axis_index(axis) // k % 2
    got = flip(v, axis, size, k)
    return jnp.where(bit == 0, jnp.concatenate([v, got], 0), jnp.concatenate([got, v], 0))


def scatter_line(v, axis, size):
    if size != 4:
        for i in range(size.bit_length() - 1):
            v = halve(v, axis, size, 1 << i)
        return v
    me = lax.axis_index(axis)
    p0, p1, p2, p3 = (flip(take(v, me ^ k, 4), axis, 4, k) if k else take(v, me, 4) for k in range(4))
    return (p0 + p1) + (p2 + p3)


def gather_line(v, axis, size):
    if size != 4:
        for i in reversed(range(size.bit_length() - 1)):
            v = double(v, axis, size, 1 << i)
        return v
    me = lax.axis_index(axis)
    out = jnp.zeros((4 * v.shape[0],) + v.shape[1:], v.dtype)
    for k in range(4):
        got = flip(v, axis, 4, k) if k else v
        out = lax.dynamic_update_slice_in_dim(out, got, (me ^ k) * v.shape[0], 0)
    return out


def sum_stages(sizes):
    dp, bucket = sizes["dp"], sizes["bucket"]
    across = [("dp", dp, 1 << i) for i in range(1, dp.bit_length() - 1)]
    stages = []
    if dp > 1:
        stages.append(lambda v: halve(v, "dp", dp, 1))
    for a, b in zip(across, across[::-1]):
        stages.append(lambda v, a=a, b=b: jnp.concatenate([halve(pieces(v, 2)[0], *a), halve(pieces(v, 2)[1], *b)], 0))
    stages.append(lambda v: scatter_line(v, "bucket", bucket))
    stages.append(lambda v: gather_line(v, "bucket", bucket))
    for a, b in zip(across[::-1], across):
        stages.append(lambda v, a=a, b=b: jnp.concatenate([double(pieces(v, 2)[0], *a), double(pieces(v, 2)[1], *b)], 0))
    if dp > 1:
        stages.append(lambda v: double(v, "dp", dp, 1))
    return stages


def sum_large(v, sizes):
    for stage in sum_stages(sizes):
        v = stage(v)
    return v


def per_device(sizes, feats, labels, valid, branch_w, branch_gain, branch_shift, branch_slope, mix_slope,
               mix_w, mix_gain, mix_shift, out_slope, head_w, head_bias):
    rows, width = feats.shape
    hops, in_w, hid = branch_w.shape
    classes = head_w.shape[1]
    mix = hops * hid
    valid = valid.reshape(rows // LANES, LANES)
    labels = labels.reshape(rows // LANES, LANES)
    mslope = mix_slope.reshape(hops, hid)
    row = lambda t: t.reshape(1, -1)
    x = feats.T

    g, st, wp = gram(valid, x, branch_w.transpose(1, 0, 2), TILES["gram"])
    st = sum_small(st, sizes)
    j, uh, ul, v, st2, mwh, mwl = forward(
        valid, x, wp, st, branch_gain, branch_shift, branch_slope, mslope, mix_w, in_w, TILES["forward"]
    )
    st2 = sum_tiny(st2, sizes)
    dy2, st3, misc = head(
        valid, labels, v, st2, st, row(mix_gain), row(mix_shift), row(out_slope), head_w.T, row(head_bias),
        TILES["head"],
    )
    st3 = sum_tiny(st3, sizes)
    core = lax.axis_index("dp") % 2
    half = lambda i: jnp.reshape(i, (1,)).astype(jnp.int32)
    away, dvh, dvl = mix_back(
        half(1 - core), valid, dy2, v, st2, st, st3, row(mix_gain), uh, ul, TILES["mix"]
    )
    got = flip(away, "dp", sizes["dp"], 1) if sizes["dp"] > 1 else None
    m = mix_back_rest(half(core), dvh, dvl, uh, ul, TILES["mix"])
    if got is None:
        m = jnp.concatenate([m, away], 0)
    else:
        m, got, x = lax.optimization_barrier((m, got, x))
        m = m + got
    stages = sum_stages(sizes)
    rest = list(stages)
    if got is not None:
        stages = stages[1:]
    per_stage = [[] for _ in range(HOP_STAGES)]
    for h in range(hops):
        per_stage[h * HOP_STAGES // hops].append(h)
    dxs, bws, sums = [], [], []
    for i, now in enumerate(per_stage):
        m, x, bws, sums = lax.optimization_barrier((m, x, bws, sums))
        if i < len(stages):
            m = stages[i](m)
        for h in now:
            dx, bw, s = hop_back(
                h, in_w, x, wp, st, branch_gain, branch_shift, branch_slope, mslope, dvh, dvl, mwh, mwl,
                j, uh, ul, TILES["hop"],
            )
            dxs, bws, sums = dxs + [dx], bws + [bw], sums + [s]
    packed = pack(g, misc, bws, sums, max(128, 2 * sizes["dp"] * sizes["bucket"]))
    for stage in stages[HOP_STAGES:]:
        m, packed = lax.optimization_barrier((m, packed))
        m = stage(m)
        for _ in range(PACK_STAGES):
            if rest:
                packed = rest.pop(0)(packed)
    for stage in rest:
        packed = stage(packed)
    m, packed = lax.optimization_barrier((m, packed))
    d_x, bw, gain_grad, shift_grad, slope_grad, mslope_grad, oslope_grad, hw_grad, hb_grad, loss = fix(
        valid, x, packed, st, branch_gain, branch_shift, wp, dxs, in_w, classes, misc.shape[0], TILES["fix"]
    )
    return (
        loss.reshape(()),
        d_x.T,
        bw.transpose(1, 0, 2),
        gain_grad,
        shift_grad,
        slope_grad,
        mslope_grad.reshape(mix),
        m,
        st3[1],
        st3[0],
        oslope_grad.reshape(hid),
        hw_grad.T,
        hb_grad.reshape(classes),
    )


def solution(mesh):
    sizes = {axis: mesh.shape[axis] for axis in ("dp", "bucket")}
    split_rows = P(("dp", "bucket"), None)
    in_specs = (split_rows, P(("dp", "bucket")), P(("dp", "bucket"))) + (P(),) * 11
    out_specs = (P(), split_rows) + (P(),) * 11
    return jax.shard_map(
        functools.partial(per_device, sizes),
        mesh=mesh,
        in_specs=in_specs,
        out_specs=out_specs,
        check_vma=False,
    )
```

time: 369 us -> 276 us (0.75)
  Pallas kernels: 177 us -> 138 us
  starting transfers between devices: 67.9 us -> 45.4 us
  waiting for transfers between devices: 74.7 us -> 56.2 us
  local copies, waits for them, and re-layouts: 25.4 us -> 10 us
  blocking collectives: 0 us -> 10.1 us
  other arithmetic: 18.1 us -> 13.9 us
    pallas_call x11, Pallas kernels: 177 us -> 138 us  [the longest x4 54 us: hop_back(): pl.pallas_call(functools.partial(hop_kernel, h, in_w), grid=(rows // tile...]
    ppermute x64 -> x39, waiting for transfers between devices: 74.7 us -> 48 us  [flip(): return lax.ppermute(v, axis, [(i, i ^ k) for i in range(size)])]
    ppermute x64 -> x39, starting transfers between devices: 67.9 us -> 42.6 us  [flip(): return lax.ppermute(v, axis, [(i, i ^ k) for i in range(size)])]
    unnamed x26 -> x7, local copies, waits for them, and re-layouts: 14.4 us -> 1.31 us
    all_to_all x0 -> x1, blocking collectives: none -> 10.1 us  [sum_tiny(): lax.all_to_all(copies, ('dp', 'bucket'), 0, 0, tiled=True)]
    all_to_all x0 -> x1, waiting for transfers between devices: none -> 8.21 us  [sum_tiny(): lax.all_to_all(copies, ('dp', 'bucket'), 0, 0, tiled=True)]
    select_n x18 -> x10, other arithmetic: 6.16 us -> 8.2 us  [double(): jnp.where(bit == 0, jnp.concatenate([v, got], 0), jnp.concatenate([got, v...]
  transfers between devices with their start and end apart: 64 -> 40, of which waited for: 41 -> 24; matrix products, arithmetic and copies ran while one was open for 6% -> 3% of each run, Pallas kernels for 5% -> 25%
where the time goes in v2:
time: 276 us; the launch traced here: 275 us
  Pallas kernels  138 us (50%)
  waiting for transfers between devices  56.2 us (20%)
  starting transfers between devices  45.4 us (16%)
  other arithmetic  13.9 us (5%)
  blocking collectives  10.1 us (4%)
  local copies, waits for them, and re-layouts  10 us (4%)
    pallas_call x4, Pallas kernels, hop_back(): pl.pallas_call(functools.partial(hop_kernel, h, in_w), grid=(rows // tile...  54 us
    ppermute x39, waiting for transfers between devices, flip(): return lax.ppermute(v, axis, [(i, i ^ k) for i in range(size)])  48 us
    ppermute x39, starting transfers between devices, flip(): return lax.ppermute(v, axis, [(i, i ^ k) for i in range(size)])  42.6 us
    pallas_call x1, Pallas kernels, forward(): pl.pallas_call(functools.partial(forward_kernel, in_w), grid=(rows // til...  32.2 us
    pallas_call x1, Pallas kernels, mix_back(): pl.pallas_call(mix_first_kernel, grid_spec=pltpu.PrefetchScalarGridSpec(n...  15 us
    pallas_call x1, Pallas kernels, mix_back_rest(): pl.pallas_call(mix_second_kernel, grid_spec=pltpu.PrefetchScalarGridSpec(...  11 us
    all_to_all x1, blocking collectives, sum_tiny(): lax.all_to_all(copies, ('dp', 'bucket'), 0, 0, tiled=True)  10.1 us
    pallas_call x1, Pallas kernels, head(): pl.pallas_call(head_kernel, grid=(rows // tile,), in_specs=[whole(valid),...  9.67 us
  transfers between devices with their start and end apart: 40, of which 24 were waited for; matrix products, arithmetic and copies ran while one was open for 3% of the time, Pallas kernels for 25%

profile of v2, /device:TPU:0, one launch (start us, length us, event | category | flops | bytes accessed | tf_op | source)
XLA Modules:
  0.0 275.5 jit_solution(3619504599623680991)
XLA Ops:
  0.7 5.2 %gram.1 = (f32[4,112,128]{2,1,0:T(8,128)}, f32[2,2176]{1,0:T(2,128)}, bf16[4,336,512]{2,1,0:T(8,128)(2,1)}) custom-call(s32[16,128]{1,0:T(8,128)} %bitcast.29, f32[400,2048]{1,0:T(8,128)} %bitcast.21, f32[100,4,512]{2,1,0:T(4,128)} %bitcast.28), custom_call_target="tpu_custom_call" | custom-call | bytes 18450000 | tf_op jit(solution)/shard_map/gram/pallas_call | solution.py:115
  8.1 2.9 %collective-permute-start.1 = (f32[2,2176]{1,0:T(2,128)S(1)}, f32[2,2176]{1,0:T(2,128)S(1)}, u32[]{:S(2)}, u32[]{:S(2)}) collective-permute-start(f32[2,2176]{1,0:T(2,128)S(1)} %add.186), channel_id=1, source_target_pairs={{0,8},{4,12},{8,0},{12,4},{16,24},{20,28},{24,16},{28,20},{1,9},{5... | collective-permute-start | bytes 52232 | tf_op jit(solution)/shard_map/ppermute | solution.py:627
  11.0 1.5 collective-permute-start.2
  12.7 2.0 collective-permute-done.2
  14.7 2.4 collective-permute-done.3
  17.2 1.6 collective-permute-start.4
  18.8 2.6 collective-permute-start.5
  23.6 3.4 %collective-permute-done.6 = f32[2,2176]{1,0:T(2,128)S(1)} collective-permute-done((f32[2,2176]{1,0:T(2,128)S(1)}, f32[2,2176]{1,0:T(2,128)S(1)}, u32[]{:S(2)}, u32[]{:S(2)}) %collective-permute-start.6) | collective-permute-done | bytes 17440 | tf_op jit(solution)/shard_map/ppermute | solution.py:627
  27.6 32.2 %forward.1 = (f32[2048,2048]{1,0:T(8,128)}, bf16[2048,2048]{1,0:T(8,128)(2,1)}, bf16[2048,2048]{1,0:T(8,128)(2,1)}, f32[2048,512]{1,0:T(8,128)}, f32[2,512]{1,0:...) custom-call(s32[16,128]{1,0:T(8,128)} %bitcast.30, f32[400,2048]{1,0:T(8,128)} %bitcast.22, ...), custom_call_target="tpu_custom_call" | custom-call | bytes 110700000 | tf_op jit(solution)/shard_map/forward/pallas_call | solution.py:213
  60.5 10.1 %all_to_all.10 = f32[32,2,512]{2,1,0:T(2,128)S(1)} all-to-all(f32[32,2,512]{2,1,0:T(2,128)S(1)} %broadcast_in_dim.8), channel_id=1, replica_groups=mesh['dp'=8,'bucket'=4] {'dp','bucket'}, dimensions={0} | all-to-all | bytes 262144 | tf_op jit(solution)/shard_map/all_to_all | solution.py:653
  71.3 9.7 %head.1 = (f32[2048,512]{1,0:T(8,128)}, f32[2,512]{1,0:T(2,128)}, f32[56,512]{1,0:T(8,128)}) custom-call(s32[16,128]{1,0:T(8,128)} %bitcast.31, s32[16,128]{1,0:T(8,128)} %bitcast.35, f32[2048,512]{1,0:T(8,128)} %get-tuple-element.82.v_ref.refs_2_, f32[2,512]{1,0:T(2,128)} %reduce_sum.18.st_ref.refs_3_, f32[2,2176]{1,0:T(2,128)} %add_add_fusion.1.st_ref.cnt_ref.refs_4_, ...), custom_call_target="tpu_custom_call" | custom-call | bytes 33210000 | tf_op jit(solution)/shard_map/head/pallas_call | solution.py:317
  80.9 1.4 broadcast_in_dim.9
  82.3 2.8 %all-to-all-start.1 = ((f32[32,2,512]{2,1,0:T(2,128)}), f32[32,2,512]{2,1,0:T(2,128)S(1)}, u32[]{:S(2)}, u32[]{:S(2)}) async-start(f32[32,2,512]{2,1,0:T(2,128)} %broadcast_in_dim.9), calls=%async_computation.1 | async-start | bytes 262144 | tf_op jit(solution)/shard_map/all_to_all | solution.py:653
  85.1 8.2 %all-to-all-done.1 = f32[32,2,512]{2,1,0:T(2,128)S(1)} async-done(((f32[32,2,512]{2,1,0:T(2,128)}), f32[32,2,512]{2,1,0:T(2,128)S(1)}, u32[]{:S(2)}, u32[]{:S(2)}) %all-to-all-start.1) | async-done | bytes 131104 | tf_op jit(solution)/shard_map/all_to_all | solution.py:653
  93.9 15.0 %mix_back.1 = (f32[1024,512]{1,0:T(8,128)}, bf16[2048,512]{1,0:T(8,128)(2,1)}, bf16[2048,512]{1,0:T(8,128)(2,1)}) custom-call(s32[1]{0:T(128)} %bitcast.2.half_ref, s32[16,128]{1,0:T(8,128)} %bitcast.32, f32[2048,512]{1,0:T(8,128)} %get-tuple-element.84.refs_1_, f32[2048,512]{1,0:T(8,128)} %get-tuple-element.82.v_ref.refs_2_, ...), custom_call_target="tpu_custom_call" | custom-call | bytes 51660000 | tf_op jit(solution)/shard_map/mix_back/pallas_call | solution.py:376
  109.1 11.0 %mix_back_rest.1 = f32[1024,512]{1,0:T(8,128)} custom-call(s32[1]{0:T(128)} %bitcast.1.half_ref, bf16[2048,512]{1,0:T(8,128)(2,1)} %get-tuple-element.88.dvh_ref, bf16[2048,512]{1,0:T(8,128)(2,1)} %get-tuple-element.89.dvl_ref, bf16[2048,2048]{1,0:T(8,128)(2,1)} %get-tuple-element.86.refs_7_.uh_ref, bf16[2048,2048]{1,0:T(8,128)(2,1)} %get-tuple-element.87.refs_8_.ul_ref), custom_call_target="tpu_custom_call" | custom-call | bytes 44280000 | tf_op jit(solution)/shard_map/mix_back_rest/pallas_call | solution.py:401
  120.0 2.1 add.193
  125.3 13.5 %hop_back_1.1 = (f32[112,2048]{1,0:T(8,128)}, f32[112,512]{1,0:T(8,128)}, f32[4,512]{1,0:T(4,128)}) custom-call(f32[400,2048]{1,0:T(8,128)} %bitcast.23, bf16[4,336,512]{2,1,0:T(8,128)(2,1)} %get-tuple-element.80.wp_ref, f32[2,2176]{1,0:T(2,128)} %add_add_fusion.1.st_ref.cnt_ref.refs_4_, f32[4,512]{1,0:T(4,128)} %gain_ref.11, f32[4,512]{1,0:T(4,128)} %shift_ref.11, ...), custom_call_target="tpu_custom_call" | custom-call | bytes 51660000 | tf_op jit(solution)/shard_map/hop_back_1/pallas_call | solution.py:491
  138.8 13.4 %hop_back_0.1 = (f32[112,2048]{1,0:T(8,128)}, f32[112,512]{1,0:T(8,128)}, f32[4,512]{1,0:T(4,128)}) custom-call(f32[400,2048]{1,0:T(8,128)} %bitcast.24, bf16[4,336,512]{2,1,0:T(8,128)(2,1)} %get-tuple-element.80.wp_ref, f32[2,2176]{1,0:T(2,128)} %add_add_fusion.1.st_ref.cnt_ref.refs_4_, f32[4,512]{1,0:T(4,128)} %gain_ref.11, f32[4,512]{1,0:T(4,128)} %shift_ref.11, ...), custom_call_target="tpu_custom_call" | custom-call | bytes 51660000 | tf_op jit(solution)/shard_map/hop_back_0/pallas_call | solution.py:491
  152.6 1.6 collective-permute-start.10
  154.2 1.3 collective-permute-start.11
  155.5 13.6 %hop_back_2.1 = (f32[112,2048]{1,0:T(8,128)}, f32[112,512]{1,0:T(8,128)}, f32[4,512]{1,0:T(4,128)}) custom-call(f32[400,2048]{1,0:T(8,128)} %bitcast.25, bf16[4,336,512]{2,1,0:T(8,128)(2,1)} %get-tuple-element.80.wp_ref, f32[2,2176]{1,0:T(2,128)} %add_add_fusion.1.st_ref.cnt_ref.refs_4_, f32[4,512]{1,0:T(4,128)} %gain_ref.11, f32[4,512]{1,0:T(4,128)} %shift_ref.11, ...), custom_call_target="tpu_custom_call" | custom-call | bytes 51660000 | tf_op jit(solution)/shard_map/hop_back_2/pallas_call | solution.py:491
  169.6 1.5 collective-permute-start.13
  171.1 2.7 collective-permute-start.14
  173.8 13.5 %hop_back_3.1 = (f32[112,2048]{1,0:T(8,128)}, f32[112,512]{1,0:T(8,128)}, f32[4,512]{1,0:T(4,128)}) custom-call(f32[400,2048]{1,0:T(8,128)} %bitcast.26, bf16[4,336,512]{2,1,0:T(8,128)(2,1)} %get-tuple-element.80.wp_ref, f32[2,2176]{1,0:T(2,128)} %add_add_fusion.1.st_ref.cnt_ref.refs_4_, f32[4,512]{1,0:T(4,128)} %gain_ref.11, f32[4,512]{1,0:T(4,128)} %shift_ref.11, ...), custom_call_target="tpu_custom_call" | custom-call | bytes 51660000 | tf_op jit(solution)/shard_map/hop_back_3/pallas_call | solution.py:491
  187.3 2.5 pack.1
  191.4 1.6 collective-permute-start.16
  192.9 2.7 collective-permute-start.17
  195.7 2.7 collective-permute-done.15
  198.5 5.8 %collective-permute-done.16 = f32[64,512]{1,0:T(8,128)S(1)} collective-permute-done((f32[64,512]{1,0:T(8,128)S(1)}, f32[64,512]{1,0:T(8,128)S(1)}, u32[]{:S(2)}, u32[]{:S(2)}) %collective-permute-start.16) | collective-permute-done | bytes 131104 | tf_op jit(solution)/shard_map/ppermute | solution.py:627
  206.0 3.9 %collective-permute-done.19 = f32[80,512]{1,0:T(8,128)S(1)} collective-permute-done((f32[80,512]{1,0:T(8,128)S(1)}, f32[80,512]{1,0:T(8,128)S(1)}, u32[]{:S(2)}, u32[]{:S(2)}) %collective-permute-start.19) | collective-permute-done | bytes 163872 | tf_op jit(solution)/shard_map/ppermute | solution.py:627
  210.9 1.3 collective-permute-start.24
  213.0 2.4 collective-permute-done.24
  216.8 1.5 collective-permute-start.25
  218.7 2.5 collective-permute-start.27
  224.7 3.0 %collective-permute-done.21 = f32[128,512]{1,0:T(8,128)S(1)} collective-permute-done((f32[128,512]{1,0:T(8,128)S(1)}, f32[128,512]{1,0:T(8,128)S(1)}, u32[]{:S(2)}, u32[]{:S(2)}) %collective-permute-start.21) | collective-permute-done | bytes 262176 | tf_op jit(solution)/shard_map/ppermute | solution.py:627
  228.9 1.6 collective-permute-start.31
  230.5 2.5 collective-permute-start.32
  236.7 1.3 collective-permute-start.33
  239.9 1.3 collective-permute-done.33
  241.2 2.6 collective-permute-done.34
  244.0 3.2 %collective-permute-done.29 = f32[256,512]{1,0:T(8,128)S(1)} collective-permute-done((f32[256,512]{1,0:T(8,128)S(1)}, f32[256,512]{1,0:T(8,128)S(1)}, u32[]{:S(2)}, u32[]{:S(2)}) %collective-permute-start.29) | collective-permute-done | bytes 524320 | tf_op jit(solution)/shard_map/ppermute | solution.py:627
  249.7 4.6 %collective-permute-done.36 = f32[80,512]{1,0:T(8,128)S(1)} collective-permute-done((f32[80,512]{1,0:T(8,128)S(1)}, f32[80,512]{1,0:T(8,128)S(1)}, u32[]{:S(2)}, u32[]{:S(2)}) %collective-permute-start.36) | collective-permute-done | bytes 163872 | tf_op jit(solution)/shard_map/ppermute | solution.py:627
  255.9 1.6 collective-permute-done.38
  257.5 2.6 maximum_select_fusion.1.p_ref
  260.1 5.3 %maximum_select_fusion = f32[2048,512]{1,0:T(8,128)} fusion(f32[1024,512]{1,0:T(8,128)} %collective-permute-done.35, f32[1024,512]{1,0:T(8,128)S(1)} %pad_maximum_fusion, pred[]{:T(512)S(6)} %eq.37), kind=kLoop, calls=%fused_computation | loop fusion | flops 3145728 | bytes 8388609 | tf_op jit(solution)/shard_map/jit(_where)/select_n | solution.py:674
  265.3 8.8 %fix.1 = (f32[400,2048]{1,0:T(8,128)}, f32[100,4,512]{2,1,0:T(4,128)}, f32[4,512]{1,0:T(4,128)}, f32[4,512]{1,0:T(4,128)}, f32[4,512]{1,0:T(4,128)}, /*index=5*/...) custom-call(s32[16,128]{1,0:T(8,128)} %bitcast.33, ...), custom_call_target="tpu_custom_call" | custom-call | bytes 29520000 | tf_op jit(solution)/shard_map/fix/pallas_call | solution.py:611
  274.2 1.3 copy.31
  (118 shorter events, 32.2 us)
Async XLA Ops:
  0.6 21.0 %copy-start.2 = (f32[2048]{0:T(1024)S(1)}, f32[2048]{0:T(1024)}, u32[]{:S(2)}) copy-start(f32[2048]{0:T(1024)} %param.21) | copy-start | bytes 24580
  5.9 1.5 collective-permute-start
  8.1 4.6 %collective-permute-start.1 = (f32[2,2176]{1,0:T(2,128)S(1)}, f32[2,2176]{1,0:T(2,128)S(1)}, u32[]{:S(2)}, u32[]{:S(2)}) collective-permute-start(f32[2,2176]{1,0:T(2,128)S(1)} %add.186), channel_id=1, source_target_pairs={{0,8},{4,12},{8,0},{12,4},{16,24},{20,28},{24,16},{28,20},{1,9},{5... | collective-permute-start | bytes 52232 | tf_op jit(solution)/shard_map/ppermute | solution.py:627
  11.0 3.8 %collective-permute-start.2 = (f32[2,2176]{1,0:T(2,128)S(1)}, f32[2,2176]{1,0:T(2,128)S(1)}, u32[]{:S(2)}, u32[]{:S(2)}) collective-permute-start(f32[2,2176]{1,0:T(2,128)S(1)} %add.186), channel_id=1, source_target_pairs={{0,16},{4,20},{8,24},{12,28},{16,0},{20,4},{24,8},{28,12},{1,17},{... | collective-permute-start | bytes 52232 | tf_op jit(solution)/shard_map/ppermute | solution.py:627
  12.5 4.6 %collective-permute-start.3 = (f32[2,2176]{1,0:T(2,128)S(1)}, f32[2,2176]{1,0:T(2,128)S(1)}, u32[]{:S(2)}, u32[]{:S(2)}) collective-permute-start(f32[2,2176]{1,0:T(2,128)S(1)} %add.186), channel_id=1, source_target_pairs={{0,24},{4,28},{8,16},{12,20},{16,8},{20,12},{24,0},{28,4},{1,25},{... | collective-permute-start | bytes 52232 | tf_op jit(solution)/shard_map/ppermute | solution.py:627
  17.2 5.1 %collective-permute-start.4 = (f32[2,2176]{1,0:T(2,128)S(1)}, f32[2,2176]{1,0:T(2,128)S(1)}, u32[]{:S(2)}, u32[]{:S(2)}) collective-permute-start(f32[2,2176]{1,0:T(2,128)S(1)} %add_add_fusion.2), channel_id=1, source_target_pairs={{0,1},{1,0},{2,3},{3,2},{4,5},{5,4},{6,7},{7,6},{8,9},{9,8},{10,11... | collective-permute-start | bytes 52232 | tf_op jit(solution)/shard_map/ppermute | solution.py:627
  18.8 4.7 %collective-permute-start.5 = (f32[2,2176]{1,0:T(2,128)S(1)}, f32[2,2176]{1,0:T(2,128)S(1)}, u32[]{:S(2)}, u32[]{:S(2)}) collective-permute-start(f32[2,2176]{1,0:T(2,128)S(1)} %add_add_fusion.2), channel_id=1, source_target_pairs={{0,2},{1,3},{2,0},{3,1},{4,6},{5,7},{6,4},{7,5},{8,10},{9,11},{10,... | collective-permute-start | bytes 52232 | tf_op jit(solution)/shard_map/ppermute | solution.py:627
  21.4 5.5 %collective-permute-start.6 = (f32[2,2176]{1,0:T(2,128)S(1)}, f32[2,2176]{1,0:T(2,128)S(1)}, u32[]{:S(2)}, u32[]{:S(2)}) collective-permute-start(f32[2,2176]{1,0:T(2,128)S(1)} %add_add_fusion.2), channel_id=1, source_target_pairs={{0,3},{1,2},{2,1},{3,0},{4,7},{5,6},{6,5},{7,4},{8,11},{9,10},{10,... | collective-permute-start | bytes 52232 | tf_op jit(solution)/shard_map/ppermute | solution.py:627
  82.3 11.0 %all-to-all-start.1 = ((f32[32,2,512]{2,1,0:T(2,128)}), f32[32,2,512]{2,1,0:T(2,128)S(1)}, u32[]{:S(2)}, u32[]{:S(2)}) async-start(f32[32,2,512]{2,1,0:T(2,128)} %broadcast_in_dim.9), calls=%async_computation.1 | async-start | bytes 262144 | tf_op jit(solution)/shard_map/all_to_all | solution.py:653
  108.9 11.1 %collective-permute-start.7 = (f32[1024,512]{1,0:T(8,128)}, f32[1024,512]{1,0:T(8,128)S(1)}, u32[]{:S(2)}, u32[]{:S(2)}) collective-permute-start(f32[1024,512]{1,0:T(8,128)} %get-tuple-element.90), channel_id=1, source_target_pairs={{0,4},{4,0},{8,12},{12,8},{16,20},{20,16},{24,28},{28,24},{1,5},{5... | collective-permute-start | bytes 6291464 | tf_op jit(solution)/shard_map/ppermute | solution.py:627
  123.1 29.1 %collective-permute-start.8 = (f32[256,512]{1,0:T(8,128)}, f32[256,512]{1,0:T(8,128)S(1)}, u32[]{:S(2)}, u32[]{:S(2)}) collective-permute-start(f32[256,512]{1,0:T(8,128)} %constant_dynamic-slice_fusion.11), channel_id=1, source_target_pairs={{0,8},{4,12},{8,0},{12,4},{16,24},{20,28},{24,16},{28,20},{1,9},{5... | collective-permute-start | bytes 1572872 | tf_op jit(solution)/shard_map/ppermute | solution.py:627
  124.7 27.6 %collective-permute-start.9 = (f32[256,512]{1,0:T(8,128)}, f32[256,512]{1,0:T(8,128)S(1)}, u32[]{:S(2)}, u32[]{:S(2)}) collective-permute-start(f32[256,512]{1,0:T(8,128)} %constant_dynamic-slice_fusion.10), channel_id=1, source_target_pairs={{0,16},{4,20},{8,24},{12,28},{16,0},{20,4},{24,8},{28,12},{1,17},{... | collective-permute-start | bytes 1572872 | tf_op jit(solution)/shard_map/ppermute | solution.py:627
  152.6 16.5 %collective-permute-start.10 = (f32[128,512]{1,0:T(8,128)S(1)}, f32[128,512]{1,0:T(8,128)S(1)}, u32[]{:S(2)}, u32[]{:S(2)}) collective-permute-start(f32[128,512]{1,0:T(8,128)S(1)} %constant_dynamic-slice_fusion.9), channel_id=1, source_target_pairs={{0,16},{4,20},{8,24},{12,28},{16,0},{20,4},{24,8},{28,12},{1,17},{... | collective-permute-start | bytes 786440 | tf_op jit(solution)/shard_map/ppermute | solution.py:627
  154.2 15.0 %collective-permute-start.11 = (f32[128,512]{1,0:T(8,128)S(1)}, f32[128,512]{1,0:T(8,128)S(1)}, u32[]{:S(2)}, u32[]{:S(2)}) collective-permute-start(f32[128,512]{1,0:T(8,128)S(1)} %constant_dynamic-slice_fusion.8), channel_id=1, source_target_pairs={{0,8},{4,12},{8,0},{12,4},{16,24},{20,28},{24,16},{28,20},{1,9},{5... | collective-permute-start | bytes 786440 | tf_op jit(solution)/shard_map/ppermute | solution.py:627
  169.3 20.5 %collective-permute-start.12 = (f32[64,512]{1,0:T(8,128)S(1)}, f32[64,512]{1,0:T(8,128)S(1)}, u32[]{:S(2)}, u32[]{:S(2)}) collective-permute-start(f32[64,512]{1,0:T(8,128)S(1)} %get-tuple-element.157), channel_id=1, source_target_pairs={{0,1},{1,0},{2,3},{3,2},{4,5},{5,4},{6,7},{7,6},{8,9},{9,8},{10,11... | collective-permute-start | bytes 393224 | tf_op jit(solution)/shard_map/ppermute | solution.py:627
  169.6 20.2 %collective-permute-start.13 = (f32[64,512]{1,0:T(8,128)S(1)}, f32[64,512]{1,0:T(8,128)S(1)}, u32[]{:S(2)}, u32[]{:S(2)}) collective-permute-start(f32[64,512]{1,0:T(8,128)S(1)} %get-tuple-element.159), channel_id=1, source_target_pairs={{0,2},{1,3},{2,0},{3,1},{4,6},{5,7},{6,4},{7,5},{8,10},{9,11},{10,... | collective-permute-start | bytes 393224 | tf_op jit(solution)/shard_map/ppermute | solution.py:627
  171.1 18.7 %collective-permute-start.14 = (f32[64,512]{1,0:T(8,128)S(1)}, f32[64,512]{1,0:T(8,128)S(1)}, u32[]{:S(2)}, u32[]{:S(2)}) collective-permute-start(f32[64,512]{1,0:T(8,128)S(1)} %get-tuple-element.158), channel_id=1, source_target_pairs={{0,3},{1,2},{2,1},{3,0},{4,7},{5,6},{6,5},{7,4},{8,11},{9,10},{10,... | collective-permute-start | bytes 393224 | tf_op jit(solution)/shard_map/ppermute | solution.py:627
  189.8 14.5 %copy-start = (f32[640,512]{1,0:T(8,128)S(1)}, f32[640,512]{1,0:T(8,128)}, u32[]{:S(2)}) copy-start(f32[640,512]{1,0:T(8,128)} %pack.1) | copy-start | bytes 3932164
  191.1 13.2 %collective-permute-start.18 = (f32[320,512]{1,0:T(8,128)S(1)}, f32[320,512]{1,0:T(8,128)S(1)}, u32[]{:S(2)}, u32[]{:S(2)}) collective-permute-start(f32[320,512]{1,0:T(8,128)S(1)} %constant_dynamic-slice_fusion.4), channel_id=1, source_target_pairs={{0,4},{4,0},{8,12},{12,8},{16,20},{20,16},{24,28},{28,24},{1,5},{5... | collective-permute-start | bytes 1966088 | tf_op jit(solution)/shard_map/ppermute | solution.py:627
  191.2 7.3 %collective-permute-start.15 = (f32[64,512]{1,0:T(8,128)S(1)}, f32[64,512]{1,0:T(8,128)S(1)}, u32[]{:S(2)}, u32[]{:S(2)}) collective-permute-start(f32[64,512]{1,0:T(8,128)S(1)} %add_add_fusion), channel_id=1, source_target_pairs={{0,1},{1,0},{2,3},{3,2},{4,5},{5,4},{6,7},{7,6},{8,9},{9,8},{10,11... | collective-permute-start | bytes 393224 | tf_op jit(solution)/shard_map/ppermute | solution.py:627
  191.4 12.9 %collective-permute-start.16 = (f32[64,512]{1,0:T(8,128)S(1)}, f32[64,512]{1,0:T(8,128)S(1)}, u32[]{:S(2)}, u32[]{:S(2)}) collective-permute-start(f32[64,512]{1,0:T(8,128)S(1)} %add_add_fusion), channel_id=1, source_target_pairs={{0,2},{1,3},{2,0},{3,1},{4,6},{5,7},{6,4},{7,5},{8,10},{9,11},{10,... | collective-permute-start | bytes 393224 | tf_op jit(solution)/shard_map/ppermute | solution.py:627
  192.9 12.4 %collective-permute-start.17 = (f32[64,512]{1,0:T(8,128)S(1)}, f32[64,512]{1,0:T(8,128)S(1)}, u32[]{:S(2)}, u32[]{:S(2)}) collective-permute-start(f32[64,512]{1,0:T(8,128)S(1)} %add_add_fusion), channel_id=1, source_target_pairs={{0,3},{1,2},{2,1},{3,0},{4,7},{5,6},{6,5},{7,4},{8,11},{9,10},{10,... | collective-permute-start | bytes 393224 | tf_op jit(solution)/shard_map/ppermute | solution.py:627
  204.5 5.4 %collective-permute-start.19 = (f32[80,512]{1,0:T(8,128)S(1)}, f32[80,512]{1,0:T(8,128)S(1)}, u32[]{:S(2)}, u32[]{:S(2)}) collective-permute-start(f32[80,512]{1,0:T(8,128)S(1)} %constant_dynamic-slice_fusion.3), channel_id=1, source_target_pairs={{0,8},{4,12},{8,0},{12,4},{16,24},{20,28},{24,16},{28,20},{1,9},{5... | collective-permute-start | bytes 491528 | tf_op jit(solution)/shard_map/ppermute | solution.py:627
  205.4 5.4 %collective-permute-start.20 = (f32[80,512]{1,0:T(8,128)S(1)}, f32[80,512]{1,0:T(8,128)S(1)}, u32[]{:S(2)}, u32[]{:S(2)}) collective-permute-start(f32[80,512]{1,0:T(8,128)S(1)} %constant_dynamic-slice_fusion.2), channel_id=1, source_target_pairs={{0,16},{4,20},{8,24},{12,28},{16,0},{20,4},{24,8},{28,12},{1,17},{... | collective-permute-start | bytes 491528 | tf_op jit(solution)/shard_map/ppermute | solution.py:627
  210.9 4.5 %collective-permute-start.24 = (f32[40,512]{1,0:T(8,128)S(1)}, f32[40,512]{1,0:T(8,128)S(1)}, u32[]{:S(2)}, u32[]{:S(2)}) collective-permute-start(f32[40,512]{1,0:T(8,128)S(1)} %constant_dynamic-slice_fusion), channel_id=1, source_target_pairs={{0,8},{4,12},{8,0},{12,4},{16,24},{20,28},{24,16},{28,20},{1,9},{5... | collective-permute-start | bytes 245768 | tf_op jit(solution)/shard_map/ppermute | solution.py:627
  212.2 4.4 %collective-permute-start.23 = (f32[40,512]{1,0:T(8,128)S(1)}, f32[40,512]{1,0:T(8,128)S(1)}, u32[]{:S(2)}, u32[]{:S(2)}) collective-permute-start(f32[40,512]{1,0:T(8,128)S(1)} %constant_dynamic-slice_fusion.1), channel_id=1, source_target_pairs={{0,16},{4,20},{8,24},{12,28},{16,0},{20,4},{24,8},{28,12},{1,17},{... | collective-permute-start | bytes 245768 | tf_op jit(solution)/shard_map/ppermute | solution.py:627
  216.8 6.1 %collective-permute-start.25 = (f32[20,512]{1,0:T(8,128)S(1)}, f32[20,512]{1,0:T(8,128)S(1)}, u32[]{:S(2)}, u32[]{:S(2)}) collective-permute-start(f32[20,512]{1,0:T(8,128)S(1)} %get-tuple-element.167), channel_id=1, source_target_pairs={{0,1},{1,0},{2,3},{3,2},{4,5},{5,4},{6,7},{7,6},{8,9},{9,8},{10,11... | collective-permute-start | bytes 122888 | tf_op jit(solution)/shard_map/ppermute | solution.py:627
  218.2 5.5 %collective-permute-start.26 = (f32[20,512]{1,0:T(8,128)S(1)}, f32[20,512]{1,0:T(8,128)S(1)}, u32[]{:S(2)}, u32[]{:S(2)}) collective-permute-start(f32[20,512]{1,0:T(8,128)S(1)} %get-tuple-element.168), channel_id=1, source_target_pairs={{0,2},{1,3},{2,0},{3,1},{4,6},{5,7},{6,4},{7,5},{8,10},{9,11},{10,... | collective-permute-start | bytes 122888 | tf_op jit(solution)/shard_map/ppermute | solution.py:627
  218.7 6.0 %collective-permute-start.27 = (f32[20,512]{1,0:T(8,128)S(1)}, f32[20,512]{1,0:T(8,128)S(1)}, u32[]{:S(2)}, u32[]{:S(2)}) collective-permute-start(f32[20,512]{1,0:T(8,128)S(1)} %get-tuple-element.166), channel_id=1, source_target_pairs={{0,3},{1,2},{2,1},{3,0},{4,7},{5,6},{6,5},{7,4},{8,11},{9,10},{10,... | collective-permute-start | bytes 122888 | tf_op jit(solution)/shard_map/ppermute | solution.py:627
  221.3 6.4 %collective-permute-start.21 = (f32[128,512]{1,0:T(8,128)S(1)}, f32[128,512]{1,0:T(8,128)S(1)}, u32[]{:S(2)}, u32[]{:S(2)}) collective-permute-start(f32[128,512]{1,0:T(8,128)S(1)} %get-tuple-element.155), channel_id=1, source_target_pairs={{0,16},{4,20},{8,24},{12,28},{16,0},{20,4},{24,8},{28,12},{1,17},{... | collective-permute-start | bytes 786440 | tf_op jit(solution)/shard_map/ppermute | solution.py:627
  222.1 6.4 %collective-permute-start.22 = (f32[128,512]{1,0:T(8,128)S(1)}, f32[128,512]{1,0:T(8,128)S(1)}, u32[]{:S(2)}, u32[]{:S(2)}) collective-permute-start(f32[128,512]{1,0:T(8,128)S(1)} %get-tuple-element.156), channel_id=1, source_target_pairs={{0,8},{4,12},{8,0},{12,4},{16,24},{20,28},{24,16},{28,20},{1,9},{5... | collective-permute-start | bytes 786440 | tf_op jit(solution)/shard_map/ppermute | solution.py:627
  228.6 5.9 %collective-permute-start.30 = (f32[20,512]{1,0:T(8,128)S(1)}, f32[20,512]{1,0:T(8,128)S(1)}, u32[]{:S(2)}, u32[]{:S(2)}) collective-permute-start(f32[20,512]{1,0:T(8,128)S(1)} %fusion.3), channel_id=1, source_target_pairs={{0,1},{1,0},{2,3},{3,2},{4,5},{5,4},{6,7},{7,6},{8,9},{9,8},{10,11... | collective-permute-start | bytes 122888 | tf_op jit(solution)/shard_map/ppermute | solution.py:627
  228.9 6.1 %collective-permute-start.31 = (f32[20,512]{1,0:T(8,128)S(1)}, f32[20,512]{1,0:T(8,128)S(1)}, u32[]{:S(2)}, u32[]{:S(2)}) collective-permute-start(f32[20,512]{1,0:T(8,128)S(1)} %fusion.3), channel_id=1, source_target_pairs={{0,2},{1,3},{2,0},{3,1},{4,6},{5,7},{6,4},{7,5},{8,10},{9,11},{10,... | collective-permute-start | bytes 122888 | tf_op jit(solution)/shard_map/ppermute | solution.py:627
  230.5 5.9 %collective-permute-start.32 = (f32[20,512]{1,0:T(8,128)S(1)}, f32[20,512]{1,0:T(8,128)S(1)}, u32[]{:S(2)}, u32[]{:S(2)}) collective-permute-start(f32[20,512]{1,0:T(8,128)S(1)} %fusion.3), channel_id=1, source_target_pairs={{0,3},{1,2},{2,1},{3,0},{4,7},{5,6},{6,5},{7,4},{8,11},{9,10},{10,... | collective-permute-start | bytes 122888 | tf_op jit(solution)/shard_map/ppermute | solution.py:627
  233.7 10.2 %collective-permute-start.28 = (f32[256,512]{1,0:T(8,128)S(1)}, f32[256,512]{1,0:T(8,128)S(1)}, u32[]{:S(2)}, u32[]{:S(2)}) collective-permute-start(f32[256,512]{1,0:T(8,128)S(1)} %get-tuple-element.149), channel_id=1, source_target_pairs={{0,8},{4,12},{8,0},{12,4},{16,24},{20,28},{24,16},{28,20},{1,9},{5... | collective-permute-start | bytes 1572872 | tf_op jit(solution)/shard_map/ppermute | solution.py:627
  236.7 4.5 %collective-permute-start.33 = (f32[40,512]{1,0:T(8,128)S(1)}, f32[40,512]{1,0:T(8,128)S(1)}, u32[]{:S(2)}, u32[]{:S(2)}) collective-permute-start(f32[40,512]{1,0:T(8,128)S(1)} %get-tuple-element.164), channel_id=1, source_target_pairs={{0,16},{4,20},{8,24},{12,28},{16,0},{20,4},{24,8},{28,12},{1,17},{... | collective-permute-start | bytes 245768 | tf_op jit(solution)/shard_map/ppermute | solution.py:627
  238.0 9.2 %collective-permute-start.29 = (f32[256,512]{1,0:T(8,128)S(1)}, f32[256,512]{1,0:T(8,128)S(1)}, u32[]{:S(2)}, u32[]{:S(2)}) collective-permute-start(f32[256,512]{1,0:T(8,128)S(1)} %get-tuple-element.150), channel_id=1, source_target_pairs={{0,16},{4,20},{8,24},{12,28},{16,0},{20,4},{24,8},{28,12},{1,17},{... | collective-permute-start | bytes 1572872 | tf_op jit(solution)/shard_map/ppermute | solution.py:627
  238.8 5.0 %collective-permute-start.34 = (f32[40,512]{1,0:T(8,128)S(1)}, f32[40,512]{1,0:T(8,128)S(1)}, u32[]{:S(2)}, u32[]{:S(2)}) collective-permute-start(f32[40,512]{1,0:T(8,128)S(1)} %get-tuple-element.165), channel_id=1, source_target_pairs={{0,8},{4,12},{8,0},{12,4},{16,24},{20,28},{24,16},{28,20},{1,9},{5... | collective-permute-start | bytes 245768 | tf_op jit(solution)/shard_map/ppermute | solution.py:627
  247.5 7.8 %copy-start.1 = (f32[2,512]{1,0:T(2,128)S(1)}, f32[2,512]{1,0:T(2,128)}, u32[]{:S(2)}) copy-start(f32[2,512]{1,0:T(2,128)} %reduce_sum.19.refs_5_) | copy-start | bytes 12292
  247.5 12.6 %collective-permute-start.35 = (f32[1024,512]{1,0:T(8,128)S(1)}, f32[1024,512]{1,0:T(8,128)}, u32[]{:S(2)}, u32[]{:S(2)}) collective-permute-start(f32[1024,512]{1,0:T(8,128)S(1)} %pad_maximum_fusion), channel_id=1, source_target_pairs={{0,4},{4,0},{8,12},{12,8},{16,20},{20,16},{24,28},{28,24},{1,5},{5... | collective-permute-start | bytes 6291464 | tf_op jit(solution)/shard_map/ppermute | solution.py:627
  247.6 6.7 %collective-permute-start.36 = (f32[80,512]{1,0:T(8,128)S(1)}, f32[80,512]{1,0:T(8,128)S(1)}, u32[]{:S(2)}, u32[]{:S(2)}) collective-permute-start(f32[80,512]{1,0:T(8,128)S(1)} %get-tuple-element.160), channel_id=1, source_target_pairs={{0,8},{4,12},{8,0},{12,4},{16,24},{20,28},{24,16},{28,20},{1,9},{5... | collective-permute-start | bytes 491528 | tf_op jit(solution)/shard_map/ppermute | solution.py:627
  248.8 6.3 %collective-permute-start.37 = (f32[80,512]{1,0:T(8,128)S(1)}, f32[80,512]{1,0:T(8,128)S(1)}, u32[]{:S(2)}, u32[]{:S(2)}) collective-permute-start(f32[80,512]{1,0:T(8,128)S(1)} %get-tuple-element.161), channel_id=1, source_target_pairs={{0,16},{4,20},{8,24},{12,28},{16,0},{20,4},{24,8},{28,12},{1,17},{... | collective-permute-start | bytes 491528 | tf_op jit(solution)/shard_map/ppermute | solution.py:627
  255.2 2.3 collective-permute-start.38

commit v3 on v2

--- a/solution.py
+++ b/solution.py
@@ -11,14 +11,13 @@
 F32 = jnp.float32
 BF16 = jnp.bfloat16
 LANES = 128
-VMEM = 56 * 1024 * 1024
 LOG2E = 1.4426950408889634
 LN2 = 0.6931471805599453
-TILES = {"gram": 1024, "forward": 512, "head": 512, "mix": 512, "hop": 512, "fix": 512}
-HOP_STAGES = 3
-PACK_STAGES = 2
+TILES = {"gram": 2048, "forward": 512, "head": 512, "mix": 512, "hop": 512, "fix": 1024}
+PACK_STEPS = 2
 SUB = 256
-CHUNK = 512
+MIX_SUB = 256
+COLS = 512
 NN = (((1,), (0,)), ((), ()))
 NT = (((1,), (1,)), ((), ()))
 TN = (((0,), (0,)), ((), ()))
@@ -44,12 +43,21 @@
     return pl.CostEstimate(flops=0, bytes_accessed=int(us * 3.69e6), transcendentals=0)
 
 
-def params(**kw):
-    return pltpu.CompilerParams(vmem_limit_bytes=VMEM, **kw)
-
-
-def whole(x):
-    return pl.BlockSpec(x.shape, lambda *_: (0,) * len(x.shape))
+def params(mib):
+    return pltpu.CompilerParams(vmem_limit_bytes=mib * 1024 * 1024)
+
+
+def near(x):
+    return pltpu.with_memory_space_constraint(x, pltpu.VMEM)
+
+
+def far(x):
+    return pltpu.with_memory_space_constraint(x, pltpu.HBM)
+
+
+def whole(x, buffers=2):
+    mode = {} if buffers == 2 else {"pipeline_mode": pl.Buffered(buffers)}
+    return pl.BlockSpec(x.shape, lambda *_: (0,) * len(x.shape), **mode)
 
 
 def row_mask(valid_ref, step, tile, axis=0):
@@ -111,17 +119,17 @@
     width, rows = x.shape
     in_w, hops, hid = w.shape
     n = -(-(in_w + 1) // 16) * 16
-    shapes = ((hops, n, LANES), F32), ((2, hops * hid + LANES), F32), ((hops, 3 * n, hid), BF16)
+    shapes = (hops, n, LANES), (2, hops * hid + LANES), (hops, 3 * n, hid)
     return pl.pallas_call(
         functools.partial(gram_kernel, in_w),
         grid=(rows // tile,),
         in_specs=[whole(valid), pl.BlockSpec((width, tile), lambda i: (0, i)), whole(w)],
-        out_specs=[pl.BlockSpec(s, lambda i, s=s: (0,) * len(s)) for s, _ in shapes],
-        out_shape=[jax.ShapeDtypeStruct(*s) for s in shapes],
-        compiler_params=params(),
+        out_specs=[pl.BlockSpec(s, lambda i, s=s: (0,) * len(s)) for s in shapes],
+        out_shape=[jax.ShapeDtypeStruct(s, F32) for s in shapes[:2]] + [pltpu.HBM(shapes[2], BF16)],
+        compiler_params=params(32),
         name="gram",
         cost_estimate=cost(5),
-    )(valid, x, w)
+    )(valid, far(x), w)
 
 
 def count_of(st_ref):
@@ -143,7 +151,7 @@
 
 def forward_kernel(
     in_w, valid_ref, x_ref, wp_ref, st_ref, gain_ref, shift_ref, slope_ref, mslope_ref, w_ref,
-    j_ref, uh_ref, ul_ref, v_ref, st2_ref, wh_ref, wl_ref,
+    j_ref, uh_ref, ul_ref, v_ref, copies_ref, wh_ref, wl_ref, st2_ref,
 ):
     step = pl.program_id(0)
     tile = x_ref.shape[1]
@@ -158,36 +166,36 @@
             wh_ref[rows, :], wl_ref[rows, :] = split(w_ref[rows, :])
 
     dot = functools.partial(lax.dot_general, preferred_element_type=F32)
-    chunks = [(h, slice(r, r + CHUNK)) for h in range(hops) for r in range(0, tile, CHUNK)]
+    chunks = [(h, c) for h in range(hops) for c in range(0, hid, COLS)]
     scales, xs = {}, {}
 
     def project(i):
-        h, rows = chunks[i]
+        h, c = chunks[i]
         if h not in xs:
             xs[h] = stack3(hop_rows(x_ref, h, in_w))
-        return dot(xs[h][:, rows], wp_ref[h], TN)
+        return dot(xs[h], wp_ref[h, :, c : c + COLS], TN)
 
     def activate(i, z):
-        h, rows = chunks[i]
-        cols = slice(h * hid, (h + 1) * hid)
+        h, c = chunks[i]
         if h not in scales:
-            scales[h] = scale_of(st_ref, cols, gain_ref, shift_ref, h)
-        a, b = scales[h]
-        s1 = slope_ref[h : h + 1, :]
-        s2 = mslope_ref[h : h + 1, :]
+            scales[h] = scale_of(st_ref, slice(h * hid, (h + 1) * hid), gain_ref, shift_ref, h)
+        part = slice(c, c + COLS)
+        cols = slice(h * hid + c, h * hid + c + COLS)
+        a, b = (t[:, part] for t in scales[h])
+        s1 = slope_ref[h : h + 1, part]
+        s2 = mslope_ref[h : h + 1, part]
         j = act2(z * a + b, s1, LOG2E * (1.0 - s1))
         u = act2(j, s2, LOG2E * (1.0 - s2))
-        j_ref[rows, cols] = j
+        j_ref[:, cols] = j
         us = split(u)
-        uh_ref[rows, cols], ul_ref[rows, cols] = us
+        uh_ref[:, cols], ul_ref[:, cols] = us
         return us
 
     def mix(i, us):
-        h, rows = chunks[i]
-        cols = slice(h * hid, (h + 1) * hid)
-        both = dot(jnp.concatenate(us, axis=0), wh_ref[cols, :], NN)
-        part = both[:CHUNK] + both[CHUNK:] + dot(us[0], wl_ref[cols, :], NN)
-        v_ref[rows, :] = part if h == 0 else v_ref[rows, :] + part
+        h, c = chunks[i]
+        cols = slice(h * hid + c, h * hid + c + COLS)
+        part = dot3(us, (wh_ref[cols, :], wl_ref[cols, :]))
+        v_ref[...] = part if i == 0 else v_ref[...] + part
 
     z = project(0)
     before = None
@@ -205,8 +213,12 @@
     st2_ref[0:1, :] += jnp.sum(vm, axis=0, keepdims=True)
     st2_ref[1:2, :] += jnp.sum(vm * vm, axis=0, keepdims=True)
 
-
-def forward(valid, x, wp, st, gain, shift, slope, mslope, w, in_w, tile):
+    @pl.when(step == pl.num_programs(0) - 1)
+    def _():
+        copies_ref[...] = jnp.broadcast_to(st2_ref[...][None], copies_ref.shape)
+
+
+def forward(valid, x, wp, st, gain, shift, slope, mslope, w, in_w, copies, tile):
     width, rows = x.shape
     mix, hid = w.shape
     by = lambda n: pl.BlockSpec((tile, n), lambda i: (i, 0))
@@ -214,22 +226,23 @@
         functools.partial(forward_kernel, in_w),
         grid=(rows // tile,),
         in_specs=[whole(valid), pl.BlockSpec((width, tile), lambda i: (0, i))]
-        + [whole(t) for t in (wp, st, gain, shift, slope, mslope, w)],
-        out_specs=[by(mix), by(mix), by(mix), by(hid)]
-        + [pl.BlockSpec(s, lambda i: (0, 0)) for s in ((2, hid), (mix, hid), (mix, hid))],
+        + [whole(t, 1) for t in (wp, st, gain, shift, slope, mslope, w)],
+        out_specs=[by(mix), by(mix), by(mix), by(hid), pl.BlockSpec((copies, 2, hid), lambda i: (0, 0, 0))]
+        + [pl.BlockSpec((mix, hid), lambda i: (0, 0), pipeline_mode=pl.Buffered(1))] * 2,
         out_shape=[
-            jax.ShapeDtypeStruct((rows, mix), F32),
-            jax.ShapeDtypeStruct((rows, mix), BF16),
-            jax.ShapeDtypeStruct((rows, mix), BF16),
-            jax.ShapeDtypeStruct((rows, hid), F32),
-            jax.ShapeDtypeStruct((2, hid), F32),
-            jax.ShapeDtypeStruct((mix, hid), BF16),
-            jax.ShapeDtypeStruct((mix, hid), BF16),
+            pltpu.HBM((rows, mix), F32),
+            pltpu.HBM((rows, mix), BF16),
+            pltpu.HBM((rows, mix), BF16),
+            pltpu.HBM((rows, hid), F32),
+            jax.ShapeDtypeStruct((copies, 2, hid), F32),
+            pltpu.HBM((mix, hid), BF16),
+            pltpu.HBM((mix, hid), BF16),
         ],
-        compiler_params=params(),
+        scratch_shapes=[pltpu.VMEM((2, hid), F32)],
+        compiler_params=params(43),
         name="forward",
         cost_estimate=cost(30),
-    )(valid, x, wp, st, gain, shift, slope, mslope, w)
+    )(valid, far(x), far(wp), st, gain, shift, slope, mslope, far(w))
 
 
 def as_column(row):
@@ -246,7 +259,7 @@
 
 def head_kernel(
     valid_ref, labels_ref, v_ref, st_ref, cnt_ref, gain_ref, shift_ref, slope_ref, hw_ref, hb_ref,
-    dy_ref, st3_ref, misc_ref,
+    dy_ref, copies_ref, misc_ref, st3_ref,
 ):
     step = pl.program_id(0)
     tile, hid = v_ref.shape
@@ -260,8 +273,9 @@
         st3_ref[...] = jnp.zeros_like(st3_ref)
         misc_ref[...] = jnp.zeros_like(misc_ref)
 
-    mean = st_ref[0:1, :] / count
-    rstd = lax.rsqrt(st_ref[1:2, :] / count - mean * mean + EPS)
+    sums = jnp.sum(st_ref[...], axis=0)
+    mean = sums[0:1, :] / count
+    rstd = lax.rsqrt(sums[1:2, :] / count - mean * mean + EPS)
     s = slope_ref[...]
     zn = (v_ref[...] - mean) * rstd
     y = gain_ref[...] * zn + shift_ref[...]
@@ -309,6 +323,10 @@
     st3_ref[0:1, :] += row(dy)
     st3_ref[1:2, :] += row(dy * zn)
 
+    @pl.when(step == pl.num_programs(0) - 1)
+    def _():
+        copies_ref[...] = jnp.broadcast_to(st3_ref[...][None], copies_ref.shape)
+
 
 def head(valid, labels, v, st2, st, gain, shift, slope, hw, hb, tile):
     rows, hid = v.shape
@@ -321,52 +339,69 @@
         + [whole(t) for t in (st2, st, gain, shift, slope, hw, hb)],
         out_specs=[
             by(hid),
-            pl.BlockSpec((2, hid), lambda i: (0, 0)),
+            whole(st2),
             pl.BlockSpec((misc, hid), lambda i: (0, 0)),
         ],
         out_shape=[
-            jax.ShapeDtypeStruct((rows, hid), F32),
-            jax.ShapeDtypeStruct((2, hid), F32),
+            pltpu.HBM((rows, hid), F32),
+            jax.ShapeDtypeStruct(st2.shape, F32),
             jax.ShapeDtypeStruct((misc, hid), F32),
         ],
-        compiler_params=params(),
+        scratch_shapes=[pltpu.VMEM((2, hid), F32)],
+        compiler_params=params(24),
         name="head",
         cost_estimate=cost(9),
-    )(valid, labels, v, st2, st, gain, shift, slope, hw, hb)
-
-
-def mix_dv(valid_ref, dy_ref, v_ref, st2_ref, cnt_ref, st3_ref, gain_ref):
-    mask = row_mask(valid_ref, pl.program_id(0), dy_ref.shape[0])
-    count = count_of(cnt_ref)
-    mean = st2_ref[0:1, :] / count
-    rstd = lax.rsqrt(st2_ref[1:2, :] / count - mean * mean + EPS)
-    a = LN2 * gain_ref[...] * rstd
-    c1 = a * st3_ref[0:1, :] / count
-    c2 = a * st3_ref[1:2, :] / count
-    zn = (v_ref[...] - mean) * rstd
-    return split(jnp.where(mask, a * dy_ref[...] - (c1 + zn * c2), 0.0))
-
-
-def mix_product(dvs, uh_ref, ul_ref, m_ref):
+    )(valid, labels, far(v), st2, st, gain, shift, slope, hw, hb)
+
+
+def mix_product(parts, uh_ref, ul_ref, m_ref):
     @pl.when(pl.program_id(0) == 0)
     def _():
         m_ref[...] = jnp.zeros_like(m_ref)
 
-    hid = dvs[0].shape[1]
-    for h in range(uh_ref.shape[1] // hid):
-        cols = slice(h * hid, (h + 1) * hid)
-        m_ref[cols, :] += dot3((uh_ref[:, cols], ul_ref[:, cols]), dvs, TN)
-
-
-def mix_first_kernel(half_ref, *refs):
-    ins, (uh_ref, ul_ref, m_ref, dvh_ref, dvl_ref) = refs[:7], refs[7:]
-    dvs = mix_dv(*ins)
-    dvh_ref[...], dvl_ref[...] = dvs
-    mix_product(dvs, uh_ref, ul_ref, m_ref)
+    ahead = parts[0][1]()
+    for k, (rows, _) in enumerate(parts):
+        dvs = ahead
+        if k + 1 < len(parts):
+            ahead = parts[k + 1][1]()
+        hid = dvs[0].shape[1]
+        for h in range(uh_ref.shape[1] // hid):
+            cols = slice(h * hid, (h + 1) * hid)
+            m_ref[cols, :] += dot3((uh_ref[rows, cols], ul_ref[rows, cols]), dvs, TN)
+
+
+def mix_first_kernel(
+    half_ref, valid_ref, dy_ref, v_ref, st2_ref, cnt_ref, st3_ref, gain_ref, uh_ref, ul_ref,
+    m_ref, dvh_ref, dvl_ref, st3_out,
+):
+    step = pl.program_id(0)
+    tile = dy_ref.shape[0]
+    mask = row_mask(valid_ref, step, tile)
+    count = count_of(cnt_ref)
+    st2 = jnp.sum(st2_ref[...], axis=0)
+    st3 = jnp.sum(st3_ref[...], axis=0)
+    mean = st2[0:1, :] / count
+    rstd = lax.rsqrt(st2[1:2, :] / count - mean * mean + EPS)
+    a = LN2 * gain_ref[...] * rstd
+    c1 = a * st3[0:1, :] / count
+    c2 = a * st3[1:2, :] / count
+
+    @pl.when(step == 0)
+    def _():
+        st3_out[...] = st3
+
+    def dv(rows):
+        zn = (v_ref[rows, :] - mean) * rstd
+        dvs = split(jnp.where(mask[rows], a * dy_ref[rows, :] - (c1 + zn * c2), 0.0))
+        dvh_ref[rows, :], dvl_ref[rows, :] = dvs
+        return dvs
+
+    parts = [slice(k, k + MIX_SUB) for k in range(0, tile, MIX_SUB)]
+    mix_product([(rows, functools.partial(dv, rows)) for rows in parts], uh_ref, ul_ref, m_ref)
 
 
 def mix_second_kernel(half_ref, dvh_ref, dvl_ref, uh_ref, ul_ref, m_ref):
-    mix_product((dvh_ref[...], dvl_ref[...]), uh_ref, ul_ref, m_ref)
+    mix_product([(slice(None), lambda: (dvh_ref[...], dvl_ref[...]))], uh_ref, ul_ref, m_ref)
 
 
 def mix_back(half, valid, dy, v, st2, st, st3, gain, uh, ul, tile):
@@ -381,17 +416,19 @@
             in_specs=[whole(valid), by(hid), by(hid)]
             + [whole(t) for t in (st2, st, st3, gain)]
             + [pl.BlockSpec((tile, part), lambda i, half: (i, half[0]))] * 2,
-            out_specs=[pl.BlockSpec((part, hid), lambda i, half: (0, 0)), by(hid), by(hid)],
+            out_specs=[pl.BlockSpec((part, hid), lambda i, half: (0, 0)), by(hid), by(hid)]
+            + [pl.BlockSpec((2, hid), lambda i, half: (0, 0))],
         ),
         out_shape=[
             jax.ShapeDtypeStruct((part, hid), F32),
-            jax.ShapeDtypeStruct((rows, hid), BF16),
-            jax.ShapeDtypeStruct((rows, hid), BF16),
+            pltpu.HBM((rows, hid), BF16),
+            pltpu.HBM((rows, hid), BF16),
+            jax.ShapeDtypeStruct((2, hid), F32),
         ],
-        compiler_params=params(),
+        compiler_params=params(28),
         name="mix_back",
         cost_estimate=cost(14),
-    )(half, valid, dy, v, st2, st, st3, gain, uh, ul)
+    )(half, valid, far(dy), far(v), st2, st, st3, gain, far(uh), far(ul))
 
 
 def mix_back_rest(half, dvh, dvl, uh, ul, tile):
@@ -408,20 +445,21 @@
             out_specs=pl.BlockSpec((part, hid), lambda i, half: (0, 0)),
         ),
         out_shape=jax.ShapeDtypeStruct((part, hid), F32),
-        compiler_params=params(),
+        compiler_params=params(28),
         name="mix_back_rest",
         cost_estimate=cost(12),
-    )(half, dvh, dvl, uh, ul)
+    )(half, far(dvh), far(dvl), far(uh), far(ul))
 
 
 def hop_kernel(
     h, in_w, x_ref, wp_ref, st_ref, gain_ref, shift_ref, slope_ref, mslope_ref, dvh_ref, dvl_ref, mwh_ref, mwl_ref,
-    j_ref, uh_ref, ul_ref,
+    j_ref,
     dx_ref, bw_ref, sums_ref,
 ):
     step = pl.program_id(0)
     n = wp_ref.shape[1] // 3
     hid = gain_ref.shape[1]
+    tile = x_ref.shape[1]
 
     @pl.when(step == 0)
     def _():
@@ -431,16 +469,13 @@
     a, b = scale_of(st_ref, slice(h * hid, (h + 1) * hid), gain_ref, shift_ref, h)
     s1 = slope_ref[h : h + 1, :]
     s2 = mslope_ref[h : h + 1, :]
-    xall = stack3(hop_rows(x_ref, h, in_w))
+    xall = stack3(hop_rows(x_ref, h, in_w, 1.0))
     wp = wp_ref[0]
-    r2 = 1.0 / (1.0 - s2)
-    r1 = 1.0 / (1.0 - s1)
     wh, wl = split((wp[:n].astype(F32) + wp[2 * n :].astype(F32)) * a)
     whl = jnp.concatenate([wh, wl], axis=0)
     dot = functools.partial(lax.dot_general, preferred_element_type=F32)
     row = lambda t: jnp.sum(t, axis=0, keepdims=True)
-    sums = [0.0] * 4
-    tile = x_ref.shape[1]
+    sums = [0.0] * 2
     parts = [slice(k, k + SUB) for k in range(0, tile, SUB)]
 
     def products(rs):
@@ -450,10 +485,9 @@
     def middle(rs, z, du):
         y = z * a + b
         j = j_ref[rs, :]
-        u = uh_ref[rs, :].astype(F32) + ul_ref[rs, :].astype(F32)
-        dj = du * (1.0 - (1.0 - s2) * jnp.exp2((s2 * r2) * j - r2 * u))
-        dy = dj * (1.0 - (1.0 - s1) * jnp.exp2((s1 * r1) * y - r1 * j))
-        for q, t in enumerate((dy, dy * y, dj * (y - j), du * (j - u))):
+        dj = du * (1.0 - (1.0 - s2) / (1.0 + jnp.exp2(j)))
+        dy = dj * (1.0 - (1.0 - s1) / (1.0 + jnp.exp2(y)))
+        for q, t in enumerate((dj * (y - j), du * j)):
             sums[q] = sums[q] + row(t)
         return split(dy)
 
@@ -474,15 +508,11 @@
         before = middle(rs, *now)
         now = ahead
     results(parts[-1], before)
-    for q, f in enumerate((1.0, 1.0, r1, r2)):
-        sums_ref[q : q + 1, :] += sums[q] * f
-
-    @pl.when(step == pl.num_programs(0) - 1)
-    def _():
-        bw_ref[...] = bw_ref[...] * a
-
-
-def hop_back(h, in_w, x, wp, st, gain, shift, slope, mslope, dvh, dvl, mwh, mwl, j, uh, ul, tile):
+    for q in range(2):
+        sums_ref[q : q + 1, :] += sums[q]
+
+
+def hop_back(h, in_w, x, wp, st, gain, shift, slope, mslope, dvh, dvl, mwh, mwl, j, tile):
     width, rows = x.shape
     hid = dvh.shape[1]
     n = wp.shape[1] // 3
@@ -494,30 +524,58 @@
         in_specs=[
             pl.BlockSpec((width, tile), lambda i: (0, i)),
             pl.BlockSpec((1, 3 * n, hid), lambda i: (h, 0, 0)),
-            whole(st),
         ]
-        + [whole(t) for t in (gain, shift, slope, mslope)]
-        + [by(hid), by(hid), block(hid), block(hid)]
-        + [by(hid, h)] * 3,
+        + [whole(t) for t in (st, gain, shift, slope, mslope)]
+        + [by(hid), by(hid), block(hid), block(hid), by(hid, h)],
         out_specs=[
             pl.BlockSpec((n, tile), lambda i: (0, i)),
             pl.BlockSpec((n, hid), lambda i: (0, 0)),
-            pl.BlockSpec((4, hid), lambda i: (0, 0)),
+            pl.BlockSpec((2, hid), lambda i: (0, 0)),
         ],
         out_shape=[
-            jax.ShapeDtypeStruct((n, rows), F32),
+            pltpu.HBM((n, rows), F32),
             jax.ShapeDtypeStruct((n, hid), F32),
-            jax.ShapeDtypeStruct((4, hid), F32),
+            jax.ShapeDtypeStruct((2, hid), F32),
         ],
-        compiler_params=params(),
+        compiler_params=params(20),
         name=f"hop_back_{h}",
-        cost_estimate=cost(14),
-    )(x, wp, st, gain, shift, slope, mslope, dvh, dvl, mwh, mwl, j, uh, ul)
+        cost_estimate=cost(11),
+    )(far(x), far(wp), st, gain, shift, slope, mslope, far(dvh), far(dvl), far(mwh), far(mwl), far(j))
+
+
+def assemble_kernel(first_ref, own_ref, got_ref, w_ref, m_ref, uu_ref):
+    mine = (pl.program_id(0) // 2) == first_ref[0]
+    m = jnp.where(mine, own_ref[...], got_ref[...])
+    m_ref[...] = m
+    ones = jnp.ones((8, m.shape[1]), BF16)
+    dot = functools.partial(lax.dot_general, dimension_numbers=NT, preferred_element_type=F32)
+    hi, lo = split(m * w_ref[...])
+    uu_ref[0] = dot(ones, hi) + dot(ones, lo)
+
+
+def assemble(first, own, got, w):
+    rows, hid = w.shape
+    block = rows // 4
+    half = pl.BlockSpec((block, hid), lambda i, first: (i % 2, 0))
+    by = pl.BlockSpec((block, hid), lambda i, first: (i, 0))
+    return pl.pallas_call(
+        assemble_kernel,
+        grid_spec=pltpu.PrefetchScalarGridSpec(
+            num_scalar_prefetch=1,
+            grid=(4,),
+            in_specs=[half, half, by],
+            out_specs=[by, pl.BlockSpec((1, 8, block), lambda i, first: (i, 0, 0))],
+        ),
+        out_shape=[jax.ShapeDtypeStruct((rows, hid), F32), jax.ShapeDtypeStruct((4, 8, block), F32)],
+        compiler_params=params(20),
+        name="assemble",
+        cost_estimate=cost(5),
+    )(first, own, got, far(w))
 
 
 def pack_rows(n, hops, misc, unit=1):
     base = hops * n
-    gram_at = base + misc + 4 * hops
+    gram_at = base + misc + 2 * hops
     used = gram_at + hops * n // 4
     return base, gram_at, -(-used // unit) * unit
 
@@ -530,8 +588,8 @@
     total = out_ref.shape[0]
     for h in range(hops):
         out_ref[h * n : (h + 1) * n, :] = refs[h][...]
-        k = base + misc_ref.shape[0] + 4 * h
-        out_ref[k : k + 4, :] = refs[hops + h][...]
+        k = base + misc_ref.shape[0] + 2 * h
+        out_ref[k : k + 2, :] = refs[hops + h][...]
         for q in range(4):
             k = gram_at + h * n // 4
             out_ref[k : k + n // 4, q * LANES : (q + 1) * LANES] = g_ref[h, q * n // 4 : (q + 1) * n // 4, :]
@@ -547,13 +605,13 @@
     return pl.pallas_call(
         pack_kernel,
         out_shape=jax.ShapeDtypeStruct((total, hid), F32),
-        compiler_params=params(),
+        compiler_params=params(24),
         name="pack",
         cost_estimate=cost(3),
     )(g, misc, *bws, *sums)
 
 
-def fix_kernel(in_w, classes, misc, valid_ref, x_ref, p_ref, st_ref, gain_ref, shift_ref, wp_ref, *refs):
+def fix_kernel(in_w, classes, misc, valid_ref, x_ref, p_ref, uu_ref, st_ref, gain_ref, slope_ref, mslope_ref, wp_ref, *refs):
     step = pl.program_id(0)
     hops, hid = gain_ref.shape
     tile = x_ref.shape[1]
@@ -574,18 +632,21 @@
             cols = slice(h * hid, (h + 1) * hid)
             mean, rstd = norm_of(st_ref, cols)
             gain = gain_ref[h : h + 1, :]
-            at = base + misc + 4 * h
-            total = LOG2E * p_ref[at : at + 1, :]
-            gsum = (p_ref[at + 1 : at + 2, :] - shift_ref[h : h + 1, :] * total) / gain
+            wh, wl = wp_ref[h, :n, :], wp_ref[h, 2 * n :, :]
+            w = wh.astype(F32) + wl.astype(F32)
+            raw = p_ref[h * n : (h + 1) * n, :]
+            total = LOG2E * raw[in_w : in_w + 1, :]
+            gsum = rstd * (LOG2E * jnp.sum(w * raw, axis=0, keepdims=True) - mean * total)
             gain_out[h : h + 1, :] = gsum
             shift_out[h : h + 1, :] = total
-            slope_out[h : h + 1, :] = p_ref[at + 2 : at + 3, :]
-            mslope_out[h : h + 1, :] = p_ref[at + 3 : at + 4, :]
+            at = base + misc + 2 * h
+            slope_out[h : h + 1, :] = p_ref[at : at + 1, :] / (1.0 - slope_ref[h : h + 1, :])
+            uu = uu_ref[h, 0:1, :]
+            mslope_out[h : h + 1, :] = (p_ref[at + 1 : at + 2, :] - uu) / (1.0 - mslope_ref[h : h + 1, :])
             a = gain * rstd / count
             c2 = a * gsum * rstd
             k0 = a * total - mean * c2
-            wh, wl = wp_ref[h, :n, :], wp_ref[h, 2 * n :, :]
-            wc = (wh.astype(F32) + wl.astype(F32)) * c2
+            wc = w * c2
             mask_row = lax.broadcasted_iota(jnp.int32, (n, hid), 0) == in_w
             wc = split(jnp.where(mask_row, k0, wc))
             q_ref[h, :, :n] = dot3((wh, wl), wc, NT)
@@ -593,7 +654,7 @@
             g = jnp.concatenate(
                 [p_ref[k : k + n // 4, q * LANES : q * LANES + n] for q in range(4)], axis=0
             )
-            bw = p_ref[h * n : (h + 1) * n, :] - dot3(split(g), wc)
+            bw = raw * (LOG2E * gain * rstd) - dot3(split(g), wc)
             bw_ref[:, h, :] = bw[:in_w]
 
     for h in range(hops):
@@ -602,7 +663,7 @@
         dx_ref[h * in_w : (h + 1) * in_w, :] = (dxs[h][...] - fix)[:in_w]
 
 
-def fix(valid, x, packed, st, gain, shift, wp, dxs, in_w, classes, misc, tile):
+def fix(valid, x, packed, uu, st, gain, slope, mslope, wp, dxs, in_w, classes, misc, tile):
     width, rows = x.shape
     hops, hid = gain.shape
     n = wp.shape[1] // 3
@@ -612,15 +673,15 @@
         functools.partial(fix_kernel, in_w, classes, misc),
         grid=(rows // tile,),
         in_specs=[whole(valid), cols(width)]
-        + [whole(t) for t in (packed, st, gain, shift, wp)]
+        + [whole(t) for t in (packed, uu, st, gain, slope, mslope, wp)]
         + [cols(n)] * hops,
         out_specs=[cols(width)] + [pl.BlockSpec(s, lambda i, s=s: (0,) * len(s)) for s in shapes],
         out_shape=[jax.ShapeDtypeStruct(s, F32) for s in ((width, rows),) + shapes],
         scratch_shapes=[pltpu.VMEM((hops, n, LANES), F32)],
-        compiler_params=params(),
+        compiler_params=params(24),
         name="fix",
         cost_estimate=cost(8),
-    )(valid, x, packed, st, gain, shift, wp, *dxs)
+    )(valid, far(x), packed, uu, st, gain, slope, mslope, far(wp), *[far(d) for d in dxs])
 
 
 def flip(v, axis, size, k):
@@ -647,10 +708,8 @@
     return v
 
 
-def sum_tiny(v, sizes):
-    n = sizes["dp"] * sizes["bucket"]
-    copies = jnp.broadcast_to(v[None], (n,) + v.shape)
-    return jnp.sum(lax.all_to_all(copies, ("dp", "bucket"), 0, 0, tiled=True), axis=0)
+def exchange(copies):
+    return lax.all_to_all(copies, ("dp", "bucket"), 0, 0, tiled=True)
 
 
 def pieces(v, n):
@@ -663,61 +722,89 @@
     return lax.dynamic_slice_in_dim(v, index * size, size, 0)
 
 
-def halve(v, axis, size, k):
+def merge(v, got, axis, size, k):
     bit = lax.axis_index(axis) // k % 2
-    return take(v, bit, 2) + flip(take(v, 1 - bit, 2), axis, size, k)
-
-
-def double(v, axis, size, k):
+    return jnp.where(bit == 0, jnp.concatenate([v, got], 0), jnp.concatenate([got, v], 0))
+
+
+def halve(parts, axis, size, k):
     bit = lax.axis_index(axis) // k % 2
-    got = flip(v, axis, size, k)
-    return jnp.where(bit == 0, jnp.concatenate([v, got], 0), jnp.concatenate([got, v], 0))
-
-
-def scatter_line(v, axis, size):
-    if size != 4:
-        for i in range(size.bit_length() - 1):
-            v = halve(v, axis, size, 1 << i)
-        return v
-    me = lax.axis_index(axis)
-    p0, p1, p2, p3 = (flip(take(v, me ^ k, 4), axis, 4, k) if k else take(v, me, 4) for k in range(4))
-    return (p0 + p1) + (p2 + p3)
-
-
-def gather_line(v, axis, size):
-    if size != 4:
-        for i in reversed(range(size.bit_length() - 1)):
-            v = double(v, axis, size, 1 << i)
-        return v
-    me = lax.axis_index(axis)
-    out = jnp.zeros((4 * v.shape[0],) + v.shape[1:], v.dtype)
-    for k in range(4):
-        got = flip(v, axis, 4, k) if k else v
-        out = lax.dynamic_update_slice_in_dim(out, got, (me ^ k) * v.shape[0], 0)
-    return out
-
-
-def sum_stages(sizes):
+    part = lambda i: functools.reduce(jnp.add, [take(p, i, 2) for p in parts])
+    return part(bit), flip(part(1 - bit), axis, size, k)
+
+
+def spread(v, axis, size, k):
+    me = lax.axis_index(axis) // k
+    return tuple(flip(take(v, me ^ i, 4), axis, size, k * i) if i else take(v, me, 4) for i in range(4))
+
+
+def collect(v, axis, size, k):
+    return (v,) + tuple(flip(v, axis, size, k * i) for i in range(1, 4))
+
+
+def in_order(parts, axis, k):
+    low, high = lax.axis_index(axis) // k % 2, lax.axis_index(axis) // (2 * k) % 2
+    pair = lambda a, b: jnp.where(low == 0, jnp.concatenate([a, b], 0), jnp.concatenate([b, a], 0))
+    near, far = pair(parts[0], parts[1]), pair(parts[2], parts[3])
+    return jnp.where(high == 0, jnp.concatenate([near, far], 0), jnp.concatenate([far, near], 0))
+
+
+def total(parts):
+    if len(parts) == 4:
+        return (parts[0] + parts[1]) + (parts[2] + parts[3])
+    return functools.reduce(jnp.add, parts)
+
+
+def sum_steps(parts, sizes, large, within):
     dp, bucket = sizes["dp"], sizes["bucket"]
     across = [("dp", dp, 1 << i) for i in range(1, dp.bit_length() - 1)]
-    stages = []
-    if dp > 1:
-        stages.append(lambda v: halve(v, "dp", dp, 1))
-    for a, b in zip(across, across[::-1]):
-        stages.append(lambda v, a=a, b=b: jnp.concatenate([halve(pieces(v, 2)[0], *a), halve(pieces(v, 2)[1], *b)], 0))
-    stages.append(lambda v: scatter_line(v, "bucket", bucket))
-    stages.append(lambda v: gather_line(v, "bucket", bucket))
-    for a, b in zip(across[::-1], across):
-        stages.append(lambda v, a=a, b=b: jnp.concatenate([double(pieces(v, 2)[0], *a), double(pieces(v, 2)[1], *b)], 0))
-    if dp > 1:
-        stages.append(lambda v: double(v, "dp", dp, 1))
-    return stages
-
-
-def sum_large(v, sizes):
-    for stage in sum_stages(sizes):
-        v = stage(v)
+    square = len(across) == 2 and not large
+    line = [("bucket", bucket, 1 << i) for i in range(bucket.bit_length() - 1)]
+    core = ("dp", dp, 1)
+    within = within and dp > 1
+    if within:
+        parts = yield halve(parts, *core)
+    if square:
+        parts = yield spread(total(parts), "dp", dp, 2)
+    elif across:
+        top, bottom = ([pieces(p, 2)[i] for p in parts] for i in range(2))
+        for a, b in zip(across, across[::-1]):
+            top, bottom = yield halve(top, *a), halve(bottom, *b)
+        parts = [jnp.concatenate([total(top), total(bottom)], 0)]
+    if bucket == 4:
+        parts = yield spread(total(parts), "bucket", bucket, 1)
+        parts = yield collect(total(parts), "bucket", bucket, 1)
+        v = in_order(parts, "bucket", 1)
+    else:
+        for s in line:
+            parts = yield halve(parts, *s)
+        v = total(parts)
+        for s in line[::-1]:
+            parts = yield v, flip(v, *s)
+            v = merge(*parts, *s)
+    if square:
+        v = in_order((yield collect(v, "dp", dp, 2)), "dp", 2)
+    elif across:
+        top, bottom = pieces(v, 2)
+        for a, b in zip(across[::-1], across):
+            got = yield top, flip(top, *a), bottom, flip(bottom, *b)
+            top, bottom = merge(*got[:2], *a), merge(*got[2:], *b)
+        v = jnp.concatenate([top, bottom], 0)
+    if within:
+        v = merge(*(yield v, flip(v, *core)), *core)
     return v
+
+
+class Steps:
+    def __init__(self, steps):
+        self.steps, self.state, self.done, self.value = steps, None, False, None
+
+    def step(self):
+        if not self.done:
+            try:
+                self.state = self.steps.send(self.state)
+            except StopIteration as end:
+                self.done, self.value, self.state = True, end.value, None
 
 
 def per_device(sizes, feats, labels, valid, branch_w, branch_gain, branch_shift, branch_slope, mix_slope,
@@ -735,56 +822,60 @@
     g, st, wp = gram(valid, x, branch_w.transpose(1, 0, 2), TILES["gram"])
     st = sum_small(st, sizes)
     j, uh, ul, v, st2, mwh, mwl = forward(
-        valid, x, wp, st, branch_gain, branch_shift, branch_slope, mslope, mix_w, in_w, TILES["forward"]
+        valid, x, wp, st, branch_gain, branch_shift, branch_slope, mslope, mix_w, in_w,
+        sizes["dp"] * sizes["bucket"], TILES["forward"],
     )
-    st2 = sum_tiny(st2, sizes)
+    st2 = exchange(st2)
     dy2, st3, misc = head(
         valid, labels, v, st2, st, row(mix_gain), row(mix_shift), row(out_slope), head_w.T, row(head_bias),
         TILES["head"],
     )
-    st3 = sum_tiny(st3, sizes)
+    st3 = exchange(st3)
     core = lax.axis_index("dp") % 2
     half = lambda i: jnp.reshape(i, (1,)).astype(jnp.int32)
-    away, dvh, dvl = mix_back(
+    away, dvh, dvl, st3 = mix_back(
         half(1 - core), valid, dy2, v, st2, st, st3, row(mix_gain), uh, ul, TILES["mix"]
     )
-    got = flip(away, "dp", sizes["dp"], 1) if sizes["dp"] > 1 else None
+    within = sizes["dp"] > 1
+    got = flip(away, "dp", sizes["dp"], 1) if within else None
     m = mix_back_rest(half(core), dvh, dvl, uh, ul, TILES["mix"])
-    if got is None:
-        m = jnp.concatenate([m, away], 0)
+    if within:
+        m, got, x = lax.optimization_barrier((m, got, x))
+        first = Steps(sum_steps((m, got), sizes, True, False))
     else:
-        m, got, x = lax.optimization_barrier((m, got, x))
-        m = m + got
-    stages = sum_stages(sizes)
-    rest = list(stages)
-    if got is not None:
-        stages = stages[1:]
-    per_stage = [[] for _ in range(HOP_STAGES)]
+        first = Steps(sum_steps((jnp.concatenate([m, away], 0),), sizes, True, False))
+    dxs, bws, sums = [], [], []
     for h in range(hops):
-        per_stage[h * HOP_STAGES // hops].append(h)
-    dxs, bws, sums = [], [], []
-    for i, now in enumerate(per_stage):
-        m, x, bws, sums = lax.optimization_barrier((m, x, bws, sums))
-        if i < len(stages):
-            m = stages[i](m)
-        for h in now:
-            dx, bw, s = hop_back(
-                h, in_w, x, wp, st, branch_gain, branch_shift, branch_slope, mslope, dvh, dvl, mwh, mwl,
-                j, uh, ul, TILES["hop"],
-            )
-            dxs, bws, sums = dxs + [dx], bws + [bw], sums + [s]
+        first.step()
+        dx, bw, s = hop_back(
+            h, in_w, x, wp, st, branch_gain, branch_shift, branch_slope, mslope, dvh, dvl, mwh, mwl,
+            j, TILES["hop"],
+        )
+        dxs, bws, sums = dxs + [dx], bws + [bw], sums + [s]
+        first.state, x, bws, sums = lax.optimization_barrier((first.state, x, bws, sums))
     packed = pack(g, misc, bws, sums, max(128, 2 * sizes["dp"] * sizes["bucket"]))
-    for stage in stages[HOP_STAGES:]:
-        m, packed = lax.optimization_barrier((m, packed))
-        m = stage(m)
-        for _ in range(PACK_STAGES):
-            if rest:
-                packed = rest.pop(0)(packed)
-    for stage in rest:
-        packed = stage(packed)
-    m, packed = lax.optimization_barrier((m, packed))
+    last = Steps(sum_steps((packed,), sizes, False, True))
+    while not first.done:
+        first.step()
+        for _ in range(PACK_STEPS):
+            last.step()
+        first.state, last.state = lax.optimization_barrier((first.state, last.state))
+    m = first.value
+    if within:
+        m, other = m, flip(m, "dp", sizes["dp"], 1)
+        last.step()
+        m, other, last.state = lax.optimization_barrier((m, other, last.state))
+    else:
+        m, other = pieces(m, 2)
+    last.step()
+    m, uu = assemble(half(core), m, other, mix_w)
+    m, uu, last.state = lax.optimization_barrier((m, uu, last.state))
+    while not last.done:
+        last.step()
+    packed = last.value
     d_x, bw, gain_grad, shift_grad, slope_grad, mslope_grad, oslope_grad, hw_grad, hb_grad, loss = fix(
-        valid, x, packed, st, branch_gain, branch_shift, wp, dxs, in_w, classes, misc.shape[0], TILES["fix"]
+        valid, x, packed, uu, st, branch_gain, branch_slope, mslope, wp, dxs, in_w, classes, misc.shape[0],
+        TILES["fix"],
     )
     return (
         loss.reshape(()),

time: 276 us -> 246 us (0.89)
  Pallas kernels: 138 us -> 128 us
  waiting for transfers between devices: 56.2 us -> 48.3 us
  other arithmetic: 13.9 us -> 6.68 us
  local copies, waits for them, and re-layouts: 10 us -> 6.08 us
    ppermute x39 -> x37, waiting for transfers between devices: 48 us -> 40.1 us  [flip(): return lax.ppermute(v, axis, [(i, i ^ k) for i in range(size)])]
    pallas_call x4, Pallas kernels: 54 us -> 46.6 us  [hop_back(): pl.pallas_call(functools.partial(hop_kernel, h, in_w), grid=(rows // tile...]
    select_n x10 -> x14, other arithmetic: 8.2 us -> 2.04 us  [the longest x5 1.78 us: merge(): jnp.where(bit == 0, jnp.concatenate([v, got], 0), jnp.concatenate([got, v...]
    pallas_call x0 -> x1, Pallas kernels: none -> 5.96 us  [assemble(): pl.pallas_call(assemble_kernel, grid_spec=pltpu.PrefetchScalarGridSpec(nu...]
    ppermute x39 -> x37, starting transfers between devices: 42.6 us -> 42.1 us  [flip(): return lax.ppermute(v, axis, [(i, i ^ k) for i in range(size)])]
  transfers between devices with their start and end apart: 40 -> 38, of which waited for: 24 -> 21; matrix products, arithmetic and copies ran while one was open for 3% -> 2% of each run, Pallas kernels for 25% -> 23%
where the time goes in v3:
time: 246 us
  Pallas kernels  128 us (52%)
  waiting for transfers between devices  48.3 us (20%)
  starting transfers between devices  44.8 us (18%)
  blocking collectives  10.1 us (4%)
  other arithmetic  6.68 us (3%)
  local copies, waits for them, and re-layouts  6.08 us (2%)
    pallas_call x4, Pallas kernels, hop_back(): pl.pallas_call(functools.partial(hop_kernel, h, in_w), grid=(rows // tile...  46.6 us
    ppermute x37, starting transfers between devices, flip(): return lax.ppermute(v, axis, [(i, i ^ k) for i in range(size)])  42.1 us
    ppermute x37, waiting for transfers between devices, flip(): return lax.ppermute(v, axis, [(i, i ^ k) for i in range(size)])  40.1 us
    pallas_call x1, Pallas kernels, forward(): pl.pallas_call(functools.partial(forward_kernel, in_w), grid=(rows // til...  32.2 us
    pallas_call x1, Pallas kernels, mix_back(): pl.pallas_call(mix_first_kernel, grid_spec=pltpu.PrefetchScalarGridSpec(n...  12.3 us
    all_to_all x1, blocking collectives, exchange(): return lax.all_to_all(copies, ('dp', 'bucket'), 0, 0, tiled=True)  10.1 us
    pallas_call x1, Pallas kernels, head(): pl.pallas_call(head_kernel, grid=(rows // tile,), in_specs=[whole(valid),...  9.65 us
    pallas_call x1, Pallas kernels, mix_back_rest(): pl.pallas_call(mix_second_kernel, grid_spec=pltpu.PrefetchScalarGridSpec(...  9.48 us
  transfers between devices with their start and end apart: 38, of which 21 were waited for; matrix products, arithmetic and copies ran while one was open for 2% of the time, Pallas kernels for 23%

profile of v3, /device:TPU:0, one launch (start us, length us, event | category | flops | bytes accessed | tf_op | source)
XLA Modules:
  0.0 245.5 jit_solution(3064782728113905398)
XLA Ops:
  2.5 4.7 %gram.1 = (f32[4,112,128]{2,1,0:T(8,128)S(1)}, f32[2,2176]{1,0:T(2,128)S(1)}, bf16[4,336,512]{2,1,0:T(8,128)(2,1)}) custom-call(s32[16,128]{1,0:T(8,128)S(1)} %bitcast.22, f32[400,2048]{1,0:T(8,128)} %bitcast.35, f32[100,4,512]{2,1,0:T(4,128)S(1)} %bitcast.21), custom_call_target="tpu_custom_call" | custom-call | bytes 18450000 | tf_op jit(solution)/shard_map/gram/pallas_call | solution.py:123
  8.5 2.9 %collective-permute-start.1 = (f32[2,2176]{1,0:T(2,128)S(1)}, f32[2,2176]{1,0:T(2,128)S(1)}, u32[]{:S(2)}, u32[]{:S(2)}) collective-permute-start(f32[2,2176]{1,0:T(2,128)S(1)} %add.189), channel_id=1, source_target_pairs={{0,8},{4,12},{8,0},{12,4},{16,24},{20,28},{24,16},{28,20},{1,9},{5... | collective-permute-start | bytes 52232 | tf_op jit(solution)/shard_map/ppermute | solution.py:688
  11.4 1.5 collective-permute-start.2
  13.1 2.0 collective-permute-done.2
  15.2 2.4 collective-permute-done.3
  17.6 1.6 collective-permute-start.4
  19.2 2.6 %collective-permute-start.5 = (f32[2,2176]{1,0:T(2,128)S(1)}, f32[2,2176]{1,0:T(2,128)S(1)}, u32[]{:S(2)}, u32[]{:S(2)}) collective-permute-start(f32[2,2176]{1,0:T(2,128)S(1)} %add_add_fusion.4), channel_id=1, source_target_pairs={{0,2},{1,3},{2,0},{3,1},{4,6},{5,7},{6,4},{7,5},{8,10},{9,11},{10,... | collective-permute-start | bytes 52232 | tf_op jit(solution)/shard_map/ppermute | solution.py:688
  22.1 1.9 collective-permute-done.5
  24.0 3.4 %collective-permute-done.6 = f32[2,2176]{1,0:T(2,128)S(1)} collective-permute-done((f32[2,2176]{1,0:T(2,128)S(1)}, f32[2,2176]{1,0:T(2,128)S(1)}, u32[]{:S(2)}, u32[]{:S(2)}) %collective-permute-start.6) | collective-permute-done | bytes 17440 | tf_op jit(solution)/shard_map/ppermute | solution.py:688
  27.5 32.2 %forward.1 = (f32[2048,2048]{1,0:T(8,128)}, bf16[2048,2048]{1,0:T(8,128)(2,1)}, bf16[2048,2048]{1,0:T(8,128)(2,1)}, f32[2048,512]{1,0:T(8,128)}, f32[32,2,512]{2...) custom-call(s32[16,128]{1,0:T(8,128)S(1)} %bitcast.23, f32[400,2048]{1,0:T(8,128)} %bitcast.36, ...), custom_call_target="tpu_custom_call" | custom-call | bytes 110700000 | tf_op jit(solution)/shard_map/forward/pallas_call | solution.py:225
  59.7 10.1 %all_to_all.10.st_ref.st2_ref = f32[32,2,512]{2,1,0:T(2,128)S(1)} all-to-all(f32[32,2,512]{2,1,0:T(2,128)S(1)} %get-tuple-element.120), channel_id=1, replica_groups=mesh['dp'=8,'bucket'=4] {'dp','bucket'}, dimensions={0} | all-to-all | bytes 262144 | tf_op jit(solution)/shard_map/all_to_all | solution.py:712
  69.9 9.6 %head.1 = (f32[2048,512]{1,0:T(8,128)}, f32[32,2,512]{2,1,0:T(2,128)}, f32[56,512]{1,0:T(8,128)S(1)}) custom-call(s32[16,128]{1,0:T(8,128)S(1)} %bitcast.24, s32[16,128]{1,0:T(8,128)S(1)} %bitcast.28, f32[2048,512]{1,0:T(8,128)} %get-tuple-element.119.v_ref, f32[32,2,512]{2,1,0:T(2,128)S(1)} %all_to_all.10.st_ref.st2_ref, ...), custom_call_target="tpu_custom_call" | custom-call | bytes 33210000 | tf_op jit(solution)/shard_map/head/pallas_call | solution.py:335
  79.5 2.8 %all-to-all-start.1 = ((f32[32,2,512]{2,1,0:T(2,128)}), f32[32,2,512]{2,1,0:T(2,128)S(1)}, u32[]{:S(2)}, u32[]{:S(2)}) async-start(f32[32,2,512]{2,1,0:T(2,128)} %get-tuple-element.122), calls=%async_computation.1 | async-start | bytes 262144 | tf_op jit(solution)/shard_map/all_to_all | solution.py:712
  82.3 8.2 %all-to-all-done.1.st3_ref = f32[32,2,512]{2,1,0:T(2,128)S(1)} async-done(((f32[32,2,512]{2,1,0:T(2,128)}), f32[32,2,512]{2,1,0:T(2,128)S(1)}, u32[]{:S(2)}, u32[]{:S(2)}) %all-to-all-start.1) | async-done | bytes 131104 | tf_op jit(solution)/shard_map/all_to_all | solution.py:712
  90.5 12.3 %mix_back.1 = (f32[1024,512]{1,0:T(8,128)}, bf16[2048,512]{1,0:T(8,128)(2,1)}, bf16[2048,512]{1,0:T(8,128)(2,1)}, f32[2,512]{1,0:T(2,128)S(1)}) custom-call(s32[1]{0:T(128)} %bitcast.2.half_ref, s32[16,128]{1,0:T(8,128)S(1)} %bitcast.25, f32[2048,512]{1,0:T(8,128)} %get-tuple-element.121.dy_ref, f32[2048,512]{1,0:T(8,128)} %get-tuple-element.119.v_ref, ...), custom_call_target="tpu_custom_call" | custom-call | bytes 51660000 | tf_op jit(solution)/shard_map/mix_back/pallas_call | solution.py:411
  103.0 9.5 %mix_back_rest.1 = f32[1024,512]{1,0:T(8,128)S(1)} custom-call(s32[1]{0:T(128)} %bitcast.1.half_ref.first_ref, bf16[2048,512]{1,0:T(8,128)(2,1)} %get-tuple-element.125.dvh_ref, bf16[2048,512]{1,0:T(8,128)(2,1)} %get-tuple-element.126.dvl_ref, bf16[2048,2048]{1,0:T(8,128)(2,1)} %get-tuple-element.123.uh_ref, bf16[2048,2048]{1,0:T(8,128)(2,1)} %get-tuple-element.124.ul_ref), custom_call_target="tpu_custom_call" | custom-call | bytes 44280000 | tf_op jit(solution)/shard_map/mix_back_rest/pallas_call | solution.py:438
  112.5 2.0 fusion.4
  117.9 11.6 %hop_back_0.1 = (f32[112,2048]{1,0:T(8,128)}, f32[112,512]{1,0:T(8,128)S(1)}, f32[2,512]{1,0:T(2,128)S(1)}) custom-call(f32[400,2048]{1,0:T(8,128)} %bitcast.37, bf16[4,336,512]{2,1,0:T(8,128)(2,1)} %get-tuple-element.117.wp_ref, f32[2,2176]{1,0:T(2,128)S(1)} %add_add_fusion.3.st_ref.cnt_ref, f32[4,512]{1,0:T(4,128)S(1)} %copy-done.1, ...), custom_call_target="tpu_custom_call" | custom-call | bytes 40590000 | tf_op jit(solution)/shard_map/hop_back_0/pallas_call | solution.py:521
  130.0 1.5 collective-permute-done.8
  132.8 1.6 collective-permute-start.10
  134.4 11.7 %hop_back_1.1 = (f32[112,2048]{1,0:T(8,128)}, f32[112,512]{1,0:T(8,128)S(1)}, f32[2,512]{1,0:T(2,128)S(1)}) custom-call(f32[400,2048]{1,0:T(8,128)} %bitcast.38, bf16[4,336,512]{2,1,0:T(8,128)(2,1)} %get-tuple-element.117.wp_ref, f32[2,2176]{1,0:T(2,128)S(1)} %add_add_fusion.3.st_ref.cnt_ref, f32[4,512]{1,0:T(4,128)S(1)} %copy-done.1, ...), custom_call_target="tpu_custom_call" | custom-call | bytes 40590000 | tf_op jit(solution)/shard_map/hop_back_1/pallas_call | solution.py:521
  146.5 1.6 collective-permute-start.13
  148.1 2.7 %collective-permute-start.14 = (f32[64,512]{1,0:T(8,128)S(1)}, f32[64,512]{1,0:T(8,128)S(1)}, u32[]{:S(2)}, u32[]{:S(2)}) collective-permute-start(f32[64,512]{1,0:T(8,128)S(1)} %get-tuple-element.239), channel_id=1, source_target_pairs={{0,3},{1,2},{2,1},{3,0},{4,7},{5,6},{6,5},{7,4},{8,11},{9,10},{10,... | collective-permute-start | bytes 393224 | tf_op jit(solution)/shard_map/ppermute | solution.py:688
  150.8 11.6 %hop_back_2.1 = (f32[112,2048]{1,0:T(8,128)}, f32[112,512]{1,0:T(8,128)S(1)}, f32[2,512]{1,0:T(2,128)S(1)}) custom-call(f32[400,2048]{1,0:T(8,128)} %bitcast.39, bf16[4,336,512]{2,1,0:T(8,128)(2,1)} %get-tuple-element.117.wp_ref, f32[2,2176]{1,0:T(2,128)S(1)} %add_add_fusion.3.st_ref.cnt_ref, f32[4,512]{1,0:T(4,128)S(1)} %copy-done.1, ...), custom_call_target="tpu_custom_call" | custom-call | bytes 40590000 | tf_op jit(solution)/shard_map/hop_back_2/pallas_call | solution.py:521
  162.6 1.6 collective-permute-start.16
  164.2 2.7 %collective-permute-start.17 = (f32[64,512]{1,0:T(8,128)S(1)}, f32[64,512]{1,0:T(8,128)S(1)}, u32[]{:S(2)}, u32[]{:S(2)}) collective-permute-start(f32[64,512]{1,0:T(8,128)S(1)} %add_add_fusion.1), channel_id=1, source_target_pairs={{0,3},{1,2},{2,1},{3,0},{4,7},{5,6},{6,5},{7,4},{8,11},{9,10},{10,... | collective-permute-start | bytes 393224 | tf_op jit(solution)/shard_map/ppermute | solution.py:688
  167.0 11.7 %hop_back_3.1 = (f32[112,2048]{1,0:T(8,128)}, f32[112,512]{1,0:T(8,128)S(1)}, f32[2,512]{1,0:T(2,128)S(1)}) custom-call(f32[400,2048]{1,0:T(8,128)} %bitcast.40, bf16[4,336,512]{2,1,0:T(8,128)(2,1)} %get-tuple-element.117.wp_ref, f32[2,2176]{1,0:T(2,128)S(1)} %add_add_fusion.3.st_ref.cnt_ref, f32[4,512]{1,0:T(4,128)S(1)} %copy-done.1, ...), custom_call_target="tpu_custom_call" | custom-call | bytes 40590000 | tf_op jit(solution)/shard_map/hop_back_3/pallas_call | solution.py:521
  180.4 1.5 collective-permute-start.19
  183.4 1.3 collective-permute-start.21
  185.5 1.5 collective-permute-start.23
  186.9 2.0 collective-permute-done.18
  189.5 3.5 %collective-permute-done.21 = f32[80,512]{1,0:T(8,128)S(1)} collective-permute-done((f32[80,512]{1,0:T(8,128)S(1)}, f32[80,512]{1,0:T(8,128)S(1)}, u32[]{:S(2)}, u32[]{:S(2)}) %collective-permute-start.21) | collective-permute-done | bytes 163872 | tf_op jit(solution)/shard_map/ppermute | solution.py:688
  193.0 3.8 %collective-permute-done.23 = f32[80,512]{1,0:T(8,128)S(1)} collective-permute-done((f32[80,512]{1,0:T(8,128)S(1)}, f32[80,512]{1,0:T(8,128)S(1)}, u32[]{:S(2)}, u32[]{:S(2)}) %collective-permute-start.23) | collective-permute-done | bytes 163872 | tf_op jit(solution)/shard_map/ppermute | solution.py:688
  197.5 1.6 collective-permute-start.24
  199.2 1.7 collective-permute-start.27
  200.9 2.7 %collective-permute-start.28 = (f32[20,512]{1,0:T(8,128)S(1)}, f32[20,512]{1,0:T(8,128)S(1)}, u32[]{:S(2)}, u32[]{:S(2)}) collective-permute-start(f32[20,512]{1,0:T(8,128)S(1)} %get-tuple-element.244), channel_id=1, source_target_pairs={{0,3},{1,2},{2,1},{3,0},{4,7},{5,6},{6,5},{7,4},{8,11},{9,10},{10,... | collective-permute-start | bytes 122888 | tf_op jit(solution)/shard_map/ppermute | solution.py:688
  204.7 2.2 collective-permute-done.28
  206.9 3.5 %collective-permute-start.30 = (f32[20,512]{1,0:T(8,128)S(1)}, f32[20,512]{1,0:T(8,128)S(1)}, u32[]{:S(2)}, u32[]{:S(2)}) collective-permute-start(f32[20,512]{1,0:T(8,128)S(1)} %add_add_fusion.2), channel_id=1, source_target_pairs={{0,2},{1,3},{2,0},{3,1},{4,6},{5,7},{6,4},{7,5},{8,10},{9,11},{10,... | collective-permute-start | bytes 122888 | tf_op jit(solution)/shard_map/ppermute | solution.py:688
  211.3 2.1 collective-permute-done.30
  213.4 2.9 %collective-permute-done.31 = f32[20,512]{1,0:T(8,128)S(1)} collective-permute-done((f32[20,512]{1,0:T(8,128)S(1)}, f32[20,512]{1,0:T(8,128)S(1)}, u32[]{:S(2)}, u32[]{:S(2)}) %collective-permute-start.31) | collective-permute-done | bytes 40992 | tf_op jit(solution)/shard_map/ppermute | solution.py:688
  217.4 1.6 collective-permute-start.33
  219.0 1.5 collective-permute-start.34
  220.5 3.5 %collective-permute-done.32 = f32[80,512]{1,0:T(8,128)S(1)} collective-permute-done((f32[80,512]{1,0:T(8,128)S(1)}, f32[80,512]{1,0:T(8,128)S(1)}, u32[]{:S(2)}, u32[]{:S(2)}) %collective-permute-start.32) | collective-permute-done | bytes 163872 | tf_op jit(solution)/shard_map/ppermute | solution.py:688
  224.0 3.8 %collective-permute-done.34 = f32[80,512]{1,0:T(8,128)S(1)} collective-permute-done((f32[80,512]{1,0:T(8,128)S(1)}, f32[80,512]{1,0:T(8,128)S(1)}, u32[]{:S(2)}, u32[]{:S(2)}) %collective-permute-start.34) | collective-permute-done | bytes 163872 | tf_op jit(solution)/shard_map/ppermute | solution.py:688
  228.5 1.6 collective-permute-done.35
  230.2 1.5 maximum_select_fusion.p_ref
  231.7 6.0 %assemble.1 = (f32[2048,512]{1,0:T(8,128)}, f32[4,8,512]{2,1,0:T(8,128)S(1)}) custom-call(s32[1]{0:T(128)} %bitcast.1.half_ref.first_ref, f32[1024,512]{1,0:T(8,128)S(1)} %pad_maximum_fusion.own_ref, f32[1024,512]{1,0:T(8,128)} %collective-permute-done.36.got_ref, f32[2048,512]{1,0:T(8,128)} %w_ref.3), custom_call_target="tpu_custom_call" | custom-call | bytes 18450000 | tf_op jit(solution)/shard_map/assemble/pallas_call | solution.py:561
  237.6 7.3 %fix.1 = (f32[400,2048]{1,0:T(8,128)}, f32[100,4,512]{2,1,0:T(4,128)}, f32[4,512]{1,0:T(4,128)}, f32[4,512]{1,0:T(4,128)}, f32[4,512]{1,0:T(4,128)}, /*index=5*/...) custom-call(s32[16,128]{1,0:T(8,128)S(1)} %bitcast.26, ...), custom_call_target="tpu_custom_call" | custom-call | bytes 29520000 | tf_op jit(solution)/shard_map/fix/pallas_call | solution.py:672
  (104 shorter events, 19.0 us)
Async XLA Ops:
  2.5 24.9 %copy-start.1 = (f32[4,512]{1,0:T(4,128)S(1)}, f32[4,512]{1,0:T(4,128)}, u32[]{:S(2)}) copy-start(f32[4,512]{1,0:T(4,128)} %gain_ref.11) | copy-start | bytes 24580
  2.5 24.9 %copy-start.2 = (f32[4,512]{1,0:T(4,128)S(1)}, f32[4,512]{1,0:T(4,128)}, u32[]{:S(2)}) copy-start(f32[4,512]{1,0:T(4,128)} %slope_ref.11) | copy-start | bytes 24580
  2.5 24.9 %copy-start.4 = (s32[2048]{0:T(1024)S(1)}, s32[2048]{0:T(1024)}, u32[]{:S(2)}) copy-start(s32[2048]{0:T(1024)} %param.16) | copy-start | bytes 24580
  2.5 24.9 %copy-start.5 = (f32[4,512]{1,0:T(4,128)S(1)}, f32[4,512]{1,0:T(4,128)}, u32[]{:S(2)}) copy-start(f32[4,512]{1,0:T(4,128)} %shift_ref.9) | copy-start | bytes 24580
  7.2 1.3 collective-permute-start
  8.5 4.6 %collective-permute-start.1 = (f32[2,2176]{1,0:T(2,128)S(1)}, f32[2,2176]{1,0:T(2,128)S(1)}, u32[]{:S(2)}, u32[]{:S(2)}) collective-permute-start(f32[2,2176]{1,0:T(2,128)S(1)} %add.189), channel_id=1, source_target_pairs={{0,8},{4,12},{8,0},{12,4},{16,24},{20,28},{24,16},{28,20},{1,9},{5... | collective-permute-start | bytes 52232 | tf_op jit(solution)/shard_map/ppermute | solution.py:688
  11.4 3.8 %collective-permute-start.2 = (f32[2,2176]{1,0:T(2,128)S(1)}, f32[2,2176]{1,0:T(2,128)S(1)}, u32[]{:S(2)}, u32[]{:S(2)}) collective-permute-start(f32[2,2176]{1,0:T(2,128)S(1)} %add.189), channel_id=1, source_target_pairs={{0,16},{4,20},{8,24},{12,28},{16,0},{20,4},{24,8},{28,12},{1,17},{... | collective-permute-start | bytes 52232 | tf_op jit(solution)/shard_map/ppermute | solution.py:688
  12.9 4.6 %collective-permute-start.3 = (f32[2,2176]{1,0:T(2,128)S(1)}, f32[2,2176]{1,0:T(2,128)S(1)}, u32[]{:S(2)}, u32[]{:S(2)}) collective-permute-start(f32[2,2176]{1,0:T(2,128)S(1)} %add.189), channel_id=1, source_target_pairs={{0,24},{4,28},{8,16},{12,20},{16,8},{20,12},{24,0},{28,4},{1,25},{... | collective-permute-start | bytes 52232 | tf_op jit(solution)/shard_map/ppermute | solution.py:688
  17.6 4.5 %collective-permute-start.4 = (f32[2,2176]{1,0:T(2,128)S(1)}, f32[2,2176]{1,0:T(2,128)S(1)}, u32[]{:S(2)}, u32[]{:S(2)}) collective-permute-start(f32[2,2176]{1,0:T(2,128)S(1)} %add_add_fusion.4), channel_id=1, source_target_pairs={{0,1},{1,0},{2,3},{3,2},{4,5},{5,4},{6,7},{7,6},{8,9},{9,8},{10,11... | collective-permute-start | bytes 52232 | tf_op jit(solution)/shard_map/ppermute | solution.py:688
  19.2 4.7 %collective-permute-start.5 = (f32[2,2176]{1,0:T(2,128)S(1)}, f32[2,2176]{1,0:T(2,128)S(1)}, u32[]{:S(2)}, u32[]{:S(2)}) collective-permute-start(f32[2,2176]{1,0:T(2,128)S(1)} %add_add_fusion.4), channel_id=1, source_target_pairs={{0,2},{1,3},{2,0},{3,1},{4,6},{5,7},{6,4},{7,5},{8,10},{9,11},{10,... | collective-permute-start | bytes 52232 | tf_op jit(solution)/shard_map/ppermute | solution.py:688
  21.8 5.5 %collective-permute-start.6 = (f32[2,2176]{1,0:T(2,128)S(1)}, f32[2,2176]{1,0:T(2,128)S(1)}, u32[]{:S(2)}, u32[]{:S(2)}) collective-permute-start(f32[2,2176]{1,0:T(2,128)S(1)} %add_add_fusion.4), channel_id=1, source_target_pairs={{0,3},{1,2},{2,1},{3,0},{4,7},{5,6},{6,5},{7,4},{8,11},{9,10},{10,... | collective-permute-start | bytes 52232 | tf_op jit(solution)/shard_map/ppermute | solution.py:688
  27.4 42.4 %copy-start.6 = (f32[512,47]{0,1:T(8,128)S(1)}, f32[512,47]{0,1:T(8,128)}, u32[]{:S(2)}) copy-start(f32[512,47]{0,1:T(8,128)} %param.26) | copy-start | bytes 288772
  27.5 42.4 %copy-start.7 = (s32[2048]{0:T(1024)S(1)}, s32[2048]{0:T(1024)}, u32[]{:S(2)}) copy-start(s32[2048]{0:T(1024)} %param.15) | copy-start | bytes 24580
  27.5 42.4 %copy-start.8 = (f32[512]{0:T(512)S(1)}, f32[512]{0:T(512)}, u32[]{:S(2)}) copy-start(f32[512]{0:T(512)} %param.23) | copy-start | bytes 6148
  27.5 42.4 %copy-start.9 = (f32[512]{0:T(512)S(1)}, f32[512]{0:T(512)}, u32[]{:S(2)}) copy-start(f32[512]{0:T(512)} %param.24) | copy-start | bytes 6148
  27.5 42.4 %copy-start.10 = (f32[512]{0:T(512)S(1)}, f32[512]{0:T(512)}, u32[]{:S(2)}) copy-start(f32[512]{0:T(512)} %param.25) | copy-start | bytes 6148
  27.5 42.4 %copy-start.11 = (f32[47]{0:T(128)S(1)}, f32[47]{0:T(128)}, u32[]{:S(2)}) copy-start(f32[47]{0:T(128)} %param.27) | copy-start | bytes 568
  79.5 11.0 %all-to-all-start.1 = ((f32[32,2,512]{2,1,0:T(2,128)}), f32[32,2,512]{2,1,0:T(2,128)S(1)}, u32[]{:S(2)}, u32[]{:S(2)}) async-start(f32[32,2,512]{2,1,0:T(2,128)} %get-tuple-element.122), calls=%async_computation.1 | async-start | bytes 262144 | tf_op jit(solution)/shard_map/all_to_all | solution.py:712
  102.9 9.7 %collective-permute-start.7 = (f32[1024,512]{1,0:T(8,128)}, f32[1024,512]{1,0:T(8,128)}, u32[]{:S(2)}, u32[]{:S(2)}) collective-permute-start(f32[1024,512]{1,0:T(8,128)} %get-tuple-element.127), channel_id=1, source_target_pairs={{0,4},{4,0},{8,12},{12,8},{16,20},{20,16},{24,28},{28,24},{1,5},{5... | collective-permute-start | bytes 6291464 | tf_op jit(solution)/shard_map/ppermute | solution.py:688
  115.5 14.4 %collective-permute-start.9 = (f32[256,512]{1,0:T(8,128)}, f32[256,512]{1,0:T(8,128)S(1)}, u32[]{:S(2)}, u32[]{:S(2)}) collective-permute-start(f32[256,512]{1,0:T(8,128)} %get-tuple-element.221), channel_id=1, source_target_pairs={{0,16},{4,20},{8,24},{12,28},{16,0},{20,4},{24,8},{28,12},{1,17},{... | collective-permute-start | bytes 1572872 | tf_op jit(solution)/shard_map/ppermute | solution.py:688
  117.3 14.1 %collective-permute-start.8 = (f32[256,512]{1,0:T(8,128)}, f32[256,512]{1,0:T(8,128)S(1)}, u32[]{:S(2)}, u32[]{:S(2)}) collective-permute-start(f32[256,512]{1,0:T(8,128)} %get-tuple-element.227), channel_id=1, source_target_pairs={{0,8},{4,12},{8,0},{12,4},{16,24},{20,28},{24,16},{28,20},{1,9},{5... | collective-permute-start | bytes 1572872 | tf_op jit(solution)/shard_map/ppermute | solution.py:688
  132.2 13.9 %collective-permute-start.11 = (f32[128,512]{1,0:T(8,128)}, f32[128,512]{1,0:T(8,128)S(1)}, u32[]{:S(2)}, u32[]{:S(2)}) collective-permute-start(f32[128,512]{1,0:T(8,128)} %get-tuple-element.229), channel_id=1, source_target_pairs={{0,8},{4,12},{8,0},{12,4},{16,24},{20,28},{24,16},{28,20},{1,9},{5... | collective-permute-start | bytes 786440 | tf_op jit(solution)/shard_map/ppermute | solution.py:688
  132.8 13.3 %collective-permute-start.10 = (f32[128,512]{1,0:T(8,128)S(1)}, f32[128,512]{1,0:T(8,128)S(1)}, u32[]{:S(2)}, u32[]{:S(2)}) collective-permute-start(f32[128,512]{1,0:T(8,128)S(1)} %get-tuple-element.231), channel_id=1, source_target_pairs={{0,16},{4,20},{8,24},{12,28},{16,0},{20,4},{24,8},{28,12},{1,17},{... | collective-permute-start | bytes 786440 | tf_op jit(solution)/shard_map/ppermute | solution.py:688
  146.4 16.1 %collective-permute-start.12 = (f32[64,512]{1,0:T(8,128)S(1)}, f32[64,512]{1,0:T(8,128)S(1)}, u32[]{:S(2)}, u32[]{:S(2)}) collective-permute-start(f32[64,512]{1,0:T(8,128)S(1)} %get-tuple-element.241), channel_id=1, source_target_pairs={{0,1},{1,0},{2,3},{3,2},{4,5},{5,4},{6,7},{7,6},{8,9},{9,8},{10,11... | collective-permute-start | bytes 393224 | tf_op jit(solution)/shard_map/ppermute | solution.py:688
  146.5 16.0 %collective-permute-start.13 = (f32[64,512]{1,0:T(8,128)S(1)}, f32[64,512]{1,0:T(8,128)S(1)}, u32[]{:S(2)}, u32[]{:S(2)}) collective-permute-start(f32[64,512]{1,0:T(8,128)S(1)} %get-tuple-element.242), channel_id=1, source_target_pairs={{0,2},{1,3},{2,0},{3,1},{4,6},{5,7},{6,4},{7,5},{8,10},{9,11},{10,... | collective-permute-start | bytes 393224 | tf_op jit(solution)/shard_map/ppermute | solution.py:688
  148.1 14.4 %collective-permute-start.14 = (f32[64,512]{1,0:T(8,128)S(1)}, f32[64,512]{1,0:T(8,128)S(1)}, u32[]{:S(2)}, u32[]{:S(2)}) collective-permute-start(f32[64,512]{1,0:T(8,128)S(1)} %get-tuple-element.239), channel_id=1, source_target_pairs={{0,3},{1,2},{2,1},{3,0},{4,7},{5,6},{6,5},{7,4},{8,11},{9,10},{10,... | collective-permute-start | bytes 393224 | tf_op jit(solution)/shard_map/ppermute | solution.py:688
  162.5 16.2 %collective-permute-start.15 = (f32[64,512]{1,0:T(8,128)S(1)}, f32[64,512]{1,0:T(8,128)S(1)}, u32[]{:S(2)}, u32[]{:S(2)}) collective-permute-start(f32[64,512]{1,0:T(8,128)S(1)} %add_add_fusion.1), channel_id=1, source_target_pairs={{0,1},{1,0},{2,3},{3,2},{4,5},{5,4},{6,7},{7,6},{8,9},{9,8},{10,11... | collective-permute-start | bytes 393224 | tf_op jit(solution)/shard_map/ppermute | solution.py:688
  162.6 16.1 %collective-permute-start.16 = (f32[64,512]{1,0:T(8,128)S(1)}, f32[64,512]{1,0:T(8,128)S(1)}, u32[]{:S(2)}, u32[]{:S(2)}) collective-permute-start(f32[64,512]{1,0:T(8,128)S(1)} %add_add_fusion.1), channel_id=1, source_target_pairs={{0,2},{1,3},{2,0},{3,1},{4,6},{5,7},{6,4},{7,5},{8,10},{9,11},{10,... | collective-permute-start | bytes 393224 | tf_op jit(solution)/shard_map/ppermute | solution.py:688
  164.2 14.5 %collective-permute-start.17 = (f32[64,512]{1,0:T(8,128)S(1)}, f32[64,512]{1,0:T(8,128)S(1)}, u32[]{:S(2)}, u32[]{:S(2)}) collective-permute-start(f32[64,512]{1,0:T(8,128)S(1)} %add_add_fusion.1), channel_id=1, source_target_pairs={{0,3},{1,2},{2,1},{3,0},{4,7},{5,6},{6,5},{7,4},{8,11},{9,10},{10,... | collective-permute-start | bytes 393224 | tf_op jit(solution)/shard_map/ppermute | solution.py:688
  179.7 2.4 collective-permute-start.20
  179.8 9.2 %collective-permute-start.18 = (f32[128,512]{1,0:T(8,128)S(1)}, f32[128,512]{1,0:T(8,128)S(1)}, u32[]{:S(2)}, u32[]{:S(2)}) collective-permute-start(f32[128,512]{1,0:T(8,128)S(1)} %get-tuple-element.184), channel_id=1, source_target_pairs={{0,16},{4,20},{8,24},{12,28},{16,0},{20,4},{24,8},{28,12},{1,17},{... | collective-permute-start | bytes 786440 | tf_op jit(solution)/shard_map/ppermute | solution.py:688
  180.4 9.1 %collective-permute-start.19 = (f32[128,512]{1,0:T(8,128)S(1)}, f32[128,512]{1,0:T(8,128)S(1)}, u32[]{:S(2)}, u32[]{:S(2)}) collective-permute-start(f32[128,512]{1,0:T(8,128)S(1)} %get-tuple-element.186), channel_id=1, source_target_pairs={{0,8},{4,12},{8,0},{12,4},{16,24},{20,28},{24,16},{28,20},{1,9},{5... | collective-permute-start | bytes 786440 | tf_op jit(solution)/shard_map/ppermute | solution.py:688
  183.4 9.6 %collective-permute-start.21 = (f32[80,512]{1,0:T(8,128)S(1)}, f32[80,512]{1,0:T(8,128)S(1)}, u32[]{:S(2)}, u32[]{:S(2)}) collective-permute-start(f32[80,512]{1,0:T(8,128)S(1)} %get-tuple-element.235), channel_id=1, source_target_pairs={{0,8},{4,12},{8,0},{12,4},{16,24},{20,28},{24,16},{28,20},{1,9},{5... | collective-permute-start | bytes 491528 | tf_op jit(solution)/shard_map/ppermute | solution.py:688
  184.7 8.4 %collective-permute-start.22 = (f32[80,512]{1,0:T(8,128)S(1)}, f32[80,512]{1,0:T(8,128)S(1)}, u32[]{:S(2)}, u32[]{:S(2)}) collective-permute-start(f32[80,512]{1,0:T(8,128)S(1)} %get-tuple-element.234), channel_id=1, source_target_pairs={{0,16},{4,20},{8,24},{12,28},{16,0},{20,4},{24,8},{28,12},{1,17},{... | collective-permute-start | bytes 491528 | tf_op jit(solution)/shard_map/ppermute | solution.py:688
  185.5 11.4 %collective-permute-start.23 = (f32[80,512]{1,0:T(8,128)S(1)}, f32[80,512]{1,0:T(8,128)S(1)}, u32[]{:S(2)}, u32[]{:S(2)}) collective-permute-start(f32[80,512]{1,0:T(8,128)S(1)} %get-tuple-element.233), channel_id=1, source_target_pairs={{0,24},{4,28},{8,16},{12,20},{16,8},{20,12},{24,0},{28,4},{1,25},{... | collective-permute-start | bytes 491528 | tf_op jit(solution)/shard_map/ppermute | solution.py:688
  196.9 19.5 %collective-permute-start.25 = (f32[256,512]{1,0:T(8,128)S(1)}, f32[256,512]{1,0:T(8,128)S(1)}, u32[]{:S(2)}, u32[]{:S(2)}) collective-permute-start(f32[256,512]{1,0:T(8,128)S(1)} %maximum_select_fusion.6), channel_id=1, source_target_pairs={{0,16},{4,20},{8,24},{12,28},{16,0},{20,4},{24,8},{28,12},{1,17},{... | collective-permute-start | bytes 1572872 | tf_op jit(solution)/shard_map/ppermute | solution.py:688
  197.5 18.9 %collective-permute-start.24 = (f32[256,512]{1,0:T(8,128)S(1)}, f32[256,512]{1,0:T(8,128)S(1)}, u32[]{:S(2)}, u32[]{:S(2)}) collective-permute-start(f32[256,512]{1,0:T(8,128)S(1)} %maximum_select_fusion.5), channel_id=1, source_target_pairs={{0,8},{4,12},{8,0},{12,4},{16,24},{20,28},{24,16},{28,20},{1,9},{5... | collective-permute-start | bytes 1572872 | tf_op jit(solution)/shard_map/ppermute | solution.py:688
  199.2 4.5 %collective-permute-start.26 = (f32[20,512]{1,0:T(8,128)S(1)}, f32[20,512]{1,0:T(8,128)S(1)}, u32[]{:S(2)}, u32[]{:S(2)}) collective-permute-start(f32[20,512]{1,0:T(8,128)S(1)} %get-tuple-element.243), channel_id=1, source_target_pairs={{0,1},{1,0},{2,3},{3,2},{4,5},{5,4},{6,7},{7,6},{8,9},{9,8},{10,11... | collective-permute-start | bytes 122888 | tf_op jit(solution)/shard_map/ppermute | solution.py:688
  199.2 5.4 %collective-permute-start.27 = (f32[20,512]{1,0:T(8,128)S(1)}, f32[20,512]{1,0:T(8,128)S(1)}, u32[]{:S(2)}, u32[]{:S(2)}) collective-permute-start(f32[20,512]{1,0:T(8,128)S(1)} %get-tuple-element.245), channel_id=1, source_target_pairs={{0,2},{1,3},{2,0},{3,1},{4,6},{5,7},{6,4},{7,5},{8,10},{9,11},{10,... | collective-permute-start | bytes 122888 | tf_op jit(solution)/shard_map/ppermute | solution.py:688
  200.9 5.9 %collective-permute-start.28 = (f32[20,512]{1,0:T(8,128)S(1)}, f32[20,512]{1,0:T(8,128)S(1)}, u32[]{:S(2)}, u32[]{:S(2)}) collective-permute-start(f32[20,512]{1,0:T(8,128)S(1)} %get-tuple-element.244), channel_id=1, source_target_pairs={{0,3},{1,2},{2,1},{3,0},{4,7},{5,6},{6,5},{7,4},{8,11},{9,10},{10,... | collective-permute-start | bytes 122888 | tf_op jit(solution)/shard_map/ppermute | solution.py:688
  206.9 4.5 %collective-permute-start.29 = (f32[20,512]{1,0:T(8,128)S(1)}, f32[20,512]{1,0:T(8,128)S(1)}, u32[]{:S(2)}, u32[]{:S(2)}) collective-permute-start(f32[20,512]{1,0:T(8,128)S(1)} %add_add_fusion.2), channel_id=1, source_target_pairs={{0,1},{1,0},{2,3},{3,2},{4,5},{5,4},{6,7},{7,6},{8,9},{9,8},{10,11... | collective-permute-start | bytes 122888 | tf_op jit(solution)/shard_map/ppermute | solution.py:688
  206.9 6.5 %collective-permute-start.30 = (f32[20,512]{1,0:T(8,128)S(1)}, f32[20,512]{1,0:T(8,128)S(1)}, u32[]{:S(2)}, u32[]{:S(2)}) collective-permute-start(f32[20,512]{1,0:T(8,128)S(1)} %add_add_fusion.2), channel_id=1, source_target_pairs={{0,2},{1,3},{2,0},{3,1},{4,6},{5,7},{6,4},{7,5},{8,10},{9,11},{10,... | collective-permute-start | bytes 122888 | tf_op jit(solution)/shard_map/ppermute | solution.py:688
  210.5 5.9 %collective-permute-start.31 = (f32[20,512]{1,0:T(8,128)S(1)}, f32[20,512]{1,0:T(8,128)S(1)}, u32[]{:S(2)}, u32[]{:S(2)}) collective-permute-start(f32[20,512]{1,0:T(8,128)S(1)} %add_add_fusion.2), channel_id=1, source_target_pairs={{0,3},{1,2},{2,1},{3,0},{4,7},{5,6},{6,5},{7,4},{8,11},{9,10},{10,... | collective-permute-start | bytes 122888 | tf_op jit(solution)/shard_map/ppermute | solution.py:688
  216.8 14.9 %collective-permute-start.36 = (f32[1024,512]{1,0:T(8,128)S(1)}, f32[1024,512]{1,0:T(8,128)}, u32[]{:S(2)}, u32[]{:S(2)}) collective-permute-start(f32[1024,512]{1,0:T(8,128)S(1)} %pad_maximum_fusion.own_ref), channel_id=1, source_target_pairs={{0,4},{4,0},{8,12},{12,8},{16,20},{20,16},{24,28},{28,24},{1,5},{5... | collective-permute-start | bytes 6291464 | tf_op jit(solution)/shard_map/ppermute | solution.py:688
  216.9 7.1 %collective-permute-start.32 = (f32[80,512]{1,0:T(8,128)S(1)}, f32[80,512]{1,0:T(8,128)S(1)}, u32[]{:S(2)}, u32[]{:S(2)}) collective-permute-start(f32[80,512]{1,0:T(8,128)S(1)} %maximum_select_fusion.11), channel_id=1, source_target_pairs={{0,8},{4,12},{8,0},{12,4},{16,24},{20,28},{24,16},{28,20},{1,9},{5... | collective-permute-start | bytes 491528 | tf_op jit(solution)/shard_map/ppermute | solution.py:688
  217.4 6.6 %collective-permute-start.33 = (f32[80,512]{1,0:T(8,128)S(1)}, f32[80,512]{1,0:T(8,128)S(1)}, u32[]{:S(2)}, u32[]{:S(2)}) collective-permute-start(f32[80,512]{1,0:T(8,128)S(1)} %maximum_select_fusion.11), channel_id=1, source_target_pairs={{0,16},{4,20},{8,24},{12,28},{16,0},{20,4},{24,8},{28,12},{1,17},{... | collective-permute-start | bytes 491528 | tf_op jit(solution)/shard_map/ppermute | solution.py:688
  219.0 8.8 %collective-permute-start.34 = (f32[80,512]{1,0:T(8,128)S(1)}, f32[80,512]{1,0:T(8,128)S(1)}, u32[]{:S(2)}, u32[]{:S(2)}) collective-permute-start(f32[80,512]{1,0:T(8,128)S(1)} %maximum_select_fusion.11), channel_id=1, source_target_pairs={{0,24},{4,28},{8,16},{12,20},{16,8},{20,12},{24,0},{28,4},{1,25},{... | collective-permute-start | bytes 491528 | tf_op jit(solution)/shard_map/ppermute | solution.py:688
  227.9 2.3 collective-permute-start.35
  (3 other events, 21.4 us)

commit v4 on v3

--- a/solution.py
+++ b/solution.py
@@ -13,11 +13,10 @@
 LANES = 128
 LOG2E = 1.4426950408889634
 LN2 = 0.6931471805599453
-TILES = {"gram": 2048, "forward": 512, "head": 512, "mix": 512, "hop": 512, "fix": 1024}
+TILES = {"gram": 2048, "project": 512, "forward": 512, "head": 512, "mix": 512, "hop": 512, "fix": 1024}
 PACK_STEPS = 2
 SUB = 256
 MIX_SUB = 256
-COLS = 512
 NN = (((1,), (0,)), ((), ()))
 NT = (((1,), (1,)), ((), ()))
 TN = (((0,), (0,)), ((), ()))
@@ -81,10 +80,11 @@
     return jnp.concatenate([hi, lo, hi], axis=0)
 
 
-def gram_kernel(in_w, valid_ref, x_ref, w_ref, g_ref, st_ref, wp_ref):
+def gram_kernel(in_w, valid_ref, x_ref, w_ref, g_ref, copies_ref, wp_ref):
     step = pl.program_id(0)
     tile = x_ref.shape[1]
     hops, hid = w_ref.shape[1:]
+    copies = copies_ref.shape[0]
     mask = row_mask(valid_ref, step, tile, 1)
 
     @pl.when(step == 0)
@@ -106,20 +106,20 @@
             w = w_ref[:, h, :]
             w = jnp.concatenate([w, jnp.zeros((n - in_w, hid), F32)], axis=0)
             ws = split(w)
-            g = g_ref[h, :, :n]
-            gw = dot3(split(g), ws)
-            cols = slice(h * hid, (h + 1) * hid)
-            st_ref[0:1, cols] = gw[in_w : in_w + 1, :]
-            st_ref[1:2, cols] = jnp.sum(w * gw, axis=0, keepdims=True)
+            gw = dot3(split(g_ref[h, :, :n]), ws)
+            squares = jnp.sum(w * gw, axis=0, keepdims=True)
+            copies_ref[:, :, h * hid : (h + 1) * hid] = jnp.broadcast_to(squares[None], (copies, 1, hid))
+            sums = g_ref[h, in_w : in_w + 1, :]
+            at = hops * hid + h * LANES
+            copies_ref[:, :, at : at + LANES] = jnp.broadcast_to(sums[None], (copies, 1, LANES))
             wp_ref[h] = jnp.concatenate([ws[0], ws[0], ws[1]], axis=0)
-        st_ref[:, hops * hid :] = jnp.broadcast_to(g_ref[0, in_w : in_w + 1, in_w : in_w + 1], (2, LANES))
-
-
-def gram(valid, x, w, tile):
+
+
+def gram(valid, x, w, copies, tile):
     width, rows = x.shape
     in_w, hops, hid = w.shape
     n = -(-(in_w + 1) // 16) * 16
-    shapes = (hops, n, LANES), (2, hops * hid + LANES), (hops, 3 * n, hid)
+    shapes = (hops, n, LANES), (copies, 1, hops * (hid + LANES)), (hops, 3 * n, hid)
     return pl.pallas_call(
         functools.partial(gram_kernel, in_w),
         grid=(rows // tile,),
@@ -129,7 +129,30 @@
         compiler_params=params(32),
         name="gram",
         cost_estimate=cost(5),
-    )(valid, far(x), w)
+    )(far(valid), far(x), far(w))
+
+
+def project_kernel(in_w, x_ref, wp_ref, z_ref):
+    hid = wp_ref.shape[2]
+    for h in range(wp_ref.shape[0]):
+        xs = stack3(hop_rows(x_ref, h, in_w))
+        cols = slice(h * hid, (h + 1) * hid)
+        z_ref[:, cols] = lax.dot_general(xs, wp_ref[h], TN, preferred_element_type=F32)
+
+
+def project(x, wp, in_w, tile):
+    width, rows = x.shape
+    hops, _, hid = wp.shape
+    return pl.pallas_call(
+        functools.partial(project_kernel, in_w),
+        grid=(rows // tile,),
+        in_specs=[pl.BlockSpec((width, tile), lambda i: (0, i)), whole(wp, 1)],
+        out_specs=pl.BlockSpec((tile, hops * hid), lambda i: (i, 0)),
+        out_shape=pltpu.HBM((rows, hops * hid), F32),
+        compiler_params=params(24),
+        name="project",
+        cost_estimate=cost(9),
+    )(far(x), far(wp))
 
 
 def count_of(st_ref):
@@ -150,62 +173,59 @@
 
 
 def forward_kernel(
-    in_w, valid_ref, x_ref, wp_ref, st_ref, gain_ref, shift_ref, slope_ref, mslope_ref, w_ref,
-    j_ref, uh_ref, ul_ref, v_ref, copies_ref, wh_ref, wl_ref, st2_ref,
+    in_w, valid_ref, z_ref, wp_ref, all_ref, gain_ref, shift_ref, slope_ref, mslope_ref, w_ref,
+    uh_ref, ul_ref, v_ref, copies_ref, wh_out, wl_out, st_ref, coef_ref,
+    st2_ref, wh_ref, wl_ref,
 ):
     step = pl.program_id(0)
-    tile = x_ref.shape[1]
+    tile = z_ref.shape[0]
     hops, hid = gain_ref.shape
     mask = row_mask(valid_ref, step, tile)
 
     @pl.when(step == 0)
     def _():
         st2_ref[...] = jnp.zeros_like(st2_ref)
+        sums = jnp.sum(all_ref[...], axis=0)
+        n = wp_ref.shape[1] // 3
         for h in range(hops):
             rows = slice(h * hid, (h + 1) * hid)
             wh_ref[rows, :], wl_ref[rows, :] = split(w_ref[rows, :])
-
-    dot = functools.partial(lax.dot_general, preferred_element_type=F32)
-    chunks = [(h, c) for h in range(hops) for c in range(0, hid, COLS)]
-    scales, xs = {}, {}
-
-    def project(i):
-        h, c = chunks[i]
-        if h not in xs:
-            xs[h] = stack3(hop_rows(x_ref, h, in_w))
-        return dot(xs[h], wp_ref[h, :, c : c + COLS], TN)
-
-    def activate(i, z):
-        h, c = chunks[i]
-        if h not in scales:
-            scales[h] = scale_of(st_ref, slice(h * hid, (h + 1) * hid), gain_ref, shift_ref, h)
-        part = slice(c, c + COLS)
-        cols = slice(h * hid + c, h * hid + c + COLS)
-        a, b = (t[:, part] for t in scales[h])
-        s1 = slope_ref[h : h + 1, part]
-        s2 = mslope_ref[h : h + 1, part]
+            at = hops * hid + h * LANES
+            xm = jnp.broadcast_to(sums[:, at : at + n], (8, n))
+            st_ref[0:1, rows] = dot3(split(xm), (wp_ref[h, :n, :], wp_ref[h, 2 * n :, :]))[0:1, :]
+            st_ref[1:2, rows] = sums[:, rows]
+        at = hops * hid + in_w
+        st_ref[:, hops * hid :] = jnp.broadcast_to(sums[:, at : at + 1], (2, LANES))
+        for h in range(hops):
+            a, b = scale_of(st_ref, slice(h * hid, (h + 1) * hid), gain_ref, shift_ref, h)
+            coef_ref[h] = jnp.concatenate(
+                [a, b, slope_ref[h : h + 1, :], mslope_ref[h : h + 1, :], jnp.zeros((4, hid), F32)], axis=0
+            )
+
+    def activate(h, z):
+        cols = slice(h * hid, (h + 1) * hid)
+        a, b = scale_of(st_ref, cols, gain_ref, shift_ref, h)
+        s1 = slope_ref[h : h + 1, :]
+        s2 = mslope_ref[h : h + 1, :]
         j = act2(z * a + b, s1, LOG2E * (1.0 - s1))
         u = act2(j, s2, LOG2E * (1.0 - s2))
-        j_ref[:, cols] = j
         us = split(u)
         uh_ref[:, cols], ul_ref[:, cols] = us
         return us
 
-    def mix(i, us):
-        h, c = chunks[i]
-        cols = slice(h * hid + c, h * hid + c + COLS)
+    def mix(h, us):
+        cols = slice(h * hid, (h + 1) * hid)
         part = dot3(us, (wh_ref[cols, :], wl_ref[cols, :]))
-        v_ref[...] = part if i == 0 else v_ref[...] + part
-
-    z = project(0)
+        v_ref[...] = part if h == 0 else v_ref[...] + part
+
     before = None
-    for i in range(len(chunks)):
-        ahead = project(i + 1) if i + 1 < len(chunks) else None
+    for h in range(hops):
         if before is not None:
-            mix(i - 1, before)
-        before = activate(i, z)
-        z = ahead
-    mix(len(chunks) - 1, before)
+            mix(h - 1, before)
+        before = activate(h, z_ref[:, h * hid : (h + 1) * hid])
+    mix(hops - 1, before)
+    piece = pl.ds(pl.multiple_of(step * wh_out.shape[0], wh_out.shape[0]), wh_out.shape[0])
+    wh_out[...], wl_out[...] = wh_ref[piece, :], wl_ref[piece, :]
     v = v_ref[...]
     v = LN2 * v
     v_ref[...] = v
@@ -218,31 +238,39 @@
         copies_ref[...] = jnp.broadcast_to(st2_ref[...][None], copies_ref.shape)
 
 
-def forward(valid, x, wp, st, gain, shift, slope, mslope, w, in_w, copies, tile):
-    width, rows = x.shape
+def forward(valid, z, wp, sums, gain, shift, slope, mslope, w, in_w, copies, tile):
+    rows = z.shape[0]
     mix, hid = w.shape
     by = lambda n: pl.BlockSpec((tile, n), lambda i: (i, 0))
     return pl.pallas_call(
         functools.partial(forward_kernel, in_w),
         grid=(rows // tile,),
-        in_specs=[whole(valid), pl.BlockSpec((width, tile), lambda i: (0, i))]
-        + [whole(t, 1) for t in (wp, st, gain, shift, slope, mslope, w)],
-        out_specs=[by(mix), by(mix), by(mix), by(hid), pl.BlockSpec((copies, 2, hid), lambda i: (0, 0, 0))]
-        + [pl.BlockSpec((mix, hid), lambda i: (0, 0), pipeline_mode=pl.Buffered(1))] * 2,
+        in_specs=[whole(valid), by(mix)]
+        + [whole(t, 1) for t in (wp, sums, gain, shift, slope, mslope, w)],
+        out_specs=[by(mix)] * 2
+        + [by(hid), pl.BlockSpec((copies, 2, hid), lambda i: (0, 0, 0))]
+        + [pl.BlockSpec((mix * tile // rows, hid), lambda i: (i, 0))] * 2
+        + [pl.BlockSpec((2, mix + LANES), lambda i: (0, 0))]
+        + [pl.BlockSpec((mix // hid, 8, hid), lambda i: (0, 0, 0))],
         out_shape=[
-            pltpu.HBM((rows, mix), F32),
             pltpu.HBM((rows, mix), BF16),
             pltpu.HBM((rows, mix), BF16),
             pltpu.HBM((rows, hid), F32),
             jax.ShapeDtypeStruct((copies, 2, hid), F32),
             pltpu.HBM((mix, hid), BF16),
             pltpu.HBM((mix, hid), BF16),
+            jax.ShapeDtypeStruct((2, mix + LANES), F32),
+            jax.ShapeDtypeStruct((mix // hid, 8, hid), F32),
         ],
-        scratch_shapes=[pltpu.VMEM((2, hid), F32)],
-        compiler_params=params(43),
+        scratch_shapes=[
+            pltpu.VMEM((2, hid), F32),
+            pltpu.VMEM((mix, hid), BF16),
+            pltpu.VMEM((mix, hid), BF16),
+        ],
+        compiler_params=params(48),
         name="forward",
         cost_estimate=cost(30),
-    )(valid, far(x), far(wp), st, gain, shift, slope, mslope, far(w))
+    )(valid, far(z), far(wp), sums, gain, shift, slope, mslope, far(w))
 
 
 def as_column(row):
@@ -452,13 +480,11 @@
 
 
 def hop_kernel(
-    h, in_w, x_ref, wp_ref, st_ref, gain_ref, shift_ref, slope_ref, mslope_ref, dvh_ref, dvl_ref, mwh_ref, mwl_ref,
-    j_ref,
+    h, in_w, x_ref, wp_ref, coef_ref, dvh_ref, dvl_ref, mwh_ref, mwl_ref,
     dx_ref, bw_ref, sums_ref,
 ):
     step = pl.program_id(0)
     n = wp_ref.shape[1] // 3
-    hid = gain_ref.shape[1]
     tile = x_ref.shape[1]
 
     @pl.when(step == 0)
@@ -466,10 +492,8 @@
         bw_ref[...] = jnp.zeros_like(bw_ref)
         sums_ref[...] = jnp.zeros_like(sums_ref)
 
-    a, b = scale_of(st_ref, slice(h * hid, (h + 1) * hid), gain_ref, shift_ref, h)
-    s1 = slope_ref[h : h + 1, :]
-    s2 = mslope_ref[h : h + 1, :]
-    xall = stack3(hop_rows(x_ref, h, in_w, 1.0))
+    a, b, s1, s2 = (coef_ref[0, k : k + 1, :] for k in range(4))
+    xall = stack3(hop_rows(x_ref, h % (x_ref.shape[0] // in_w), in_w, 1.0))
     wp = wp_ref[0]
     wh, wl = split((wp[:n].astype(F32) + wp[2 * n :].astype(F32)) * a)
     whl = jnp.concatenate([wh, wl], axis=0)
@@ -484,9 +508,10 @@
 
     def middle(rs, z, du):
         y = z * a + b
-        j = j_ref[rs, :]
+        e = 1.0 + jnp.exp2(jnp.minimum(y, 30.0))
+        j = jnp.maximum(s1 * y + (LOG2E * (1.0 - s1)) * jnp.log(e), y)
         dj = du * (1.0 - (1.0 - s2) / (1.0 + jnp.exp2(j)))
-        dy = dj * (1.0 - (1.0 - s1) / (1.0 + jnp.exp2(y)))
+        dy = dj * (1.0 - (1.0 - s1) / e)
         for q, t in enumerate((dj * (y - j), du * j)):
             sums[q] = sums[q] + row(t)
         return split(dy)
@@ -512,8 +537,10 @@
         sums_ref[q : q + 1, :] += sums[q]
 
 
-def hop_back(h, in_w, x, wp, st, gain, shift, slope, mslope, dvh, dvl, mwh, mwl, j, tile):
+def hop_back(h, in_w, x, wp, coef, dvh, dvl, mwh, mwl, tile):
     width, rows = x.shape
+    some = 2 * in_w if width % (2 * in_w) == 0 and in_w % 4 == 0 else width
+    at = h * in_w // some
     hid = dvh.shape[1]
     n = wp.shape[1] // 3
     by = lambda w, k=0: pl.BlockSpec((tile, w), lambda i: (i, k))
@@ -522,11 +549,11 @@
         functools.partial(hop_kernel, h, in_w),
         grid=(rows // tile,),
         in_specs=[
-            pl.BlockSpec((width, tile), lambda i: (0, i)),
+            pl.BlockSpec((some, tile), lambda i: (at, i)),
             pl.BlockSpec((1, 3 * n, hid), lambda i: (h, 0, 0)),
+            pl.BlockSpec((1, 8, hid), lambda i: (h, 0, 0)),
         ]
-        + [whole(t) for t in (st, gain, shift, slope, mslope)]
-        + [by(hid), by(hid), block(hid), block(hid), by(hid, h)],
+        + [by(hid), by(hid), block(hid), block(hid)],
         out_specs=[
             pl.BlockSpec((n, tile), lambda i: (0, i)),
             pl.BlockSpec((n, hid), lambda i: (0, 0)),
@@ -540,7 +567,7 @@
         compiler_params=params(20),
         name=f"hop_back_{h}",
         cost_estimate=cost(11),
-    )(far(x), far(wp), st, gain, shift, slope, mslope, far(dvh), far(dvl), far(mwh), far(mwl), far(j))
+    )(far(x), far(wp), coef, far(dvh), far(dvl), far(mwh), far(mwl))
 
 
 def assemble_kernel(first_ref, own_ref, got_ref, w_ref, m_ref, uu_ref):
@@ -688,26 +715,6 @@
     return lax.ppermute(v, axis, [(i, i ^ k) for i in range(size)])
 
 
-def sum_small(v, sizes):
-    steps = []
-    for axis, size in sizes.items():
-        k = 1
-        if axis == "dp" and size >= 2:
-            steps.append((axis, size, 1, 2))
-            k = 2
-        while k < size:
-            wide = 4 if 4 * k <= size else 2
-            steps.append((axis, size, k, wide))
-            k *= wide
-    for axis, size, k, wide in steps:
-        if wide == 2:
-            v = v + flip(v, axis, size, k)
-        else:
-            p1, p2, p3 = (flip(v, axis, size, k * m) for m in (1, 2, 3))
-            v = (v + p1) + (p2 + p3)
-    return v
-
-
 def exchange(copies):
     return lax.all_to_all(copies, ("dp", "bucket"), 0, 0, tiled=True)
 
@@ -727,10 +734,13 @@
     return jnp.where(bit == 0, jnp.concatenate([v, got], 0), jnp.concatenate([got, v], 0))
 
 
-def halve(parts, axis, size, k):
+def halve(v, axis, size, k):
     bit = lax.axis_index(axis) // k % 2
-    part = lambda i: functools.reduce(jnp.add, [take(p, i, 2) for p in parts])
-    return part(bit), flip(part(1 - bit), axis, size, k)
+    return v, flip(take(v, 1 - bit, 2), axis, size, k)
+
+
+def kept(v, got, axis, size, k):
+    return take(v, lax.axis_index(axis) // k % 2, 2) + got
 
 
 def spread(v, axis, size, k):
@@ -763,22 +773,28 @@
     core = ("dp", dp, 1)
     within = within and dp > 1
     if within:
-        parts = yield halve(parts, *core)
+        parts = [kept(*(yield halve(total(parts), *core)), *core)]
     if square:
         parts = yield spread(total(parts), "dp", dp, 2)
     elif across:
-        top, bottom = ([pieces(p, 2)[i] for p in parts] for i in range(2))
-        for a, b in zip(across, across[::-1]):
-            top, bottom = yield halve(top, *a), halve(bottom, *b)
-        parts = [jnp.concatenate([total(top), total(bottom)], 0)]
+        a, b = across[0], across[-1]
+        bits = [lax.axis_index("dp") // s[2] % 2 for s in (a, b)]
+        quarter = lambda i: functools.reduce(jnp.add, [take(p, i, 4) for p in parts])
+        gone = flip(quarter(1 - bits[0]), *a), flip(quarter(3 - bits[1]), *b)
+        parts, got = yield tuple(parts), gone
+        top, bottom = quarter(bits[0]) + got[0], quarter(2 + bits[1]) + got[1]
+        for a, b in list(zip(across, across[::-1]))[1:]:
+            got = yield halve(top, *a), halve(bottom, *b)
+            top, bottom = kept(*got[0], *a), kept(*got[1], *b)
+        parts = [jnp.concatenate([top, bottom], 0)]
     if bucket == 4:
         parts = yield spread(total(parts), "bucket", bucket, 1)
         parts = yield collect(total(parts), "bucket", bucket, 1)
         v = in_order(parts, "bucket", 1)
     else:
+        v = total(parts)
         for s in line:
-            parts = yield halve(parts, *s)
-        v = total(parts)
+            v = kept(*(yield halve(v, *s)), *s)
         for s in line[::-1]:
             parts = yield v, flip(v, *s)
             v = merge(*parts, *s)
@@ -819,11 +835,13 @@
     row = lambda t: t.reshape(1, -1)
     x = feats.T
 
-    g, st, wp = gram(valid, x, branch_w.transpose(1, 0, 2), TILES["gram"])
-    st = sum_small(st, sizes)
-    j, uh, ul, v, st2, mwh, mwl = forward(
-        valid, x, wp, st, branch_gain, branch_shift, branch_slope, mslope, mix_w, in_w,
-        sizes["dp"] * sizes["bucket"], TILES["forward"],
+    devices = sizes["dp"] * sizes["bucket"]
+    g, sums, wp = gram(valid, x, branch_w.transpose(1, 0, 2), devices, TILES["gram"])
+    sums = exchange(sums)
+    z = project(x, wp, in_w, TILES["project"])
+    uh, ul, v, st2, mwh, mwl, st, coef = forward(
+        valid, z, wp, sums, branch_gain, branch_shift, branch_slope, mslope, mix_w, in_w, devices,
+        TILES["forward"],
     )
     st2 = exchange(st2)
     dy2, st3, misc = head(
@@ -848,25 +866,25 @@
     for h in range(hops):
         first.step()
         dx, bw, s = hop_back(
-            h, in_w, x, wp, st, branch_gain, branch_shift, branch_slope, mslope, dvh, dvl, mwh, mwl,
-            j, TILES["hop"],
+            h, in_w, x, wp, coef, dvh, dvl, mwh, mwl, TILES["hop"],
         )
         dxs, bws, sums = dxs + [dx], bws + [bw], sums + [s]
         first.state, x, bws, sums = lax.optimization_barrier((first.state, x, bws, sums))
     packed = pack(g, misc, bws, sums, max(128, 2 * sizes["dp"] * sizes["bucket"]))
     last = Steps(sum_steps((packed,), sizes, False, True))
+    first.step()
+    last.step()
+    last.step()
+    first.state, last.state = lax.optimization_barrier((first.state, last.state))
+    first.step()
+    last.step()
+    first.state, last.state = lax.optimization_barrier((first.state, last.state))
     while not first.done:
         first.step()
-        for _ in range(PACK_STEPS):
-            last.step()
-        first.state, last.state = lax.optimization_barrier((first.state, last.state))
     m = first.value
-    if within:
-        m, other = m, flip(m, "dp", sizes["dp"], 1)
-        last.step()
-        m, other, last.state = lax.optimization_barrier((m, other, last.state))
-    else:
-        m, other = pieces(m, 2)
+    m, other = (m, flip(m, "dp", sizes["dp"], 1)) if within else pieces(m, 2)
+    last.step()
+    m, other, last.state = lax.optimization_barrier((m, other, last.state))
     last.step()
     m, uu = assemble(half(core), m, other, mix_w)
     m, uu, last.state = lax.optimization_barrier((m, uu, last.state))

time: 246 us -> 235 us (0.955)
  waiting for transfers between devices: 48.3 us -> 34.7 us
  Pallas kernels: 128 us -> 133 us
  local copies, waits for them, and re-layouts: 6.08 us -> 2.55 us
  blocking collectives: 10.1 us -> 13.1 us
    ppermute x37 -> x30, waiting for transfers between devices: 40.1 us -> 25.5 us  [flip(): return lax.ppermute(v, axis, [(i, i ^ k) for i in range(size)])]
    pallas_call x0 -> x1, Pallas kernels: none -> 9.85 us  [project(): pl.pallas_call(functools.partial(project_kernel, in_w), grid=(rows // til...]
    ppermute x37 -> x30, starting transfers between devices: 42.1 us -> 33 us  [flip(): return lax.ppermute(v, axis, [(i, i ^ k) for i in range(size)])]
    all_to_all x1 -> x2, starting transfers between devices: 2.76 us -> 10.1 us  [exchange(): return lax.all_to_all(copies, ('dp', 'bucket'), 0, 0, tiled=True)]
    pallas_call x1, Pallas kernels: 32.2 us -> 28.5 us  [forward(): pl.pallas_call(functools.partial(forward_kernel, in_w), grid=(rows // til...]
    all_to_all x1, blocking collectives: 10.1 us -> 13.1 us  [exchange(): return lax.all_to_all(copies, ('dp', 'bucket'), 0, 0, tiled=True)]
    all_to_all x1 -> x2, waiting for transfers between devices: 8.21 us -> 9.2 us  [exchange(): return lax.all_to_all(copies, ('dp', 'bucket'), 0, 0, tiled=True)]
  transfers between devices with their start and end apart: 38 -> 32, of which waited for: 21 -> 16; matrix products, arithmetic and copies ran while one was open for 2% -> 1% of each run, Pallas kernels for 23% -> 30%
where the time goes in v4:
time: 235 us
  Pallas kernels  133 us (57%)
  starting transfers between devices  43 us (18%)
  waiting for transfers between devices  34.7 us (15%)
  blocking collectives  13.1 us (6%)
  other arithmetic  7.39 us (3%)
  local copies, waits for them, and re-layouts  2.55 us (1%)
    pallas_call x4, Pallas kernels, hop_back(): pl.pallas_call(functools.partial(hop_kernel, h, in_w), grid=(rows // tile...  45.3 us
    ppermute x30, starting transfers between devices, flip(): return lax.ppermute(v, axis, [(i, i ^ k) for i in range(size)])  33 us
    pallas_call x1, Pallas kernels, forward(): pl.pallas_call(functools.partial(forward_kernel, in_w), grid=(rows // til...  28.5 us
    ppermute x30, waiting for transfers between devices, flip(): return lax.ppermute(v, axis, [(i, i ^ k) for i in range(size)])  25.5 us
    all_to_all x1, blocking collectives, exchange(): return lax.all_to_all(copies, ('dp', 'bucket'), 0, 0, tiled=True)  13.1 us
    pallas_call x1, Pallas kernels, mix_back(): pl.pallas_call(mix_first_kernel, grid_spec=pltpu.PrefetchScalarGridSpec(n...  12.3 us
    all_to_all x2, starting transfers between devices, exchange(): return lax.all_to_all(copies, ('dp', 'bucket'), 0, 0, tiled=True)  10.1 us
    pallas_call x1, Pallas kernels, project(): pl.pallas_call(functools.partial(project_kernel, in_w), grid=(rows // til...  9.85 us
  transfers between devices with their start and end apart: 32, of which 16 were waited for; matrix products, arithmetic and copies ran while one was open for 1% of the time, Pallas kernels for 30%

profile of v4, /device:TPU:0, one launch (start us, length us, event | category | flops | bytes accessed | tf_op | source)
XLA Modules:
  0.0 234.9 jit_solution(12236308483203135479)
XLA Ops:
  0.6 5.0 %gram.1 = (f32[4,112,128]{2,1,0:T(8,128)S(1)}, f32[32,1,2560]{2,1,0:T(1,128)}, bf16[4,336,512]{2,1,0:T(8,128)(2,1)}) custom-call(s32[16,128]{1,0:T(8,128)} %bitcast.21, f32[400,2048]{1,0:T(8,128)} %bitcast.34, f32[100,4,512]{2,1,0:T(4,128)} %bitcast.41), custom_call_target="tpu_custom_call" | custom-call | bytes 18450000 | tf_op jit(solution)/shard_map/gram/pallas_call | solution.py:123
  5.6 7.3 %all-to-all-start = ((f32[32,1,2560]{2,1,0:T(1,128)}), f32[32,1,2560]{2,1,0:T(1,128)S(1)}, u32[]{:S(2)}, u32[]{:S(2)}) async-start(f32[32,1,2560]{2,1,0:T(1,128)} %get-tuple-element.127), calls=%async_computation | async-start | bytes 655360 | tf_op jit(solution)/shard_map/all_to_all | solution.py:719
  13.0 9.8 %project.1.z_ref = f32[2048,2048]{1,0:T(8,128)} custom-call(f32[400,2048]{1,0:T(8,128)} %bitcast.35, bf16[4,336,512]{2,1,0:T(8,128)(2,1)} %get-tuple-element.126.wp_ref), custom_call_target="tpu_custom_call" | custom-call | bytes 33210000 | tf_op jit(solution)/shard_map/project/pallas_call | solution.py:146
  22.9 1.0 all-to-all-done.all_ref
  23.9 28.5 %forward.1 = (bf16[2048,2048]{1,0:T(8,128)(2,1)}, bf16[2048,2048]{1,0:T(8,128)(2,1)}, f32[2048,512]{1,0:T(8,128)}, f32[32,2,512]{2,1,0:T(2,128)S(1)}, bf16[2048,...) custom-call(s32[16,128]{1,0:T(8,128)S(1)} %bitcast.22, ...), custom_call_target="tpu_custom_call" | custom-call | bytes 110700000 | tf_op jit(solution)/shard_map/forward/pallas_call | solution.py:245
  52.5 13.1 %all_to_all.15.st_ref.st2_ref = f32[32,2,512]{2,1,0:T(2,128)S(1)} all-to-all(f32[32,2,512]{2,1,0:T(2,128)S(1)} %get-tuple-element.129), channel_id=1, replica_groups=mesh['dp'=8,'bucket'=4] {'dp','bucket'}, dimensions={0} | all-to-all | bytes 262144 | tf_op jit(solution)/shard_map/all_to_all | solution.py:719
  65.6 9.7 %head.1 = (f32[2048,512]{1,0:T(8,128)}, f32[32,2,512]{2,1,0:T(2,128)}, f32[56,512]{1,0:T(8,128)S(1)}) custom-call(s32[16,128]{1,0:T(8,128)S(1)} %bitcast.23, s32[16,128]{1,0:T(8,128)S(1)} %bitcast.27, f32[2048,512]{1,0:T(8,128)} %get-tuple-element.128.v_ref, f32[32,2,512]{2,1,0:T(2,128)S(1)} %all_to_all.15.st_ref.st2_ref, ...), custom_call_target="tpu_custom_call" | custom-call | bytes 33210000 | tf_op jit(solution)/shard_map/head/pallas_call | solution.py:363
  75.2 2.8 %all-to-all-start.2 = ((f32[32,2,512]{2,1,0:T(2,128)}), f32[32,2,512]{2,1,0:T(2,128)S(1)}, u32[]{:S(2)}, u32[]{:S(2)}) async-start(f32[32,2,512]{2,1,0:T(2,128)} %get-tuple-element.132), calls=%async_computation.2 | async-start | bytes 262144 | tf_op jit(solution)/shard_map/all_to_all | solution.py:719
  78.0 8.2 %all-to-all-done.2.st3_ref = f32[32,2,512]{2,1,0:T(2,128)S(1)} async-done(((f32[32,2,512]{2,1,0:T(2,128)}), f32[32,2,512]{2,1,0:T(2,128)S(1)}, u32[]{:S(2)}, u32[]{:S(2)}) %all-to-all-start.2) | async-done | bytes 131104 | tf_op jit(solution)/shard_map/all_to_all | solution.py:719
  86.2 12.3 %mix_back.1 = (f32[1024,512]{1,0:T(8,128)}, bf16[2048,512]{1,0:T(8,128)(2,1)}, bf16[2048,512]{1,0:T(8,128)(2,1)}, f32[2,512]{1,0:T(2,128)S(1)}) custom-call(s32[1]{0:T(128)} %bitcast.2.half_ref, s32[16,128]{1,0:T(8,128)S(1)} %bitcast.24, f32[2048,512]{1,0:T(8,128)} %get-tuple-element.131.dy_ref, f32[2048,512]{1,0:T(8,128)} %get-tuple-element.128.v_ref, ...), custom_call_target="tpu_custom_call" | custom-call | bytes 51660000 | tf_op jit(solution)/shard_map/mix_back/pallas_call | solution.py:439
  98.7 9.5 %mix_back_rest.1 = f32[1024,512]{1,0:T(8,128)S(1)} custom-call(s32[1]{0:T(128)} %bitcast.1.half_ref.first_ref, bf16[2048,512]{1,0:T(8,128)(2,1)} %get-tuple-element.135.dvh_ref, bf16[2048,512]{1,0:T(8,128)(2,1)} %get-tuple-element.136.dvl_ref, bf16[2048,2048]{1,0:T(8,128)(2,1)} %get-tuple-element.133.uh_ref, bf16[2048,2048]{1,0:T(8,128)(2,1)} %get-tuple-element.134.ul_ref), custom_call_target="tpu_custom_call" | custom-call | bytes 44280000 | tf_op jit(solution)/shard_map/mix_back_rest/pallas_call | solution.py:466
  108.2 2.3 dynamic-slice_add_fusion.1
  111.8 11.3 %hop_back_0.1 = (f32[112,2048]{1,0:T(8,128)}, f32[112,512]{1,0:T(8,128)S(1)}, f32[2,512]{1,0:T(2,128)S(1)}) custom-call(f32[400,2048]{1,0:T(8,128)} %bitcast.36, bf16[4,336,512]{2,1,0:T(8,128)(2,1)} %get-tuple-element.126.wp_ref, f32[4,8,512]{2,1,0:T(8,128)S(1)} %get-tuple-element.141.coef_ref, bf16[2048,512]{1,0:T(8,128)(2,1)} %get-tuple-element.135.dvh_ref, ...), custom_call_target="tpu_custom_call" | custom-call | bytes 40590000 | tf_op jit(solution)/shard_map/hop_back_0/pallas_call | solution.py:548
  123.2 1.9 collective-permute-done.1
  125.8 1.7 add_add_fusion
  127.6 1.1 collective-permute-start.4
  129.6 11.4 %hop_back_1.1 = (f32[112,2048]{1,0:T(8,128)}, f32[112,512]{1,0:T(8,128)S(1)}, f32[2,512]{1,0:T(2,128)S(1)}) custom-call(f32[400,2048]{1,0:T(8,128)} %bitcast.37, bf16[4,336,512]{2,1,0:T(8,128)(2,1)} %get-tuple-element.126.wp_ref, f32[4,8,512]{2,1,0:T(8,128)S(1)} %get-tuple-element.141.coef_ref, bf16[2048,512]{1,0:T(8,128)(2,1)} %get-tuple-element.135.dvh_ref, ...), custom_call_target="tpu_custom_call" | custom-call | bytes 40590000 | tf_op jit(solution)/shard_map/hop_back_1/pallas_call | solution.py:548
  141.4 1.6 collective-permute-start.6
  143.0 2.7 %collective-permute-start.7 = (f32[64,512]{1,0:T(8,128)S(1)}, f32[64,512]{1,0:T(8,128)S(1)}, u32[]{:S(2)}, u32[]{:S(2)}) collective-permute-start(f32[64,512]{1,0:T(8,128)S(1)} %get-tuple-element.249), channel_id=1, source_target_pairs={{0,3},{1,2},{2,1},{3,0},{4,7},{5,6},{6,5},{7,4},{8,11},{9,10},{10,... | collective-permute-start | bytes 393224 | tf_op jit(solution)/shard_map/ppermute | solution.py:715
  145.8 11.2 %hop_back_2.1 = (f32[112,2048]{1,0:T(8,128)}, f32[112,512]{1,0:T(8,128)S(1)}, f32[2,512]{1,0:T(2,128)S(1)}) custom-call(f32[400,2048]{1,0:T(8,128)} %bitcast.38, bf16[4,336,512]{2,1,0:T(8,128)(2,1)} %get-tuple-element.126.wp_ref, f32[4,8,512]{2,1,0:T(8,128)S(1)} %get-tuple-element.141.coef_ref, bf16[2048,512]{1,0:T(8,128)(2,1)} %get-tuple-element.135.dvh_ref, ...), custom_call_target="tpu_custom_call" | custom-call | bytes 40590000 | tf_op jit(solution)/shard_map/hop_back_2/pallas_call | solution.py:548
  157.1 1.2 collective-permute-start.10
  158.2 3.3 %collective-permute-start.9 = (f32[64,512]{1,0:T(8,128)S(1)}, f32[64,512]{1,0:T(8,128)S(1)}, u32[]{:S(2)}, u32[]{:S(2)}) collective-permute-start(f32[64,512]{1,0:T(8,128)S(1)} %add_add_fusion.3), channel_id=1, source_target_pairs={{0,2},{1,3},{2,0},{3,1},{4,6},{5,7},{6,4},{7,5},{8,10},{9,11},{10,... | collective-permute-start | bytes 393224 | tf_op jit(solution)/shard_map/ppermute | solution.py:715
  161.5 11.3 %hop_back_3.1 = (f32[112,2048]{1,0:T(8,128)}, f32[112,512]{1,0:T(8,128)S(1)}, f32[2,512]{1,0:T(2,128)S(1)}) custom-call(f32[400,2048]{1,0:T(8,128)} %bitcast.39, bf16[4,336,512]{2,1,0:T(8,128)(2,1)} %get-tuple-element.126.wp_ref, f32[4,8,512]{2,1,0:T(8,128)S(1)} %get-tuple-element.141.coef_ref, bf16[2048,512]{1,0:T(8,128)(2,1)} %get-tuple-element.135.dvh_ref, ...), custom_call_target="tpu_custom_call" | custom-call | bytes 40590000 | tf_op jit(solution)/shard_map/hop_back_3/pallas_call | solution.py:548
  174.0 1.3 collective-permute-start.11
  176.5 1.1 collective-permute-start.14
  177.6 1.0 collective-permute-start.15
  178.6 1.4 collective-permute-start.16
  180.0 3.2 %collective-permute-done.11 = f32[128,512]{1,0:T(8,128)S(1)} collective-permute-done((f32[128,512]{1,0:T(8,128)S(1)}, f32[128,512]{1,0:T(8,128)S(1)}, u32[]{:S(2)}, u32[]{:S(2)}) %collective-permute-start.11) | collective-permute-done | bytes 262176 | tf_op jit(solution)/shard_map/ppermute | solution.py:715
  183.2 1.4 collective-permute-done.12
  184.6 3.4 %collective-permute-done.14 = f32[80,512]{1,0:T(8,128)S(1)} collective-permute-done((f32[80,512]{1,0:T(8,128)S(1)}, f32[80,512]{1,0:T(8,128)S(1)}, u32[]{:S(2)}, u32[]{:S(2)}) %collective-permute-start.14) | collective-permute-done | bytes 163872 | tf_op jit(solution)/shard_map/ppermute | solution.py:715
  188.0 3.1 %collective-permute-done.16 = f32[80,512]{1,0:T(8,128)} collective-permute-done((f32[80,512]{1,0:T(8,128)S(1)}, f32[80,512]{1,0:T(8,128)}, u32[]{:S(2)}, u32[]{:S(2)}) %collective-permute-start.16) | collective-permute-done | bytes 163872 | tf_op jit(solution)/shard_map/ppermute | solution.py:715
  191.1 1.1 maximum_select_fusion.6
  192.2 1.3 collective-permute-start.18
  193.5 1.0 collective-permute-start.17
  195.7 1.7 collective-permute-start.20
  197.4 2.7 %collective-permute-start.21 = (f32[20,512]{1,0:T(8,128)S(1)}, f32[20,512]{1,0:T(8,128)S(1)}, u32[]{:S(2)}, u32[]{:S(2)}) collective-permute-start(f32[20,512]{1,0:T(8,128)S(1)} %get-tuple-element.253), channel_id=1, source_target_pairs={{0,3},{1,2},{2,1},{3,0},{4,7},{5,6},{6,5},{7,4},{8,11},{9,10},{10,... | collective-permute-start | bytes 122888 | tf_op jit(solution)/shard_map/ppermute | solution.py:715
  200.1 1.1 collective-permute-done.20
  201.1 2.2 collective-permute-done.21
  203.3 2.2 collective-permute-done.18
  205.5 1.1 collective-permute-done.17
  207.2 1.7 collective-permute-start.24
  208.9 2.6 %collective-permute-start.25 = (f32[20,512]{1,0:T(8,128)S(1)}, f32[20,512]{1,0:T(8,128)S(1)}, u32[]{:S(2)}, u32[]{:S(2)}) collective-permute-start(f32[20,512]{1,0:T(8,128)S(1)} %add_add_fusion.4), channel_id=1, source_target_pairs={{0,3},{1,2},{2,1},{3,0},{4,7},{5,6},{6,5},{7,4},{8,11},{9,10},{10,... | collective-permute-start | bytes 122888 | tf_op jit(solution)/shard_map/ppermute | solution.py:715
  211.6 2.7 %collective-permute-done.24 = f32[20,512]{1,0:T(8,128)S(1)} collective-permute-done((f32[20,512]{1,0:T(8,128)S(1)}, f32[20,512]{1,0:T(8,128)S(1)}, u32[]{:S(2)}, u32[]{:S(2)}) %collective-permute-start.24) | collective-permute-done | bytes 40992 | tf_op jit(solution)/shard_map/ppermute | solution.py:715
  214.9 1.0 collective-permute-start.26
  216.7 1.8 collective-permute-start.28
  218.5 5.3 %assemble.1 = (f32[2048,512]{1,0:T(8,128)}, f32[4,8,512]{2,1,0:T(8,128)S(1)}) custom-call(s32[1]{0:T(128)} %bitcast.1.half_ref.first_ref, f32[1024,512]{1,0:T(8,128)S(1)} %pad_maximum_fusion.own_ref, f32[1024,512]{1,0:T(8,128)S(1)} %collective-permute-done.22.got_ref, f32[2048,512]{1,0:T(8,128)} %w_ref.3), custom_call_target="tpu_custom_call" | custom-call | bytes 18450000 | tf_op jit(solution)/shard_map/assemble/pallas_call | solution.py:588
  225.3 1.5 collective-permute-done.29
  226.9 7.3 %fix.1 = (f32[400,2048]{1,0:T(8,128)}, f32[100,4,512]{2,1,0:T(4,128)}, f32[4,512]{1,0:T(4,128)}, f32[4,512]{1,0:T(4,128)}, f32[4,512]{1,0:T(4,128)}, /*index=5*/...) custom-call(s32[16,128]{1,0:T(8,128)S(1)} %bitcast.25, ...), custom_call_target="tpu_custom_call" | custom-call | bytes 29520000 | tf_op jit(solution)/shard_map/fix/pallas_call | solution.py:699
  (90 shorter events, 11.1 us)
Async XLA Ops:
  5.6 18.3 %all-to-all-start = ((f32[32,1,2560]{2,1,0:T(1,128)}), f32[32,1,2560]{2,1,0:T(1,128)S(1)}, u32[]{:S(2)}, u32[]{:S(2)}) async-start(f32[32,1,2560]{2,1,0:T(1,128)} %get-tuple-element.127), calls=%async_computation | async-start | bytes 655360 | tf_op jit(solution)/shard_map/all_to_all | solution.py:719
  12.9 9.9 %copy-start.13 = (f32[2048]{0:T(1024)S(1)}, f32[2048]{0:T(1024)}, u32[]{:S(2)}) copy-start(f32[2048]{0:T(1024)} %param.21) | copy-start | bytes 24580
  12.9 11.0 %copy-start = (s32[2048]{0:T(1024)S(1)}, s32[2048]{0:T(1024)}, u32[]{:S(2)}) copy-start(s32[2048]{0:T(1024)} %param.16) | copy-start | bytes 24580
  13.0 11.0 %copy-start.2 = (f32[4,512]{1,0:T(4,128)S(1)}, f32[4,512]{1,0:T(4,128)}, u32[]{:S(2)}) copy-start(f32[4,512]{1,0:T(4,128)} %gain_ref.3) | copy-start | bytes 24580
  13.0 11.0 %copy-start.3 = (f32[4,512]{1,0:T(4,128)S(1)}, f32[4,512]{1,0:T(4,128)}, u32[]{:S(2)}) copy-start(f32[4,512]{1,0:T(4,128)} %slope_ref.3) | copy-start | bytes 24580
  13.0 11.0 %copy-start.4 = (f32[4,512]{1,0:T(4,128)S(1)}, f32[4,512]{1,0:T(4,128)}, u32[]{:S(2)}) copy-start(f32[4,512]{1,0:T(4,128)} %shift_ref.1) | copy-start | bytes 24580
  22.9 42.7 %copy-start.1 = (f32[512,47]{0,1:T(8,128)S(1)}, f32[512,47]{0,1:T(8,128)}, u32[]{:S(2)}) copy-start(f32[512,47]{0,1:T(8,128)} %param.26) | copy-start | bytes 288772
  22.9 42.7 %copy-start.5 = (s32[2048]{0:T(1024)S(1)}, s32[2048]{0:T(1024)}, u32[]{:S(2)}) copy-start(s32[2048]{0:T(1024)} %param.15) | copy-start | bytes 24580
  22.9 42.7 %copy-start.6 = (f32[512]{0:T(512)S(1)}, f32[512]{0:T(512)}, u32[]{:S(2)}) copy-start(f32[512]{0:T(512)} %param.23) | copy-start | bytes 6148
  22.9 42.6 %copy-start.7 = (f32[512]{0:T(512)S(1)}, f32[512]{0:T(512)}, u32[]{:S(2)}) copy-start(f32[512]{0:T(512)} %param.24) | copy-start | bytes 6148
  22.9 42.6 %copy-start.8 = (f32[512]{0:T(512)S(1)}, f32[512]{0:T(512)}, u32[]{:S(2)}) copy-start(f32[512]{0:T(512)} %param.25) | copy-start | bytes 6148
  22.9 42.6 %copy-start.9 = (f32[47]{0:T(128)S(1)}, f32[47]{0:T(128)}, u32[]{:S(2)}) copy-start(f32[47]{0:T(128)} %param.27) | copy-start | bytes 568
  75.2 11.0 %all-to-all-start.2 = ((f32[32,2,512]{2,1,0:T(2,128)}), f32[32,2,512]{2,1,0:T(2,128)S(1)}, u32[]{:S(2)}, u32[]{:S(2)}) async-start(f32[32,2,512]{2,1,0:T(2,128)} %get-tuple-element.132), calls=%async_computation.2 | async-start | bytes 262144 | tf_op jit(solution)/shard_map/all_to_all | solution.py:719
  98.5 9.7 %collective-permute-start = (f32[1024,512]{1,0:T(8,128)}, f32[1024,512]{1,0:T(8,128)}, u32[]{:S(2)}, u32[]{:S(2)}) collective-permute-start(f32[1024,512]{1,0:T(8,128)} %get-tuple-element.137), channel_id=1, source_target_pairs={{0,4},{4,0},{8,12},{12,8},{16,20},{20,16},{24,28},{28,24},{1,5},{5... | collective-permute-start | bytes 6291464 | tf_op jit(solution)/shard_map/ppermute | solution.py:715
  110.5 14.5 %collective-permute-start.1 = (f32[256,512]{1,0:T(8,128)}, f32[256,512]{1,0:T(8,128)S(1)}, u32[]{:S(2)}, u32[]{:S(2)}) collective-permute-start(f32[256,512]{1,0:T(8,128)} %get-tuple-element.242), channel_id=1, source_target_pairs={{0,8},{4,12},{8,0},{12,4},{16,24},{20,28},{24,16},{28,20},{1,9},{5... | collective-permute-start | bytes 1572872 | tf_op jit(solution)/shard_map/ppermute | solution.py:715
  111.3 14.3 %collective-permute-start.2 = (f32[256,512]{1,0:T(8,128)}, f32[256,512]{1,0:T(8,128)}, u32[]{:S(2)}, u32[]{:S(2)}) collective-permute-start(f32[256,512]{1,0:T(8,128)} %get-tuple-element.241), channel_id=1, source_target_pairs={{0,16},{4,20},{8,24},{12,28},{16,0},{20,4},{24,8},{28,12},{1,17},{... | collective-permute-start | bytes 1572872 | tf_op jit(solution)/shard_map/ppermute | solution.py:715
  125.0 0.8 copy-start.12
  127.6 1.2 copy-start.10
  127.6 13.4 %collective-permute-start.4 = (f32[128,512]{1,0:T(8,128)S(1)}, f32[128,512]{1,0:T(8,128)S(1)}, u32[]{:S(2)}, u32[]{:S(2)}) collective-permute-start(f32[128,512]{1,0:T(8,128)S(1)} %constant_dynamic-slice_fusion.9), channel_id=1, source_target_pairs={{0,8},{4,12},{8,0},{12,4},{16,24},{20,28},{24,16},{28,20},{1,9},{5... | collective-permute-start | bytes 786440 | tf_op jit(solution)/shard_map/ppermute | solution.py:715
  128.8 12.3 %collective-permute-start.3 = (f32[128,512]{1,0:T(8,128)S(1)}, f32[128,512]{1,0:T(8,128)S(1)}, u32[]{:S(2)}, u32[]{:S(2)}) collective-permute-start(f32[128,512]{1,0:T(8,128)S(1)} %constant_dynamic-slice_fusion.10), channel_id=1, source_target_pairs={{0,16},{4,20},{8,24},{12,28},{16,0},{20,4},{24,8},{28,12},{1,17},{... | collective-permute-start | bytes 786440 | tf_op jit(solution)/shard_map/ppermute | solution.py:715
  129.6 11.4 %copy-start.11 = (f32[256,512]{1,0:T(8,128)S(1)}, f32[256,512]{1,0:T(8,128)}, u32[]{:S(2)}) copy-start(f32[256,512]{1,0:T(8,128)} %copy-done.10) | copy-start | bytes 1572868
  141.3 15.7 %collective-permute-start.5 = (f32[64,512]{1,0:T(8,128)S(1)}, f32[64,512]{1,0:T(8,128)S(1)}, u32[]{:S(2)}, u32[]{:S(2)}) collective-permute-start(f32[64,512]{1,0:T(8,128)S(1)} %get-tuple-element.251), channel_id=1, source_target_pairs={{0,1},{1,0},{2,3},{3,2},{4,5},{5,4},{6,7},{7,6},{8,9},{9,8},{10,11... | collective-permute-start | bytes 393224 | tf_op jit(solution)/shard_map/ppermute | solution.py:715
  141.4 15.6 %collective-permute-start.6 = (f32[64,512]{1,0:T(8,128)S(1)}, f32[64,512]{1,0:T(8,128)S(1)}, u32[]{:S(2)}, u32[]{:S(2)}) collective-permute-start(f32[64,512]{1,0:T(8,128)S(1)} %get-tuple-element.252), channel_id=1, source_target_pairs={{0,2},{1,3},{2,0},{3,1},{4,6},{5,7},{6,4},{7,5},{8,10},{9,11},{10,... | collective-permute-start | bytes 393224 | tf_op jit(solution)/shard_map/ppermute | solution.py:715
  143.0 14.0 %collective-permute-start.7 = (f32[64,512]{1,0:T(8,128)S(1)}, f32[64,512]{1,0:T(8,128)S(1)}, u32[]{:S(2)}, u32[]{:S(2)}) collective-permute-start(f32[64,512]{1,0:T(8,128)S(1)} %get-tuple-element.249), channel_id=1, source_target_pairs={{0,3},{1,2},{2,1},{3,0},{4,7},{5,6},{6,5},{7,4},{8,11},{9,10},{10,... | collective-permute-start | bytes 393224 | tf_op jit(solution)/shard_map/ppermute | solution.py:715
  157.1 15.8 %collective-permute-start.10 = (f32[64,512]{1,0:T(8,128)S(1)}, f32[64,512]{1,0:T(8,128)S(1)}, u32[]{:S(2)}, u32[]{:S(2)}) collective-permute-start(f32[64,512]{1,0:T(8,128)S(1)} %add_add_fusion.3), channel_id=1, source_target_pairs={{0,3},{1,2},{2,1},{3,0},{4,7},{5,6},{6,5},{7,4},{8,11},{9,10},{10,... | collective-permute-start | bytes 393224 | tf_op jit(solution)/shard_map/ppermute | solution.py:715
  158.2 14.6 %collective-permute-start.8 = (f32[64,512]{1,0:T(8,128)S(1)}, f32[64,512]{1,0:T(8,128)S(1)}, u32[]{:S(2)}, u32[]{:S(2)}) collective-permute-start(f32[64,512]{1,0:T(8,128)S(1)} %add_add_fusion.3), channel_id=1, source_target_pairs={{0,1},{1,0},{2,3},{3,2},{4,5},{5,4},{6,7},{7,6},{8,9},{9,8},{10,11... | collective-permute-start | bytes 393224 | tf_op jit(solution)/shard_map/ppermute | solution.py:715
  158.2 14.6 %collective-permute-start.9 = (f32[64,512]{1,0:T(8,128)S(1)}, f32[64,512]{1,0:T(8,128)S(1)}, u32[]{:S(2)}, u32[]{:S(2)}) collective-permute-start(f32[64,512]{1,0:T(8,128)S(1)} %add_add_fusion.3), channel_id=1, source_target_pairs={{0,2},{1,3},{2,0},{3,1},{4,6},{5,7},{6,4},{7,5},{8,10},{9,11},{10,... | collective-permute-start | bytes 393224 | tf_op jit(solution)/shard_map/ppermute | solution.py:715
  173.9 2.4 %collective-permute-start.13 = (f32[320,512]{1,0:T(8,128)}, f32[320,512]{1,0:T(8,128)S(1)}, u32[]{:S(2)}, u32[]{:S(2)}) collective-permute-start(f32[320,512]{1,0:T(8,128)} %constant_dynamic-slice_fusion.6), channel_id=1, source_target_pairs={{0,4},{4,0},{8,12},{12,8},{16,20},{20,16},{24,28},{28,24},{1,5},{5... | collective-permute-start | bytes 1966088 | tf_op jit(solution)/shard_map/ppermute | solution.py:715
  174.0 9.2 %collective-permute-start.11 = (f32[128,512]{1,0:T(8,128)S(1)}, f32[128,512]{1,0:T(8,128)S(1)}, u32[]{:S(2)}, u32[]{:S(2)}) collective-permute-start(f32[128,512]{1,0:T(8,128)S(1)} %get-tuple-element.194), channel_id=1, source_target_pairs={{0,16},{4,20},{8,24},{12,28},{16,0},{20,4},{24,8},{28,12},{1,17},{... | collective-permute-start | bytes 786440 | tf_op jit(solution)/shard_map/ppermute | solution.py:715
  175.3 9.2 %collective-permute-start.12 = (f32[128,512]{1,0:T(8,128)S(1)}, f32[128,512]{1,0:T(8,128)}, u32[]{:S(2)}, u32[]{:S(2)}) collective-permute-start(f32[128,512]{1,0:T(8,128)S(1)} %get-tuple-element.196), channel_id=1, source_target_pairs={{0,8},{4,12},{8,0},{12,4},{16,24},{20,28},{24,16},{28,20},{1,9},{5... | collective-permute-start | bytes 786440 | tf_op jit(solution)/shard_map/ppermute | solution.py:715
  176.5 11.5 %collective-permute-start.14 = (f32[80,512]{1,0:T(8,128)S(1)}, f32[80,512]{1,0:T(8,128)S(1)}, u32[]{:S(2)}, u32[]{:S(2)}) collective-permute-start(f32[80,512]{1,0:T(8,128)S(1)} %get-tuple-element.245), channel_id=1, source_target_pairs={{0,8},{4,12},{8,0},{12,4},{16,24},{20,28},{24,16},{28,20},{1,9},{5... | collective-permute-start | bytes 491528 | tf_op jit(solution)/shard_map/ppermute | solution.py:715
  177.6 10.4 %collective-permute-start.15 = (f32[80,512]{1,0:T(8,128)S(1)}, f32[80,512]{1,0:T(8,128)S(1)}, u32[]{:S(2)}, u32[]{:S(2)}) collective-permute-start(f32[80,512]{1,0:T(8,128)S(1)} %get-tuple-element.244), channel_id=1, source_target_pairs={{0,16},{4,20},{8,24},{12,28},{16,0},{20,4},{24,8},{28,12},{1,17},{... | collective-permute-start | bytes 491528 | tf_op jit(solution)/shard_map/ppermute | solution.py:715
  178.6 12.5 %collective-permute-start.16 = (f32[80,512]{1,0:T(8,128)S(1)}, f32[80,512]{1,0:T(8,128)}, u32[]{:S(2)}, u32[]{:S(2)}) collective-permute-start(f32[80,512]{1,0:T(8,128)S(1)} %get-tuple-element.243), channel_id=1, source_target_pairs={{0,24},{4,28},{8,16},{12,20},{16,8},{20,12},{24,0},{28,4},{1,25},{... | collective-permute-start | bytes 491528 | tf_op jit(solution)/shard_map/ppermute | solution.py:715
  192.2 13.3 %collective-permute-start.18 = (f32[256,512]{1,0:T(8,128)S(1)}, f32[256,512]{1,0:T(8,128)S(1)}, u32[]{:S(2)}, u32[]{:S(2)}) collective-permute-start(f32[256,512]{1,0:T(8,128)S(1)} %maximum_select_fusion.6), channel_id=1, source_target_pairs={{0,16},{4,20},{8,24},{12,28},{16,0},{20,4},{24,8},{28,12},{1,17},{... | collective-permute-start | bytes 1572872 | tf_op jit(solution)/shard_map/ppermute | solution.py:715
  193.5 13.0 %collective-permute-start.17 = (f32[256,512]{1,0:T(8,128)S(1)}, f32[256,512]{1,0:T(8,128)S(1)}, u32[]{:S(2)}, u32[]{:S(2)}) collective-permute-start(f32[256,512]{1,0:T(8,128)S(1)} %maximum_select_fusion.5), channel_id=1, source_target_pairs={{0,8},{4,12},{8,0},{12,4},{16,24},{20,28},{24,16},{28,20},{1,9},{5... | collective-permute-start | bytes 1572872 | tf_op jit(solution)/shard_map/ppermute | solution.py:715
  195.6 4.5 %collective-permute-start.19 = (f32[20,512]{1,0:T(8,128)S(1)}, f32[20,512]{1,0:T(8,128)S(1)}, u32[]{:S(2)}, u32[]{:S(2)}) collective-permute-start(f32[20,512]{1,0:T(8,128)S(1)} %get-tuple-element.255), channel_id=1, source_target_pairs={{0,1},{1,0},{2,3},{3,2},{4,5},{5,4},{6,7},{7,6},{8,9},{9,8},{10,11... | collective-permute-start | bytes 122888 | tf_op jit(solution)/shard_map/ppermute | solution.py:715
  195.7 5.5 %collective-permute-start.20 = (f32[20,512]{1,0:T(8,128)S(1)}, f32[20,512]{1,0:T(8,128)S(1)}, u32[]{:S(2)}, u32[]{:S(2)}) collective-permute-start(f32[20,512]{1,0:T(8,128)S(1)} %get-tuple-element.254), channel_id=1, source_target_pairs={{0,2},{1,3},{2,0},{3,1},{4,6},{5,7},{6,4},{7,5},{8,10},{9,11},{10,... | collective-permute-start | bytes 122888 | tf_op jit(solution)/shard_map/ppermute | solution.py:715
  197.4 5.9 %collective-permute-start.21 = (f32[20,512]{1,0:T(8,128)S(1)}, f32[20,512]{1,0:T(8,128)S(1)}, u32[]{:S(2)}, u32[]{:S(2)}) collective-permute-start(f32[20,512]{1,0:T(8,128)S(1)} %get-tuple-element.253), channel_id=1, source_target_pairs={{0,3},{1,2},{2,1},{3,0},{4,7},{5,6},{6,5},{7,4},{8,11},{9,10},{10,... | collective-permute-start | bytes 122888 | tf_op jit(solution)/shard_map/ppermute | solution.py:715
  207.0 7.9 %collective-permute-start.22 = (f32[1024,512]{1,0:T(8,128)S(1)}, f32[1024,512]{1,0:T(8,128)S(1)}, u32[]{:S(2)}, u32[]{:S(2)}) collective-permute-start(f32[1024,512]{1,0:T(8,128)S(1)} %pad_maximum_fusion.own_ref), channel_id=1, source_target_pairs={{0,4},{4,0},{8,12},{12,8},{16,20},{20,16},{24,28},{28,24},{1,5},{5... | collective-permute-start | bytes 6291464 | tf_op jit(solution)/shard_map/ppermute | solution.py:715
  207.1 4.5 %collective-permute-start.23 = (f32[20,512]{1,0:T(8,128)S(1)}, f32[20,512]{1,0:T(8,128)S(1)}, u32[]{:S(2)}, u32[]{:S(2)}) collective-permute-start(f32[20,512]{1,0:T(8,128)S(1)} %add_add_fusion.4), channel_id=1, source_target_pairs={{0,1},{1,0},{2,3},{3,2},{4,5},{5,4},{6,7},{7,6},{8,9},{9,8},{10,11... | collective-permute-start | bytes 122888 | tf_op jit(solution)/shard_map/ppermute | solution.py:715
  207.2 7.1 %collective-permute-start.24 = (f32[20,512]{1,0:T(8,128)S(1)}, f32[20,512]{1,0:T(8,128)S(1)}, u32[]{:S(2)}, u32[]{:S(2)}) collective-permute-start(f32[20,512]{1,0:T(8,128)S(1)} %add_add_fusion.4), channel_id=1, source_target_pairs={{0,2},{1,3},{2,0},{3,1},{4,6},{5,7},{6,4},{7,5},{8,10},{9,11},{10,... | collective-permute-start | bytes 122888 | tf_op jit(solution)/shard_map/ppermute | solution.py:715
  208.9 5.9 %collective-permute-start.25 = (f32[20,512]{1,0:T(8,128)S(1)}, f32[20,512]{1,0:T(8,128)S(1)}, u32[]{:S(2)}, u32[]{:S(2)}) collective-permute-start(f32[20,512]{1,0:T(8,128)S(1)} %add_add_fusion.4), channel_id=1, source_target_pairs={{0,3},{1,2},{2,1},{3,0},{4,7},{5,6},{6,5},{7,4},{8,11},{9,10},{10,... | collective-permute-start | bytes 122888 | tf_op jit(solution)/shard_map/ppermute | solution.py:715
  214.9 8.8 %collective-permute-start.26 = (f32[80,512]{1,0:T(8,128)S(1)}, f32[80,512]{1,0:T(8,128)S(1)}, u32[]{:S(2)}, u32[]{:S(2)}) collective-permute-start(f32[80,512]{1,0:T(8,128)S(1)} %maximum_select_fusion.11), channel_id=1, source_target_pairs={{0,8},{4,12},{8,0},{12,4},{16,24},{20,28},{24,16},{28,20},{1,9},{5... | collective-permute-start | bytes 491528 | tf_op jit(solution)/shard_map/ppermute | solution.py:715
  216.0 8.5 %collective-permute-start.27 = (f32[80,512]{1,0:T(8,128)S(1)}, f32[80,512]{1,0:T(8,128)S(1)}, u32[]{:S(2)}, u32[]{:S(2)}) collective-permute-start(f32[80,512]{1,0:T(8,128)S(1)} %maximum_select_fusion.11), channel_id=1, source_target_pairs={{0,16},{4,20},{8,24},{12,28},{16,0},{20,4},{24,8},{28,12},{1,17},{... | collective-permute-start | bytes 491528 | tf_op jit(solution)/shard_map/ppermute | solution.py:715
  216.7 7.7 %collective-permute-start.28 = (f32[80,512]{1,0:T(8,128)S(1)}, f32[80,512]{1,0:T(8,128)S(1)}, u32[]{:S(2)}, u32[]{:S(2)}) collective-permute-start(f32[80,512]{1,0:T(8,128)S(1)} %maximum_select_fusion.11), channel_id=1, source_target_pairs={{0,24},{4,28},{8,16},{12,20},{16,8},{20,12},{24,0},{28,4},{1,25},{... | collective-permute-start | bytes 491528 | tf_op jit(solution)/shard_map/ppermute | solution.py:715
  224.6 2.2 collective-permute-start.29

commit v5 on v4

--- a/solution.py
+++ b/solution.py
@@ -13,7 +13,7 @@
 LANES = 128
 LOG2E = 1.4426950408889634
 LN2 = 0.6931471805599453
-TILES = {"gram": 2048, "project": 512, "forward": 512, "head": 512, "mix": 512, "hop": 512, "fix": 1024}
+TILES = {"gram": 2048, "project": 512, "forward": 512, "head": 1024, "mix": 512, "hop": 512, "fix": 1024}
 PACK_STEPS = 2
 SUB = 256
 MIX_SUB = 256
@@ -382,10 +382,19 @@
     )(valid, labels, far(v), st2, st, gain, shift, slope, hw, hb)
 
 
-def mix_product(parts, uh_ref, ul_ref, m_ref):
+def mix_product(parts, half_ref, g_ref, uh_ref, ul_ref, m_ref):
+    mix = uh_ref.shape[1]
+    some, n = g_ref.shape[0] // 2, g_ref.shape[1]
+
     @pl.when(pl.program_id(0) == 0)
     def _():
         m_ref[...] = jnp.zeros_like(m_ref)
+        for h in range(some):
+            g = g_ref[half_ref[0] * some + h]
+            at = mix + h * n // 4
+            m_ref[at : at + n // 4, :] = jnp.concatenate(
+                [g[q * n // 4 : (q + 1) * n // 4] for q in range(4)], axis=1
+            )
 
     ahead = parts[0][1]()
     for k, (rows, _) in enumerate(parts):
@@ -399,7 +408,7 @@
 
 
 def mix_first_kernel(
-    half_ref, valid_ref, dy_ref, v_ref, st2_ref, cnt_ref, st3_ref, gain_ref, uh_ref, ul_ref,
+    half_ref, valid_ref, dy_ref, v_ref, st2_ref, cnt_ref, st3_ref, gain_ref, g_ref, uh_ref, ul_ref,
     m_ref, dvh_ref, dvl_ref, st3_out,
 ):
     step = pl.program_id(0)
@@ -425,14 +434,14 @@
         return dvs
 
     parts = [slice(k, k + MIX_SUB) for k in range(0, tile, MIX_SUB)]
-    mix_product([(rows, functools.partial(dv, rows)) for rows in parts], uh_ref, ul_ref, m_ref)
-
-
-def mix_second_kernel(half_ref, dvh_ref, dvl_ref, uh_ref, ul_ref, m_ref):
-    mix_product([(slice(None), lambda: (dvh_ref[...], dvl_ref[...]))], uh_ref, ul_ref, m_ref)
-
-
-def mix_back(half, valid, dy, v, st2, st, st3, gain, uh, ul, tile):
+    mix_product([(rows, functools.partial(dv, rows)) for rows in parts], half_ref, g_ref, uh_ref, ul_ref, m_ref)
+
+
+def mix_second_kernel(half_ref, dvh_ref, dvl_ref, g_ref, uh_ref, ul_ref, m_ref):
+    mix_product([(slice(None), lambda: (dvh_ref[...], dvl_ref[...]))], half_ref, g_ref, uh_ref, ul_ref, m_ref)
+
+
+def mix_back(half, valid, dy, v, st2, st, st3, gain, g, uh, ul, extra, tile):
     rows, hid = dy.shape
     part = uh.shape[1] // 2
     by = lambda n: pl.BlockSpec((tile, n), lambda i, half: (i, 0))
@@ -442,13 +451,13 @@
             num_scalar_prefetch=1,
             grid=(rows // tile,),
             in_specs=[whole(valid), by(hid), by(hid)]
-            + [whole(t) for t in (st2, st, st3, gain)]
+            + [whole(t) for t in (st2, st, st3, gain, g)]
             + [pl.BlockSpec((tile, part), lambda i, half: (i, half[0]))] * 2,
-            out_specs=[pl.BlockSpec((part, hid), lambda i, half: (0, 0)), by(hid), by(hid)]
+            out_specs=[pl.BlockSpec((part + extra, hid), lambda i, half: (0, 0)), by(hid), by(hid)]
             + [pl.BlockSpec((2, hid), lambda i, half: (0, 0))],
         ),
         out_shape=[
-            jax.ShapeDtypeStruct((part, hid), F32),
+            jax.ShapeDtypeStruct((part + extra, hid), F32),
             pltpu.HBM((rows, hid), BF16),
             pltpu.HBM((rows, hid), BF16),
             jax.ShapeDtypeStruct((2, hid), F32),
@@ -456,10 +465,10 @@
         compiler_params=params(28),
         name="mix_back",
         cost_estimate=cost(14),
-    )(half, valid, far(dy), far(v), st2, st, st3, gain, far(uh), far(ul))
-
-
-def mix_back_rest(half, dvh, dvl, uh, ul, tile):
+    )(half, valid, far(dy), far(v), st2, st, st3, gain, g, far(uh), far(ul))
+
+
+def mix_back_rest(half, dvh, dvl, g, uh, ul, extra, tile):
     rows, hid = dvh.shape
     part = uh.shape[1] // 2
     by = lambda n: pl.BlockSpec((tile, n), lambda i, half: (i, 0))
@@ -468,15 +477,15 @@
         grid_spec=pltpu.PrefetchScalarGridSpec(
             num_scalar_prefetch=1,
             grid=(rows // tile,),
-            in_specs=[by(hid), by(hid)]
+            in_specs=[by(hid), by(hid), whole(g)]
             + [pl.BlockSpec((tile, part), lambda i, half: (i, half[0]))] * 2,
-            out_specs=pl.BlockSpec((part, hid), lambda i, half: (0, 0)),
+            out_specs=pl.BlockSpec((part + extra, hid), lambda i, half: (0, 0)),
         ),
-        out_shape=jax.ShapeDtypeStruct((part, hid), F32),
+        out_shape=jax.ShapeDtypeStruct((part + extra, hid), F32),
         compiler_params=params(28),
         name="mix_back_rest",
         cost_estimate=cost(12),
-    )(half, far(dvh), far(dvl), far(uh), far(ul))
+    )(half, far(dvh), far(dvl), g, far(uh), far(ul))
 
 
 def hop_kernel(
@@ -570,7 +579,7 @@
     )(far(x), far(wp), coef, far(dvh), far(dvl), far(mwh), far(mwl))
 
 
-def assemble_kernel(first_ref, own_ref, got_ref, w_ref, m_ref, uu_ref):
+def assemble_kernel(first_ref, own_ref, got_ref, own_g_ref, got_g_ref, w_ref, m_ref, uu_ref, g_ref):
     mine = (pl.program_id(0) // 2) == first_ref[0]
     m = jnp.where(mine, own_ref[...], got_ref[...])
     m_ref[...] = m
@@ -579,73 +588,75 @@
     hi, lo = split(m * w_ref[...])
     uu_ref[0] = dot(ones, hi) + dot(ones, lo)
 
+    @pl.when(pl.program_id(0) % 2 == 0)
+    def _():
+        g_ref[...] = jnp.where(mine, own_g_ref[...], got_g_ref[...])
+
 
 def assemble(first, own, got, w):
     rows, hid = w.shape
     block = rows // 4
+    extra = own.shape[0] - rows // 2
     half = pl.BlockSpec((block, hid), lambda i, first: (i % 2, 0))
+    tail = pl.BlockSpec((extra, hid), lambda i, first: (rows // 2 // extra, 0))
     by = pl.BlockSpec((block, hid), lambda i, first: (i, 0))
     return pl.pallas_call(
         assemble_kernel,
         grid_spec=pltpu.PrefetchScalarGridSpec(
             num_scalar_prefetch=1,
             grid=(4,),
-            in_specs=[half, half, by],
-            out_specs=[by, pl.BlockSpec((1, 8, block), lambda i, first: (i, 0, 0))],
+            in_specs=[half, half, tail, tail, by],
+            out_specs=[
+                by,
+                pl.BlockSpec((1, 8, block), lambda i, first: (i, 0, 0)),
+                pl.BlockSpec((extra, hid), lambda i, first: (i // 2, 0)),
+            ],
         ),
-        out_shape=[jax.ShapeDtypeStruct((rows, hid), F32), jax.ShapeDtypeStruct((4, 8, block), F32)],
+        out_shape=[
+            jax.ShapeDtypeStruct((rows, hid), F32),
+            jax.ShapeDtypeStruct((4, 8, block), F32),
+            jax.ShapeDtypeStruct((2 * extra, hid), F32),
+        ],
         compiler_params=params(20),
         name="assemble",
         cost_estimate=cost(5),
-    )(first, own, got, far(w))
-
-
-def pack_rows(n, hops, misc, unit=1):
+    )(first, own, got, own, got, far(w))
+
+
+def pack_kernel(misc_ref, *refs):
+    hops = (len(refs) - 1) // 2
+    n = refs[0].shape[0]
+    out_ref = refs[-1]
     base = hops * n
-    gram_at = base + misc + 2 * hops
-    used = gram_at + hops * n // 4
-    return base, gram_at, -(-used // unit) * unit
-
-
-def pack_kernel(g_ref, misc_ref, *refs):
-    hops = g_ref.shape[0]
-    n = g_ref.shape[1]
-    out_ref = refs[-1]
-    base, gram_at, _ = pack_rows(n, hops, misc_ref.shape[0])
-    total = out_ref.shape[0]
+    at = base + misc_ref.shape[0]
     for h in range(hops):
         out_ref[h * n : (h + 1) * n, :] = refs[h][...]
-        k = base + misc_ref.shape[0] + 2 * h
-        out_ref[k : k + 2, :] = refs[hops + h][...]
-        for q in range(4):
-            k = gram_at + h * n // 4
-            out_ref[k : k + n // 4, q * LANES : (q + 1) * LANES] = g_ref[h, q * n // 4 : (q + 1) * n // 4, :]
-    out_ref[base : base + misc_ref.shape[0], :] = misc_ref[...]
-    used = gram_at + hops * n // 4
-    if used < total:
-        out_ref[used:, :] = jnp.zeros((total - used, out_ref.shape[1]), F32)
-
-
-def pack(g, misc, bws, sums, unit):
-    hid = misc.shape[1]
-    total = pack_rows(g.shape[1], g.shape[0], misc.shape[0], unit)[2]
+        out_ref[at + 2 * h : at + 2 * h + 2, :] = refs[hops + h][...]
+    out_ref[base:at, :] = misc_ref[...]
+    used = at + 2 * hops
+    if used < out_ref.shape[0]:
+        out_ref[used:, :] = jnp.zeros((out_ref.shape[0] - used, out_ref.shape[1]), F32)
+
+
+def pack(misc, bws, sums, unit):
+    used = len(bws) * (bws[0].shape[0] + 2) + misc.shape[0]
     return pl.pallas_call(
         pack_kernel,
-        out_shape=jax.ShapeDtypeStruct((total, hid), F32),
+        out_shape=jax.ShapeDtypeStruct((-(-used // unit) * unit, misc.shape[1]), F32),
         compiler_params=params(24),
         name="pack",
         cost_estimate=cost(3),
-    )(g, misc, *bws, *sums)
-
-
-def fix_kernel(in_w, classes, misc, valid_ref, x_ref, p_ref, uu_ref, st_ref, gain_ref, slope_ref, mslope_ref, wp_ref, *refs):
+    )(misc, *bws, *sums)
+
+
+def fix_kernel(in_w, classes, misc, valid_ref, x_ref, p_ref, uu_ref, g_ref, st_ref, gain_ref, slope_ref, mslope_ref, wp_ref, *refs):
     step = pl.program_id(0)
     hops, hid = gain_ref.shape
     tile = x_ref.shape[1]
     n = wp_ref.shape[1] // 3
     dxs, rest = refs[:hops], refs[hops:]
     dx_ref, bw_ref, gain_out, shift_out, slope_out, mslope_out, oslope_out, hw_out, hb_out, loss_out, q_ref = rest
-    base, gram_at, _ = pack_rows(n, hops, misc)
+    base = hops * n
     mask = row_mask(valid_ref, step, tile, 1)
 
     @pl.when(step == 0)
@@ -677,9 +688,9 @@
             mask_row = lax.broadcasted_iota(jnp.int32, (n, hid), 0) == in_w
             wc = split(jnp.where(mask_row, k0, wc))
             q_ref[h, :, :n] = dot3((wh, wl), wc, NT)
-            k = gram_at + h * n // 4
+            k = h // (hops // 2) * (g_ref.shape[0] // 2) + h % (hops // 2) * n // 4
             g = jnp.concatenate(
-                [p_ref[k : k + n // 4, q * LANES : q * LANES + n] for q in range(4)], axis=0
+                [g_ref[k : k + n // 4, q * LANES : q * LANES + n] for q in range(4)], axis=0
             )
             bw = raw * (LOG2E * gain * rstd) - dot3(split(g), wc)
             bw_ref[:, h, :] = bw[:in_w]
@@ -690,7 +701,7 @@
         dx_ref[h * in_w : (h + 1) * in_w, :] = (dxs[h][...] - fix)[:in_w]
 
 
-def fix(valid, x, packed, uu, st, gain, slope, mslope, wp, dxs, in_w, classes, misc, tile):
+def fix(valid, x, packed, uu, g, st, gain, slope, mslope, wp, dxs, in_w, classes, misc, tile):
     width, rows = x.shape
     hops, hid = gain.shape
     n = wp.shape[1] // 3
@@ -700,7 +711,7 @@
         functools.partial(fix_kernel, in_w, classes, misc),
         grid=(rows // tile,),
         in_specs=[whole(valid), cols(width)]
-        + [whole(t) for t in (packed, uu, st, gain, slope, mslope, wp)]
+        + [whole(t) for t in (packed, uu, g, st, gain, slope, mslope, wp)]
         + [cols(n)] * hops,
         out_specs=[cols(width)] + [pl.BlockSpec(s, lambda i, s=s: (0,) * len(s)) for s in shapes],
         out_shape=[jax.ShapeDtypeStruct(s, F32) for s in ((width, rows),) + shapes],
@@ -708,7 +719,7 @@
         compiler_params=params(24),
         name="fix",
         cost_estimate=cost(8),
-    )(valid, far(x), packed, uu, st, gain, slope, mslope, far(wp), *[far(d) for d in dxs])
+    )(valid, far(x), packed, uu, g, st, gain, slope, mslope, far(wp), *[far(d) for d in dxs])
 
 
 def flip(v, axis, size, k):
@@ -850,13 +861,15 @@
     )
     st3 = exchange(st3)
     core = lax.axis_index("dp") % 2
+    unit = max(devices, 64)
+    extra = -(-(hops // 2 * g.shape[1] // 4) // unit) * unit
     half = lambda i: jnp.reshape(i, (1,)).astype(jnp.int32)
     away, dvh, dvl, st3 = mix_back(
-        half(1 - core), valid, dy2, v, st2, st, st3, row(mix_gain), uh, ul, TILES["mix"]
+        half(1 - core), valid, dy2, v, st2, st, st3, row(mix_gain), g, uh, ul, extra, TILES["mix"]
     )
     within = sizes["dp"] > 1
     got = flip(away, "dp", sizes["dp"], 1) if within else None
-    m = mix_back_rest(half(core), dvh, dvl, uh, ul, TILES["mix"])
+    m = mix_back_rest(half(core), dvh, dvl, g, uh, ul, extra, TILES["mix"])
     if within:
         m, got, x = lax.optimization_barrier((m, got, x))
         first = Steps(sum_steps((m, got), sizes, True, False))
@@ -870,7 +883,7 @@
         )
         dxs, bws, sums = dxs + [dx], bws + [bw], sums + [s]
         first.state, x, bws, sums = lax.optimization_barrier((first.state, x, bws, sums))
-    packed = pack(g, misc, bws, sums, max(128, 2 * sizes["dp"] * sizes["bucket"]))
+    packed = pack(misc, bws, sums, max(128, 2 * devices))
     last = Steps(sum_steps((packed,), sizes, False, True))
     first.step()
     last.step()
@@ -878,21 +891,20 @@
     first.state, last.state = lax.optimization_barrier((first.state, last.state))
     first.step()
     last.step()
+    last.step()
     first.state, last.state = lax.optimization_barrier((first.state, last.state))
     while not first.done:
         first.step()
     m = first.value
     m, other = (m, flip(m, "dp", sizes["dp"], 1)) if within else pieces(m, 2)
     last.step()
-    m, other, last.state = lax.optimization_barrier((m, other, last.state))
-    last.step()
-    m, uu = assemble(half(core), m, other, mix_w)
+    m, uu, g = assemble(half(core), m, other, mix_w)
     m, uu, last.state = lax.optimization_barrier((m, uu, last.state))
     while not last.done:
         last.step()
     packed = last.value
     d_x, bw, gain_grad, shift_grad, slope_grad, mslope_grad, oslope_grad, hw_grad, hb_grad, loss = fix(
-        valid, x, packed, uu, st, branch_gain, branch_slope, mslope, wp, dxs, in_w, classes, misc.shape[0],
+        valid, x, packed, uu, g, st, branch_gain, branch_slope, mslope, wp, dxs, in_w, classes, misc.shape[0],
         TILES["fix"],
     )
     return (

time: 235 us -> 230 us (0.979)
  waiting for transfers between devices: 34.7 us -> 32 us
    ppermute x30, waiting for transfers between devices: 25.5 us -> 22.6 us  [flip(): return lax.ppermute(v, axis, [(i, i ^ k) for i in range(size)])]
  transfers between devices with their start and end apart: 32 -> 32, of which waited for: 16 -> 14; matrix products, arithmetic and copies ran while one was open for 1% -> 0% of each run, Pallas kernels for 30% -> 31%
where the time goes in v5:
time: 230 us; the launch traced here: 229 us
  Pallas kernels  133 us (58%)
  starting transfers between devices  43.1 us (19%)
  waiting for transfers between devices  32 us (14%)
  blocking collectives  13.1 us (6%)
  other arithmetic  5.55 us (2%)
    pallas_call x4, Pallas kernels, hop_back(): pl.pallas_call(functools.partial(hop_kernel, h, in_w), grid=(rows // tile...  45.3 us
    ppermute x30, starting transfers between devices, flip(): return lax.ppermute(v, axis, [(i, i ^ k) for i in range(size)])  33.2 us
    pallas_call x1, Pallas kernels, forward(): pl.pallas_call(functools.partial(forward_kernel, in_w), grid=(rows // til...  28.5 us
    ppermute x30, waiting for transfers between devices, flip(): return lax.ppermute(v, axis, [(i, i ^ k) for i in range(size)])  22.6 us
    all_to_all x1, blocking collectives, exchange(): return lax.all_to_all(copies, ('dp', 'bucket'), 0, 0, tiled=True)  13.1 us
    pallas_call x1, Pallas kernels, mix_back(): pl.pallas_call(mix_first_kernel, grid_spec=pltpu.PrefetchScalarGridSpec(n...  12.4 us
    all_to_all x2, starting transfers between devices, exchange(): return lax.all_to_all(copies, ('dp', 'bucket'), 0, 0, tiled=True)  9.88 us
    pallas_call x1, Pallas kernels, project(): pl.pallas_call(functools.partial(project_kernel, in_w), grid=(rows // til...  9.85 us
  transfers between devices with their start and end apart: 32, of which 14 were waited for; matrix products, arithmetic and copies ran while one was open for 0% of the time, Pallas kernels for 31%

profile of v5, /device:TPU:0, one launch (start us, length us, event | category | flops | bytes accessed | tf_op | source)
XLA Modules:
  0.0 229.3 jit_solution(10199137494033931352)
XLA Ops:
  0.6 5.0 %gram.1 = (f32[4,112,128]{2,1,0:T(8,128)S(1)}, f32[32,1,2560]{2,1,0:T(1,128)}, bf16[4,336,512]{2,1,0:T(8,128)(2,1)}) custom-call(s32[16,128]{1,0:T(8,128)} %bitcast.21, f32[400,2048]{1,0:T(8,128)} %bitcast.34, f32[100,4,512]{2,1,0:T(4,128)} %bitcast.41), custom_call_target="tpu_custom_call" | custom-call | bytes 18450000 | tf_op jit(solution)/shard_map/gram/pallas_call | solution.py:123
  5.6 7.3 %all-to-all-start = ((f32[32,1,2560]{2,1,0:T(1,128)}), f32[32,1,2560]{2,1,0:T(1,128)S(1)}, u32[]{:S(2)}, u32[]{:S(2)}) async-start(f32[32,1,2560]{2,1,0:T(1,128)} %get-tuple-element.122), calls=%async_computation | async-start | bytes 655360 | tf_op jit(solution)/shard_map/all_to_all | solution.py:730
  13.0 9.8 %project.1.z_ref = f32[2048,2048]{1,0:T(8,128)} custom-call(f32[400,2048]{1,0:T(8,128)} %bitcast.35, bf16[4,336,512]{2,1,0:T(8,128)(2,1)} %get-tuple-element.121.wp_ref), custom_call_target="tpu_custom_call" | custom-call | bytes 33210000 | tf_op jit(solution)/shard_map/project/pallas_call | solution.py:146
  22.9 1.0 all-to-all-done.all_ref
  23.9 28.5 %forward.1 = (bf16[2048,2048]{1,0:T(8,128)(2,1)}, bf16[2048,2048]{1,0:T(8,128)(2,1)}, f32[2048,512]{1,0:T(8,128)}, f32[32,2,512]{2,1,0:T(2,128)S(1)}, bf16[2048,...) custom-call(s32[16,128]{1,0:T(8,128)S(1)} %bitcast.22, ...), custom_call_target="tpu_custom_call" | custom-call | bytes 110700000 | tf_op jit(solution)/shard_map/forward/pallas_call | solution.py:245
  52.5 13.1 %all_to_all.15.st_ref.st2_ref = f32[32,2,512]{2,1,0:T(2,128)S(1)} all-to-all(f32[32,2,512]{2,1,0:T(2,128)S(1)} %get-tuple-element.124), channel_id=1, replica_groups=mesh['dp'=8,'bucket'=4] {'dp','bucket'}, dimensions={0} | all-to-all | bytes 262144 | tf_op jit(solution)/shard_map/all_to_all | solution.py:730
  65.6 9.2 %head.1 = (f32[2048,512]{1,0:T(8,128)}, f32[32,2,512]{2,1,0:T(2,128)}, f32[56,512]{1,0:T(8,128)S(1)}) custom-call(s32[16,128]{1,0:T(8,128)S(1)} %bitcast.23, s32[16,128]{1,0:T(8,128)S(1)} %bitcast.27, f32[2048,512]{1,0:T(8,128)} %get-tuple-element.123.v_ref, f32[32,2,512]{2,1,0:T(2,128)S(1)} %all_to_all.15.st_ref.st2_ref, ...), custom_call_target="tpu_custom_call" | custom-call | bytes 33210000 | tf_op jit(solution)/shard_map/head/pallas_call | solution.py:363
  74.8 2.6 %all-to-all-start.2 = ((f32[32,2,512]{2,1,0:T(2,128)}), f32[32,2,512]{2,1,0:T(2,128)S(1)}, u32[]{:S(2)}, u32[]{:S(2)}) async-start(f32[32,2,512]{2,1,0:T(2,128)} %get-tuple-element.127), calls=%async_computation.2 | async-start | bytes 262144 | tf_op jit(solution)/shard_map/all_to_all | solution.py:730
  77.4 8.4 %all-to-all-done.2.st3_ref = f32[32,2,512]{2,1,0:T(2,128)S(1)} async-done(((f32[32,2,512]{2,1,0:T(2,128)}), f32[32,2,512]{2,1,0:T(2,128)S(1)}, u32[]{:S(2)}, u32[]{:S(2)}) %all-to-all-start.2) | async-done | bytes 131104 | tf_op jit(solution)/shard_map/all_to_all | solution.py:730
  85.8 12.4 %mix_back.1 = (f32[1088,512]{1,0:T(8,128)}, bf16[2048,512]{1,0:T(8,128)(2,1)}, bf16[2048,512]{1,0:T(8,128)(2,1)}, f32[2,512]{1,0:T(2,128)S(1)}) custom-call(s32[1]{0:T(128)} %bitcast.2.half_ref, s32[16,128]{1,0:T(8,128)S(1)} %bitcast.24, f32[2048,512]{1,0:T(8,128)} %get-tuple-element.126.dy_ref, f32[2048,512]{1,0:T(8,128)} %get-tuple-element.123.v_ref, ...), custom_call_target="tpu_custom_call" | custom-call | bytes 51660000 | tf_op jit(solution)/shard_map/mix_back/pallas_call | solution.py:448
  98.3 9.5 %mix_back_rest.1 = f32[1088,512]{1,0:T(8,128)S(1)} custom-call(s32[1]{0:T(128)} %bitcast.1.half_ref.first_ref, bf16[2048,512]{1,0:T(8,128)(2,1)} %get-tuple-element.131.dvh_ref, bf16[2048,512]{1,0:T(8,128)(2,1)} %get-tuple-element.132.dvl_ref, f32[4,112,128]{2,1,0:T(8,128)S(1)} %get-tuple-element.128.g_ref, bf16[2048,2048]{1,0:T(8,128)(2,1)} %get-tuple-element.129.uh_ref, ...), custom_call_target="tpu_custom_call" | custom-call | bytes 44280000 | tf_op jit(solution)/shard_map/mix_back_rest/pallas_call | solution.py:475
  107.8 2.4 %dynamic-slice_add_fusion = (f32[272,512]{1,0:T(8,128)}, f32[272,512]{1,0:T(8,128)}) fusion(f32[1088,512]{1,0:T(8,128)} %collective-permute-done, s32[]{:T(128)S(6)} %select_n.252, f32[1088,512]{1,0:T(8,128)S(1)} %mix_back_rest.1, s32[]{:T(128)S(6)} %select_n.249), kind=kLoop, calls=%fused_computation.17 | loop fusion | flops 278528 | bytes 3342344 | tf_op jit(solution)/shard_map/add | solution.py:793
  111.5 11.3 %hop_back_0.1 = (f32[112,2048]{1,0:T(8,128)}, f32[112,512]{1,0:T(8,128)S(1)}, f32[2,512]{1,0:T(2,128)S(1)}) custom-call(f32[400,2048]{1,0:T(8,128)} %bitcast.36, bf16[4,336,512]{2,1,0:T(8,128)(2,1)} %get-tuple-element.121.wp_ref, f32[4,8,512]{2,1,0:T(8,128)S(1)} %get-tuple-element.137.coef_ref, bf16[2048,512]{1,0:T(8,128)(2,1)} %get-tuple-element.131.dvh_ref, ...), custom_call_target="tpu_custom_call" | custom-call | bytes 40590000 | tf_op jit(solution)/shard_map/hop_back_0/pallas_call | solution.py:557
  122.8 2.6 %collective-permute-done.1 = f32[272,512]{1,0:T(8,128)S(1)} collective-permute-done((f32[272,512]{1,0:T(8,128)}, f32[272,512]{1,0:T(8,128)S(1)}, u32[]{:S(2)}, u32[]{:S(2)}) %collective-permute-start.1) | collective-permute-done | bytes 557088 | tf_op jit(solution)/shard_map/ppermute | solution.py:726
  126.1 1.8 add_add_fusion
  128.0 1.1 collective-permute-start.4
  129.1 0.8 collective-permute-start.3
  130.0 11.4 %hop_back_1.1 = (f32[112,2048]{1,0:T(8,128)}, f32[112,512]{1,0:T(8,128)S(1)}, f32[2,512]{1,0:T(2,128)S(1)}) custom-call(f32[400,2048]{1,0:T(8,128)} %bitcast.37, bf16[4,336,512]{2,1,0:T(8,128)(2,1)} %get-tuple-element.121.wp_ref, f32[4,8,512]{2,1,0:T(8,128)S(1)} %get-tuple-element.137.coef_ref, bf16[2048,512]{1,0:T(8,128)(2,1)} %get-tuple-element.131.dvh_ref, ...), custom_call_target="tpu_custom_call" | custom-call | bytes 40590000 | tf_op jit(solution)/shard_map/hop_back_1/pallas_call | solution.py:557
  141.9 1.7 collective-permute-start.6
  143.5 2.7 %collective-permute-start.7 = (f32[68,512]{1,0:T(8,128)S(1)}, f32[68,512]{1,0:T(8,128)S(1)}, u32[]{:S(2)}, u32[]{:S(2)}) collective-permute-start(f32[68,512]{1,0:T(8,128)S(1)} %get-tuple-element.235), channel_id=1, source_target_pairs={{0,3},{1,2},{2,1},{3,0},{4,7},{5,6},{6,5},{7,4},{8,11},{9,10},{10,... | collective-permute-start | bytes 417800 | tf_op jit(solution)/shard_map/ppermute | solution.py:726
  146.2 11.2 %hop_back_2.1 = (f32[112,2048]{1,0:T(8,128)}, f32[112,512]{1,0:T(8,128)S(1)}, f32[2,512]{1,0:T(2,128)S(1)}) custom-call(f32[400,2048]{1,0:T(8,128)} %bitcast.38, bf16[4,336,512]{2,1,0:T(8,128)(2,1)} %get-tuple-element.121.wp_ref, f32[4,8,512]{2,1,0:T(8,128)S(1)} %get-tuple-element.137.coef_ref, bf16[2048,512]{1,0:T(8,128)(2,1)} %get-tuple-element.131.dvh_ref, ...), custom_call_target="tpu_custom_call" | custom-call | bytes 40590000 | tf_op jit(solution)/shard_map/hop_back_2/pallas_call | solution.py:557
  157.5 1.2 collective-permute-start.10
  158.7 3.3 %collective-permute-start.9 = (f32[68,512]{1,0:T(8,128)S(1)}, f32[68,512]{1,0:T(8,128)S(1)}, u32[]{:S(2)}, u32[]{:S(2)}) collective-permute-start(f32[68,512]{1,0:T(8,128)S(1)} %add_add_fusion.2), channel_id=1, source_target_pairs={{0,2},{1,3},{2,0},{3,1},{4,6},{5,7},{6,4},{7,5},{8,10},{9,11},{10,... | collective-permute-start | bytes 417800 | tf_op jit(solution)/shard_map/ppermute | solution.py:726
  162.0 11.4 %hop_back_3.1 = (f32[112,2048]{1,0:T(8,128)}, f32[112,512]{1,0:T(8,128)S(1)}, f32[2,512]{1,0:T(2,128)S(1)}) custom-call(f32[400,2048]{1,0:T(8,128)} %bitcast.39, bf16[4,336,512]{2,1,0:T(8,128)(2,1)} %get-tuple-element.121.wp_ref, f32[4,8,512]{2,1,0:T(8,128)S(1)} %get-tuple-element.137.coef_ref, bf16[2048,512]{1,0:T(8,128)(2,1)} %get-tuple-element.131.dvh_ref, ...), custom_call_target="tpu_custom_call" | custom-call | bytes 40590000 | tf_op jit(solution)/shard_map/hop_back_3/pallas_call | solution.py:557
  173.8 1.3 collective-permute-start.11
  175.1 1.0 collective-permute-start.12
  176.2 1.1 collective-permute-start.14
  177.3 0.8 collective-permute-start.15
  178.1 1.7 collective-permute-start.16
  179.8 3.5 %collective-permute-done.11 = f32[136,512]{1,0:T(8,128)S(1)} collective-permute-done((f32[136,512]{1,0:T(8,128)S(1)}, f32[136,512]{1,0:T(8,128)S(1)}, u32[]{:S(2)}, u32[]{:S(2)}) %collective-permute-start.11) | collective-permute-done | bytes 278560 | tf_op jit(solution)/shard_map/ppermute | solution.py:726
  183.3 1.3 collective-permute-done.12
  184.6 2.8 %collective-permute-done.14 = f32[64,512]{1,0:T(8,128)S(1)} collective-permute-done((f32[64,512]{1,0:T(8,128)S(1)}, f32[64,512]{1,0:T(8,128)S(1)}, u32[]{:S(2)}, u32[]{:S(2)}) %collective-permute-start.14) | collective-permute-done | bytes 131104 | tf_op jit(solution)/shard_map/ppermute | solution.py:726
  187.4 2.3 %collective-permute-done.16 = f32[64,512]{1,0:T(8,128)S(1)} collective-permute-done((f32[64,512]{1,0:T(8,128)S(1)}, f32[64,512]{1,0:T(8,128)S(1)}, u32[]{:S(2)}, u32[]{:S(2)}) %collective-permute-start.16) | collective-permute-done | bytes 131104 | tf_op jit(solution)/shard_map/ppermute | solution.py:726
  189.8 1.3 collective-permute-start.18
  191.1 1.0 collective-permute-start.17
  192.3 1.7 collective-permute-start.20
  194.0 2.7 %collective-permute-start.21 = (f32[16,512]{1,0:T(8,128)S(1)}, f32[16,512]{1,0:T(8,128)S(1)}, u32[]{:S(2)}, u32[]{:S(2)}) collective-permute-start(f32[16,512]{1,0:T(8,128)S(1)} %get-tuple-element.244), channel_id=1, source_target_pairs={{0,3},{1,2},{2,1},{3,0},{4,7},{5,6},{6,5},{7,4},{8,11},{9,10},{10,... | collective-permute-start | bytes 98312 | tf_op jit(solution)/shard_map/ppermute | solution.py:726
  197.4 2.4 %collective-permute-done.21 = f32[16,512]{1,0:T(8,128)S(1)} collective-permute-done((f32[16,512]{1,0:T(8,128)S(1)}, f32[16,512]{1,0:T(8,128)S(1)}, u32[]{:S(2)}, u32[]{:S(2)}) %collective-permute-start.21) | collective-permute-done | bytes 32800 | tf_op jit(solution)/shard_map/ppermute | solution.py:726
  199.8 3.2 %collective-permute-start.23 = (f32[16,512]{1,0:T(8,128)S(1)}, f32[16,512]{1,0:T(8,128)S(1)}, u32[]{:S(2)}, u32[]{:S(2)}) collective-permute-start(f32[16,512]{1,0:T(8,128)S(1)} %add_add_fusion.4), channel_id=1, source_target_pairs={{0,2},{1,3},{2,0},{3,1},{4,6},{5,7},{6,4},{7,5},{8,10},{9,11},{10,... | collective-permute-start | bytes 98312 | tf_op jit(solution)/shard_map/ppermute | solution.py:726
  203.0 1.2 collective-permute-start.24
  204.2 0.9 collective-permute-done.23
  205.1 3.7 %collective-permute-done.24 = f32[16,512]{1,0:T(8,128)S(1)} collective-permute-done((f32[16,512]{1,0:T(8,128)S(1)}, f32[16,512]{1,0:T(8,128)S(1)}, u32[]{:S(2)}, u32[]{:S(2)}) %collective-permute-start.24) | collective-permute-done | bytes 32800 | tf_op jit(solution)/shard_map/ppermute | solution.py:726
  209.3 1.1 collective-permute-start.26
  210.4 0.8 collective-permute-start.27
  211.2 1.7 collective-permute-start.28
  213.6 5.5 %assemble.1 = (f32[2048,512]{1,0:T(8,128)}, f32[4,8,512]{2,1,0:T(8,128)S(1)}, f32[128,512]{1,0:T(8,128)S(1)}) custom-call(s32[1]{0:T(128)} %bitcast.1.half_ref.first_ref, f32[1088,512]{1,0:T(8,128)S(1)} %pad_maximum_fusion.own_ref.own_g_ref, f32[1088,512]{1,0:T(8,128)S(1)} %collective-permute-done.25.got_ref.got_g_ref, ...), custom_call_target="tpu_custom_call" | custom-call | bytes 18450000 | tf_op jit(solution)/shard_map/assemble/pallas_call | solution.py:603
  220.0 1.2 collective-permute-done.29
  221.3 7.4 %fix.1 = (f32[400,2048]{1,0:T(8,128)}, f32[100,4,512]{2,1,0:T(4,128)}, f32[4,512]{1,0:T(4,128)}, f32[4,512]{1,0:T(4,128)}, f32[4,512]{1,0:T(4,128)}, /*index=5*/...) custom-call(s32[16,128]{1,0:T(8,128)S(1)} %bitcast.25, ...), custom_call_target="tpu_custom_call" | custom-call | bytes 29520000 | tf_op jit(solution)/shard_map/fix/pallas_call | solution.py:710
  (90 shorter events, 7.1 us)
Async XLA Ops:
  5.6 18.3 %all-to-all-start = ((f32[32,1,2560]{2,1,0:T(1,128)}), f32[32,1,2560]{2,1,0:T(1,128)S(1)}, u32[]{:S(2)}, u32[]{:S(2)}) async-start(f32[32,1,2560]{2,1,0:T(1,128)} %get-tuple-element.122), calls=%async_computation | async-start | bytes 655360 | tf_op jit(solution)/shard_map/all_to_all | solution.py:730
  12.9 9.9 %copy-start.13 = (f32[2048]{0:T(1024)S(1)}, f32[2048]{0:T(1024)}, u32[]{:S(2)}) copy-start(f32[2048]{0:T(1024)} %param.21) | copy-start | bytes 24580
  12.9 11.0 %copy-start = (s32[2048]{0:T(1024)S(1)}, s32[2048]{0:T(1024)}, u32[]{:S(2)}) copy-start(s32[2048]{0:T(1024)} %param.16) | copy-start | bytes 24580
  13.0 11.0 %copy-start.2 = (f32[4,512]{1,0:T(4,128)S(1)}, f32[4,512]{1,0:T(4,128)}, u32[]{:S(2)}) copy-start(f32[4,512]{1,0:T(4,128)} %gain_ref.3) | copy-start | bytes 24580
  13.0 11.0 %copy-start.3 = (f32[4,512]{1,0:T(4,128)S(1)}, f32[4,512]{1,0:T(4,128)}, u32[]{:S(2)}) copy-start(f32[4,512]{1,0:T(4,128)} %slope_ref.3) | copy-start | bytes 24580
  13.0 11.0 %copy-start.4 = (f32[4,512]{1,0:T(4,128)S(1)}, f32[4,512]{1,0:T(4,128)}, u32[]{:S(2)}) copy-start(f32[4,512]{1,0:T(4,128)} %shift_ref.1) | copy-start | bytes 24580
  22.9 42.7 %copy-start.1 = (f32[512,47]{0,1:T(8,128)S(1)}, f32[512,47]{0,1:T(8,128)}, u32[]{:S(2)}) copy-start(f32[512,47]{0,1:T(8,128)} %param.26) | copy-start | bytes 288772
  22.9 42.7 %copy-start.5 = (s32[2048]{0:T(1024)S(1)}, s32[2048]{0:T(1024)}, u32[]{:S(2)}) copy-start(s32[2048]{0:T(1024)} %param.15) | copy-start | bytes 24580
  22.9 42.7 %copy-start.6 = (f32[512]{0:T(512)S(1)}, f32[512]{0:T(512)}, u32[]{:S(2)}) copy-start(f32[512]{0:T(512)} %param.23) | copy-start | bytes 6148
  22.9 42.7 %copy-start.7 = (f32[512]{0:T(512)S(1)}, f32[512]{0:T(512)}, u32[]{:S(2)}) copy-start(f32[512]{0:T(512)} %param.24) | copy-start | bytes 6148
  22.9 42.7 %copy-start.8 = (f32[512]{0:T(512)S(1)}, f32[512]{0:T(512)}, u32[]{:S(2)}) copy-start(f32[512]{0:T(512)} %param.25) | copy-start | bytes 6148
  22.9 42.7 %copy-start.9 = (f32[47]{0:T(128)S(1)}, f32[47]{0:T(128)}, u32[]{:S(2)}) copy-start(f32[47]{0:T(128)} %param.27) | copy-start | bytes 568
  74.8 11.0 %all-to-all-start.2 = ((f32[32,2,512]{2,1,0:T(2,128)}), f32[32,2,512]{2,1,0:T(2,128)S(1)}, u32[]{:S(2)}, u32[]{:S(2)}) async-start(f32[32,2,512]{2,1,0:T(2,128)} %get-tuple-element.127), calls=%async_computation.2 | async-start | bytes 262144 | tf_op jit(solution)/shard_map/all_to_all | solution.py:730
  98.2 9.7 %collective-permute-start = (f32[1088,512]{1,0:T(8,128)}, f32[1088,512]{1,0:T(8,128)}, u32[]{:S(2)}, u32[]{:S(2)}) collective-permute-start(f32[1088,512]{1,0:T(8,128)} %get-tuple-element.133), channel_id=1, source_target_pairs={{0,4},{4,0},{8,12},{12,8},{16,20},{20,16},{24,28},{28,24},{1,5},{5... | collective-permute-start | bytes 6684680 | tf_op jit(solution)/shard_map/ppermute | solution.py:726
  110.2 15.2 %collective-permute-start.1 = (f32[272,512]{1,0:T(8,128)}, f32[272,512]{1,0:T(8,128)S(1)}, u32[]{:S(2)}, u32[]{:S(2)}) collective-permute-start(f32[272,512]{1,0:T(8,128)} %get-tuple-element.232), channel_id=1, source_target_pairs={{0,8},{4,12},{8,0},{12,4},{16,24},{20,28},{24,16},{28,20},{1,9},{5... | collective-permute-start | bytes 1671176 | tf_op jit(solution)/shard_map/ppermute | solution.py:726
  110.9 15.0 %collective-permute-start.2 = (f32[272,512]{1,0:T(8,128)}, f32[272,512]{1,0:T(8,128)}, u32[]{:S(2)}, u32[]{:S(2)}) collective-permute-start(f32[272,512]{1,0:T(8,128)} %get-tuple-element.231), channel_id=1, source_target_pairs={{0,16},{4,20},{8,24},{12,28},{16,0},{20,4},{24,8},{28,12},{1,17},{... | collective-permute-start | bytes 1671176 | tf_op jit(solution)/shard_map/ppermute | solution.py:726
  125.3 0.8 copy-start.12
  128.0 1.2 copy-start.10
  128.0 13.4 %collective-permute-start.4 = (f32[136,512]{1,0:T(8,128)S(1)}, f32[136,512]{1,0:T(8,128)S(1)}, u32[]{:S(2)}, u32[]{:S(2)}) collective-permute-start(f32[136,512]{1,0:T(8,128)S(1)} %constant_dynamic-slice_fusion.8), channel_id=1, source_target_pairs={{0,8},{4,12},{8,0},{12,4},{16,24},{20,28},{24,16},{28,20},{1,9},{5... | collective-permute-start | bytes 835592 | tf_op jit(solution)/shard_map/ppermute | solution.py:726
  129.1 12.2 %collective-permute-start.3 = (f32[136,512]{1,0:T(8,128)S(1)}, f32[136,512]{1,0:T(8,128)S(1)}, u32[]{:S(2)}, u32[]{:S(2)}) collective-permute-start(f32[136,512]{1,0:T(8,128)S(1)} %constant_dynamic-slice_fusion.9), channel_id=1, source_target_pairs={{0,16},{4,20},{8,24},{12,28},{16,0},{20,4},{24,8},{28,12},{1,17},{... | collective-permute-start | bytes 835592 | tf_op jit(solution)/shard_map/ppermute | solution.py:726
  130.0 11.4 %copy-start.11 = (f32[272,512]{1,0:T(8,128)S(1)}, f32[272,512]{1,0:T(8,128)}, u32[]{:S(2)}) copy-start(f32[272,512]{1,0:T(8,128)} %copy-done.10) | copy-start | bytes 1671172
  141.8 15.7 %collective-permute-start.5 = (f32[68,512]{1,0:T(8,128)S(1)}, f32[68,512]{1,0:T(8,128)S(1)}, u32[]{:S(2)}, u32[]{:S(2)}) collective-permute-start(f32[68,512]{1,0:T(8,128)S(1)} %get-tuple-element.237), channel_id=1, source_target_pairs={{0,1},{1,0},{2,3},{3,2},{4,5},{5,4},{6,7},{7,6},{8,9},{9,8},{10,11... | collective-permute-start | bytes 417800 | tf_op jit(solution)/shard_map/ppermute | solution.py:726
  141.9 15.6 %collective-permute-start.6 = (f32[68,512]{1,0:T(8,128)S(1)}, f32[68,512]{1,0:T(8,128)S(1)}, u32[]{:S(2)}, u32[]{:S(2)}) collective-permute-start(f32[68,512]{1,0:T(8,128)S(1)} %get-tuple-element.238), channel_id=1, source_target_pairs={{0,2},{1,3},{2,0},{3,1},{4,6},{5,7},{6,4},{7,5},{8,10},{9,11},{10,... | collective-permute-start | bytes 417800 | tf_op jit(solution)/shard_map/ppermute | solution.py:726
  143.5 14.0 %collective-permute-start.7 = (f32[68,512]{1,0:T(8,128)S(1)}, f32[68,512]{1,0:T(8,128)S(1)}, u32[]{:S(2)}, u32[]{:S(2)}) collective-permute-start(f32[68,512]{1,0:T(8,128)S(1)} %get-tuple-element.235), channel_id=1, source_target_pairs={{0,3},{1,2},{2,1},{3,0},{4,7},{5,6},{6,5},{7,4},{8,11},{9,10},{10,... | collective-permute-start | bytes 417800 | tf_op jit(solution)/shard_map/ppermute | solution.py:726
  157.5 15.8 %collective-permute-start.10 = (f32[68,512]{1,0:T(8,128)S(1)}, f32[68,512]{1,0:T(8,128)S(1)}, u32[]{:S(2)}, u32[]{:S(2)}) collective-permute-start(f32[68,512]{1,0:T(8,128)S(1)} %add_add_fusion.2), channel_id=1, source_target_pairs={{0,3},{1,2},{2,1},{3,0},{4,7},{5,6},{6,5},{7,4},{8,11},{9,10},{10,... | collective-permute-start | bytes 417800 | tf_op jit(solution)/shard_map/ppermute | solution.py:726
  158.7 14.7 %collective-permute-start.8 = (f32[68,512]{1,0:T(8,128)S(1)}, f32[68,512]{1,0:T(8,128)S(1)}, u32[]{:S(2)}, u32[]{:S(2)}) collective-permute-start(f32[68,512]{1,0:T(8,128)S(1)} %add_add_fusion.2), channel_id=1, source_target_pairs={{0,1},{1,0},{2,3},{3,2},{4,5},{5,4},{6,7},{7,6},{8,9},{9,8},{10,11... | collective-permute-start | bytes 417800 | tf_op jit(solution)/shard_map/ppermute | solution.py:726
  158.7 14.7 %collective-permute-start.9 = (f32[68,512]{1,0:T(8,128)S(1)}, f32[68,512]{1,0:T(8,128)S(1)}, u32[]{:S(2)}, u32[]{:S(2)}) collective-permute-start(f32[68,512]{1,0:T(8,128)S(1)} %add_add_fusion.2), channel_id=1, source_target_pairs={{0,2},{1,3},{2,0},{3,1},{4,6},{5,7},{6,4},{7,5},{8,10},{9,11},{10,... | collective-permute-start | bytes 417800 | tf_op jit(solution)/shard_map/ppermute | solution.py:726
  173.5 2.6 %collective-permute-start.13 = (f32[256,512]{1,0:T(8,128)S(1)}, f32[256,512]{1,0:T(8,128)S(1)}, u32[]{:S(2)}, u32[]{:S(2)}) collective-permute-start(f32[256,512]{1,0:T(8,128)S(1)} %constant_dynamic-slice_fusion.5), channel_id=1, source_target_pairs={{0,4},{4,0},{8,12},{12,8},{16,20},{20,16},{24,28},{28,24},{1,5},{5... | collective-permute-start | bytes 1572872 | tf_op jit(solution)/shard_map/ppermute | solution.py:726
  173.8 9.5 %collective-permute-start.11 = (f32[136,512]{1,0:T(8,128)S(1)}, f32[136,512]{1,0:T(8,128)S(1)}, u32[]{:S(2)}, u32[]{:S(2)}) collective-permute-start(f32[136,512]{1,0:T(8,128)S(1)} %get-tuple-element.189), channel_id=1, source_target_pairs={{0,16},{4,20},{8,24},{12,28},{16,0},{20,4},{24,8},{28,12},{1,17},{... | collective-permute-start | bytes 835592 | tf_op jit(solution)/shard_map/ppermute | solution.py:726
  175.1 9.5 %collective-permute-start.12 = (f32[136,512]{1,0:T(8,128)S(1)}, f32[136,512]{1,0:T(8,128)S(1)}, u32[]{:S(2)}, u32[]{:S(2)}) collective-permute-start(f32[136,512]{1,0:T(8,128)S(1)} %get-tuple-element.191), channel_id=1, source_target_pairs={{0,8},{4,12},{8,0},{12,4},{16,24},{20,28},{24,16},{28,20},{1,9},{5... | collective-permute-start | bytes 835592 | tf_op jit(solution)/shard_map/ppermute | solution.py:726
  176.2 11.2 %collective-permute-start.14 = (f32[64,512]{1,0:T(8,128)S(1)}, f32[64,512]{1,0:T(8,128)S(1)}, u32[]{:S(2)}, u32[]{:S(2)}) collective-permute-start(f32[64,512]{1,0:T(8,128)S(1)} %get-tuple-element.241), channel_id=1, source_target_pairs={{0,8},{4,12},{8,0},{12,4},{16,24},{20,28},{24,16},{28,20},{1,9},{5... | collective-permute-start | bytes 393224 | tf_op jit(solution)/shard_map/ppermute | solution.py:726
  177.3 10.1 %collective-permute-start.15 = (f32[64,512]{1,0:T(8,128)S(1)}, f32[64,512]{1,0:T(8,128)S(1)}, u32[]{:S(2)}, u32[]{:S(2)}) collective-permute-start(f32[64,512]{1,0:T(8,128)S(1)} %get-tuple-element.240), channel_id=1, source_target_pairs={{0,16},{4,20},{8,24},{12,28},{16,0},{20,4},{24,8},{28,12},{1,17},{... | collective-permute-start | bytes 393224 | tf_op jit(solution)/shard_map/ppermute | solution.py:726
  178.1 11.6 %collective-permute-start.16 = (f32[64,512]{1,0:T(8,128)S(1)}, f32[64,512]{1,0:T(8,128)S(1)}, u32[]{:S(2)}, u32[]{:S(2)}) collective-permute-start(f32[64,512]{1,0:T(8,128)S(1)} %get-tuple-element.239), channel_id=1, source_target_pairs={{0,24},{4,28},{8,16},{12,20},{16,8},{20,12},{24,0},{28,4},{1,25},{... | collective-permute-start | bytes 393224 | tf_op jit(solution)/shard_map/ppermute | solution.py:726
  189.8 19.0 %collective-permute-start.18 = (f32[272,512]{1,0:T(8,128)S(1)}, f32[272,512]{1,0:T(8,128)S(1)}, u32[]{:S(2)}, u32[]{:S(2)}) collective-permute-start(f32[272,512]{1,0:T(8,128)S(1)} %maximum_select_fusion.5), channel_id=1, source_target_pairs={{0,16},{4,20},{8,24},{12,28},{16,0},{20,4},{24,8},{28,12},{1,17},{... | collective-permute-start | bytes 1671176 | tf_op jit(solution)/shard_map/ppermute | solution.py:726
  191.1 17.6 %collective-permute-start.17 = (f32[272,512]{1,0:T(8,128)S(1)}, f32[272,512]{1,0:T(8,128)S(1)}, u32[]{:S(2)}, u32[]{:S(2)}) collective-permute-start(f32[272,512]{1,0:T(8,128)S(1)} %maximum_select_fusion.4), channel_id=1, source_target_pairs={{0,8},{4,12},{8,0},{12,4},{16,24},{20,28},{24,16},{28,20},{1,9},{5... | collective-permute-start | bytes 1671176 | tf_op jit(solution)/shard_map/ppermute | solution.py:726
  192.2 4.5 %collective-permute-start.19 = (f32[16,512]{1,0:T(8,128)S(1)}, f32[16,512]{1,0:T(8,128)S(1)}, u32[]{:S(2)}, u32[]{:S(2)}) collective-permute-start(f32[16,512]{1,0:T(8,128)S(1)} %get-tuple-element.243), channel_id=1, source_target_pairs={{0,1},{1,0},{2,3},{3,2},{4,5},{5,4},{6,7},{7,6},{8,9},{9,8},{10,11... | collective-permute-start | bytes 98312 | tf_op jit(solution)/shard_map/ppermute | solution.py:726
  192.3 5.1 %collective-permute-start.20 = (f32[16,512]{1,0:T(8,128)S(1)}, f32[16,512]{1,0:T(8,128)S(1)}, u32[]{:S(2)}, u32[]{:S(2)}) collective-permute-start(f32[16,512]{1,0:T(8,128)S(1)} %get-tuple-element.245), channel_id=1, source_target_pairs={{0,2},{1,3},{2,0},{3,1},{4,6},{5,7},{6,4},{7,5},{8,10},{9,11},{10,... | collective-permute-start | bytes 98312 | tf_op jit(solution)/shard_map/ppermute | solution.py:726
  194.0 5.7 %collective-permute-start.21 = (f32[16,512]{1,0:T(8,128)S(1)}, f32[16,512]{1,0:T(8,128)S(1)}, u32[]{:S(2)}, u32[]{:S(2)}) collective-permute-start(f32[16,512]{1,0:T(8,128)S(1)} %get-tuple-element.244), channel_id=1, source_target_pairs={{0,3},{1,2},{2,1},{3,0},{4,7},{5,6},{6,5},{7,4},{8,11},{9,10},{10,... | collective-permute-start | bytes 98312 | tf_op jit(solution)/shard_map/ppermute | solution.py:726
  199.8 4.5 %collective-permute-start.22 = (f32[16,512]{1,0:T(8,128)S(1)}, f32[16,512]{1,0:T(8,128)S(1)}, u32[]{:S(2)}, u32[]{:S(2)}) collective-permute-start(f32[16,512]{1,0:T(8,128)S(1)} %add_add_fusion.4), channel_id=1, source_target_pairs={{0,1},{1,0},{2,3},{3,2},{4,5},{5,4},{6,7},{7,6},{8,9},{9,8},{10,11... | collective-permute-start | bytes 98312 | tf_op jit(solution)/shard_map/ppermute | solution.py:726
  199.8 5.2 %collective-permute-start.23 = (f32[16,512]{1,0:T(8,128)S(1)}, f32[16,512]{1,0:T(8,128)S(1)}, u32[]{:S(2)}, u32[]{:S(2)}) collective-permute-start(f32[16,512]{1,0:T(8,128)S(1)} %add_add_fusion.4), channel_id=1, source_target_pairs={{0,2},{1,3},{2,0},{3,1},{4,6},{5,7},{6,4},{7,5},{8,10},{9,11},{10,... | collective-permute-start | bytes 98312 | tf_op jit(solution)/shard_map/ppermute | solution.py:726
  203.0 5.7 %collective-permute-start.24 = (f32[16,512]{1,0:T(8,128)S(1)}, f32[16,512]{1,0:T(8,128)S(1)}, u32[]{:S(2)}, u32[]{:S(2)}) collective-permute-start(f32[16,512]{1,0:T(8,128)S(1)} %add_add_fusion.4), channel_id=1, source_target_pairs={{0,3},{1,2},{2,1},{3,0},{4,7},{5,6},{6,5},{7,4},{8,11},{9,10},{10,... | collective-permute-start | bytes 98312 | tf_op jit(solution)/shard_map/ppermute | solution.py:726
  209.2 4.4 %collective-permute-start.25 = (f32[1088,512]{1,0:T(8,128)S(1)}, f32[1088,512]{1,0:T(8,128)S(1)}, u32[]{:S(2)}, u32[]{:S(2)}) collective-permute-start(f32[1088,512]{1,0:T(8,128)S(1)} %pad_maximum_fusion.own_ref.own_g_ref), channel_id=1, source_target_pairs={{0,4},{4,0},{8,12},{12,8},{16,20},{20,16},{24,28},{28,24},{1,5},{5... | collective-permute-start | bytes 6684680 | tf_op jit(solution)/shard_map/ppermute | solution.py:726
  209.3 9.8 %collective-permute-start.26 = (f32[64,512]{1,0:T(8,128)S(1)}, f32[64,512]{1,0:T(8,128)S(1)}, u32[]{:S(2)}, u32[]{:S(2)}) collective-permute-start(f32[64,512]{1,0:T(8,128)S(1)} %maximum_select_fusion.11), channel_id=1, source_target_pairs={{0,8},{4,12},{8,0},{12,4},{16,24},{20,28},{24,16},{28,20},{1,9},{5... | collective-permute-start | bytes 393224 | tf_op jit(solution)/shard_map/ppermute | solution.py:726
  210.4 8.7 %collective-permute-start.27 = (f32[64,512]{1,0:T(8,128)S(1)}, f32[64,512]{1,0:T(8,128)S(1)}, u32[]{:S(2)}, u32[]{:S(2)}) collective-permute-start(f32[64,512]{1,0:T(8,128)S(1)} %maximum_select_fusion.11), channel_id=1, source_target_pairs={{0,16},{4,20},{8,24},{12,28},{16,0},{20,4},{24,8},{28,12},{1,17},{... | collective-permute-start | bytes 393224 | tf_op jit(solution)/shard_map/ppermute | solution.py:726
  211.2 7.9 %collective-permute-start.28 = (f32[64,512]{1,0:T(8,128)S(1)}, f32[64,512]{1,0:T(8,128)S(1)}, u32[]{:S(2)}, u32[]{:S(2)}) collective-permute-start(f32[64,512]{1,0:T(8,128)S(1)} %maximum_select_fusion.11), channel_id=1, source_target_pairs={{0,24},{4,28},{8,16},{12,20},{16,8},{20,12},{24,0},{28,4},{1,25},{... | collective-permute-start | bytes 393224 | tf_op jit(solution)/shard_map/ppermute | solution.py:726
  219.2 2.0 collective-permute-start.29

commit v6 on v5

--- a/solution.py
+++ b/solution.py
@@ -488,8 +488,26 @@
     )(half, far(dvh), far(dvl), g, far(uh), far(ul))
 
 
+def scale_kernel(wp_ref, coef_ref, ws_ref):
+    n = wp_ref.shape[1] // 3
+    for h in range(wp_ref.shape[0]):
+        w = wp_ref[h, :n, :].astype(F32) + wp_ref[h, 2 * n :, :].astype(F32)
+        ws_ref[h] = jnp.concatenate(split(w * coef_ref[h, 0:1, :]), axis=0)
+
+
+def scale_weights(wp, coef):
+    hops, n, hid = wp.shape
+    return pl.pallas_call(
+        scale_kernel,
+        out_shape=pltpu.HBM((hops, n // 3 * 2, hid), BF16),
+        compiler_params=params(16),
+        name="scale_weights",
+        cost_estimate=cost(3),
+    )(wp, coef)
+
+
 def hop_kernel(
-    h, in_w, x_ref, wp_ref, coef_ref, dvh_ref, dvl_ref, mwh_ref, mwl_ref,
+    h, in_w, x_ref, wp_ref, ws_ref, coef_ref, dvh_ref, dvl_ref, mwh_ref, mwl_ref,
     dx_ref, bw_ref, sums_ref,
 ):
     step = pl.program_id(0)
@@ -504,8 +522,8 @@
     a, b, s1, s2 = (coef_ref[0, k : k + 1, :] for k in range(4))
     xall = stack3(hop_rows(x_ref, h % (x_ref.shape[0] // in_w), in_w, 1.0))
     wp = wp_ref[0]
-    wh, wl = split((wp[:n].astype(F32) + wp[2 * n :].astype(F32)) * a)
-    whl = jnp.concatenate([wh, wl], axis=0)
+    whl = ws_ref[0]
+    wh = whl[:n]
     dot = functools.partial(lax.dot_general, preferred_element_type=F32)
     row = lambda t: jnp.sum(t, axis=0, keepdims=True)
     sums = [0.0] * 2
@@ -546,7 +564,7 @@
         sums_ref[q : q + 1, :] += sums[q]
 
 
-def hop_back(h, in_w, x, wp, coef, dvh, dvl, mwh, mwl, tile):
+def hop_back(h, in_w, x, wp, ws, coef, dvh, dvl, mwh, mwl, tile):
     width, rows = x.shape
     some = 2 * in_w if width % (2 * in_w) == 0 and in_w % 4 == 0 else width
     at = h * in_w // some
@@ -560,6 +578,7 @@
         in_specs=[
             pl.BlockSpec((some, tile), lambda i: (at, i)),
             pl.BlockSpec((1, 3 * n, hid), lambda i: (h, 0, 0)),
+            pl.BlockSpec((1, 2 * n, hid), lambda i: (h, 0, 0)),
             pl.BlockSpec((1, 8, hid), lambda i: (h, 0, 0)),
         ]
         + [by(hid), by(hid), block(hid), block(hid)],
@@ -576,7 +595,7 @@
         compiler_params=params(20),
         name=f"hop_back_{h}",
         cost_estimate=cost(11),
-    )(far(x), far(wp), coef, far(dvh), far(dvl), far(mwh), far(mwl))
+    )(far(x), far(wp), far(ws), coef, far(dvh), far(dvl), far(mwh), far(mwl))
 
 
 def assemble_kernel(first_ref, own_ref, got_ref, own_g_ref, got_g_ref, w_ref, m_ref, uu_ref, g_ref):
@@ -855,6 +874,7 @@
         TILES["forward"],
     )
     st2 = exchange(st2)
+    st2, ws = lax.optimization_barrier((st2, scale_weights(wp, coef)))
     dy2, st3, misc = head(
         valid, labels, v, st2, st, row(mix_gain), row(mix_shift), row(out_slope), head_w.T, row(head_bias),
         TILES["head"],
@@ -879,7 +899,7 @@
     for h in range(hops):
         first.step()
         dx, bw, s = hop_back(
-            h, in_w, x, wp, coef, dvh, dvl, mwh, mwl, TILES["hop"],
+            h, in_w, x, wp, ws, coef, dvh, dvl, mwh, mwl, TILES["hop"],
         )
         dxs, bws, sums = dxs + [dx], bws + [bw], sums + [s]
         first.state, x, bws, sums = lax.optimization_barrier((first.state, x, bws, sums))

time: 230 us -> 230 us (level)
  blocking collectives: 13.1 us -> 0 us
  waiting for transfers between devices: 32 us -> 39.2 us
  starting transfers between devices: 43.1 us -> 48.1 us
    all_to_all x1 -> x0, blocking collectives: 13.1 us -> none  [exchange(): return lax.all_to_all(copies, ('dp', 'bucket'), 0, 0, tiled=True)]
    all_to_all x2 -> x3, waiting for transfers between devices: 9.38 us -> 16.5 us  [exchange(): return lax.all_to_all(copies, ('dp', 'bucket'), 0, 0, tiled=True)]
    all_to_all x2 -> x3, starting transfers between devices: 9.88 us -> 14.9 us  [exchange(): return lax.all_to_all(copies, ('dp', 'bucket'), 0, 0, tiled=True)]
  transfers between devices with their start and end apart: 32 -> 33, of which waited for: 14 -> 15; matrix products, arithmetic and copies ran while one was open for 0% -> 0% of each run, Pallas kernels for 31% -> 31%
where the time goes in v6:
time: 230 us; the launch traced here: 229 us
  Pallas kernels  134 us (58%)
  starting transfers between devices  48.1 us (21%)
  waiting for transfers between devices  39.2 us (17%)
  other arithmetic  5.55 us (2%)
    pallas_call x4, Pallas kernels, hop_back(): pl.pallas_call(functools.partial(hop_kernel, h, in_w), grid=(rows // tile...  45.1 us
    ppermute x30, starting transfers between devices, flip(): return lax.ppermute(v, axis, [(i, i ^ k) for i in range(size)])  33.2 us
    pallas_call x1, Pallas kernels, forward(): pl.pallas_call(functools.partial(forward_kernel, in_w), grid=(rows // til...  28.5 us
    ppermute x30, waiting for transfers between devices, flip(): return lax.ppermute(v, axis, [(i, i ^ k) for i in range(size)])  22.7 us
    all_to_all x3, waiting for transfers between devices, exchange(): return lax.all_to_all(copies, ('dp', 'bucket'), 0, 0, tiled=True)  16.5 us
    all_to_all x3, starting transfers between devices, exchange(): return lax.all_to_all(copies, ('dp', 'bucket'), 0, 0, tiled=True)  14.9 us
    pallas_call x1, Pallas kernels, mix_back(): pl.pallas_call(mix_first_kernel, grid_spec=pltpu.PrefetchScalarGridSpec(n...  12.4 us
    pallas_call x1, Pallas kernels, project(): pl.pallas_call(functools.partial(project_kernel, in_w), grid=(rows // til...  9.85 us
  transfers between devices with their start and end apart: 33, of which 15 were waited for; matrix products, arithmetic and copies ran while one was open for 0% of the time, Pallas kernels for 31%

profile of v6, /device:TPU:0, one launch (start us, length us, event | category | flops | bytes accessed | tf_op | source)
XLA Modules:
  0.0 229.4 jit_solution(9653271936104314496)
XLA Ops:
  0.6 5.0 %gram.1 = (f32[4,112,128]{2,1,0:T(8,128)S(1)}, f32[32,1,2560]{2,1,0:T(1,128)}, bf16[4,336,512]{2,1,0:T(8,128)(2,1)}) custom-call(s32[16,128]{1,0:T(8,128)} %bitcast.21, f32[400,2048]{1,0:T(8,128)} %bitcast.34, f32[100,4,512]{2,1,0:T(4,128)} %bitcast.41), custom_call_target="tpu_custom_call" | custom-call | bytes 18450000 | tf_op jit(solution)/shard_map/gram/pallas_call | solution.py:123
  5.6 7.3 %all-to-all-start = ((f32[32,1,2560]{2,1,0:T(1,128)}), f32[32,1,2560]{2,1,0:T(1,128)S(1)}, u32[]{:S(2)}, u32[]{:S(2)}) async-start(f32[32,1,2560]{2,1,0:T(1,128)} %get-tuple-element.124), calls=%async_computation | async-start | bytes 655360 | tf_op jit(solution)/shard_map/all_to_all | solution.py:749
  13.0 9.9 %project.1.z_ref = f32[2048,2048]{1,0:T(8,128)} custom-call(f32[400,2048]{1,0:T(8,128)} %bitcast.35, bf16[4,336,512]{2,1,0:T(8,128)(2,1)} %get-tuple-element.123.wp_ref), custom_call_target="tpu_custom_call" | custom-call | bytes 33210000 | tf_op jit(solution)/shard_map/project/pallas_call | solution.py:146
  22.9 1.1 all-to-all-done.all_ref
  23.9 28.5 %forward.1 = (bf16[2048,2048]{1,0:T(8,128)(2,1)}, bf16[2048,2048]{1,0:T(8,128)(2,1)}, f32[2048,512]{1,0:T(8,128)}, f32[32,2,512]{2,1,0:T(2,128)}, bf16[2048,512]...) custom-call(s32[16,128]{1,0:T(8,128)S(1)} %bitcast.22, ...), custom_call_target="tpu_custom_call" | custom-call | bytes 110700000 | tf_op jit(solution)/shard_map/forward/pallas_call | solution.py:245
  52.6 5.1 %all-to-all-start.1 = ((f32[32,2,512]{2,1,0:T(2,128)}), f32[32,2,512]{2,1,0:T(2,128)S(1)}, u32[]{:S(2)}, u32[]{:S(2)}) async-start(f32[32,2,512]{2,1,0:T(2,128)} %get-tuple-element.126), calls=%async_computation.1 | async-start | bytes 262144 | tf_op jit(solution)/shard_map/all_to_all | solution.py:749
  57.6 1.1 scale_weights.1.ws_ref
  58.8 7.1 %all-to-all-done.1.st_ref.st2_ref = f32[32,2,512]{2,1,0:T(2,128)S(1)} async-done(((f32[32,2,512]{2,1,0:T(2,128)}), f32[32,2,512]{2,1,0:T(2,128)S(1)}, u32[]{:S(2)}, u32[]{:S(2)}) %all-to-all-start.1) | async-done | bytes 131104 | tf_op jit(solution)/shard_map/all_to_all | solution.py:749
  65.9 9.2 %head.1 = (f32[2048,512]{1,0:T(8,128)}, f32[32,2,512]{2,1,0:T(2,128)}, f32[56,512]{1,0:T(8,128)S(1)}) custom-call(s32[16,128]{1,0:T(8,128)S(1)} %bitcast.23, s32[16,128]{1,0:T(8,128)S(1)} %bitcast.27, f32[2048,512]{1,0:T(8,128)} %get-tuple-element.125.v_ref, f32[32,2,512]{2,1,0:T(2,128)S(1)} %all-to-all-done.1.st_ref.st2_ref, ...), custom_call_target="tpu_custom_call" | custom-call | bytes 33210000 | tf_op jit(solution)/shard_map/head/pallas_call | solution.py:363
  75.1 2.6 %all-to-all-start.2 = ((f32[32,2,512]{2,1,0:T(2,128)}), f32[32,2,512]{2,1,0:T(2,128)S(1)}, u32[]{:S(2)}, u32[]{:S(2)}) async-start(f32[32,2,512]{2,1,0:T(2,128)} %get-tuple-element.131), calls=%async_computation.2 | async-start | bytes 262144 | tf_op jit(solution)/shard_map/all_to_all | solution.py:749
  77.7 8.4 %all-to-all-done.2.st3_ref = f32[32,2,512]{2,1,0:T(2,128)S(1)} async-done(((f32[32,2,512]{2,1,0:T(2,128)}), f32[32,2,512]{2,1,0:T(2,128)S(1)}, u32[]{:S(2)}, u32[]{:S(2)}) %all-to-all-start.2) | async-done | bytes 131104 | tf_op jit(solution)/shard_map/all_to_all | solution.py:749
  86.1 12.4 %mix_back.1 = (f32[1088,512]{1,0:T(8,128)}, bf16[2048,512]{1,0:T(8,128)(2,1)}, bf16[2048,512]{1,0:T(8,128)(2,1)}, f32[2,512]{1,0:T(2,128)S(1)}) custom-call(s32[1]{0:T(128)} %bitcast.2.half_ref, s32[16,128]{1,0:T(8,128)S(1)} %bitcast.24, f32[2048,512]{1,0:T(8,128)} %get-tuple-element.130.dy_ref, f32[2048,512]{1,0:T(8,128)} %get-tuple-element.125.v_ref, ...), custom_call_target="tpu_custom_call" | custom-call | bytes 51660000 | tf_op jit(solution)/shard_map/mix_back/pallas_call | solution.py:448
  98.6 9.5 %mix_back_rest.1 = f32[1088,512]{1,0:T(8,128)S(1)} custom-call(s32[1]{0:T(128)} %bitcast.1.half_ref.first_ref, bf16[2048,512]{1,0:T(8,128)(2,1)} %get-tuple-element.135.dvh_ref, bf16[2048,512]{1,0:T(8,128)(2,1)} %get-tuple-element.136.dvl_ref, f32[4,112,128]{2,1,0:T(8,128)S(1)} %get-tuple-element.132.g_ref, bf16[2048,2048]{1,0:T(8,128)(2,1)} %get-tuple-element.133.uh_ref, ...), custom_call_target="tpu_custom_call" | custom-call | bytes 44280000 | tf_op jit(solution)/shard_map/mix_back_rest/pallas_call | solution.py:475
  108.1 2.4 %dynamic-slice_add_fusion = (f32[272,512]{1,0:T(8,128)}, f32[272,512]{1,0:T(8,128)}) fusion(f32[1088,512]{1,0:T(8,128)} %collective-permute-done, s32[]{:T(128)S(6)} %select_n.252, f32[1088,512]{1,0:T(8,128)S(1)} %mix_back_rest.1, s32[]{:T(128)S(6)} %select_n.249), kind=kLoop, calls=%fused_computation.17 | loop fusion | flops 278528 | bytes 3342344 | tf_op jit(solution)/shard_map/add | solution.py:812
  111.8 11.2 %hop_back_0.1 = (f32[112,2048]{1,0:T(8,128)}, f32[112,512]{1,0:T(8,128)S(1)}, f32[2,512]{1,0:T(2,128)S(1)}) custom-call(f32[400,2048]{1,0:T(8,128)} %bitcast.36, bf16[4,336,512]{2,1,0:T(8,128)(2,1)} %get-tuple-element.123.wp_ref, bf16[4,224,512]{2,1,0:T(8,128)(2,1)} %scale_weights.1.ws_ref, f32[4,8,512]{2,1,0:T(8,128)S(1)} %get-tuple-element.127.coef_ref, ...), custom_call_target="tpu_custom_call" | custom-call | bytes 40590000 | tf_op jit(solution)/shard_map/hop_back_0/pallas_call | solution.py:575
  123.0 2.6 %collective-permute-done.1 = f32[272,512]{1,0:T(8,128)S(1)} collective-permute-done((f32[272,512]{1,0:T(8,128)}, f32[272,512]{1,0:T(8,128)S(1)}, u32[]{:S(2)}, u32[]{:S(2)}) %collective-permute-start.1) | collective-permute-done | bytes 557088 | tf_op jit(solution)/shard_map/ppermute | solution.py:745
  126.4 1.8 add_add_fusion
  128.3 1.1 collective-permute-start.4
  129.4 0.8 collective-permute-start.3
  130.3 11.3 %hop_back_1.1 = (f32[112,2048]{1,0:T(8,128)}, f32[112,512]{1,0:T(8,128)S(1)}, f32[2,512]{1,0:T(2,128)S(1)}) custom-call(f32[400,2048]{1,0:T(8,128)} %bitcast.37, bf16[4,336,512]{2,1,0:T(8,128)(2,1)} %get-tuple-element.123.wp_ref, bf16[4,224,512]{2,1,0:T(8,128)(2,1)} %scale_weights.1.ws_ref, f32[4,8,512]{2,1,0:T(8,128)S(1)} %get-tuple-element.127.coef_ref, ...), custom_call_target="tpu_custom_call" | custom-call | bytes 40590000 | tf_op jit(solution)/shard_map/hop_back_1/pallas_call | solution.py:575
  142.1 1.6 collective-permute-start.6
  143.8 2.7 %collective-permute-start.7 = (f32[68,512]{1,0:T(8,128)S(1)}, f32[68,512]{1,0:T(8,128)S(1)}, u32[]{:S(2)}, u32[]{:S(2)}) collective-permute-start(f32[68,512]{1,0:T(8,128)S(1)} %get-tuple-element.239), channel_id=1, source_target_pairs={{0,3},{1,2},{2,1},{3,0},{4,7},{5,6},{6,5},{7,4},{8,11},{9,10},{10,... | collective-permute-start | bytes 417800 | tf_op jit(solution)/shard_map/ppermute | solution.py:745
  146.5 11.2 %hop_back_2.1 = (f32[112,2048]{1,0:T(8,128)}, f32[112,512]{1,0:T(8,128)S(1)}, f32[2,512]{1,0:T(2,128)S(1)}) custom-call(f32[400,2048]{1,0:T(8,128)} %bitcast.38, bf16[4,336,512]{2,1,0:T(8,128)(2,1)} %get-tuple-element.123.wp_ref, bf16[4,224,512]{2,1,0:T(8,128)(2,1)} %scale_weights.1.ws_ref, f32[4,8,512]{2,1,0:T(8,128)S(1)} %get-tuple-element.127.coef_ref, ...), custom_call_target="tpu_custom_call" | custom-call | bytes 40590000 | tf_op jit(solution)/shard_map/hop_back_2/pallas_call | solution.py:575
  157.8 1.2 collective-permute-start.10
  158.9 3.3 %collective-permute-start.9 = (f32[68,512]{1,0:T(8,128)S(1)}, f32[68,512]{1,0:T(8,128)S(1)}, u32[]{:S(2)}, u32[]{:S(2)}) collective-permute-start(f32[68,512]{1,0:T(8,128)S(1)} %add_add_fusion.2), channel_id=1, source_target_pairs={{0,2},{1,3},{2,0},{3,1},{4,6},{5,7},{6,4},{7,5},{8,10},{9,11},{10,... | collective-permute-start | bytes 417800 | tf_op jit(solution)/shard_map/ppermute | solution.py:745
  162.2 11.3 %hop_back_3.1 = (f32[112,2048]{1,0:T(8,128)}, f32[112,512]{1,0:T(8,128)S(1)}, f32[2,512]{1,0:T(2,128)S(1)}) custom-call(f32[400,2048]{1,0:T(8,128)} %bitcast.39, bf16[4,336,512]{2,1,0:T(8,128)(2,1)} %get-tuple-element.123.wp_ref, bf16[4,224,512]{2,1,0:T(8,128)(2,1)} %scale_weights.1.ws_ref, f32[4,8,512]{2,1,0:T(8,128)S(1)} %get-tuple-element.127.coef_ref, ...), custom_call_target="tpu_custom_call" | custom-call | bytes 40590000 | tf_op jit(solution)/shard_map/hop_back_3/pallas_call | solution.py:575
  173.9 1.3 collective-permute-start.11
  175.2 1.0 collective-permute-start.12
  176.3 1.1 collective-permute-start.14
  178.2 1.7 collective-permute-start.16
  179.9 3.5 %collective-permute-done.11 = f32[136,512]{1,0:T(8,128)S(1)} collective-permute-done((f32[136,512]{1,0:T(8,128)S(1)}, f32[136,512]{1,0:T(8,128)S(1)}, u32[]{:S(2)}, u32[]{:S(2)}) %collective-permute-start.11) | collective-permute-done | bytes 278560 | tf_op jit(solution)/shard_map/ppermute | solution.py:745
  183.4 1.3 collective-permute-done.12
  184.7 2.8 %collective-permute-done.14 = f32[64,512]{1,0:T(8,128)S(1)} collective-permute-done((f32[64,512]{1,0:T(8,128)S(1)}, f32[64,512]{1,0:T(8,128)S(1)}, u32[]{:S(2)}, u32[]{:S(2)}) %collective-permute-start.14) | collective-permute-done | bytes 131104 | tf_op jit(solution)/shard_map/ppermute | solution.py:745
  187.5 2.3 %collective-permute-done.16 = f32[64,512]{1,0:T(8,128)S(1)} collective-permute-done((f32[64,512]{1,0:T(8,128)S(1)}, f32[64,512]{1,0:T(8,128)S(1)}, u32[]{:S(2)}, u32[]{:S(2)}) %collective-permute-start.16) | collective-permute-done | bytes 131104 | tf_op jit(solution)/shard_map/ppermute | solution.py:745
  189.9 1.3 collective-permute-start.18
  191.3 1.0 collective-permute-start.17
  192.4 1.7 collective-permute-start.20
  194.1 2.7 %collective-permute-start.21 = (f32[16,512]{1,0:T(8,128)S(1)}, f32[16,512]{1,0:T(8,128)S(1)}, u32[]{:S(2)}, u32[]{:S(2)}) collective-permute-start(f32[16,512]{1,0:T(8,128)S(1)} %get-tuple-element.248), channel_id=1, source_target_pairs={{0,3},{1,2},{2,1},{3,0},{4,7},{5,6},{6,5},{7,4},{8,11},{9,10},{10,... | collective-permute-start | bytes 98312 | tf_op jit(solution)/shard_map/ppermute | solution.py:745
  197.5 2.4 %collective-permute-done.21 = f32[16,512]{1,0:T(8,128)S(1)} collective-permute-done((f32[16,512]{1,0:T(8,128)S(1)}, f32[16,512]{1,0:T(8,128)S(1)}, u32[]{:S(2)}, u32[]{:S(2)}) %collective-permute-start.21) | collective-permute-done | bytes 32800 | tf_op jit(solution)/shard_map/ppermute | solution.py:745
  200.0 3.2 %collective-permute-start.23 = (f32[16,512]{1,0:T(8,128)S(1)}, f32[16,512]{1,0:T(8,128)S(1)}, u32[]{:S(2)}, u32[]{:S(2)}) collective-permute-start(f32[16,512]{1,0:T(8,128)S(1)} %add_add_fusion.4), channel_id=1, source_target_pairs={{0,2},{1,3},{2,0},{3,1},{4,6},{5,7},{6,4},{7,5},{8,10},{9,11},{10,... | collective-permute-start | bytes 98312 | tf_op jit(solution)/shard_map/ppermute | solution.py:745
  203.2 1.2 collective-permute-start.24
  204.3 0.9 collective-permute-done.23
  205.2 3.7 %collective-permute-done.24 = f32[16,512]{1,0:T(8,128)S(1)} collective-permute-done((f32[16,512]{1,0:T(8,128)S(1)}, f32[16,512]{1,0:T(8,128)S(1)}, u32[]{:S(2)}, u32[]{:S(2)}) %collective-permute-start.24) | collective-permute-done | bytes 32800 | tf_op jit(solution)/shard_map/ppermute | solution.py:745
  209.4 1.1 collective-permute-start.26
  211.3 1.7 collective-permute-start.28
  213.7 5.5 %assemble.1 = (f32[2048,512]{1,0:T(8,128)}, f32[4,8,512]{2,1,0:T(8,128)S(1)}, f32[128,512]{1,0:T(8,128)S(1)}) custom-call(s32[1]{0:T(128)} %bitcast.1.half_ref.first_ref, f32[1088,512]{1,0:T(8,128)S(1)} %pad_maximum_fusion.own_ref.own_g_ref, f32[1088,512]{1,0:T(8,128)S(1)} %collective-permute-done.25.got_ref.got_g_ref, ...), custom_call_target="tpu_custom_call" | custom-call | bytes 18450000 | tf_op jit(solution)/shard_map/assemble/pallas_call | solution.py:622
  220.1 1.2 collective-permute-done.29
  221.4 7.3 %fix.1 = (f32[400,2048]{1,0:T(8,128)}, f32[100,4,512]{2,1,0:T(4,128)}, f32[4,512]{1,0:T(4,128)}, f32[4,512]{1,0:T(4,128)}, f32[4,512]{1,0:T(4,128)}, /*index=5*/...) custom-call(s32[16,128]{1,0:T(8,128)S(1)} %bitcast.25, ...), custom_call_target="tpu_custom_call" | custom-call | bytes 29520000 | tf_op jit(solution)/shard_map/fix/pallas_call | solution.py:729
  (94 shorter events, 8.7 us)
Async XLA Ops:
  5.6 18.3 %all-to-all-start = ((f32[32,1,2560]{2,1,0:T(1,128)}), f32[32,1,2560]{2,1,0:T(1,128)S(1)}, u32[]{:S(2)}, u32[]{:S(2)}) async-start(f32[32,1,2560]{2,1,0:T(1,128)} %get-tuple-element.124), calls=%async_computation | async-start | bytes 655360 | tf_op jit(solution)/shard_map/all_to_all | solution.py:749
  12.9 9.9 %copy-start.14 = (f32[2048]{0:T(1024)S(1)}, f32[2048]{0:T(1024)}, u32[]{:S(2)}) copy-start(f32[2048]{0:T(1024)} %param.21) | copy-start | bytes 24580
  12.9 11.0 %copy-start.1 = (s32[2048]{0:T(1024)S(1)}, s32[2048]{0:T(1024)}, u32[]{:S(2)}) copy-start(s32[2048]{0:T(1024)} %param.16) | copy-start | bytes 24580
  13.0 11.0 %copy-start.3 = (f32[4,512]{1,0:T(4,128)S(1)}, f32[4,512]{1,0:T(4,128)}, u32[]{:S(2)}) copy-start(f32[4,512]{1,0:T(4,128)} %gain_ref.3) | copy-start | bytes 24580
  13.0 11.0 %copy-start.4 = (f32[4,512]{1,0:T(4,128)S(1)}, f32[4,512]{1,0:T(4,128)}, u32[]{:S(2)}) copy-start(f32[4,512]{1,0:T(4,128)} %slope_ref.3) | copy-start | bytes 24580
  13.0 11.0 %copy-start.5 = (f32[4,512]{1,0:T(4,128)S(1)}, f32[4,512]{1,0:T(4,128)}, u32[]{:S(2)}) copy-start(f32[4,512]{1,0:T(4,128)} %shift_ref.1) | copy-start | bytes 24580
  22.9 34.8 %copy-start = (bf16[4,336,512]{2,1,0:T(8,128)(2,1)S(1)}, bf16[4,336,512]{2,1,0:T(8,128)(2,1)}, u32[]{:S(2)}) copy-start(bf16[4,336,512]{2,1,0:T(8,128)(2,1)} %get-tuple-element.123.wp_ref) | copy-start | bytes 4128772
  52.5 13.4 %copy-start.2 = (f32[512,47]{0,1:T(8,128)S(1)}, f32[512,47]{0,1:T(8,128)}, u32[]{:S(2)}) copy-start(f32[512,47]{0,1:T(8,128)} %param.26) | copy-start | bytes 288772
  52.5 13.4 %copy-start.6 = (s32[2048]{0:T(1024)S(1)}, s32[2048]{0:T(1024)}, u32[]{:S(2)}) copy-start(s32[2048]{0:T(1024)} %param.15) | copy-start | bytes 24580
  52.5 13.3 %copy-start.7 = (f32[512]{0:T(512)S(1)}, f32[512]{0:T(512)}, u32[]{:S(2)}) copy-start(f32[512]{0:T(512)} %param.23) | copy-start | bytes 6148
  52.5 13.3 %copy-start.8 = (f32[512]{0:T(512)S(1)}, f32[512]{0:T(512)}, u32[]{:S(2)}) copy-start(f32[512]{0:T(512)} %param.24) | copy-start | bytes 6148
  52.5 13.3 %copy-start.9 = (f32[512]{0:T(512)S(1)}, f32[512]{0:T(512)}, u32[]{:S(2)}) copy-start(f32[512]{0:T(512)} %param.25) | copy-start | bytes 6148
  52.6 13.3 %copy-start.10 = (f32[47]{0:T(128)S(1)}, f32[47]{0:T(128)}, u32[]{:S(2)}) copy-start(f32[47]{0:T(128)} %param.27) | copy-start | bytes 568
  52.6 13.3 %all-to-all-start.1 = ((f32[32,2,512]{2,1,0:T(2,128)}), f32[32,2,512]{2,1,0:T(2,128)S(1)}, u32[]{:S(2)}, u32[]{:S(2)}) async-start(f32[32,2,512]{2,1,0:T(2,128)} %get-tuple-element.126), calls=%async_computation.1 | async-start | bytes 262144 | tf_op jit(solution)/shard_map/all_to_all | solution.py:749
  75.1 11.0 %all-to-all-start.2 = ((f32[32,2,512]{2,1,0:T(2,128)}), f32[32,2,512]{2,1,0:T(2,128)S(1)}, u32[]{:S(2)}, u32[]{:S(2)}) async-start(f32[32,2,512]{2,1,0:T(2,128)} %get-tuple-element.131), calls=%async_computation.2 | async-start | bytes 262144 | tf_op jit(solution)/shard_map/all_to_all | solution.py:749
  98.5 9.6 %collective-permute-start = (f32[1088,512]{1,0:T(8,128)}, f32[1088,512]{1,0:T(8,128)}, u32[]{:S(2)}, u32[]{:S(2)}) collective-permute-start(f32[1088,512]{1,0:T(8,128)} %get-tuple-element.137), channel_id=1, source_target_pairs={{0,4},{4,0},{8,12},{12,8},{16,20},{20,16},{24,28},{28,24},{1,5},{5... | collective-permute-start | bytes 6684680 | tf_op jit(solution)/shard_map/ppermute | solution.py:745
  110.5 15.2 %collective-permute-start.1 = (f32[272,512]{1,0:T(8,128)}, f32[272,512]{1,0:T(8,128)S(1)}, u32[]{:S(2)}, u32[]{:S(2)}) collective-permute-start(f32[272,512]{1,0:T(8,128)} %get-tuple-element.236), channel_id=1, source_target_pairs={{0,8},{4,12},{8,0},{12,4},{16,24},{20,28},{24,16},{28,20},{1,9},{5... | collective-permute-start | bytes 1671176 | tf_op jit(solution)/shard_map/ppermute | solution.py:745
  111.2 15.0 %collective-permute-start.2 = (f32[272,512]{1,0:T(8,128)}, f32[272,512]{1,0:T(8,128)}, u32[]{:S(2)}, u32[]{:S(2)}) collective-permute-start(f32[272,512]{1,0:T(8,128)} %get-tuple-element.235), channel_id=1, source_target_pairs={{0,16},{4,20},{8,24},{12,28},{16,0},{20,4},{24,8},{28,12},{1,17},{... | collective-permute-start | bytes 1671176 | tf_op jit(solution)/shard_map/ppermute | solution.py:745
  125.6 0.8 copy-start.13
  128.3 1.2 copy-start.11
  128.3 13.3 %collective-permute-start.4 = (f32[136,512]{1,0:T(8,128)S(1)}, f32[136,512]{1,0:T(8,128)S(1)}, u32[]{:S(2)}, u32[]{:S(2)}) collective-permute-start(f32[136,512]{1,0:T(8,128)S(1)} %constant_dynamic-slice_fusion.8), channel_id=1, source_target_pairs={{0,8},{4,12},{8,0},{12,4},{16,24},{20,28},{24,16},{28,20},{1,9},{5... | collective-permute-start | bytes 835592 | tf_op jit(solution)/shard_map/ppermute | solution.py:745
  129.4 12.2 %collective-permute-start.3 = (f32[136,512]{1,0:T(8,128)S(1)}, f32[136,512]{1,0:T(8,128)S(1)}, u32[]{:S(2)}, u32[]{:S(2)}) collective-permute-start(f32[136,512]{1,0:T(8,128)S(1)} %constant_dynamic-slice_fusion.9), channel_id=1, source_target_pairs={{0,16},{4,20},{8,24},{12,28},{16,0},{20,4},{24,8},{28,12},{1,17},{... | collective-permute-start | bytes 835592 | tf_op jit(solution)/shard_map/ppermute | solution.py:745
  130.3 11.3 %copy-start.12 = (f32[272,512]{1,0:T(8,128)S(1)}, f32[272,512]{1,0:T(8,128)}, u32[]{:S(2)}) copy-start(f32[272,512]{1,0:T(8,128)} %copy-done.11) | copy-start | bytes 1671172
  142.0 15.7 %collective-permute-start.5 = (f32[68,512]{1,0:T(8,128)S(1)}, f32[68,512]{1,0:T(8,128)S(1)}, u32[]{:S(2)}, u32[]{:S(2)}) collective-permute-start(f32[68,512]{1,0:T(8,128)S(1)} %get-tuple-element.241), channel_id=1, source_target_pairs={{0,1},{1,0},{2,3},{3,2},{4,5},{5,4},{6,7},{7,6},{8,9},{9,8},{10,11... | collective-permute-start | bytes 417800 | tf_op jit(solution)/shard_map/ppermute | solution.py:745
  142.1 15.6 %collective-permute-start.6 = (f32[68,512]{1,0:T(8,128)S(1)}, f32[68,512]{1,0:T(8,128)S(1)}, u32[]{:S(2)}, u32[]{:S(2)}) collective-permute-start(f32[68,512]{1,0:T(8,128)S(1)} %get-tuple-element.242), channel_id=1, source_target_pairs={{0,2},{1,3},{2,0},{3,1},{4,6},{5,7},{6,4},{7,5},{8,10},{9,11},{10,... | collective-permute-start | bytes 417800 | tf_op jit(solution)/shard_map/ppermute | solution.py:745
  143.8 13.9 %collective-permute-start.7 = (f32[68,512]{1,0:T(8,128)S(1)}, f32[68,512]{1,0:T(8,128)S(1)}, u32[]{:S(2)}, u32[]{:S(2)}) collective-permute-start(f32[68,512]{1,0:T(8,128)S(1)} %get-tuple-element.239), channel_id=1, source_target_pairs={{0,3},{1,2},{2,1},{3,0},{4,7},{5,6},{6,5},{7,4},{8,11},{9,10},{10,... | collective-permute-start | bytes 417800 | tf_op jit(solution)/shard_map/ppermute | solution.py:745
  157.8 15.7 %collective-permute-start.10 = (f32[68,512]{1,0:T(8,128)S(1)}, f32[68,512]{1,0:T(8,128)S(1)}, u32[]{:S(2)}, u32[]{:S(2)}) collective-permute-start(f32[68,512]{1,0:T(8,128)S(1)} %add_add_fusion.2), channel_id=1, source_target_pairs={{0,3},{1,2},{2,1},{3,0},{4,7},{5,6},{6,5},{7,4},{8,11},{9,10},{10,... | collective-permute-start | bytes 417800 | tf_op jit(solution)/shard_map/ppermute | solution.py:745
  158.9 14.6 %collective-permute-start.8 = (f32[68,512]{1,0:T(8,128)S(1)}, f32[68,512]{1,0:T(8,128)S(1)}, u32[]{:S(2)}, u32[]{:S(2)}) collective-permute-start(f32[68,512]{1,0:T(8,128)S(1)} %add_add_fusion.2), channel_id=1, source_target_pairs={{0,1},{1,0},{2,3},{3,2},{4,5},{5,4},{6,7},{7,6},{8,9},{9,8},{10,11... | collective-permute-start | bytes 417800 | tf_op jit(solution)/shard_map/ppermute | solution.py:745
  158.9 14.6 %collective-permute-start.9 = (f32[68,512]{1,0:T(8,128)S(1)}, f32[68,512]{1,0:T(8,128)S(1)}, u32[]{:S(2)}, u32[]{:S(2)}) collective-permute-start(f32[68,512]{1,0:T(8,128)S(1)} %add_add_fusion.2), channel_id=1, source_target_pairs={{0,2},{1,3},{2,0},{3,1},{4,6},{5,7},{6,4},{7,5},{8,10},{9,11},{10,... | collective-permute-start | bytes 417800 | tf_op jit(solution)/shard_map/ppermute | solution.py:745
  173.6 2.6 %collective-permute-start.13 = (f32[256,512]{1,0:T(8,128)S(1)}, f32[256,512]{1,0:T(8,128)S(1)}, u32[]{:S(2)}, u32[]{:S(2)}) collective-permute-start(f32[256,512]{1,0:T(8,128)S(1)} %constant_dynamic-slice_fusion.5), channel_id=1, source_target_pairs={{0,4},{4,0},{8,12},{12,8},{16,20},{20,16},{24,28},{28,24},{1,5},{5... | collective-permute-start | bytes 1572872 | tf_op jit(solution)/shard_map/ppermute | solution.py:745
  173.9 9.5 %collective-permute-start.11 = (f32[136,512]{1,0:T(8,128)S(1)}, f32[136,512]{1,0:T(8,128)S(1)}, u32[]{:S(2)}, u32[]{:S(2)}) collective-permute-start(f32[136,512]{1,0:T(8,128)S(1)} %get-tuple-element.193), channel_id=1, source_target_pairs={{0,16},{4,20},{8,24},{12,28},{16,0},{20,4},{24,8},{28,12},{1,17},{... | collective-permute-start | bytes 835592 | tf_op jit(solution)/shard_map/ppermute | solution.py:745
  175.2 9.5 %collective-permute-start.12 = (f32[136,512]{1,0:T(8,128)S(1)}, f32[136,512]{1,0:T(8,128)S(1)}, u32[]{:S(2)}, u32[]{:S(2)}) collective-permute-start(f32[136,512]{1,0:T(8,128)S(1)} %get-tuple-element.195), channel_id=1, source_target_pairs={{0,8},{4,12},{8,0},{12,4},{16,24},{20,28},{24,16},{28,20},{1,9},{5... | collective-permute-start | bytes 835592 | tf_op jit(solution)/shard_map/ppermute | solution.py:745
  176.3 11.2 %collective-permute-start.14 = (f32[64,512]{1,0:T(8,128)S(1)}, f32[64,512]{1,0:T(8,128)S(1)}, u32[]{:S(2)}, u32[]{:S(2)}) collective-permute-start(f32[64,512]{1,0:T(8,128)S(1)} %get-tuple-element.245), channel_id=1, source_target_pairs={{0,8},{4,12},{8,0},{12,4},{16,24},{20,28},{24,16},{28,20},{1,9},{5... | collective-permute-start | bytes 393224 | tf_op jit(solution)/shard_map/ppermute | solution.py:745
  177.5 10.1 %collective-permute-start.15 = (f32[64,512]{1,0:T(8,128)S(1)}, f32[64,512]{1,0:T(8,128)S(1)}, u32[]{:S(2)}, u32[]{:S(2)}) collective-permute-start(f32[64,512]{1,0:T(8,128)S(1)} %get-tuple-element.244), channel_id=1, source_target_pairs={{0,16},{4,20},{8,24},{12,28},{16,0},{20,4},{24,8},{28,12},{1,17},{... | collective-permute-start | bytes 393224 | tf_op jit(solution)/shard_map/ppermute | solution.py:745
  178.2 11.6 %collective-permute-start.16 = (f32[64,512]{1,0:T(8,128)S(1)}, f32[64,512]{1,0:T(8,128)S(1)}, u32[]{:S(2)}, u32[]{:S(2)}) collective-permute-start(f32[64,512]{1,0:T(8,128)S(1)} %get-tuple-element.243), channel_id=1, source_target_pairs={{0,24},{4,28},{8,16},{12,20},{16,8},{20,12},{24,0},{28,4},{1,25},{... | collective-permute-start | bytes 393224 | tf_op jit(solution)/shard_map/ppermute | solution.py:745
  189.9 19.0 %collective-permute-start.18 = (f32[272,512]{1,0:T(8,128)S(1)}, f32[272,512]{1,0:T(8,128)S(1)}, u32[]{:S(2)}, u32[]{:S(2)}) collective-permute-start(f32[272,512]{1,0:T(8,128)S(1)} %maximum_select_fusion.5), channel_id=1, source_target_pairs={{0,16},{4,20},{8,24},{12,28},{16,0},{20,4},{24,8},{28,12},{1,17},{... | collective-permute-start | bytes 1671176 | tf_op jit(solution)/shard_map/ppermute | solution.py:745
  191.3 17.6 %collective-permute-start.17 = (f32[272,512]{1,0:T(8,128)S(1)}, f32[272,512]{1,0:T(8,128)S(1)}, u32[]{:S(2)}, u32[]{:S(2)}) collective-permute-start(f32[272,512]{1,0:T(8,128)S(1)} %maximum_select_fusion.4), channel_id=1, source_target_pairs={{0,8},{4,12},{8,0},{12,4},{16,24},{20,28},{24,16},{28,20},{1,9},{5... | collective-permute-start | bytes 1671176 | tf_op jit(solution)/shard_map/ppermute | solution.py:745
  192.4 4.5 %collective-permute-start.19 = (f32[16,512]{1,0:T(8,128)S(1)}, f32[16,512]{1,0:T(8,128)S(1)}, u32[]{:S(2)}, u32[]{:S(2)}) collective-permute-start(f32[16,512]{1,0:T(8,128)S(1)} %get-tuple-element.247), channel_id=1, source_target_pairs={{0,1},{1,0},{2,3},{3,2},{4,5},{5,4},{6,7},{7,6},{8,9},{9,8},{10,11... | collective-permute-start | bytes 98312 | tf_op jit(solution)/shard_map/ppermute | solution.py:745
  192.4 5.1 %collective-permute-start.20 = (f32[16,512]{1,0:T(8,128)S(1)}, f32[16,512]{1,0:T(8,128)S(1)}, u32[]{:S(2)}, u32[]{:S(2)}) collective-permute-start(f32[16,512]{1,0:T(8,128)S(1)} %get-tuple-element.249), channel_id=1, source_target_pairs={{0,2},{1,3},{2,0},{3,1},{4,6},{5,7},{6,4},{7,5},{8,10},{9,11},{10,... | collective-permute-start | bytes 98312 | tf_op jit(solution)/shard_map/ppermute | solution.py:745
  194.1 5.7 %collective-permute-start.21 = (f32[16,512]{1,0:T(8,128)S(1)}, f32[16,512]{1,0:T(8,128)S(1)}, u32[]{:S(2)}, u32[]{:S(2)}) collective-permute-start(f32[16,512]{1,0:T(8,128)S(1)} %get-tuple-element.248), channel_id=1, source_target_pairs={{0,3},{1,2},{2,1},{3,0},{4,7},{5,6},{6,5},{7,4},{8,11},{9,10},{10,... | collective-permute-start | bytes 98312 | tf_op jit(solution)/shard_map/ppermute | solution.py:745
  199.9 4.5 %collective-permute-start.22 = (f32[16,512]{1,0:T(8,128)S(1)}, f32[16,512]{1,0:T(8,128)S(1)}, u32[]{:S(2)}, u32[]{:S(2)}) collective-permute-start(f32[16,512]{1,0:T(8,128)S(1)} %add_add_fusion.4), channel_id=1, source_target_pairs={{0,1},{1,0},{2,3},{3,2},{4,5},{5,4},{6,7},{7,6},{8,9},{9,8},{10,11... | collective-permute-start | bytes 98312 | tf_op jit(solution)/shard_map/ppermute | solution.py:745
  200.0 5.2 %collective-permute-start.23 = (f32[16,512]{1,0:T(8,128)S(1)}, f32[16,512]{1,0:T(8,128)S(1)}, u32[]{:S(2)}, u32[]{:S(2)}) collective-permute-start(f32[16,512]{1,0:T(8,128)S(1)} %add_add_fusion.4), channel_id=1, source_target_pairs={{0,2},{1,3},{2,0},{3,1},{4,6},{5,7},{6,4},{7,5},{8,10},{9,11},{10,... | collective-permute-start | bytes 98312 | tf_op jit(solution)/shard_map/ppermute | solution.py:745
  203.2 5.7 %collective-permute-start.24 = (f32[16,512]{1,0:T(8,128)S(1)}, f32[16,512]{1,0:T(8,128)S(1)}, u32[]{:S(2)}, u32[]{:S(2)}) collective-permute-start(f32[16,512]{1,0:T(8,128)S(1)} %add_add_fusion.4), channel_id=1, source_target_pairs={{0,3},{1,2},{2,1},{3,0},{4,7},{5,6},{6,5},{7,4},{8,11},{9,10},{10,... | collective-permute-start | bytes 98312 | tf_op jit(solution)/shard_map/ppermute | solution.py:745
  209.3 4.4 %collective-permute-start.25 = (f32[1088,512]{1,0:T(8,128)S(1)}, f32[1088,512]{1,0:T(8,128)S(1)}, u32[]{:S(2)}, u32[]{:S(2)}) collective-permute-start(f32[1088,512]{1,0:T(8,128)S(1)} %pad_maximum_fusion.own_ref.own_g_ref), channel_id=1, source_target_pairs={{0,4},{4,0},{8,12},{12,8},{16,20},{20,16},{24,28},{28,24},{1,5},{5... | collective-permute-start | bytes 6684680 | tf_op jit(solution)/shard_map/ppermute | solution.py:745
  209.4 9.8 %collective-permute-start.26 = (f32[64,512]{1,0:T(8,128)S(1)}, f32[64,512]{1,0:T(8,128)S(1)}, u32[]{:S(2)}, u32[]{:S(2)}) collective-permute-start(f32[64,512]{1,0:T(8,128)S(1)} %maximum_select_fusion.11), channel_id=1, source_target_pairs={{0,8},{4,12},{8,0},{12,4},{16,24},{20,28},{24,16},{28,20},{1,9},{5... | collective-permute-start | bytes 393224 | tf_op jit(solution)/shard_map/ppermute | solution.py:745
  210.6 8.7 %collective-permute-start.27 = (f32[64,512]{1,0:T(8,128)S(1)}, f32[64,512]{1,0:T(8,128)S(1)}, u32[]{:S(2)}, u32[]{:S(2)}) collective-permute-start(f32[64,512]{1,0:T(8,128)S(1)} %maximum_select_fusion.11), channel_id=1, source_target_pairs={{0,16},{4,20},{8,24},{12,28},{16,0},{20,4},{24,8},{28,12},{1,17},{... | collective-permute-start | bytes 393224 | tf_op jit(solution)/shard_map/ppermute | solution.py:745
  211.3 7.9 %collective-permute-start.28 = (f32[64,512]{1,0:T(8,128)S(1)}, f32[64,512]{1,0:T(8,128)S(1)}, u32[]{:S(2)}, u32[]{:S(2)}) collective-permute-start(f32[64,512]{1,0:T(8,128)S(1)} %maximum_select_fusion.11), channel_id=1, source_target_pairs={{0,24},{4,28},{8,16},{12,20},{16,8},{20,12},{24,0},{28,4},{1,25},{... | collective-permute-start | bytes 393224 | tf_op jit(solution)/shard_map/ppermute | solution.py:745
  219.3 2.0 collective-permute-start.29

commit v7 on v5

--- a/solution.py
+++ b/solution.py
@@ -16,7 +16,7 @@
 TILES = {"gram": 2048, "project": 512, "forward": 512, "head": 1024, "mix": 512, "hop": 512, "fix": 1024}
 PACK_STEPS = 2
 SUB = 256
-MIX_SUB = 256
+MIX_SUB = 512
 NN = (((1,), (0,)), ((), ()))
 NT = (((1,), (1,)), ((), ()))
 TN = (((0,), (0,)), ((), ()))

time: 230 us -> 230 us (level)
  no operation moved by 1% of the time
where the time goes in v7:
time: 230 us
  Pallas kernels  133 us (58%)
  starting transfers between devices  43.1 us (19%)
  waiting for transfers between devices  32 us (14%)
  blocking collectives  13.1 us (6%)
  other arithmetic  5.55 us (2%)
    pallas_call x4, Pallas kernels, hop_back(): pl.pallas_call(functools.partial(hop_kernel, h, in_w), grid=(rows // tile...  45.3 us
    ppermute x30, starting transfers between devices, flip(): return lax.ppermute(v, axis, [(i, i ^ k) for i in range(size)])  33.2 us
    pallas_call x1, Pallas kernels, forward(): pl.pallas_call(functools.partial(forward_kernel, in_w), grid=(rows // til...  28.5 us
    ppermute x30, waiting for transfers between devices, flip(): return lax.ppermute(v, axis, [(i, i ^ k) for i in range(size)])  22.6 us
    all_to_all x1, blocking collectives, exchange(): return lax.all_to_all(copies, ('dp', 'bucket'), 0, 0, tiled=True)  13.1 us
    pallas_call x1, Pallas kernels, mix_back(): pl.pallas_call(mix_first_kernel, grid_spec=pltpu.PrefetchScalarGridSpec(n...  12.7 us
    all_to_all x2, starting transfers between devices, exchange(): return lax.all_to_all(copies, ('dp', 'bucket'), 0, 0, tiled=True)  9.88 us
    pallas_call x1, Pallas kernels, project(): pl.pallas_call(functools.partial(project_kernel, in_w), grid=(rows // til...  9.85 us
  transfers between devices with their start and end apart: 32, of which 14 were waited for; matrix products, arithmetic and copies ran while one was open for 0% of the time, Pallas kernels for 31%

profile of v7, /device:TPU:0, one launch (start us, length us, event | category | flops | bytes accessed | tf_op | source)
XLA Modules:
  0.0 229.6 jit_solution(4018906985914676065)
XLA Ops:
  0.6 5.0 %gram.1 = (f32[4,112,128]{2,1,0:T(8,128)S(1)}, f32[32,1,2560]{2,1,0:T(1,128)}, bf16[4,336,512]{2,1,0:T(8,128)(2,1)}) custom-call(s32[16,128]{1,0:T(8,128)} %bitcast.21, f32[400,2048]{1,0:T(8,128)} %bitcast.34, f32[100,4,512]{2,1,0:T(4,128)} %bitcast.41), custom_call_target="tpu_custom_call" | custom-call | bytes 18450000 | tf_op jit(solution)/shard_map/gram/pallas_call | solution.py:123
  5.6 7.3 %all-to-all-start = ((f32[32,1,2560]{2,1,0:T(1,128)}), f32[32,1,2560]{2,1,0:T(1,128)S(1)}, u32[]{:S(2)}, u32[]{:S(2)}) async-start(f32[32,1,2560]{2,1,0:T(1,128)} %get-tuple-element.122), calls=%async_computation | async-start | bytes 655360 | tf_op jit(solution)/shard_map/all_to_all | solution.py:730
  13.0 9.8 %project.1.z_ref = f32[2048,2048]{1,0:T(8,128)} custom-call(f32[400,2048]{1,0:T(8,128)} %bitcast.35, bf16[4,336,512]{2,1,0:T(8,128)(2,1)} %get-tuple-element.121.wp_ref), custom_call_target="tpu_custom_call" | custom-call | bytes 33210000 | tf_op jit(solution)/shard_map/project/pallas_call | solution.py:146
  22.9 1.0 all-to-all-done.all_ref
  23.9 28.5 %forward.1 = (bf16[2048,2048]{1,0:T(8,128)(2,1)}, bf16[2048,2048]{1,0:T(8,128)(2,1)}, f32[2048,512]{1,0:T(8,128)}, f32[32,2,512]{2,1,0:T(2,128)S(1)}, bf16[2048,...) custom-call(s32[16,128]{1,0:T(8,128)S(1)} %bitcast.22, ...), custom_call_target="tpu_custom_call" | custom-call | bytes 110700000 | tf_op jit(solution)/shard_map/forward/pallas_call | solution.py:245
  52.5 13.1 %all_to_all.15.st_ref.st2_ref = f32[32,2,512]{2,1,0:T(2,128)S(1)} all-to-all(f32[32,2,512]{2,1,0:T(2,128)S(1)} %get-tuple-element.124), channel_id=1, replica_groups=mesh['dp'=8,'bucket'=4] {'dp','bucket'}, dimensions={0} | all-to-all | bytes 262144 | tf_op jit(solution)/shard_map/all_to_all | solution.py:730
  65.6 9.2 %head.1 = (f32[2048,512]{1,0:T(8,128)}, f32[32,2,512]{2,1,0:T(2,128)}, f32[56,512]{1,0:T(8,128)S(1)}) custom-call(s32[16,128]{1,0:T(8,128)S(1)} %bitcast.23, s32[16,128]{1,0:T(8,128)S(1)} %bitcast.27, f32[2048,512]{1,0:T(8,128)} %get-tuple-element.123.v_ref, f32[32,2,512]{2,1,0:T(2,128)S(1)} %all_to_all.15.st_ref.st2_ref, ...), custom_call_target="tpu_custom_call" | custom-call | bytes 33210000 | tf_op jit(solution)/shard_map/head/pallas_call | solution.py:363
  74.8 2.6 %all-to-all-start.2 = ((f32[32,2,512]{2,1,0:T(2,128)}), f32[32,2,512]{2,1,0:T(2,128)S(1)}, u32[]{:S(2)}, u32[]{:S(2)}) async-start(f32[32,2,512]{2,1,0:T(2,128)} %get-tuple-element.127), calls=%async_computation.2 | async-start | bytes 262144 | tf_op jit(solution)/shard_map/all_to_all | solution.py:730
  77.4 8.4 %all-to-all-done.2.st3_ref = f32[32,2,512]{2,1,0:T(2,128)S(1)} async-done(((f32[32,2,512]{2,1,0:T(2,128)}), f32[32,2,512]{2,1,0:T(2,128)S(1)}, u32[]{:S(2)}, u32[]{:S(2)}) %all-to-all-start.2) | async-done | bytes 131104 | tf_op jit(solution)/shard_map/all_to_all | solution.py:730
  85.8 12.7 %mix_back.1 = (f32[1088,512]{1,0:T(8,128)}, bf16[2048,512]{1,0:T(8,128)(2,1)}, bf16[2048,512]{1,0:T(8,128)(2,1)}, f32[2,512]{1,0:T(2,128)S(1)}) custom-call(s32[1]{0:T(128)} %bitcast.2.half_ref, s32[16,128]{1,0:T(8,128)S(1)} %bitcast.24, f32[2048,512]{1,0:T(8,128)} %get-tuple-element.126.dy_ref, f32[2048,512]{1,0:T(8,128)} %get-tuple-element.123.v_ref, ...), custom_call_target="tpu_custom_call" | custom-call | bytes 51660000 | tf_op jit(solution)/shard_map/mix_back/pallas_call | solution.py:448
  98.7 9.5 %mix_back_rest.1 = f32[1088,512]{1,0:T(8,128)S(1)} custom-call(s32[1]{0:T(128)} %bitcast.1.half_ref.first_ref, bf16[2048,512]{1,0:T(8,128)(2,1)} %get-tuple-element.131.dvh_ref, bf16[2048,512]{1,0:T(8,128)(2,1)} %get-tuple-element.132.dvl_ref, f32[4,112,128]{2,1,0:T(8,128)S(1)} %get-tuple-element.128.g_ref, bf16[2048,2048]{1,0:T(8,128)(2,1)} %get-tuple-element.129.uh_ref, ...), custom_call_target="tpu_custom_call" | custom-call | bytes 44280000 | tf_op jit(solution)/shard_map/mix_back_rest/pallas_call | solution.py:475
  108.2 2.4 %dynamic-slice_add_fusion = (f32[272,512]{1,0:T(8,128)}, f32[272,512]{1,0:T(8,128)}) fusion(f32[1088,512]{1,0:T(8,128)} %collective-permute-done, s32[]{:T(128)S(6)} %select_n.252, f32[1088,512]{1,0:T(8,128)S(1)} %mix_back_rest.1, s32[]{:T(128)S(6)} %select_n.249), kind=kLoop, calls=%fused_computation.17 | loop fusion | flops 278528 | bytes 3342344 | tf_op jit(solution)/shard_map/add | solution.py:793
  111.8 11.3 %hop_back_0.1 = (f32[112,2048]{1,0:T(8,128)}, f32[112,512]{1,0:T(8,128)S(1)}, f32[2,512]{1,0:T(2,128)S(1)}) custom-call(f32[400,2048]{1,0:T(8,128)} %bitcast.36, bf16[4,336,512]{2,1,0:T(8,128)(2,1)} %get-tuple-element.121.wp_ref, f32[4,8,512]{2,1,0:T(8,128)S(1)} %get-tuple-element.137.coef_ref, bf16[2048,512]{1,0:T(8,128)(2,1)} %get-tuple-element.131.dvh_ref, ...), custom_call_target="tpu_custom_call" | custom-call | bytes 40590000 | tf_op jit(solution)/shard_map/hop_back_0/pallas_call | solution.py:557
  123.1 2.6 %collective-permute-done.1 = f32[272,512]{1,0:T(8,128)S(1)} collective-permute-done((f32[272,512]{1,0:T(8,128)}, f32[272,512]{1,0:T(8,128)S(1)}, u32[]{:S(2)}, u32[]{:S(2)}) %collective-permute-start.1) | collective-permute-done | bytes 557088 | tf_op jit(solution)/shard_map/ppermute | solution.py:726
  126.5 1.8 add_add_fusion
  128.4 1.1 collective-permute-start.4
  129.5 0.8 collective-permute-start.3
  130.4 11.4 %hop_back_1.1 = (f32[112,2048]{1,0:T(8,128)}, f32[112,512]{1,0:T(8,128)S(1)}, f32[2,512]{1,0:T(2,128)S(1)}) custom-call(f32[400,2048]{1,0:T(8,128)} %bitcast.37, bf16[4,336,512]{2,1,0:T(8,128)(2,1)} %get-tuple-element.121.wp_ref, f32[4,8,512]{2,1,0:T(8,128)S(1)} %get-tuple-element.137.coef_ref, bf16[2048,512]{1,0:T(8,128)(2,1)} %get-tuple-element.131.dvh_ref, ...), custom_call_target="tpu_custom_call" | custom-call | bytes 40590000 | tf_op jit(solution)/shard_map/hop_back_1/pallas_call | solution.py:557
  142.2 1.7 collective-permute-start.6
  143.9 2.7 %collective-permute-start.7 = (f32[68,512]{1,0:T(8,128)S(1)}, f32[68,512]{1,0:T(8,128)S(1)}, u32[]{:S(2)}, u32[]{:S(2)}) collective-permute-start(f32[68,512]{1,0:T(8,128)S(1)} %get-tuple-element.235), channel_id=1, source_target_pairs={{0,3},{1,2},{2,1},{3,0},{4,7},{5,6},{6,5},{7,4},{8,11},{9,10},{10,... | collective-permute-start | bytes 417800 | tf_op jit(solution)/shard_map/ppermute | solution.py:726
  146.6 11.2 %hop_back_2.1 = (f32[112,2048]{1,0:T(8,128)}, f32[112,512]{1,0:T(8,128)S(1)}, f32[2,512]{1,0:T(2,128)S(1)}) custom-call(f32[400,2048]{1,0:T(8,128)} %bitcast.38, bf16[4,336,512]{2,1,0:T(8,128)(2,1)} %get-tuple-element.121.wp_ref, f32[4,8,512]{2,1,0:T(8,128)S(1)} %get-tuple-element.137.coef_ref, bf16[2048,512]{1,0:T(8,128)(2,1)} %get-tuple-element.131.dvh_ref, ...), custom_call_target="tpu_custom_call" | custom-call | bytes 40590000 | tf_op jit(solution)/shard_map/hop_back_2/pallas_call | solution.py:557
  157.9 1.2 collective-permute-start.10
  159.1 3.3 %collective-permute-start.9 = (f32[68,512]{1,0:T(8,128)S(1)}, f32[68,512]{1,0:T(8,128)S(1)}, u32[]{:S(2)}, u32[]{:S(2)}) collective-permute-start(f32[68,512]{1,0:T(8,128)S(1)} %add_add_fusion.2), channel_id=1, source_target_pairs={{0,2},{1,3},{2,0},{3,1},{4,6},{5,7},{6,4},{7,5},{8,10},{9,11},{10,... | collective-permute-start | bytes 417800 | tf_op jit(solution)/shard_map/ppermute | solution.py:726
  162.4 11.4 %hop_back_3.1 = (f32[112,2048]{1,0:T(8,128)}, f32[112,512]{1,0:T(8,128)S(1)}, f32[2,512]{1,0:T(2,128)S(1)}) custom-call(f32[400,2048]{1,0:T(8,128)} %bitcast.39, bf16[4,336,512]{2,1,0:T(8,128)(2,1)} %get-tuple-element.121.wp_ref, f32[4,8,512]{2,1,0:T(8,128)S(1)} %get-tuple-element.137.coef_ref, bf16[2048,512]{1,0:T(8,128)(2,1)} %get-tuple-element.131.dvh_ref, ...), custom_call_target="tpu_custom_call" | custom-call | bytes 40590000 | tf_op jit(solution)/shard_map/hop_back_3/pallas_call | solution.py:557
  174.2 1.3 collective-permute-start.11
  175.5 1.0 collective-permute-start.12
  176.6 1.1 collective-permute-start.14
  177.7 0.8 collective-permute-start.15
  178.5 1.7 collective-permute-start.16
  180.1 3.5 %collective-permute-done.11 = f32[136,512]{1,0:T(8,128)S(1)} collective-permute-done((f32[136,512]{1,0:T(8,128)S(1)}, f32[136,512]{1,0:T(8,128)S(1)}, u32[]{:S(2)}, u32[]{:S(2)}) %collective-permute-start.11) | collective-permute-done | bytes 278560 | tf_op jit(solution)/shard_map/ppermute | solution.py:726
  183.7 1.3 collective-permute-done.12
  185.0 2.8 %collective-permute-done.14 = f32[64,512]{1,0:T(8,128)S(1)} collective-permute-done((f32[64,512]{1,0:T(8,128)S(1)}, f32[64,512]{1,0:T(8,128)S(1)}, u32[]{:S(2)}, u32[]{:S(2)}) %collective-permute-start.14) | collective-permute-done | bytes 131104 | tf_op jit(solution)/shard_map/ppermute | solution.py:726
  187.8 2.3 %collective-permute-done.16 = f32[64,512]{1,0:T(8,128)S(1)} collective-permute-done((f32[64,512]{1,0:T(8,128)S(1)}, f32[64,512]{1,0:T(8,128)S(1)}, u32[]{:S(2)}, u32[]{:S(2)}) %collective-permute-start.16) | collective-permute-done | bytes 131104 | tf_op jit(solution)/shard_map/ppermute | solution.py:726
  190.1 1.3 collective-permute-start.18
  191.5 1.0 collective-permute-start.17
  192.7 1.7 collective-permute-start.20
  194.4 2.7 %collective-permute-start.21 = (f32[16,512]{1,0:T(8,128)S(1)}, f32[16,512]{1,0:T(8,128)S(1)}, u32[]{:S(2)}, u32[]{:S(2)}) collective-permute-start(f32[16,512]{1,0:T(8,128)S(1)} %get-tuple-element.244), channel_id=1, source_target_pairs={{0,3},{1,2},{2,1},{3,0},{4,7},{5,6},{6,5},{7,4},{8,11},{9,10},{10,... | collective-permute-start | bytes 98312 | tf_op jit(solution)/shard_map/ppermute | solution.py:726
  197.7 2.4 %collective-permute-done.21 = f32[16,512]{1,0:T(8,128)S(1)} collective-permute-done((f32[16,512]{1,0:T(8,128)S(1)}, f32[16,512]{1,0:T(8,128)S(1)}, u32[]{:S(2)}, u32[]{:S(2)}) %collective-permute-start.21) | collective-permute-done | bytes 32800 | tf_op jit(solution)/shard_map/ppermute | solution.py:726
  200.2 3.2 %collective-permute-start.23 = (f32[16,512]{1,0:T(8,128)S(1)}, f32[16,512]{1,0:T(8,128)S(1)}, u32[]{:S(2)}, u32[]{:S(2)}) collective-permute-start(f32[16,512]{1,0:T(8,128)S(1)} %add_add_fusion.4), channel_id=1, source_target_pairs={{0,2},{1,3},{2,0},{3,1},{4,6},{5,7},{6,4},{7,5},{8,10},{9,11},{10,... | collective-permute-start | bytes 98312 | tf_op jit(solution)/shard_map/ppermute | solution.py:726
  203.4 1.2 collective-permute-start.24
  204.6 0.9 collective-permute-done.23
  205.4 3.7 %collective-permute-done.24 = f32[16,512]{1,0:T(8,128)S(1)} collective-permute-done((f32[16,512]{1,0:T(8,128)S(1)}, f32[16,512]{1,0:T(8,128)S(1)}, u32[]{:S(2)}, u32[]{:S(2)}) %collective-permute-start.24) | collective-permute-done | bytes 32800 | tf_op jit(solution)/shard_map/ppermute | solution.py:726
  209.7 1.1 collective-permute-start.26
  210.8 0.8 collective-permute-start.27
  211.6 1.7 collective-permute-start.28
  214.0 5.5 %assemble.1 = (f32[2048,512]{1,0:T(8,128)}, f32[4,8,512]{2,1,0:T(8,128)S(1)}, f32[128,512]{1,0:T(8,128)S(1)}) custom-call(s32[1]{0:T(128)} %bitcast.1.half_ref.first_ref, f32[1088,512]{1,0:T(8,128)S(1)} %pad_maximum_fusion.own_ref.own_g_ref, f32[1088,512]{1,0:T(8,128)S(1)} %collective-permute-done.25.got_ref.got_g_ref, ...), custom_call_target="tpu_custom_call" | custom-call | bytes 18450000 | tf_op jit(solution)/shard_map/assemble/pallas_call | solution.py:603
  220.4 1.2 collective-permute-done.29
  221.7 7.4 %fix.1 = (f32[400,2048]{1,0:T(8,128)}, f32[100,4,512]{2,1,0:T(4,128)}, f32[4,512]{1,0:T(4,128)}, f32[4,512]{1,0:T(4,128)}, f32[4,512]{1,0:T(4,128)}, /*index=5*/...) custom-call(s32[16,128]{1,0:T(8,128)S(1)} %bitcast.25, ...), custom_call_target="tpu_custom_call" | custom-call | bytes 29520000 | tf_op jit(solution)/shard_map/fix/pallas_call | solution.py:710
  (90 shorter events, 7.1 us)
Async XLA Ops:
  5.6 18.3 %all-to-all-start = ((f32[32,1,2560]{2,1,0:T(1,128)}), f32[32,1,2560]{2,1,0:T(1,128)S(1)}, u32[]{:S(2)}, u32[]{:S(2)}) async-start(f32[32,1,2560]{2,1,0:T(1,128)} %get-tuple-element.122), calls=%async_computation | async-start | bytes 655360 | tf_op jit(solution)/shard_map/all_to_all | solution.py:730
  12.9 9.9 %copy-start.13 = (f32[2048]{0:T(1024)S(1)}, f32[2048]{0:T(1024)}, u32[]{:S(2)}) copy-start(f32[2048]{0:T(1024)} %param.21) | copy-start | bytes 24580
  12.9 11.0 %copy-start = (s32[2048]{0:T(1024)S(1)}, s32[2048]{0:T(1024)}, u32[]{:S(2)}) copy-start(s32[2048]{0:T(1024)} %param.16) | copy-start | bytes 24580
  13.0 11.0 %copy-start.2 = (f32[4,512]{1,0:T(4,128)S(1)}, f32[4,512]{1,0:T(4,128)}, u32[]{:S(2)}) copy-start(f32[4,512]{1,0:T(4,128)} %gain_ref.3) | copy-start | bytes 24580
  13.0 11.0 %copy-start.3 = (f32[4,512]{1,0:T(4,128)S(1)}, f32[4,512]{1,0:T(4,128)}, u32[]{:S(2)}) copy-start(f32[4,512]{1,0:T(4,128)} %slope_ref.3) | copy-start | bytes 24580
  13.0 11.0 %copy-start.4 = (f32[4,512]{1,0:T(4,128)S(1)}, f32[4,512]{1,0:T(4,128)}, u32[]{:S(2)}) copy-start(f32[4,512]{1,0:T(4,128)} %shift_ref.1) | copy-start | bytes 24580
  22.9 42.7 %copy-start.1 = (f32[512,47]{0,1:T(8,128)S(1)}, f32[512,47]{0,1:T(8,128)}, u32[]{:S(2)}) copy-start(f32[512,47]{0,1:T(8,128)} %param.26) | copy-start | bytes 288772
  22.9 42.7 %copy-start.5 = (s32[2048]{0:T(1024)S(1)}, s32[2048]{0:T(1024)}, u32[]{:S(2)}) copy-start(s32[2048]{0:T(1024)} %param.15) | copy-start | bytes 24580
  22.9 42.7 %copy-start.6 = (f32[512]{0:T(512)S(1)}, f32[512]{0:T(512)}, u32[]{:S(2)}) copy-start(f32[512]{0:T(512)} %param.23) | copy-start | bytes 6148
  22.9 42.7 %copy-start.7 = (f32[512]{0:T(512)S(1)}, f32[512]{0:T(512)}, u32[]{:S(2)}) copy-start(f32[512]{0:T(512)} %param.24) | copy-start | bytes 6148
  22.9 42.7 %copy-start.8 = (f32[512]{0:T(512)S(1)}, f32[512]{0:T(512)}, u32[]{:S(2)}) copy-start(f32[512]{0:T(512)} %param.25) | copy-start | bytes 6148
  22.9 42.7 %copy-start.9 = (f32[47]{0:T(128)S(1)}, f32[47]{0:T(128)}, u32[]{:S(2)}) copy-start(f32[47]{0:T(128)} %param.27) | copy-start | bytes 568
  74.8 11.0 %all-to-all-start.2 = ((f32[32,2,512]{2,1,0:T(2,128)}), f32[32,2,512]{2,1,0:T(2,128)S(1)}, u32[]{:S(2)}, u32[]{:S(2)}) async-start(f32[32,2,512]{2,1,0:T(2,128)} %get-tuple-element.127), calls=%async_computation.2 | async-start | bytes 262144 | tf_op jit(solution)/shard_map/all_to_all | solution.py:730
  98.5 9.6 %collective-permute-start = (f32[1088,512]{1,0:T(8,128)}, f32[1088,512]{1,0:T(8,128)}, u32[]{:S(2)}, u32[]{:S(2)}) collective-permute-start(f32[1088,512]{1,0:T(8,128)} %get-tuple-element.133), channel_id=1, source_target_pairs={{0,4},{4,0},{8,12},{12,8},{16,20},{20,16},{24,28},{28,24},{1,5},{5... | collective-permute-start | bytes 6684680 | tf_op jit(solution)/shard_map/ppermute | solution.py:726
  110.5 15.2 %collective-permute-start.1 = (f32[272,512]{1,0:T(8,128)}, f32[272,512]{1,0:T(8,128)S(1)}, u32[]{:S(2)}, u32[]{:S(2)}) collective-permute-start(f32[272,512]{1,0:T(8,128)} %get-tuple-element.232), channel_id=1, source_target_pairs={{0,8},{4,12},{8,0},{12,4},{16,24},{20,28},{24,16},{28,20},{1,9},{5... | collective-permute-start | bytes 1671176 | tf_op jit(solution)/shard_map/ppermute | solution.py:726
  111.3 15.0 %collective-permute-start.2 = (f32[272,512]{1,0:T(8,128)}, f32[272,512]{1,0:T(8,128)}, u32[]{:S(2)}, u32[]{:S(2)}) collective-permute-start(f32[272,512]{1,0:T(8,128)} %get-tuple-element.231), channel_id=1, source_target_pairs={{0,16},{4,20},{8,24},{12,28},{16,0},{20,4},{24,8},{28,12},{1,17},{... | collective-permute-start | bytes 1671176 | tf_op jit(solution)/shard_map/ppermute | solution.py:726
  125.7 0.8 copy-start.12
  128.3 1.2 copy-start.10
  128.4 13.4 %collective-permute-start.4 = (f32[136,512]{1,0:T(8,128)S(1)}, f32[136,512]{1,0:T(8,128)S(1)}, u32[]{:S(2)}, u32[]{:S(2)}) collective-permute-start(f32[136,512]{1,0:T(8,128)S(1)} %constant_dynamic-slice_fusion.8), channel_id=1, source_target_pairs={{0,8},{4,12},{8,0},{12,4},{16,24},{20,28},{24,16},{28,20},{1,9},{5... | collective-permute-start | bytes 835592 | tf_op jit(solution)/shard_map/ppermute | solution.py:726
  129.5 12.3 %collective-permute-start.3 = (f32[136,512]{1,0:T(8,128)S(1)}, f32[136,512]{1,0:T(8,128)S(1)}, u32[]{:S(2)}, u32[]{:S(2)}) collective-permute-start(f32[136,512]{1,0:T(8,128)S(1)} %constant_dynamic-slice_fusion.9), channel_id=1, source_target_pairs={{0,16},{4,20},{8,24},{12,28},{16,0},{20,4},{24,8},{28,12},{1,17},{... | collective-permute-start | bytes 835592 | tf_op jit(solution)/shard_map/ppermute | solution.py:726
  130.4 11.4 %copy-start.11 = (f32[272,512]{1,0:T(8,128)S(1)}, f32[272,512]{1,0:T(8,128)}, u32[]{:S(2)}) copy-start(f32[272,512]{1,0:T(8,128)} %copy-done.10) | copy-start | bytes 1671172
  142.2 15.7 %collective-permute-start.5 = (f32[68,512]{1,0:T(8,128)S(1)}, f32[68,512]{1,0:T(8,128)S(1)}, u32[]{:S(2)}, u32[]{:S(2)}) collective-permute-start(f32[68,512]{1,0:T(8,128)S(1)} %get-tuple-element.237), channel_id=1, source_target_pairs={{0,1},{1,0},{2,3},{3,2},{4,5},{5,4},{6,7},{7,6},{8,9},{9,8},{10,11... | collective-permute-start | bytes 417800 | tf_op jit(solution)/shard_map/ppermute | solution.py:726
  142.2 15.6 %collective-permute-start.6 = (f32[68,512]{1,0:T(8,128)S(1)}, f32[68,512]{1,0:T(8,128)S(1)}, u32[]{:S(2)}, u32[]{:S(2)}) collective-permute-start(f32[68,512]{1,0:T(8,128)S(1)} %get-tuple-element.238), channel_id=1, source_target_pairs={{0,2},{1,3},{2,0},{3,1},{4,6},{5,7},{6,4},{7,5},{8,10},{9,11},{10,... | collective-permute-start | bytes 417800 | tf_op jit(solution)/shard_map/ppermute | solution.py:726
  143.9 14.0 %collective-permute-start.7 = (f32[68,512]{1,0:T(8,128)S(1)}, f32[68,512]{1,0:T(8,128)S(1)}, u32[]{:S(2)}, u32[]{:S(2)}) collective-permute-start(f32[68,512]{1,0:T(8,128)S(1)} %get-tuple-element.235), channel_id=1, source_target_pairs={{0,3},{1,2},{2,1},{3,0},{4,7},{5,6},{6,5},{7,4},{8,11},{9,10},{10,... | collective-permute-start | bytes 417800 | tf_op jit(solution)/shard_map/ppermute | solution.py:726
  157.9 15.8 %collective-permute-start.10 = (f32[68,512]{1,0:T(8,128)S(1)}, f32[68,512]{1,0:T(8,128)S(1)}, u32[]{:S(2)}, u32[]{:S(2)}) collective-permute-start(f32[68,512]{1,0:T(8,128)S(1)} %add_add_fusion.2), channel_id=1, source_target_pairs={{0,3},{1,2},{2,1},{3,0},{4,7},{5,6},{6,5},{7,4},{8,11},{9,10},{10,... | collective-permute-start | bytes 417800 | tf_op jit(solution)/shard_map/ppermute | solution.py:726
  159.1 14.6 %collective-permute-start.8 = (f32[68,512]{1,0:T(8,128)S(1)}, f32[68,512]{1,0:T(8,128)S(1)}, u32[]{:S(2)}, u32[]{:S(2)}) collective-permute-start(f32[68,512]{1,0:T(8,128)S(1)} %add_add_fusion.2), channel_id=1, source_target_pairs={{0,1},{1,0},{2,3},{3,2},{4,5},{5,4},{6,7},{7,6},{8,9},{9,8},{10,11... | collective-permute-start | bytes 417800 | tf_op jit(solution)/shard_map/ppermute | solution.py:726
  159.1 14.7 %collective-permute-start.9 = (f32[68,512]{1,0:T(8,128)S(1)}, f32[68,512]{1,0:T(8,128)S(1)}, u32[]{:S(2)}, u32[]{:S(2)}) collective-permute-start(f32[68,512]{1,0:T(8,128)S(1)} %add_add_fusion.2), channel_id=1, source_target_pairs={{0,2},{1,3},{2,0},{3,1},{4,6},{5,7},{6,4},{7,5},{8,10},{9,11},{10,... | collective-permute-start | bytes 417800 | tf_op jit(solution)/shard_map/ppermute | solution.py:726
  173.9 2.6 %collective-permute-start.13 = (f32[256,512]{1,0:T(8,128)S(1)}, f32[256,512]{1,0:T(8,128)S(1)}, u32[]{:S(2)}, u32[]{:S(2)}) collective-permute-start(f32[256,512]{1,0:T(8,128)S(1)} %constant_dynamic-slice_fusion.5), channel_id=1, source_target_pairs={{0,4},{4,0},{8,12},{12,8},{16,20},{20,16},{24,28},{28,24},{1,5},{5... | collective-permute-start | bytes 1572872 | tf_op jit(solution)/shard_map/ppermute | solution.py:726
  174.2 9.5 %collective-permute-start.11 = (f32[136,512]{1,0:T(8,128)S(1)}, f32[136,512]{1,0:T(8,128)S(1)}, u32[]{:S(2)}, u32[]{:S(2)}) collective-permute-start(f32[136,512]{1,0:T(8,128)S(1)} %get-tuple-element.189), channel_id=1, source_target_pairs={{0,16},{4,20},{8,24},{12,28},{16,0},{20,4},{24,8},{28,12},{1,17},{... | collective-permute-start | bytes 835592 | tf_op jit(solution)/shard_map/ppermute | solution.py:726
  175.5 9.5 %collective-permute-start.12 = (f32[136,512]{1,0:T(8,128)S(1)}, f32[136,512]{1,0:T(8,128)S(1)}, u32[]{:S(2)}, u32[]{:S(2)}) collective-permute-start(f32[136,512]{1,0:T(8,128)S(1)} %get-tuple-element.191), channel_id=1, source_target_pairs={{0,8},{4,12},{8,0},{12,4},{16,24},{20,28},{24,16},{28,20},{1,9},{5... | collective-permute-start | bytes 835592 | tf_op jit(solution)/shard_map/ppermute | solution.py:726
  176.6 11.2 %collective-permute-start.14 = (f32[64,512]{1,0:T(8,128)S(1)}, f32[64,512]{1,0:T(8,128)S(1)}, u32[]{:S(2)}, u32[]{:S(2)}) collective-permute-start(f32[64,512]{1,0:T(8,128)S(1)} %get-tuple-element.241), channel_id=1, source_target_pairs={{0,8},{4,12},{8,0},{12,4},{16,24},{20,28},{24,16},{28,20},{1,9},{5... | collective-permute-start | bytes 393224 | tf_op jit(solution)/shard_map/ppermute | solution.py:726
  177.7 10.1 %collective-permute-start.15 = (f32[64,512]{1,0:T(8,128)S(1)}, f32[64,512]{1,0:T(8,128)S(1)}, u32[]{:S(2)}, u32[]{:S(2)}) collective-permute-start(f32[64,512]{1,0:T(8,128)S(1)} %get-tuple-element.240), channel_id=1, source_target_pairs={{0,16},{4,20},{8,24},{12,28},{16,0},{20,4},{24,8},{28,12},{1,17},{... | collective-permute-start | bytes 393224 | tf_op jit(solution)/shard_map/ppermute | solution.py:726
  178.5 11.6 %collective-permute-start.16 = (f32[64,512]{1,0:T(8,128)S(1)}, f32[64,512]{1,0:T(8,128)S(1)}, u32[]{:S(2)}, u32[]{:S(2)}) collective-permute-start(f32[64,512]{1,0:T(8,128)S(1)} %get-tuple-element.239), channel_id=1, source_target_pairs={{0,24},{4,28},{8,16},{12,20},{16,8},{20,12},{24,0},{28,4},{1,25},{... | collective-permute-start | bytes 393224 | tf_op jit(solution)/shard_map/ppermute | solution.py:726
  190.1 19.0 %collective-permute-start.18 = (f32[272,512]{1,0:T(8,128)S(1)}, f32[272,512]{1,0:T(8,128)S(1)}, u32[]{:S(2)}, u32[]{:S(2)}) collective-permute-start(f32[272,512]{1,0:T(8,128)S(1)} %maximum_select_fusion.5), channel_id=1, source_target_pairs={{0,16},{4,20},{8,24},{12,28},{16,0},{20,4},{24,8},{28,12},{1,17},{... | collective-permute-start | bytes 1671176 | tf_op jit(solution)/shard_map/ppermute | solution.py:726
  191.5 17.6 %collective-permute-start.17 = (f32[272,512]{1,0:T(8,128)S(1)}, f32[272,512]{1,0:T(8,128)S(1)}, u32[]{:S(2)}, u32[]{:S(2)}) collective-permute-start(f32[272,512]{1,0:T(8,128)S(1)} %maximum_select_fusion.4), channel_id=1, source_target_pairs={{0,8},{4,12},{8,0},{12,4},{16,24},{20,28},{24,16},{28,20},{1,9},{5... | collective-permute-start | bytes 1671176 | tf_op jit(solution)/shard_map/ppermute | solution.py:726
  192.6 4.5 %collective-permute-start.19 = (f32[16,512]{1,0:T(8,128)S(1)}, f32[16,512]{1,0:T(8,128)S(1)}, u32[]{:S(2)}, u32[]{:S(2)}) collective-permute-start(f32[16,512]{1,0:T(8,128)S(1)} %get-tuple-element.243), channel_id=1, source_target_pairs={{0,1},{1,0},{2,3},{3,2},{4,5},{5,4},{6,7},{7,6},{8,9},{9,8},{10,11... | collective-permute-start | bytes 98312 | tf_op jit(solution)/shard_map/ppermute | solution.py:726
  192.7 5.1 %collective-permute-start.20 = (f32[16,512]{1,0:T(8,128)S(1)}, f32[16,512]{1,0:T(8,128)S(1)}, u32[]{:S(2)}, u32[]{:S(2)}) collective-permute-start(f32[16,512]{1,0:T(8,128)S(1)} %get-tuple-element.245), channel_id=1, source_target_pairs={{0,2},{1,3},{2,0},{3,1},{4,6},{5,7},{6,4},{7,5},{8,10},{9,11},{10,... | collective-permute-start | bytes 98312 | tf_op jit(solution)/shard_map/ppermute | solution.py:726
  194.4 5.7 %collective-permute-start.21 = (f32[16,512]{1,0:T(8,128)S(1)}, f32[16,512]{1,0:T(8,128)S(1)}, u32[]{:S(2)}, u32[]{:S(2)}) collective-permute-start(f32[16,512]{1,0:T(8,128)S(1)} %get-tuple-element.244), channel_id=1, source_target_pairs={{0,3},{1,2},{2,1},{3,0},{4,7},{5,6},{6,5},{7,4},{8,11},{9,10},{10,... | collective-permute-start | bytes 98312 | tf_op jit(solution)/shard_map/ppermute | solution.py:726
  200.1 4.5 %collective-permute-start.22 = (f32[16,512]{1,0:T(8,128)S(1)}, f32[16,512]{1,0:T(8,128)S(1)}, u32[]{:S(2)}, u32[]{:S(2)}) collective-permute-start(f32[16,512]{1,0:T(8,128)S(1)} %add_add_fusion.4), channel_id=1, source_target_pairs={{0,1},{1,0},{2,3},{3,2},{4,5},{5,4},{6,7},{7,6},{8,9},{9,8},{10,11... | collective-permute-start | bytes 98312 | tf_op jit(solution)/shard_map/ppermute | solution.py:726
  200.2 5.2 %collective-permute-start.23 = (f32[16,512]{1,0:T(8,128)S(1)}, f32[16,512]{1,0:T(8,128)S(1)}, u32[]{:S(2)}, u32[]{:S(2)}) collective-permute-start(f32[16,512]{1,0:T(8,128)S(1)} %add_add_fusion.4), channel_id=1, source_target_pairs={{0,2},{1,3},{2,0},{3,1},{4,6},{5,7},{6,4},{7,5},{8,10},{9,11},{10,... | collective-permute-start | bytes 98312 | tf_op jit(solution)/shard_map/ppermute | solution.py:726
  203.4 5.7 %collective-permute-start.24 = (f32[16,512]{1,0:T(8,128)S(1)}, f32[16,512]{1,0:T(8,128)S(1)}, u32[]{:S(2)}, u32[]{:S(2)}) collective-permute-start(f32[16,512]{1,0:T(8,128)S(1)} %add_add_fusion.4), channel_id=1, source_target_pairs={{0,3},{1,2},{2,1},{3,0},{4,7},{5,6},{6,5},{7,4},{8,11},{9,10},{10,... | collective-permute-start | bytes 98312 | tf_op jit(solution)/shard_map/ppermute | solution.py:726
  209.5 4.4 %collective-permute-start.25 = (f32[1088,512]{1,0:T(8,128)S(1)}, f32[1088,512]{1,0:T(8,128)S(1)}, u32[]{:S(2)}, u32[]{:S(2)}) collective-permute-start(f32[1088,512]{1,0:T(8,128)S(1)} %pad_maximum_fusion.own_ref.own_g_ref), channel_id=1, source_target_pairs={{0,4},{4,0},{8,12},{12,8},{16,20},{20,16},{24,28},{28,24},{1,5},{5... | collective-permute-start | bytes 6684680 | tf_op jit(solution)/shard_map/ppermute | solution.py:726
  209.7 9.8 %collective-permute-start.26 = (f32[64,512]{1,0:T(8,128)S(1)}, f32[64,512]{1,0:T(8,128)S(1)}, u32[]{:S(2)}, u32[]{:S(2)}) collective-permute-start(f32[64,512]{1,0:T(8,128)S(1)} %maximum_select_fusion.11), channel_id=1, source_target_pairs={{0,8},{4,12},{8,0},{12,4},{16,24},{20,28},{24,16},{28,20},{1,9},{5... | collective-permute-start | bytes 393224 | tf_op jit(solution)/shard_map/ppermute | solution.py:726
  210.8 8.7 %collective-permute-start.27 = (f32[64,512]{1,0:T(8,128)S(1)}, f32[64,512]{1,0:T(8,128)S(1)}, u32[]{:S(2)}, u32[]{:S(2)}) collective-permute-start(f32[64,512]{1,0:T(8,128)S(1)} %maximum_select_fusion.11), channel_id=1, source_target_pairs={{0,16},{4,20},{8,24},{12,28},{16,0},{20,4},{24,8},{28,12},{1,17},{... | collective-permute-start | bytes 393224 | tf_op jit(solution)/shard_map/ppermute | solution.py:726
  211.6 7.9 %collective-permute-start.28 = (f32[64,512]{1,0:T(8,128)S(1)}, f32[64,512]{1,0:T(8,128)S(1)}, u32[]{:S(2)}, u32[]{:S(2)}) collective-permute-start(f32[64,512]{1,0:T(8,128)S(1)} %maximum_select_fusion.11), channel_id=1, source_target_pairs={{0,24},{4,28},{8,16},{12,20},{16,8},{20,12},{24,0},{28,4},{1,25},{... | collective-permute-start | bytes 393224 | tf_op jit(solution)/shard_map/ppermute | solution.py:726
  219.6 2.0 collective-permute-start.29
